TPU v7x, 128 devices: a whole 4x4x4 slice. The times are simulated.
128 devices in a mesh: nodes: 32 (over y, z, core), feat: 4 (over x).
Axes of the slice: x: 4, y: 4, z: 4, core: 2. Of those that a mesh axis runs over, the one named last changes fastest.
Arguments:
- features: bfloat16 [131072, 1024], P('nodes', 'feat'), may hold values from -6 to 6
- pair_count: int32 [32, 32], P('nodes'), may hold values from 1 to 2, as said below
- send_blocks: int32 [32, 32, 2], P('nodes'), may hold values from 0 to 31
- tile_src: int32 [1024, 4], P('nodes'), may hold values from 0 to 63, as said below
- tiles: bfloat16 [1024, 4, 128, 128], P('nodes'), may hold values from -0.25 to 0.25
- labels: int32 [131072], P('nodes'), may hold values from 0 to 15
- w_first: bfloat16 [1024, 1024], P('feat'), may hold values from -0.1875 to 0.1875
- b_first: float32 [1024], P('feat'), may hold values from -3 to 3
- w_second: bfloat16 [1024, 16], P('feat'), may hold values from -0.1875 to 0.1875
Outputs:
- grad_first: float32 [1024, 1024], P('feat', 'nodes')
- grad_bias: float32 [1024], P('feat')
- grad_second: float32 [1024, 16], P('feat')
Inputs may be any that keep to these rules, and one draw needn't show every extreme that they name: pair_count[p, p] is 2 for every p. `tile_src`: the 32 rows of one partition name every slot 0 to 63 at least once.
All inputs are finite; a program needn't handle non-finite values.
Results may differ from a plain program's by a relative error of at most 0.015.
The roundings to bfloat16 on the way count: a program that leaves them out, or rounds other values in their place, can miss the bound.
Values may be sent and summed in bfloat16 or wider, within the bound.
No kernel may reach another device: no remote copies, remote signals or barrier semaphores. Data moves between devices by JAX's collectives and lax.ppermute only.
A program may use at most 128 MiB of HBM per device.

v0:
```python
import math

import jax
import jax.numpy as jnp
from jax import lax
from jax.sharding import PartitionSpec as P


def shards(features, pair_count, send_blocks, tile_src, tiles, labels, w_first, b_first, w_second):
    high = lax.Precision.HIGHEST
    rows, width = features.shape
    nblocks, per_block = tile_src.shape
    blk = tiles.shape[2]
    parts = lax.axis_size("nodes")
    slots = send_blocks.shape[2]
    grades = w_second.shape[1]
    hq = w_first.shape[1] // lax.axis_size("feat")
    owner = tile_src // slots
    slot_in = tile_src % slots
    counts = pair_count[0]
    live = slot_in < counts[owner]
    weights = tiles * live[:, :, None, None].astype(jnp.bfloat16)
    table = send_blocks[0]

    def gather_sources(received):
        flat = received.reshape(parts * slots, blk, received.shape[-1])
        return flat[tile_src]

    own_one = features.reshape(nblocks, blk, width)
    arrived = lax.all_to_all(own_one[table], "nodes", split_axis=0, concat_axis=0, tiled=True)
    summed = jnp.einsum(
        "btij,btjf->bif", weights, gather_sources(arrived), preferred_element_type=jnp.float32
    )
    agg_first = (summed + own_one).astype(jnp.bfloat16).reshape(rows, width)
    partial_pre = jnp.dot(agg_first, w_first, preferred_element_type=jnp.float32)
    pre = lax.psum_scatter(partial_pre, "feat", scatter_dimension=1, tiled=True)
    pre = pre + b_first
    hidden = jnp.maximum(pre, 0.0).astype(jnp.bfloat16)
    own_two = hidden.reshape(nblocks, blk, hq)
    arrived_two = lax.all_to_all(own_two[table], "nodes", split_axis=0, concat_axis=0, tiled=True)
    agg_second = (
        jnp.einsum(
            "btij,btjf->bif",
            weights,
            gather_sources(arrived_two),
            preferred_element_type=jnp.float32,
        )
        + own_two
    )
    partial_logits = jnp.dot(
        agg_second.reshape(rows, hq), w_second.astype(jnp.float32), precision=high
    )
    logits = lax.psum(partial_logits, "feat")
    expo = jnp.exp(logits)
    probs = expo / jnp.sum(expo, axis=1, keepdims=True)
    onehot = (labels[:, None] == jnp.arange(grades, dtype=jnp.int32)[None, :]).astype(jnp.float32)
    dlog = (probs - onehot) * (1.0 / math.sqrt(rows * parts))
    dlog_b = dlog.astype(jnp.bfloat16).reshape(nblocks, blk, grades)
    contrib = jnp.einsum("btij,bif->btjf", weights, dlog_b, preferred_element_type=jnp.float32)
    slot_hit = (
        tile_src.reshape(-1)[:, None] == jnp.arange(parts * slots, dtype=jnp.int32)[None, :]
    ).astype(jnp.float32)
    slotsum = lax.dot_general(
        slot_hit,
        contrib.reshape(nblocks * per_block, blk * grades),
        (((0,), (0,)), ((), ())),
        precision=high,
    )
    returned = lax.all_to_all(
        slotsum.reshape(parts, slots, blk, grades).astype(jnp.bfloat16),
        "nodes",
        split_axis=0,
        concat_axis=0,
        tiled=True,
    ).astype(jnp.float32)
    placing = (table.reshape(-1)[None, :] == jnp.arange(nblocks, dtype=jnp.int32)[:, None]).astype(
        jnp.float32
    )
    spread = jnp.dot(placing, returned.reshape(parts * slots, blk * grades), precision=high)
    dproj_b = (dlog + spread.reshape(rows, grades)).astype(jnp.bfloat16)
    grad_second = lax.dot_general(
        hidden, dproj_b, (((0,), (0,)), ((), ())), preferred_element_type=jnp.float32
    )
    dhid = lax.dot_general(
        dproj_b, w_second, (((1,), (1,)), ((), ())), preferred_element_type=jnp.float32
    )
    dpre = jnp.where(pre > 0, dhid, 0.0)
    grad_bias = jnp.sum(dpre, axis=0)
    grad_second, grad_bias = lax.psum((grad_second, grad_bias), "nodes")
    dpre_b = dpre.astype(jnp.bfloat16)
    grad_part = lax.dot_general(
        agg_first,
        lax.all_gather(dpre_b, "feat", axis=1, tiled=True),
        (((0,), (0,)), ((), ())),
        preferred_element_type=jnp.float32,
    )
    grad_first = lax.psum_scatter(
        grad_part.astype(jnp.bfloat16), "nodes", scatter_dimension=1, tiled=True
    ).astype(jnp.float32)
    return (grad_first, grad_bias, grad_second)


def solution(mesh):
    placed = (
        P("nodes", "feat"),
        P("nodes", None),
        P("nodes", None, None),
        P("nodes", None),
        P("nodes", None, None, None),
        P("nodes"),
        P("feat", None),
        P("feat"),
        P("feat", None),
    )
    return jax.shard_map(
        shards,
        mesh=mesh,
        in_specs=placed,
        out_specs=(P("feat", "nodes"), P("feat"), P("feat", None)),
        check_vma=False,
    )
```

profile of v0, /device:TPU:1, one launch (start us, length us, event | category | flops | bytes accessed | tf_op | source)
XLA Modules:
  0.0 646.0 jit_solution(7798856695492343430)
XLA Ops:
  7.2 0.0 copy-start
  7.2 0.7 compare_select_fusion.1
  7.9 0.1 copy.59
  8.0 0.1 reshape.111
  8.1 4.4 gather_fusion.1
  12.5 9.8 %all-to-all-start = ((bf16[32,2,128,256]{3,2,1,0:T(8,128)(2,1)}), bf16[32,2,128,256]{3,2,1,0:T(8,128)(2,1)}, u32[]{:S(2)}, u32[]{:S(2)}) async-start(bf16[32,2,128,256]{3,2,1,0:T(8,128)(2,1)} %bitcast.63), calls=%async_computation | async-start | bytes 8388608 | tf_op jit(solution)/shard_map/all_to_all | solution.py:30
  22.3 0.0 reduce-scatter.3.cloned.1.call-start
  22.4 0.1 copy.60
  22.5 0.1 reshape.119
  22.6 0.1 copy.56
  22.7 0.1 reshape.103
  22.8 0.0 copy-done.2
  22.8 1.2 gather_fusion
  24.0 0.1 reshape.102
  24.1 0.1 copy.57
  24.2 0.1 copy.58
  24.3 50.2 %all-to-all-done = bf16[32,2,128,256]{3,2,1,0:T(8,128)(2,1)} async-done(((bf16[32,2,128,256]{3,2,1,0:T(8,128)(2,1)}), bf16[32,2,128,256]{3,2,1,0:T(8,128)(2,1)}, u32[]{:S(2)}, u32[]{:S(2)}) %all-to-all-start) | async-done | bytes 4194336 | tf_op jit(solution)/shard_map/all_to_all | solution.py:30
  74.5 8.9 %gather_fusion.2 = bf16[128,128,256]{2,1,0:T(8,128)(2,1)} fusion(bf16[64,128,256]{2,1,0:T(8,128)(2,1)} %bitcast.4, s32[1024]{0:T(1024)S(1)} %pad_clamp_fusion), kind=kCustom, calls=%fused_computation.2 | custom fusion | bytes 16777728 | tf_op jit(solution)/shard_map/gather | solution.py:27
  83.4 6.5 fusion
  89.9 1.3 copy-done.5
  91.2 8.1 %fusion.27 = f32[4096,1024]{1,0:T(8,128)} fusion(bf16[4096,256]{1,0:T(8,128)(2,1)S(1)} %bitcast.70, bf16[256,1024]{1,0:T(8,128)(2,1)S(1)} %copy-done), kind=kOutput, calls=%fused_computation.54 | convolution fusion | flops 2147483648 | bytes 19398656 | tf_op jit(solution)/shard_map/dot_general | solution.py:35
  99.3 0.0 reduce-scatter.3.cloned.1.call-update
  99.3 0.0 all-reduce.3.cloned.1.call-start
  99.4 148.8 %reduce-scatter.3.cloned.1.call-done = f32[4096,256]{1,0:T(8,128)} async-done(((f32[4096,1024]{1,0:T(8,128)}), f32[4096,256]{1,0:T(8,128)}) %reduce-scatter.3.cloned.1.call-update) | async-done | bytes 4194320 | tf_op jit(solution)/shard_map/reduce_scatter | solution.py:36
  248.1 2.6 maximum_convert_fusion
  250.7 2.7 gather_fusion.3
  253.5 58.4 %all_to_all.15 = bf16[32,2,128,256]{3,2,1,0:T(8,128)(2,1)} all-to-all(bf16[32,2,128,256]{3,2,1,0:T(8,128)(2,1)} %bitcast.64), channel_id=1, replica_groups=mesh['nodes'=32,'feat'=4] {'nodes'}, dimensions={0} | all-to-all | bytes 8388608 | tf_op jit(solution)/shard_map/all_to_all | solution.py:40
  311.8 8.8 %gather_fusion.4 = bf16[128,128,256]{2,1,0:T(8,128)(2,1)} fusion(bf16[64,128,256]{2,1,0:T(8,128)(2,1)} %bitcast.61, s32[1024]{0:T(1024)S(1)} %pad_clamp_fusion), kind=kCustom, calls=%fused_computation.4 | custom fusion | bytes 16777728 | tf_op jit(solution)/shard_map/gather | solution.py:27
  320.6 6.5 %bitcast_add_fusion = f32[32,128,256]{2,1,0:T(8,128)S(1)} fusion(bf16[32,128,256]{2,1,0:T(8,128)(2,1)S(1)} %bitcast.59, bf16[32,4,128,256]{3,2,1,0:T(8,128)(2,1)} %bitcast.60, bf16[32,4,128,128]{3,2,1,0:T(8,128)(2,1)} %param.13, bf16[32,4]{1,0:T(8,128)(2,1)S(1)} %copy.58), kind=kOutput, calls=%fused_computation.6 | convolution fusion | flops 1077936128 | bytes 18874624 | tf_op jit(solution)/shard_map/btij,btjf->bif/dot_general | solution.py:42
  327.1 0.0 copy-start.6
  327.1 2.7 fusion.28
  329.8 0.0 all-reduce.3.cloned.1.call-update
  329.8 0.1 copy.62
  329.9 0.1 eq.68
  330.0 35.4 %all-reduce.3.cloned.1.call-done = f32[4096,16]{0,1:T(8,128)} async-done(((f32[4096,16]{0,1:T(8,128)}), f32[4096,16]{0,1:T(8,128)}) %all-reduce.3.cloned.1.call-update) | async-done | bytes 262160 | tf_op jit(solution)/shard_map/psum | solution.py:53
  365.5 1.0 exponential_reduce_fusion
  366.5 0.0 copy-done.6
  366.5 1.0 convert_bitcast_fusion
  367.5 6.9 %fusion.1 = f32[32,4,128,16]{3,2,1,0:T(8,128)} fusion(bf16[32,4,128,128]{3,2,1,0:T(8,128)(2,1)} %param.13, bf16[32,4]{1,0:T(8,128)(2,1)S(1)} %copy.58, bf16[32,128,16,1]{1,0,2,3:T(8,128)(2,1)S(1)} %bitcast.72), kind=kOutput, calls=%fused_computation.10 | convolution fusion | flops 69206016 | bytes 5374208 | tf_op jit(solution)/shard_map/btij,bif->btjf/dot_general | solution.py:59
  374.4 8.7 %reshape.98 = f32[128,2048]{1,0:T(8,128)} reshape(f32[32,4,128,16]{3,2,1,0:T(8,128)} %fusion.1) | data formatting | bytes 2097152 | tf_op jit(solution)/shard_map/reshape | solution.py:65
  383.1 2.5 copy.65
  385.7 2.2 convolution_convert_fusion.1
  387.9 0.8 copy.67
  388.7 9.8 %all-to-all-start.2 = ((bf16[32,2,128,16]{2,3,1,0:T(8,128)(2,1)}), bf16[32,2,128,16]{2,3,1,0:T(8,128)(2,1)S(1)}, u32[]{:S(2)}, u32[]{:S(2)}) async-start(bf16[32,2,128,16]{2,3,1,0:T(8,128)(2,1)} %copy.67), calls=%async_computation.3 | async-start | bytes 524288 | tf_op jit(solution)/shard_map/all_to_all | solution.py:69
  398.5 0.3 all-gather.2.cloned.1.call-start
  398.8 0.1 copy.61
  398.9 0.1 eq.64
  399.0 8.5 %all-to-all-done.2 = bf16[32,2,128,16]{2,3,1,0:T(8,128)(2,1)S(1)} async-done(((bf16[32,2,128,16]{2,3,1,0:T(8,128)(2,1)}), bf16[32,2,128,16]{2,3,1,0:T(8,128)(2,1)S(1)}, u32[]{:S(2)}, u32[]{:S(2)}) %all-to-all-start.2) | async-done | bytes 262176 | tf_op jit(solution)/shard_map/all_to_all | solution.py:69
  407.5 1.7 copy.68
  409.3 4.7 reshape.99
  414.0 0.2 fusion.21
  414.2 2.1 reshape.100
  416.2 2.2 copy.69
  418.4 0.0 copy-done.4
  418.4 0.1 add_convert_fusion
  418.5 4.5 fusion.26
  423.0 0.0 all-gather.2.cloned.1.call-update
  423.0 0.0 reduce-scatter.5.cloned.1.call-start
  423.0 83.0 %all-gather.2.cloned.1.call-done = bf16[4096,1024]{1,0:T(8,128)(2,1)} async-done(((bf16[4096,256]{1,0:T(8,128)(2,1)}), bf16[4096,1024]{1,0:T(8,128)(2,1)}) %all-gather.2.cloned.1.call-update) | async-done | bytes 8388624 | tf_op jit(solution)/shard_map/all_gather | solution.py:93
  506.1 8.2 %convolution_convert_fusion = bf16[256,1024]{0,1:T(8,128)(2,1)} fusion(bf16[4096,256]{1,0:T(8,128)(2,1)} %bitcast.71, bf16[4096,1024]{1,0:T(8,128)(2,1)} %all-gather.2.cloned.1.call-done), kind=kOutput, calls=%fused_computation.19 | convolution fusion | flops 2147745792 | bytes 11010048 | tf_op jit(solution)/shard_map/dot_general | solution.py:91
  514.3 0.0 reduce-scatter.5.cloned.1.call-update
  514.4 0.4 fusion.29
  514.8 123.4 %all-reduce = (f32[256]{0:T(256)}, f32[256,16]{0,1:T(8,128)}) all-reduce(f32[256]{0:T(256)S(1)} %get-tuple-element.5, f32[256,16]{0,1:T(8,128)S(1)} %fusion.29), channel_id=1, replica_groups=mesh['nodes'=32,'feat'=4] {'nodes'}, use_global_device_ids=true, to_apply=%region_5.6 | all-reduce | flops 4352 | bytes 34816 | tf_op jit(solution)/shard_map/psum | solution.py:89
  638.2 1.3 convert_element_type.52
  (24 shorter events, 0.1 us)
Async XLA Ops:
  7.2 84.0 %copy-start = (bf16[256,1024]{1,0:T(8,128)(2,1)S(1)}, bf16[256,1024]{1,0:T(8,128)(2,1)}, u32[]{:S(2)}) copy-start(bf16[256,1024]{1,0:T(8,128)(2,1)} %param.15) | copy-start | bytes 1572868
  12.5 9.9 %copy-start.8 = (s32[32,4]{0,1:T(4,128)S(1)}, s32[32,4]{0,1:T(4,128)}, u32[]{:S(2)}) copy-start(s32[32,4]{0,1:T(4,128)} %param.12) | copy-start | bytes 1540
  12.5 10.3 %copy-start.2 = (s32[1,32]{1,0:T(1,128)S(1)}, s32[1,32]{1,0:T(1,128)}, u32[]{:S(2)}) copy-start(s32[1,32]{1,0:T(1,128)} %param.10) | copy-start | bytes 388
  12.5 62.0 %all-to-all-start = ((bf16[32,2,128,256]{3,2,1,0:T(8,128)(2,1)}), bf16[32,2,128,256]{3,2,1,0:T(8,128)(2,1)}, u32[]{:S(2)}, u32[]{:S(2)}) async-start(bf16[32,2,128,256]{3,2,1,0:T(8,128)(2,1)} %bitcast.63), calls=%async_computation | async-start | bytes 8388608 | tf_op jit(solution)/shard_map/all_to_all | solution.py:30
  22.3 225.8 %reduce-scatter.3.cloned.1.call-start = ((), (), s32[]{:S(2)}) async-start(), calls=%async_computation.5 | async-start | bytes 20971520 | tf_op jit(solution)/shard_map/reduce_scatter | solution.py:36
  74.5 8.9 %copy-start.3 = (bf16[4096,256]{1,0:T(8,128)(2,1)S(1)}, bf16[4096,256]{1,0:T(8,128)(2,1)}, u32[]{:S(2)}) copy-start(bf16[4096,256]{1,0:T(8,128)(2,1)} %param.9) | copy-start | bytes 6291460
  89.9 1.3 copy-start.5
  99.3 148.8 %copy-start.10 = (f32[256]{0:T(256)S(1)}, f32[256]{0:T(256)}, u32[]{:S(2)}) copy-start(f32[256]{0:T(256)} %param.16) | copy-start | bytes 3076
  99.3 266.1 %all-reduce.3.cloned.1.call-start = ((), (), s32[]{:S(2)}) async-start(), calls=%async_computation.6 | async-start | bytes 524288 | tf_op jit(solution)/shard_map/psum | solution.py:53
  320.6 6.5 %copy-start.7 = (bf16[256,16]{0,1:T(8,128)(2,1)S(1)}, bf16[256,16]{0,1:T(8,128)(2,1)}, u32[]{:S(2)}) copy-start(bf16[256,16]{0,1:T(8,128)(2,1)} %param.17) | copy-start | bytes 24580
  327.1 39.4 %copy-start.6 = (s32[4096]{0:T(1024)S(1)}, s32[4096]{0:T(1024)}, u32[]{:S(2)}) copy-start(s32[4096]{0:T(1024)} %param.14) | copy-start | bytes 49156
  383.1 15.7 %copy-start.9 = (s32[1,32,2]{1,2,0:T(2,128)S(1)}, s32[1,32,2]{1,2,0:T(2,128)}, u32[]{:S(2)}) copy-start(s32[1,32,2]{1,2,0:T(2,128)} %param.11) | copy-start | bytes 772
  388.7 18.8 %all-to-all-start.2 = ((bf16[32,2,128,16]{2,3,1,0:T(8,128)(2,1)}), bf16[32,2,128,16]{2,3,1,0:T(8,128)(2,1)S(1)}, u32[]{:S(2)}, u32[]{:S(2)}) async-start(bf16[32,2,128,16]{2,3,1,0:T(8,128)(2,1)} %copy.67), calls=%async_computation.3 | async-start | bytes 524288 | tf_op jit(solution)/shard_map/all_to_all | solution.py:69
  398.5 107.6 %all-gather.2.cloned.1.call-start = ((), (), s32[]{:S(2)}) async-start(), calls=%async_computation.7 | async-start | bytes 10485760 | tf_op jit(solution)/shard_map/all_gather | solution.py:93
  409.3 9.1 %copy-start.4 = (f32[4096,16]{0,1:T(8,128)S(1)}, f32[4096,16]{0,1:T(8,128)}, u32[]{:S(2)}) copy-start(f32[4096,16]{0,1:T(8,128)} %all-reduce.3.cloned.1.call-done) | copy-start | bytes 786436
  423.0 215.2 %reduce-scatter.5.cloned.1.call-start = ((), (), s32[]{:S(2)}) async-start(), calls=%async_computation.8 | async-start | bytes 540672 | tf_op jit(solution)/shard_map/reduce_scatter | solution.py:97
  506.1 133.4 %copy-start.1 = (bf16[256,1024]{1,0:T(8,128)(2,1)S(1)}, bf16[256,1024]{1,0:T(8,128)(2,1)}, u32[]{:S(2)}) copy-start(bf16[256,1024]{1,0:T(8,128)(2,1)} %param.15) | copy-start | bytes 1572868
Sparse Core Ops, SparseCore 0:
  99.4 148.6 reduce-scatter.2
  330.0 35.4 all-reduce.2
  423.1 82.9 all-gather.1
  514.5 77.0 reduce-scatter.4
where the time goes:
time: 651 us; the launch traced here: 646 us
  waiting for transfers between devices  326 us (50%)
  blocking collectives  182 us (28%)
  local copies, waits for them, and re-layouts  51.3 us (8%)
  matrix products  46.1 us (7%)
  starting transfers between devices  20 us (3%)
  between operations  14 us (2%)
  other arithmetic  6.85 us (1%)
    reduce_scatter x1, waiting for transfers between devices, shards(): pre = lax.psum_scatter(partial_pre, 'feat', scatter_dimension=1, tiled=True)  149 us
    psum x1, blocking collectives, shards(): grad_second, grad_bias = lax.psum((grad_second, grad_bias), 'nodes')  123 us
    all_gather x1, waiting for transfers between devices, shards(): lax.all_gather(dpre_b, 'feat', axis=1, tiled=True)  83 us
    all_to_all x1, blocking collectives, shards(): lax.all_to_all(own_two[table], 'nodes', split_axis=0, concat_axis=0, tile...  58.4 us
    all_to_all x1, waiting for transfers between devices, shards(): lax.all_to_all(own_one[table], 'nodes', split_axis=0, concat_axis=0, tile...  50.2 us
    psum x1, waiting for transfers between devices, shards(): logits = lax.psum(partial_logits, 'feat')  35.4 us
    gather x2, local copies, waits for them, and re-layouts, gather_sources(): return flat[tile_src]  17.7 us
  transfers between devices with their start and end apart: 6, of which 5 were waited for; matrix products, arithmetic and copies ran while one was open for 0% of the time, Pallas kernels for 0%

commit v1 on v0

v1 whole, which is shorter than its diff:
```python
import functools
import math

import jax
import jax.numpy as jnp
from jax import lax
from jax.experimental import pallas as pl
from jax.experimental.pallas import tpu as pltpu
from jax.sharding import PartitionSpec as P

F32 = jnp.float32
BF16 = jnp.bfloat16
NT = (((1,), (1,)), ((), ()))
NN = (((1,), (0,)), ((), ()))
BLK = 128
MIB = 1 << 20


def params(mib):
    return pltpu.CompilerParams(vmem_limit_bytes=mib * MIB)


def cost(flops, nbytes):
    return pl.CostEstimate(flops=flops, bytes_accessed=nbytes, transcendentals=0)


def dot(a, b, dims):
    return lax.dot_general(a, b, dims, preferred_element_type=F32)


def pick_kernel(chunk, table, features, out, sems):
    slots = out.shape[0]

    def copy(k):
        rows = pl.ds(pl.multiple_of(table[k] * BLK, BLK), BLK)
        return pltpu.make_async_copy(
            features.at[rows, pl.ds(chunk * BLK, BLK)], out.at[k], sems.at[k]
        )

    @pl.loop(0, slots)
    def _(k):
        copy(k).start()

    @pl.loop(0, slots)
    def _(k):
        copy(k).wait()


def pick(features, table, chunk):
    slots = table.shape[0]
    return pl.pallas_call(
        functools.partial(pick_kernel, chunk),
        grid_spec=pltpu.PrefetchScalarGridSpec(
            num_scalar_prefetch=1,
            grid=(),
            in_specs=[pl.BlockSpec(memory_space=pl.ANY)],
            out_specs=pl.BlockSpec(memory_space=pl.ANY),
            scratch_shapes=[pltpu.SemaphoreType.DMA((slots,))],
        ),
        out_shape=jax.ShapeDtypeStruct((slots, BLK, BLK), BF16),
        compiler_params=params(4),
        cost_estimate=cost(0, 4 * MIB),
        name="pick",
    )(table, features)


def agg_kernel(src, counts, me, arrived, tiles, own, o0, o1, o2, o3, buf):
    group, per = tiles.shape[0], tiles.shape[1]
    g = pl.program_id(0)
    first = lax.rem(me[0] + g, pl.num_programs(0)) * group

    for b in range(group):
        rows, weights = [], []
        for t in range(per):
            slot = src[(first + b) * per + t]
            live = lax.rem(slot, 2) < counts[lax.div(slot, 2)]
            rows.append(arrived[slot])
            weights.append(tiles[b, t] * jnp.where(live, 1.0, 0.0).astype(BF16))
        total = dot(jnp.concatenate(weights, 1), jnp.concatenate(rows, 0), NN)
        mine = own[pl.ds(b * BLK, BLK), :].astype(F32)
        buf[pl.ds(b * BLK, BLK), :] = (mine + total).astype(BF16)
    for k, out in enumerate((o0, o1, o2, o3)):

        @pl.when(g == k)
        def _():
            out[...] = buf[...]


def aggregate(src, counts, me, arrived, tiles, features, chunk, nfeat):
    nblocks, per = tiles.shape[:2]
    group = nblocks // nfeat
    piece = jax.ShapeDtypeStruct((group * BLK, BLK), BF16)
    turn = lambda g, m: lax.rem(m[0] + g, nfeat)
    return pl.pallas_call(
        agg_kernel,
        grid_spec=pltpu.PrefetchScalarGridSpec(
            num_scalar_prefetch=3,
            grid=(nfeat,),
            in_specs=[
                pl.BlockSpec(arrived.shape, lambda g, s, c, m: (0, 0, 0)),
                pl.BlockSpec((group, per, BLK, BLK), lambda g, s, c, m: (turn(g, m), 0, 0, 0)),
                pl.BlockSpec((group * BLK, BLK), lambda g, s, c, m: (turn(g, m), chunk)),
            ],
            out_specs=[pl.BlockSpec(piece.shape, lambda g, s, c, m: (0, 0))] * nfeat,
            scratch_shapes=[pltpu.VMEM(piece.shape, BF16)],
        ),
        out_shape=[piece] * nfeat,
        compiler_params=params(20),
        cost_estimate=cost(nblocks * per * 2 * BLK**3, 8 * MIB),
        name="aggregate",
    )(src, counts, me, arrived, tiles, features)


def dense_kernel(nfeat, *refs):
    pieces, rest = refs[: 2 * nfeat], refs[2 * nfeat :]
    weights, (bias, second, hidden, proj) = rest[:nfeat], rest[nfeat:]
    pre = bias[...] + dot(
        weights[0][...], jnp.concatenate([pieces[0][...], pieces[nfeat][...]], 1), NT
    )
    for k in range(1, nfeat):
        pre += dot(
            weights[k][...], jnp.concatenate([pieces[k][...], pieces[nfeat + k][...]], 1), NT
        )
    hid = jnp.maximum(pre, 0.0).astype(BF16)
    hidden[...] = hid
    out = dot(second[...], hid, NN)
    for b in range(proj.shape[0]):
        proj[b] = out[:, b * BLK : (b + 1) * BLK]


def dense(pieces, weights, bias, second):
    nodes, nfeat = pieces[0].shape[0], len(weights)
    hid, width = weights[0].shape
    grades = second.shape[0]
    step = 256
    return pl.pallas_call(
        functools.partial(dense_kernel, nfeat),
        grid=(nodes // step,),
        in_specs=[pl.BlockSpec((step, BLK), lambda g: (g, 0))] * (2 * nfeat)
        + [pl.BlockSpec((hid, width), lambda g: (0, 0))] * nfeat
        + [
            pl.BlockSpec((hid, 1), lambda g: (0, 0)),
            pl.BlockSpec((grades, hid), lambda g: (0, 0)),
        ],
        out_specs=[
            pl.BlockSpec((hid, step), lambda g: (0, g)),
            pl.BlockSpec((step // BLK, grades, BLK), lambda g: (g, 0, 0)),
        ],
        out_shape=[
            jax.ShapeDtypeStruct((hid, nodes), BF16),
            jax.ShapeDtypeStruct((nodes // BLK, grades, BLK), F32),
        ],
        compiler_params=params(28),
        cost_estimate=cost(2 * nodes * hid * width * nfeat, 7 * MIB),
        name="dense",
    )(*pieces, *weights, bias, second)


def spread_kernel(table, me, p0, p1, p2, p3, whole, out):
    nfeat, group = 4, p0.shape[0]
    for k, piece in enumerate((p0, p1, p2, p3)):
        owner = lax.rem(me[0] + nfeat - k, nfeat)
        whole[pl.ds(owner * group, group)] = piece[...]

    @pl.loop(0, out.shape[0], unroll=8)
    def _(k):
        out[k] = whole[table[k]]


def spread(table, me, pieces):
    group, grades, _ = pieces[0].shape
    slots = table.shape[0]
    vmem = pl.BlockSpec(memory_space=pltpu.VMEM)
    return pl.pallas_call(
        spread_kernel,
        grid_spec=pltpu.PrefetchScalarGridSpec(
            num_scalar_prefetch=2,
            grid=(),
            in_specs=[vmem] * 4,
            out_specs=[vmem] * 2,
        ),
        out_shape=[
            jax.ShapeDtypeStruct((group * 4, grades, BLK), F32),
            jax.ShapeDtypeStruct((slots, grades, BLK), F32),
        ],
        compiler_params=params(4),
        cost_estimate=cost(0, MIB),
        name="spread",
    )(table, me, *pieces)


def logits_kernel(scale, src, counts, me, arrived, own, labels, tiles, dlog_out, slots_out, parts, sums):
    group, per = tiles.shape[0], tiles.shape[1]
    nslots, grades, _ = arrived.shape
    mine = dlog_out.shape[0]
    g = pl.program_id(0)

    @pl.when(g == 0)
    def _():
        sums[...] = jnp.zeros_like(sums)

        @pl.loop(0, nslots, unroll=4)
        def _(k):
            x = arrived[k]
            for i in range(3):
                y = x.astype(BF16)
                parts[k, pl.ds(i * grades, grades), :] = y
                x = x - y.astype(F32)

    for b in range(group):
        block = g * group + b
        slots, lives, rows = [], [], []
        for t in range(per):
            slot = src[block * per + t]
            live = jnp.where(lax.rem(slot, 2) < counts[lax.div(slot, 2)], 1.0, 0.0)
            slots.append(slot)
            lives.append(live)
            rows.append(parts[slot] * live.astype(BF16))
        weights = jnp.concatenate([tiles[b, t] for t in range(per)], 1)
        triple = dot(jnp.concatenate(rows, 1), weights, NT)
        logits = own[b] + (
            triple[:grades] + (triple[grades : 2 * grades] + triple[2 * grades :])
        )
        expo = jnp.exp(logits)
        probs = expo / jnp.sum(expo, axis=0, keepdims=True)
        grade = lax.broadcasted_iota(jnp.int32, (grades, BLK), 0)
        onehot = jnp.where(labels[pl.ds(b, 1), :] == grade, 1.0, 0.0)
        dlog = (probs - onehot) * scale

        @pl.when(lax.div(block, mine) == me[0])
        def _():
            dlog_out[lax.rem(block, mine)] = dlog

        back = dot(dlog.astype(BF16), weights, NN)
        for t in range(per):
            sums[slots[t]] += back[:, t * BLK : (t + 1) * BLK] * lives[t]

    @pl.when(g == pl.num_programs(0) - 1)
    def _():
        slots_out[...] = sums[...].astype(BF16)


def logits_back(src, counts, me, arrived, own, labels, tiles, scale, nfeat):
    nblocks, per = tiles.shape[:2]
    nslots, grades, _ = arrived.shape
    group = 8
    whole = lambda g, s, c, m: (0, 0, 0)
    return pl.pallas_call(
        functools.partial(logits_kernel, scale),
        grid_spec=pltpu.PrefetchScalarGridSpec(
            num_scalar_prefetch=3,
            grid=(nblocks // group,),
            in_specs=[
                pl.BlockSpec(arrived.shape, whole),
                pl.BlockSpec((group, grades, BLK), lambda g, s, c, m: (g, 0, 0)),
                pl.BlockSpec((group, BLK), lambda g, s, c, m: (g, 0)),
                pl.BlockSpec((group, per, BLK, BLK), lambda g, s, c, m: (g, 0, 0, 0)),
            ],
            out_specs=[
                pl.BlockSpec((nblocks // nfeat, grades, BLK), whole),
                pl.BlockSpec(arrived.shape, whole),
            ],
            scratch_shapes=[
                pltpu.VMEM((nslots, 3 * grades, BLK), BF16),
                pltpu.VMEM(arrived.shape, F32),
            ],
        ),
        out_shape=[
            jax.ShapeDtypeStruct((nblocks // nfeat, grades, BLK), F32),
            jax.ShapeDtypeStruct(arrived.shape, BF16),
        ],
        compiler_params=params(20),
        cost_estimate=cost(nblocks * per * 2 * 64 * BLK**2, 6 * MIB),
        name="logits",
    )(src, counts, me, arrived, own, labels, tiles)


def grads_kernel(nfeat, table, me, returned, dlog, hidden, second, *refs):
    pieces = refs[: 2 * nfeat]
    big = refs[2 * nfeat]
    small = refs[2 * nfeat + 1 : 3 * nfeat + 1]
    total, dproj, buf = refs[3 * nfeat + 1 :]
    group, grades, _ = dlog.shape
    g = pl.program_id(0)
    width = hidden.shape[0]

    @pl.when(g == 0)
    def _():
        total[pl.ds(0, group)] = dlog[...]

        @pl.loop(0, returned.shape[0], unroll=8)
        def _(k):
            at = table[k] - me[0] * group
            at = jnp.where((at >= 0) & (at < group), at, group)
            total[at] += returned[k].astype(F32)

        for b in range(group):
            dproj[:, b * BLK : (b + 1) * BLK] = total[b].astype(BF16)

    active = hidden[...]
    dproj_b = dproj[...]
    dpre = jnp.where(active > 0, dot(second[...], dproj_b, NN), 0.0)
    buf[pl.ds(0, grades), :] = dot(dproj_b, active, NT)
    part = dpre[:, :BLK]
    for i in range(1, dpre.shape[1] // BLK):
        part += dpre[:, i * BLK : (i + 1) * BLK]
    buf[pl.ds(grades, 8), :] = jnp.broadcast_to(
        jnp.sum(part.T, axis=0, keepdims=True), (8, width)
    )
    dpre_b = dpre.astype(BF16)
    for k in range(nfeat):
        owner = lax.rem(me[0] + nfeat - k, nfeat)
        both = jnp.concatenate([pieces[k][...], pieces[nfeat + k][...]], 1)
        grad = dot(dpre_b, both, NN).astype(BF16)
        big[:, owner] = grad.reshape(big.shape[0], big.shape[2], big.shape[3])
    for k in range(nfeat):

        @pl.when(g == k)
        def _():
            small[k][...] = buf[...]


def gradients(table, me, returned, dlog, hidden, second, pieces, parts):
    nfeat = len(pieces) // 2
    hid, nodes = hidden.shape
    group, grades, _ = dlog.shape
    width = hid // nfeat
    per = parts // nfeat
    turn = lambda g, m: lax.rem(m[0] + nfeat - g, nfeat)
    whole3 = lambda g, t, m: (0, 0, 0)
    whole2 = lambda g, t, m: (0, 0)
    small = jax.ShapeDtypeStruct((grades + 8, width), F32)
    return pl.pallas_call(
        functools.partial(grads_kernel, nfeat),
        grid_spec=pltpu.PrefetchScalarGridSpec(
            num_scalar_prefetch=2,
            grid=(nfeat,),
            in_specs=[
                pl.BlockSpec(returned.shape, whole3),
                pl.BlockSpec(dlog.shape, whole3),
                pl.BlockSpec((width, nodes), lambda g, t, m: (turn(g, m), 0)),
                pl.BlockSpec((width, grades), lambda g, t, m: (turn(g, m), 0)),
            ]
            + [pl.BlockSpec((nodes, BLK), whole2)] * (2 * nfeat),
            out_specs=[
                pl.BlockSpec(
                    (per, nfeat, hid // parts, width), lambda g, t, m: (turn(g, m), 0, 0, 0)
                )
            ]
            + [pl.BlockSpec(small.shape, whole2)] * nfeat,
            scratch_shapes=[
                pltpu.VMEM((group + 1, grades, BLK), F32),
                pltpu.VMEM((grades, nodes), BF16),
                pltpu.VMEM(small.shape, F32),
            ],
        ),
        out_shape=[jax.ShapeDtypeStruct((parts, nfeat, hid // parts, width), BF16)]
        + [small] * nfeat,
        compiler_params=params(32),
        cost_estimate=cost(2 * nodes * hid * hid, 8 * MIB),
        name="gradients",
    )(table, me, returned, dlog, hidden, second, *pieces)


def total_kernel(arrived, out, acc):
    g = pl.program_id(0)

    @pl.when(g == 0)
    def _():
        acc[...] = jnp.zeros_like(acc)

    total = arrived[0].astype(F32)
    for i in range(1, arrived.shape[0]):
        total += arrived[i].astype(F32)
    acc[...] += total

    @pl.when(g == pl.num_programs(0) - 1)
    def _():
        out[...] = acc[...].T


def total(arrived):
    n, cols, rows = arrived.shape
    step = 16
    return pl.pallas_call(
        total_kernel,
        grid=(n // step,),
        in_specs=[pl.BlockSpec((step, cols, rows), lambda g: (g, 0, 0))],
        out_specs=pl.BlockSpec((rows, cols), lambda g: (0, 0)),
        out_shape=jax.ShapeDtypeStruct((rows, cols), F32),
        scratch_shapes=[pltpu.VMEM((cols, rows), F32)],
        compiler_params=params(8),
        cost_estimate=cost(0, 2 * MIB),
        name="total",
    )(arrived)


def shards(features, pair_count, send_blocks, tile_src, tiles, labels, w_first, b_first, w_second):
    nblocks = tile_src.shape[0]
    parts = lax.axis_size("nodes")
    nfeat = lax.axis_size("feat")
    slots = send_blocks.shape[2]
    grades = w_second.shape[1]
    hid = w_first.shape[1]
    axis = lax.axis_index("feat").astype(jnp.int32)
    me = axis.reshape(1)
    table = send_blocks.reshape(parts * slots)
    src = tile_src.reshape(-1)
    counts = pair_count.reshape(-1)

    def ahead(x, k):
        return lax.ppermute(x, "feat", [(i, (i + k) % nfeat) for i in range(nfeat)])

    def swap(x):
        shaped = x.reshape(parts, slots, *x.shape[1:])
        moved = lax.all_to_all(shaped, "nodes", split_axis=0, concat_axis=0, tiled=True)
        return moved.reshape(x.shape)

    arrived = [swap(pick(features, table, c)) for c in range(2)]

    flat = w_first.T
    weights = [flat] + [ahead(flat, k) for k in range(1, nfeat)]
    consts = jnp.concatenate(
        [w_second.T.astype(F32), jnp.broadcast_to(b_first[None], (8, b_first.shape[0]))], 0
    )
    turned = [consts] + [ahead(consts, k) for k in range(1, nfeat)]
    ring = jnp.stack([turned[k] for k in (3, 2, 1, 0, 3, 2, 1)])
    ordered = lax.dynamic_slice_in_dim(ring, nfeat - 1 - axis, nfeat, 0)
    second_t = ordered[:, :grades].transpose(1, 0, 2).reshape(grades, hid).astype(BF16)
    bias = ordered[:, grades].reshape(hid, 1)
    second = second_t.T

    pieces = []
    for c in range(2):
        made = aggregate(src, counts, me, arrived[c], tiles, features, c, nfeat)
        pieces += [made[0]] + [ahead(made[k], k) for k in range(1, nfeat)]
    hidden, proj = dense(pieces, weights, bias, second_t)

    projs = [proj] + [ahead(proj, k) for k in range(1, nfeat)]
    own, send = spread(table, me, projs)
    scale = 1.0 / math.sqrt(nblocks * BLK * parts)
    dlog, slotsum = logits_back(
        src, counts, me, swap(send), own, labels.reshape(nblocks, BLK), tiles, scale, nfeat
    )
    big, *small = gradients(
        table, me, swap(slotsum), dlog, hidden, second, pieces, parts
    )
    moved = lax.all_to_all(
        big.reshape(parts * nfeat, *big.shape[2:]),
        ("nodes", "feat"),
        split_axis=0,
        concat_axis=0,
        tiled=True,
    )
    rest = small[0]
    for k in range(1, nfeat):
        rest = rest + ahead(small[k], nfeat - k)
    for bit in (1, 2, 4, 8, 16):
        rest = rest + lax.ppermute(rest, "nodes", [(i, i ^ bit) for i in range(parts)])
    return total(moved), rest[grades], rest[:grades].T


def solution(mesh):
    placed = (
        P("nodes", "feat"),
        P("nodes", None),
        P("nodes", None, None),
        P("nodes", None),
        P("nodes", None, None, None),
        P("nodes"),
        P("feat", None),
        P("feat"),
        P("feat", None),
    )
    return jax.shard_map(
        shards,
        mesh=mesh,
        in_specs=placed,
        out_specs=(P("feat", "nodes"), P("feat"), P("feat", None)),
        check_vma=False,
    )
```

time: 651 us -> 220 us (0.34)
  waiting for transfers between devices: 326 us -> 77.5 us
  blocking collectives: 182 us -> 30.1 us
  matrix products: 46.1 us -> 0 us
  Pallas kernels: 0 us -> 36.8 us
  local copies, waits for them, and re-layouts: 51.3 us -> 18.2 us
  starting transfers between devices: 20 us -> 52.2 us
  between operations: 14 us -> 0.93 us
  other arithmetic: 6.85 us -> 0.05 us
    reduce_scatter x2 -> x0, waiting for transfers between devices: 149 us -> none  [the longest x1 149 us: shards(): pre = lax.psum_scatter(partial_pre, 'feat', scatter_dimension=1, tiled=True)]
    psum x1 -> x0, blocking collectives: 123 us -> none  [shards(): grad_second, grad_bias = lax.psum((grad_second, grad_bias), 'nodes')]
    all_gather x1 -> x0, waiting for transfers between devices: 83 us -> none  [shards(): lax.all_gather(dpre_b, 'feat', axis=1, tiled=True)]
    dot_general x10 -> x0, matrix products: 46.1 us -> none  [the longest x1 8.25 us: shards(): lax.dot_general(agg_first, lax.all_gather(dpre_b, 'feat', axis=1, tiled=T...]
    ppermute x0 -> x23, waiting for transfers between devices: none -> 43.1 us  [the longest x18 36.8 us: ahead(): return lax.ppermute(x, 'feat', [(i, (i + k) % nfeat) for i in range(nfeat)])]
    pallas_call x0 -> x9, Pallas kernels: none -> 36.8 us  [the longest x2 10.7 us: aggregate(): pl.pallas_call(agg_kernel, grid_spec=pltpu.PrefetchScalarGridSpec(num_sca...]
    psum x1 -> x0, waiting for transfers between devices: 35.4 us -> none  [shards(): logits = lax.psum(partial_logits, 'feat')]
    ppermute x0 -> x23, starting transfers between devices: none -> 33 us  [the longest x18 23.3 us: ahead(): return lax.ppermute(x, 'feat', [(i, (i + k) % nfeat) for i in range(nfeat)])]
  transfers between devices with their start and end apart: 6 -> 26, of which waited for: 5 -> 16; matrix products, arithmetic and copies ran while one was open for 0% -> 2% of each run, Pallas kernels for 0% -> 6%
where the time goes in v1:
time: 220 us; the launch traced here: 216 us
  waiting for transfers between devices  77.5 us (35%)
  starting transfers between devices  52.2 us (24%)
  Pallas kernels  36.8 us (17%)
  blocking collectives  30.1 us (14%)
  local copies, waits for them, and re-layouts  18.2 us (8%)
    ppermute x18, waiting for transfers between devices, ahead(): return lax.ppermute(x, 'feat', [(i, (i + k) % nfeat) for i in range(nfeat)])  36.8 us
    all_to_all x2, waiting for transfers between devices, swap(): lax.all_to_all(shaped, 'nodes', split_axis=0, concat_axis=0, tiled=True)  34.4 us
    all_to_all x2, blocking collectives, swap(): lax.all_to_all(shaped, 'nodes', split_axis=0, concat_axis=0, tiled=True)  30.1 us
    ppermute x18, starting transfers between devices, ahead(): return lax.ppermute(x, 'feat', [(i, (i + k) % nfeat) for i in range(nfeat)])  23.3 us
    all_to_all x2, starting transfers between devices, swap(): lax.all_to_all(shaped, 'nodes', split_axis=0, concat_axis=0, tiled=True)  15.1 us
    unnamed x45, local copies, waits for them, and re-layouts  14.1 us
    pallas_call x2, Pallas kernels, aggregate(): pl.pallas_call(agg_kernel, grid_spec=pltpu.PrefetchScalarGridSpec(num_sca...  10.7 us
    ppermute x5, starting transfers between devices, shards(): lax.ppermute(rest, 'nodes', [(i, i ^ bit) for i in range(parts)])  9.66 us
  transfers between devices with their start and end apart: 26, of which 16 were waited for; matrix products, arithmetic and copies ran while one was open for 2% of the time, Pallas kernels for 6%

profile of v1, /device:TPU:1, one launch (start us, length us, event | category | flops | bytes accessed | tf_op | source)
XLA Modules:
  0.0 215.7 jit_solution(16963056239087493058)
XLA Ops:
  0.6 0.8 copy.18
  1.5 1.6 copy-done.3
  3.1 2.5 %pick.2 = bf16[64,128,128]{2,1,0:T(8,128)(2,1)S(1)} custom-call(s32[64]{0:T(128)S(1)} %reshape.51.table, bf16[4096,256]{1,0:T(8,128)(2,1)S(1)} %copy-done.3), custom_call_target="tpu_custom_call" | custom-call | bytes 4194304 | tf_op jit(solution)/shard_map/pick/pallas_call | solution.py:51
  5.6 1.3 copy-done.6
  7.0 9.8 %all-to-all-start = ((bf16[32,2,128,128]{3,2,1,0:T(8,128)(2,1)}), bf16[32,2,128,128]{3,2,1,0:T(8,128)(2,1)}, u32[]{:S(2)}, u32[]{:S(2)}) async-start(bf16[32,2,128,128]{3,2,1,0:T(8,128)(2,1)} %bitcast.36), calls=%async_computation | async-start | bytes 4194304 | tf_op jit(solution)/shard_map/all_to_all | solution.py:416
  16.8 2.5 %pick.3 = bf16[64,128,128]{2,1,0:T(8,128)(2,1)S(1)} custom-call(s32[64]{0:T(128)S(1)} %reshape.51.table, bf16[4096,256]{1,0:T(8,128)(2,1)S(1)} %copy-done.4), custom_call_target="tpu_custom_call" | custom-call | bytes 4194304 | tf_op jit(solution)/shard_map/pick/pallas_call | solution.py:51
  19.3 1.3 copy-done.5
  20.6 24.5 %all-to-all-done = bf16[32,2,128,128]{3,2,1,0:T(8,128)(2,1)} async-done(((bf16[32,2,128,128]{3,2,1,0:T(8,128)(2,1)}), bf16[32,2,128,128]{3,2,1,0:T(8,128)(2,1)}, u32[]{:S(2)}, u32[]{:S(2)}) %all-to-all-start) | async-done | bytes 2097184 | tf_op jit(solution)/shard_map/all_to_all | solution.py:416
  45.1 5.4 %all-to-all-start.1 = ((bf16[32,2,128,128]{3,2,1,0:T(8,128)(2,1)}), bf16[32,2,128,128]{3,2,1,0:T(8,128)(2,1)}, u32[]{:S(2)}, u32[]{:S(2)}) async-start(bf16[32,2,128,128]{3,2,1,0:T(8,128)(2,1)} %bitcast.35), calls=%async_computation.1 | async-start | bytes 4194304 | tf_op jit(solution)/shard_map/all_to_all | solution.py:416
  50.5 2.5 %collective-permute-start.9 = (f32[24,256]{1,0:T(8,128)S(1)}, f32[24,256]{1,0:T(8,128)S(1)}, u32[]{:S(2)}, u32[]{:S(2)}) collective-permute-start(f32[24,256]{1,0:T(8,128)S(1)} %pad_maximum_fusion), channel_id=1, source_target_pairs={{0,3},{1,0},{2,1},{3,2},{4,7},{5,4},{6,5},{7,6},{8,11},{9,8},{10,9... | collective-permute-start | bytes 73736 | tf_op jit(solution)/shard_map/ppermute | solution.py:412
  53.6 0.6 collective-permute-start.11
  54.4 1.6 collective-permute-start.6
  56.0 1.7 collective-permute-start.7
  58.0 0.8 collective-permute-start.8
  58.9 2.2 %copy-done = bf16[32,4,128,128]{3,2,1,0:T(8,128)(2,1)S(1)} copy-done((bf16[32,4,128,128]{3,2,1,0:T(8,128)(2,1)S(1)}, bf16[32,4,128,128]{3,2,1,0:T(8,128)(2,1)}, u32[]{:S(2)}) %copy-start) | copy-done | bytes 4194328
  61.0 5.4 %aggregate.2 = (bf16[1024,128]{1,0:T(8,128)(2,1)S(1)}, bf16[1024,128]{1,0:T(8,128)(2,1)}, bf16[1024,128]{1,0:T(8,128)(2,1)}, bf16[1024,128]{1,0:T(8,128)(2,1)}) custom-call(s32[128]{0:T(128)S(1)} %reshape.53.src, s32[32]{0:T(128)S(1)} %bitcast.49, s32[1]{0:T(128)} %bitcast.me, bf16[64,128,128]{2,1,0:T(8,128)(2,1)} %bitcast.3.arrived, ...), custom_call_target="tpu_custom_call" | custom-call | flops 536870912 | bytes 8388608 | tf_op jit(solution)/shard_map/aggregate/pallas_call | solution.py:94
  66.4 0.7 collective-permute-start
  67.1 0.7 copy-done.14
  67.8 1.2 collective-permute-start.1
  69.0 9.9 %all-to-all-done.1 = bf16[32,2,128,128]{3,2,1,0:T(8,128)(2,1)} async-done(((bf16[32,2,128,128]{3,2,1,0:T(8,128)(2,1)}), bf16[32,2,128,128]{3,2,1,0:T(8,128)(2,1)}, u32[]{:S(2)}, u32[]{:S(2)}) %all-to-all-start.1) | async-done | bytes 2097184 | tf_op jit(solution)/shard_map/all_to_all | solution.py:416
  78.9 2.2 %copy-done.1 = bf16[32,4,128,128]{3,2,1,0:T(8,128)(2,1)S(1)} copy-done((bf16[32,4,128,128]{3,2,1,0:T(8,128)(2,1)S(1)}, bf16[32,4,128,128]{3,2,1,0:T(8,128)(2,1)}, u32[]{:S(2)}) %copy-start.1) | copy-done | bytes 4194328
  81.1 5.3 %aggregate.3 = (bf16[1024,128]{1,0:T(8,128)(2,1)S(1)}, bf16[1024,128]{1,0:T(8,128)(2,1)}, bf16[1024,128]{1,0:T(8,128)(2,1)}, bf16[1024,128]{1,0:T(8,128)(2,1)}) custom-call(s32[128]{0:T(128)S(1)} %reshape.53.src, s32[32]{0:T(128)S(1)} %bitcast.50, s32[1]{0:T(128)} %bitcast.me, bf16[64,128,128]{2,1,0:T(8,128)(2,1)} %bitcast.5.arrived, ...), custom_call_target="tpu_custom_call" | custom-call | flops 536870912 | bytes 8388608 | tf_op jit(solution)/shard_map/aggregate/pallas_call | solution.py:94
  86.4 0.7 copy-done.10
  87.1 2.5 %collective-permute-start.2 = (bf16[1024,128]{1,0:T(8,128)(2,1)}, bf16[1024,128]{1,0:T(8,128)(2,1)S(1)}, u32[]{:S(2)}, u32[]{:S(2)}) collective-permute-start(bf16[1024,128]{1,0:T(8,128)(2,1)} %get-tuple-element.25), channel_id=1, source_target_pairs={{0,3},{1,0},{2,1},{3,2},{4,7},{5,4},{6,5},{7,6},{8,11},{9,8},{10,9... | collective-permute-start | bytes 786440 | tf_op jit(solution)/shard_map/ppermute | solution.py:412
  89.6 1.7 collective-permute-start.4
  91.4 1.0 collective-permute-start.5
  92.4 0.6 bitcast_dynamic-update-slice_fusion.2
  93.0 0.8 fusion
  94.1 0.8 constant_dynamic-slice_fusion
  95.4 3.2 %collective-permute-done.3.refs_5_ = bf16[1024,128]{1,0:T(8,128)(2,1)S(1)} collective-permute-done((bf16[1024,128]{1,0:T(8,128)(2,1)}, bf16[1024,128]{1,0:T(8,128)(2,1)S(1)}, u32[]{:S(2)}, u32[]{:S(2)}) %collective-permute-start.3) | collective-permute-done | bytes 262176 | tf_op jit(solution)/shard_map/ppermute | solution.py:412
  98.6 3.8 %collective-permute-done.4.refs_6_ = bf16[1024,128]{1,0:T(8,128)(2,1)S(1)} collective-permute-done((bf16[1024,128]{1,0:T(8,128)(2,1)}, bf16[1024,128]{1,0:T(8,128)(2,1)S(1)}, u32[]{:S(2)}, u32[]{:S(2)}) %collective-permute-start.4) | collective-permute-done | bytes 262176 | tf_op jit(solution)/shard_map/ppermute | solution.py:412
  102.4 3.5 %collective-permute-done.5.refs_7_ = bf16[1024,128]{1,0:T(8,128)(2,1)S(1)} collective-permute-done((bf16[1024,128]{1,0:T(8,128)(2,1)}, bf16[1024,128]{1,0:T(8,128)(2,1)S(1)}, u32[]{:S(2)}, u32[]{:S(2)}) %collective-permute-start.5) | collective-permute-done | bytes 262176 | tf_op jit(solution)/shard_map/ppermute | solution.py:412
  105.9 0.9 copy-done.11
  106.9 5.6 %dense.1 = (bf16[1024,1024]{1,0:T(8,128)(2,1)S(1)}, f32[8,16,128]{2,1,0:T(8,128)S(1)}) custom-call(bf16[1024,128]{1,0:T(8,128)(2,1)S(1)} %get-tuple-element.22.refs_0_, bf16[1024,128]{1,0:T(8,128)(2,1)} %collective-permute-done.refs_1_, bf16[1024,128]{1,0:T(8,128)(2,1)} %collective-permute-done.1.refs_2_, ...), custom_call_target="tpu_custom_call" | custom-call | flops 2147483648 | bytes 7340032 | tf_op jit(solution)/shard_map/dense/pallas_call | solution.py:136
  112.5 1.2 collective-permute-start.12
  113.7 3.3 %collective-permute-start.13 = (f32[8,16,128]{2,1,0:T(8,128)S(1)}, f32[8,16,128]{2,1,0:T(8,128)S(1)}, u32[]{:S(2)}, u32[]{:S(2)}) collective-permute-start(f32[8,16,128]{2,1,0:T(8,128)S(1)} %get-tuple-element.30.p0), channel_id=1, source_target_pairs={{0,2},{1,3},{2,0},{3,1},{4,6},{5,7},{6,4},{7,5},{8,10},{9,11},{10,... | collective-permute-start | bytes 196616 | tf_op jit(solution)/shard_map/ppermute | solution.py:412
  117.5 1.9 collective-permute-done.13.p2
  119.4 1.4 collective-permute-done.14.p3
  120.9 0.7 spread.1
  121.5 17.7 %all_to_all.25 = f32[32,2,16,128]{3,2,1,0:T(8,128)S(1)} all-to-all(f32[32,2,16,128]{3,2,1,0:T(8,128)S(1)} %bitcast.45), channel_id=1, replica_groups=mesh['nodes'=32,'feat'=4] {'nodes'}, dimensions={0} | all-to-all | bytes 1048576 | tf_op jit(solution)/shard_map/all_to_all | solution.py:416
  139.2 7.9 %logits.1 = (f32[8,16,128]{2,1,0:T(8,128)S(1)}, bf16[64,16,128]{2,1,0:T(8,128)(2,1)S(1)}) custom-call(s32[128]{0:T(128)S(1)} %reshape.53.src, s32[32]{0:T(128)S(1)} %bitcast.51, s32[1]{0:T(128)} %bitcast.me, f32[64,16,128]{2,1,0:T(8,128)S(1)} %bitcast.37, f32[32,16,128]{2,1,0:T(8,128)S(1)} %get-tuple-element.32.own, s32[32,128]{1,0:T(8,128)S(1)} %bitcast.48, ...), custom_call_target="tpu_custom_call" | custom-call | flops 268435456 | bytes 6291456 | tf_op jit(solution)/shard_map/logits/pallas_call | solution.py:248
  147.1 12.4 %all_to_all.26 = bf16[32,2,16,128]{3,2,1,0:T(8,128)(2,1)S(1)} all-to-all(bf16[32,2,16,128]{3,2,1,0:T(8,128)(2,1)S(1)} %bitcast.47), channel_id=1, replica_groups=mesh['nodes'=32,'feat'=4] {'nodes'}, dimensions={0} | all-to-all | bytes 524288 | tf_op jit(solution)/shard_map/all_to_all | solution.py:416
  159.5 6.4 %gradients.1 = (bf16[32,4,32,256]{3,2,1,0:T(8,128)(2,1)S(1)}, f32[24,256]{1,0:T(8,128)S(1)}, f32[24,256]{1,0:T(8,128)S(1)}, f32[24,256]{1,0:T(8,128)S(1)}, f32[24,256]{1,0:T(8,128)S(1)}) custom-call(s32[64]{0:T(128)S(1)} %reshape.51.table, s32[1]{0:T(128)} %bitcast.me, bf16[64,16,128]{2,1,0:T(8,128)(2,1)S(1)} %bitcast.46, ...), custom_call_target="tpu_custom_call" | custom-call | flops 2147483648 | bytes 8388608 | tf_op jit(solution)/shard_map/gradients/pallas_call | solution.py:333
  165.9 1.3 copy-done.7
  167.3 4.0 %all-to-all-start.4 = ((bf16[128,32,256]{2,1,0:T(8,128)(2,1)}), bf16[128,32,256]{2,1,0:T(8,128)(2,1)S(1)}, u32[]{:S(2)}, u32[]{:S(2)}) async-start(bf16[128,32,256]{2,1,0:T(8,128)(2,1)} %bitcast.38), calls=%async_computation.4 | async-start | bytes 4194304 | tf_op jit(solution)/shard_map/all_to_all | solution.py:448
  171.3 2.7 %collective-permute-start.15 = (f32[24,256]{1,0:T(8,128)S(1)}, f32[24,256]{1,0:T(8,128)S(1)}, u32[]{:S(2)}, u32[]{:S(2)}) collective-permute-start(f32[24,256]{1,0:T(8,128)S(1)} %get-tuple-element.38), channel_id=1, source_target_pairs={{0,3},{1,0},{2,1},{3,2},{4,7},{5,4},{6,5},{7,6},{8,11},{9,8},{10,9... | collective-permute-start | bytes 73736 | tf_op jit(solution)/shard_map/ppermute | solution.py:412
  174.0 0.6 collective-permute-start.16
  174.6 0.6 collective-permute-start.17
  175.1 20.7 %collective-permute-done.15 = f32[24,256]{1,0:T(8,128)S(1)} collective-permute-done((f32[24,256]{1,0:T(8,128)S(1)}, f32[24,256]{1,0:T(8,128)S(1)}, u32[]{:S(2)}, u32[]{:S(2)}) %collective-permute-start.15) | collective-permute-done | bytes 24608 | tf_op jit(solution)/shard_map/ppermute | solution.py:412
  195.8 1.5 collective-permute-done.16
  197.3 1.2 collective-permute-start.18
  198.5 0.8 collective-permute-done.18
  199.4 1.3 collective-permute-start.19
  200.7 1.4 collective-permute-done.19
  202.1 3.0 %collective-permute-start.20 = (f32[24,256]{1,0:T(8,128)S(1)}, f32[24,256]{1,0:T(8,128)S(1)}, u32[]{:S(2)}, u32[]{:S(2)}) collective-permute-start(f32[24,256]{1,0:T(8,128)S(1)} %add.33), channel_id=1, source_target_pairs={{0,16},{4,20},{8,24},{12,28},{16,0},{20,4},{24,8},{28,12},{32,48},... | collective-permute-start | bytes 73736 | tf_op jit(solution)/shard_map/ppermute | solution.py:459
  205.2 1.2 collective-permute-done.20
  206.4 1.2 collective-permute-start.21
  207.7 1.4 collective-permute-done.21
  209.1 2.8 %collective-permute-start.22 = (f32[24,256]{1,0:T(8,128)S(1)}, f32[24,256]{1,0:T(8,128)S(1)}, u32[]{:S(2)}, u32[]{:S(2)}) collective-permute-start(f32[24,256]{1,0:T(8,128)S(1)} %add.35), channel_id=1, source_target_pairs={{0,64},{4,68},{8,72},{12,76},{16,80},{20,84},{24,88},{28,92},{32,9... | collective-permute-start | bytes 73736 | tf_op jit(solution)/shard_map/ppermute | solution.py:459
  211.9 1.4 collective-permute-done.22
  213.3 0.6 slice.17
  213.8 0.6 slice_bitcast_fusion
  214.5 0.5 total.1
  215.0 0.7 copy.24
  (64 shorter events, 2.4 us)
Async XLA Ops:
  1.5 1.6 copy-start.3
  5.6 1.3 copy-start.6
  7.0 9.8 %copy-start.4 = (bf16[4096,256]{1,0:T(8,128)(2,1)S(1)}, bf16[4096,256]{1,0:T(8,128)(2,1)}, u32[]{:S(2)}) copy-start(bf16[4096,256]{1,0:T(8,128)(2,1)} %own.3) | copy-start | bytes 6291460
  7.0 38.1 %all-to-all-start = ((bf16[32,2,128,128]{3,2,1,0:T(8,128)(2,1)}), bf16[32,2,128,128]{3,2,1,0:T(8,128)(2,1)}, u32[]{:S(2)}, u32[]{:S(2)}) async-start(bf16[32,2,128,128]{3,2,1,0:T(8,128)(2,1)} %bitcast.36), calls=%async_computation | async-start | bytes 4194304 | tf_op jit(solution)/shard_map/all_to_all | solution.py:416
  19.3 1.3 copy-start.5
  45.1 5.4 %copy-start.15 = (bf16[256,16]{0,1:T(8,128)(2,1)S(1)}, bf16[256,16]{0,1:T(8,128)(2,1)}, u32[]{:S(2)}) copy-start(bf16[256,16]{0,1:T(8,128)(2,1)} %param.17) | copy-start | bytes 24580
  45.1 5.4 %copy-start.17 = (f32[256]{0:T(256)S(1)}, f32[256]{0:T(256)}, u32[]{:S(2)}) copy-start(f32[256]{0:T(256)} %param.16) | copy-start | bytes 3076
  45.1 9.1 %copy-start.13 = (bf16[256,1024]{1,0:T(8,128)(2,1)S(1)}, bf16[256,1024]{1,0:T(8,128)(2,1)}, u32[]{:S(2)}) copy-start(bf16[256,1024]{1,0:T(8,128)(2,1)} %param.15) | copy-start | bytes 1572868
  45.1 12.6 %copy-start.16 = (s32[32,4]{0,1:T(4,128)S(1)}, s32[32,4]{0,1:T(4,128)}, u32[]{:S(2)}) copy-start(s32[32,4]{0,1:T(4,128)} %param.12) | copy-start | bytes 1540
  45.1 13.7 %copy-start.9 = (s32[1,32]{1,0:T(1,128)S(1)}, s32[1,32]{1,0:T(1,128)}, u32[]{:S(2)}) copy-start(s32[1,32]{1,0:T(1,128)} %param.10) | copy-start | bytes 388
  45.1 33.8 %all-to-all-start.1 = ((bf16[32,2,128,128]{3,2,1,0:T(8,128)(2,1)}), bf16[32,2,128,128]{3,2,1,0:T(8,128)(2,1)}, u32[]{:S(2)}, u32[]{:S(2)}) async-start(bf16[32,2,128,128]{3,2,1,0:T(8,128)(2,1)} %bitcast.35), calls=%async_computation.1 | async-start | bytes 4194304 | tf_op jit(solution)/shard_map/all_to_all | solution.py:416
  50.5 7.4 %collective-permute-start.9 = (f32[24,256]{1,0:T(8,128)S(1)}, f32[24,256]{1,0:T(8,128)S(1)}, u32[]{:S(2)}, u32[]{:S(2)}) collective-permute-start(f32[24,256]{1,0:T(8,128)S(1)} %pad_maximum_fusion), channel_id=1, source_target_pairs={{0,3},{1,0},{2,1},{3,2},{4,7},{5,4},{6,5},{7,6},{8,11},{9,8},{10,9... | collective-permute-start | bytes 73736 | tf_op jit(solution)/shard_map/ppermute | solution.py:412
  53.1 5.7 %collective-permute-start.10 = (f32[24,256]{1,0:T(8,128)S(1)}, f32[24,256]{1,0:T(8,128)S(1)}, u32[]{:S(2)}, u32[]{:S(2)}) collective-permute-start(f32[24,256]{1,0:T(8,128)S(1)} %pad_maximum_fusion), channel_id=1, source_target_pairs={{0,2},{1,3},{2,0},{3,1},{4,6},{5,7},{6,4},{7,5},{8,10},{9,11},{10,... | collective-permute-start | bytes 73736 | tf_op jit(solution)/shard_map/ppermute | solution.py:412
  53.6 5.2 %collective-permute-start.11 = (f32[24,256]{1,0:T(8,128)S(1)}, f32[24,256]{1,0:T(8,128)S(1)}, u32[]{:S(2)}, u32[]{:S(2)}) collective-permute-start(f32[24,256]{1,0:T(8,128)S(1)} %pad_maximum_fusion), channel_id=1, source_target_pairs={{0,1},{1,2},{2,3},{3,0},{4,5},{5,6},{6,7},{7,4},{8,9},{9,10},{10,1... | collective-permute-start | bytes 73736 | tf_op jit(solution)/shard_map/ppermute | solution.py:412
  54.4 32.7 %collective-permute-start.6 = (bf16[1024,256]{1,0:T(8,128)(2,1)S(1)}, bf16[1024,256]{1,0:T(8,128)(2,1)S(1)}, u32[]{:S(2)}, u32[]{:S(2)}) collective-permute-start(bf16[1024,256]{1,0:T(8,128)(2,1)S(1)} %bitcast.41), channel_id=1, source_target_pairs={{0,1},{1,2},{2,3},{3,0},{4,5},{5,6},{6,7},{7,4},{8,9},{9,10},{10,1... | collective-permute-start | bytes 1572872 | tf_op jit(solution)/shard_map/ppermute | solution.py:412
  56.0 33.6 %collective-permute-start.7 = (bf16[1024,256]{1,0:T(8,128)(2,1)S(1)}, bf16[1024,256]{1,0:T(8,128)(2,1)}, u32[]{:S(2)}, u32[]{:S(2)}) collective-permute-start(bf16[1024,256]{1,0:T(8,128)(2,1)S(1)} %bitcast.42), channel_id=1, source_target_pairs={{0,2},{1,3},{2,0},{3,1},{4,6},{5,7},{6,4},{7,5},{8,10},{9,11},{10,... | collective-permute-start | bytes 1572872 | tf_op jit(solution)/shard_map/ppermute | solution.py:412
  58.0 31.7 %collective-permute-start.8 = (bf16[1024,256]{1,0:T(8,128)(2,1)S(1)}, bf16[1024,256]{1,0:T(8,128)(2,1)}, u32[]{:S(2)}, u32[]{:S(2)}) collective-permute-start(bf16[1024,256]{1,0:T(8,128)(2,1)S(1)} %bitcast.43), channel_id=1, source_target_pairs={{0,3},{1,0},{2,1},{3,2},{4,7},{5,4},{6,5},{7,6},{8,11},{9,8},{10,9... | collective-permute-start | bytes 1572872 | tf_op jit(solution)/shard_map/ppermute | solution.py:412
  58.9 2.2 %copy-start = (bf16[32,4,128,128]{3,2,1,0:T(8,128)(2,1)S(1)}, bf16[32,4,128,128]{3,2,1,0:T(8,128)(2,1)}, u32[]{:S(2)}) copy-start(bf16[32,4,128,128]{3,2,1,0:T(8,128)(2,1)} %tiles.5) | copy-start | bytes 12582916
  66.4 24.9 %collective-permute-start = (bf16[1024,128]{1,0:T(8,128)(2,1)}, bf16[1024,128]{1,0:T(8,128)(2,1)}, u32[]{:S(2)}, u32[]{:S(2)}) collective-permute-start(bf16[1024,128]{1,0:T(8,128)(2,1)} %get-tuple-element.23), channel_id=1, source_target_pairs={{0,1},{1,2},{2,3},{3,0},{4,5},{5,6},{6,7},{7,4},{8,9},{9,10},{10,1... | collective-permute-start | bytes 786440 | tf_op jit(solution)/shard_map/ppermute | solution.py:412
  67.1 0.7 copy-start.14
  67.8 27.3 %collective-permute-start.1 = (bf16[1024,128]{1,0:T(8,128)(2,1)}, bf16[1024,128]{1,0:T(8,128)(2,1)}, u32[]{:S(2)}, u32[]{:S(2)}) collective-permute-start(bf16[1024,128]{1,0:T(8,128)(2,1)} %get-tuple-element.24), channel_id=1, source_target_pairs={{0,2},{1,3},{2,0},{3,1},{4,6},{5,7},{6,4},{7,5},{8,10},{9,11},{10,... | collective-permute-start | bytes 786440 | tf_op jit(solution)/shard_map/ppermute | solution.py:412
  78.9 2.2 %copy-start.1 = (bf16[32,4,128,128]{3,2,1,0:T(8,128)(2,1)S(1)}, bf16[32,4,128,128]{3,2,1,0:T(8,128)(2,1)}, u32[]{:S(2)}) copy-start(bf16[32,4,128,128]{3,2,1,0:T(8,128)(2,1)} %tiles.5) | copy-start | bytes 12582916
  86.4 0.7 copy-start.10
  87.1 8.2 %collective-permute-start.2 = (bf16[1024,128]{1,0:T(8,128)(2,1)}, bf16[1024,128]{1,0:T(8,128)(2,1)S(1)}, u32[]{:S(2)}, u32[]{:S(2)}) collective-permute-start(bf16[1024,128]{1,0:T(8,128)(2,1)} %get-tuple-element.25), channel_id=1, source_target_pairs={{0,3},{1,0},{2,1},{3,2},{4,7},{5,4},{6,5},{7,6},{8,11},{9,8},{10,9... | collective-permute-start | bytes 786440 | tf_op jit(solution)/shard_map/ppermute | solution.py:412
  89.6 9.0 %collective-permute-start.3 = (bf16[1024,128]{1,0:T(8,128)(2,1)}, bf16[1024,128]{1,0:T(8,128)(2,1)S(1)}, u32[]{:S(2)}, u32[]{:S(2)}) collective-permute-start(bf16[1024,128]{1,0:T(8,128)(2,1)} %get-tuple-element.27), channel_id=1, source_target_pairs={{0,1},{1,2},{2,3},{3,0},{4,5},{5,6},{6,7},{7,4},{8,9},{9,10},{10,1... | collective-permute-start | bytes 786440 | tf_op jit(solution)/shard_map/ppermute | solution.py:412
  89.6 12.8 %collective-permute-start.4 = (bf16[1024,128]{1,0:T(8,128)(2,1)}, bf16[1024,128]{1,0:T(8,128)(2,1)S(1)}, u32[]{:S(2)}, u32[]{:S(2)}) collective-permute-start(bf16[1024,128]{1,0:T(8,128)(2,1)} %get-tuple-element.28), channel_id=1, source_target_pairs={{0,2},{1,3},{2,0},{3,1},{4,6},{5,7},{6,4},{7,5},{8,10},{9,11},{10,... | collective-permute-start | bytes 786440 | tf_op jit(solution)/shard_map/ppermute | solution.py:412
  91.4 14.6 %collective-permute-start.5 = (bf16[1024,128]{1,0:T(8,128)(2,1)}, bf16[1024,128]{1,0:T(8,128)(2,1)S(1)}, u32[]{:S(2)}, u32[]{:S(2)}) collective-permute-start(bf16[1024,128]{1,0:T(8,128)(2,1)} %get-tuple-element.29), channel_id=1, source_target_pairs={{0,3},{1,0},{2,1},{3,2},{4,7},{5,4},{6,5},{7,6},{8,11},{9,8},{10,9... | collective-permute-start | bytes 786440 | tf_op jit(solution)/shard_map/ppermute | solution.py:412
  105.9 0.9 copy-start.11
  106.9 32.3 %copy-start.2 = (bf16[32,4,128,128]{3,2,1,0:T(8,128)(2,1)S(1)}, bf16[32,4,128,128]{3,2,1,0:T(8,128)(2,1)}, u32[]{:S(2)}) copy-start(bf16[32,4,128,128]{3,2,1,0:T(8,128)(2,1)} %tiles.5) | copy-start | bytes 12582916
  106.9 32.3 %copy-start.8 = (s32[4096]{0:T(1024)S(1)}, s32[4096]{0:T(1024)}, u32[]{:S(2)}) copy-start(s32[4096]{0:T(1024)} %param.14) | copy-start | bytes 49156
  112.5 5.0 %collective-permute-start.12 = (f32[8,16,128]{2,1,0:T(8,128)S(1)}, f32[8,16,128]{2,1,0:T(8,128)S(1)}, u32[]{:S(2)}, u32[]{:S(2)}) collective-permute-start(f32[8,16,128]{2,1,0:T(8,128)S(1)} %get-tuple-element.30.p0), channel_id=1, source_target_pairs={{0,1},{1,2},{2,3},{3,0},{4,5},{5,6},{6,7},{7,4},{8,9},{9,10},{10,1... | collective-permute-start | bytes 196616 | tf_op jit(solution)/shard_map/ppermute | solution.py:412
  113.7 5.7 %collective-permute-start.13 = (f32[8,16,128]{2,1,0:T(8,128)S(1)}, f32[8,16,128]{2,1,0:T(8,128)S(1)}, u32[]{:S(2)}, u32[]{:S(2)}) collective-permute-start(f32[8,16,128]{2,1,0:T(8,128)S(1)} %get-tuple-element.30.p0), channel_id=1, source_target_pairs={{0,2},{1,3},{2,0},{3,1},{4,6},{5,7},{6,4},{7,5},{8,10},{9,11},{10,... | collective-permute-start | bytes 196616 | tf_op jit(solution)/shard_map/ppermute | solution.py:412
  117.0 3.9 %collective-permute-start.14 = (f32[8,16,128]{2,1,0:T(8,128)S(1)}, f32[8,16,128]{2,1,0:T(8,128)S(1)}, u32[]{:S(2)}, u32[]{:S(2)}) collective-permute-start(f32[8,16,128]{2,1,0:T(8,128)S(1)} %get-tuple-element.30.p0), channel_id=1, source_target_pairs={{0,3},{1,0},{2,1},{3,2},{4,7},{5,4},{6,5},{7,6},{8,11},{9,8},{10,9... | collective-permute-start | bytes 196616 | tf_op jit(solution)/shard_map/ppermute | solution.py:412
  139.2 20.3 %copy-start.12 = (bf16[1024,128]{1,0:T(8,128)(2,1)S(1)}, bf16[1024,128]{1,0:T(8,128)(2,1)}, u32[]{:S(2)}) copy-start(bf16[1024,128]{1,0:T(8,128)(2,1)} %copy-done.10) | copy-start | bytes 786436
  165.9 1.3 copy-start.7
  167.3 47.2 %all-to-all-start.4 = ((bf16[128,32,256]{2,1,0:T(8,128)(2,1)}), bf16[128,32,256]{2,1,0:T(8,128)(2,1)S(1)}, u32[]{:S(2)}, u32[]{:S(2)}) async-start(bf16[128,32,256]{2,1,0:T(8,128)(2,1)} %bitcast.38), calls=%async_computation.4 | async-start | bytes 4194304 | tf_op jit(solution)/shard_map/all_to_all | solution.py:448
  171.3 24.5 %collective-permute-start.15 = (f32[24,256]{1,0:T(8,128)S(1)}, f32[24,256]{1,0:T(8,128)S(1)}, u32[]{:S(2)}, u32[]{:S(2)}) collective-permute-start(f32[24,256]{1,0:T(8,128)S(1)} %get-tuple-element.38), channel_id=1, source_target_pairs={{0,3},{1,0},{2,1},{3,2},{4,7},{5,4},{6,5},{7,6},{8,11},{9,8},{10,9... | collective-permute-start | bytes 73736 | tf_op jit(solution)/shard_map/ppermute | solution.py:412
  174.0 23.3 %collective-permute-start.16 = (f32[24,256]{1,0:T(8,128)S(1)}, f32[24,256]{1,0:T(8,128)S(1)}, u32[]{:S(2)}, u32[]{:S(2)}) collective-permute-start(f32[24,256]{1,0:T(8,128)S(1)} %get-tuple-element.39), channel_id=1, source_target_pairs={{0,2},{1,3},{2,0},{3,1},{4,6},{5,7},{6,4},{7,5},{8,10},{9,11},{10,... | collective-permute-start | bytes 73736 | tf_op jit(solution)/shard_map/ppermute | solution.py:412
  174.6 22.8 %collective-permute-start.17 = (f32[24,256]{1,0:T(8,128)S(1)}, f32[24,256]{1,0:T(8,128)S(1)}, u32[]{:S(2)}, u32[]{:S(2)}) collective-permute-start(f32[24,256]{1,0:T(8,128)S(1)} %get-tuple-element.40), channel_id=1, source_target_pairs={{0,1},{1,2},{2,3},{3,0},{4,5},{5,6},{6,7},{7,4},{8,9},{9,10},{10,1... | collective-permute-start | bytes 73736 | tf_op jit(solution)/shard_map/ppermute | solution.py:412
  197.3 2.1 collective-permute-start.18
  199.4 2.8 %collective-permute-start.19 = (f32[24,256]{1,0:T(8,128)S(1)}, f32[24,256]{1,0:T(8,128)S(1)}, u32[]{:S(2)}, u32[]{:S(2)}) collective-permute-start(f32[24,256]{1,0:T(8,128)S(1)} %add.32), channel_id=1, source_target_pairs={{0,8},{4,12},{8,0},{12,4},{16,24},{20,28},{24,16},{28,20},{32,40},... | collective-permute-start | bytes 73736 | tf_op jit(solution)/shard_map/ppermute | solution.py:459
  202.1 4.3 %collective-permute-start.20 = (f32[24,256]{1,0:T(8,128)S(1)}, f32[24,256]{1,0:T(8,128)S(1)}, u32[]{:S(2)}, u32[]{:S(2)}) collective-permute-start(f32[24,256]{1,0:T(8,128)S(1)} %add.33), channel_id=1, source_target_pairs={{0,16},{4,20},{8,24},{12,28},{16,0},{20,4},{24,8},{28,12},{32,48},... | collective-permute-start | bytes 73736 | tf_op jit(solution)/shard_map/ppermute | solution.py:459
  206.4 2.7 %collective-permute-start.21 = (f32[24,256]{1,0:T(8,128)S(1)}, f32[24,256]{1,0:T(8,128)S(1)}, u32[]{:S(2)}, u32[]{:S(2)}) collective-permute-start(f32[24,256]{1,0:T(8,128)S(1)} %add.34), channel_id=1, source_target_pairs={{0,32},{4,36},{8,40},{12,44},{16,48},{20,52},{24,56},{28,60},{32,0... | collective-permute-start | bytes 73736 | tf_op jit(solution)/shard_map/ppermute | solution.py:459
  209.1 4.2 %collective-permute-start.22 = (f32[24,256]{1,0:T(8,128)S(1)}, f32[24,256]{1,0:T(8,128)S(1)}, u32[]{:S(2)}, u32[]{:S(2)}) collective-permute-start(f32[24,256]{1,0:T(8,128)S(1)} %add.35), channel_id=1, source_target_pairs={{0,64},{4,68},{8,72},{12,76},{16,80},{20,84},{24,88},{28,92},{32,9... | collective-permute-start | bytes 73736 | tf_op jit(solution)/shard_map/ppermute | solution.py:459

commit v2 on v1

v2 whole, which is shorter than its diff:
```python
import functools
import math

import jax
import jax.numpy as jnp
from jax import lax
from jax.experimental import pallas as pl
from jax.experimental.pallas import tpu as pltpu
from jax.sharding import PartitionSpec as P

F32 = jnp.float32
BF16 = jnp.bfloat16
NT = (((1,), (1,)), ((), ()))
NN = (((1,), (0,)), ((), ()))
BLK = 128
MIB = 1 << 20


def params(mib):
    return pltpu.CompilerParams(vmem_limit_bytes=mib * MIB)


def cost(flops, nbytes):
    return pl.CostEstimate(flops=flops, bytes_accessed=nbytes, transcendentals=0)


def dot(a, b, dims):
    return lax.dot_general(a, b, dims, preferred_element_type=F32)


def pick_kernel(chunk, table, features, out, sem):
    slots = out.shape[0]

    @pl.loop(0, slots, unroll=8)
    def _(k):
        rows = pl.ds(pl.multiple_of(table[k] * BLK, BLK), BLK)
        pltpu.make_async_copy(
            features.at[rows, pl.ds(chunk * BLK, BLK)], out.at[k], sem
        ).start()

    pltpu.make_async_copy(out, out, sem).wait()


def pick(features, table, chunk):
    slots = table.shape[0]
    return pl.pallas_call(
        functools.partial(pick_kernel, chunk),
        grid_spec=pltpu.PrefetchScalarGridSpec(
            num_scalar_prefetch=1,
            grid=(),
            in_specs=[pl.BlockSpec(memory_space=pltpu.HBM)],
            out_specs=pl.BlockSpec(memory_space=pltpu.HBM),
            scratch_shapes=[pltpu.SemaphoreType.DMA],
        ),
        out_shape=pltpu.HBM((slots, BLK, BLK), BF16),
        compiler_params=params(4),
        cost_estimate=cost(0, 4 * MIB),
        name="pick",
    )(table, features)


def stage_kernel(x, out, sem):
    copy = pltpu.make_async_copy(x, out, sem)
    copy.start()
    copy.wait()


def stage(x):
    return pl.pallas_call(
        stage_kernel,
        in_specs=[pl.BlockSpec(memory_space=pltpu.HBM)],
        out_specs=pl.BlockSpec(memory_space=pltpu.VMEM),
        out_shape=pltpu.VMEM(x.shape, x.dtype),
        scratch_shapes=[pltpu.SemaphoreType.DMA],
        compiler_params=params(4),
        cost_estimate=cost(0, x.size * 2),
        name="stage",
    )(x)


def agg_kernel(which, group, nfeat, src, counts, me, arrived, tiles, own, *outs):
    per = tiles.shape[1]
    for k, out in zip(which, outs):
        first = lax.rem(me[0] + k, nfeat) * group
        for b in range(group):
            rows, weights = [], []
            for t in range(per):
                slot = src[(first + b) * per + t]
                live = lax.rem(slot, 2) < counts[lax.div(slot, 2)]
                rows.append(arrived[slot])
                weights.append(tiles[first + b, t] * jnp.where(live, 1.0, 0.0).astype(BF16))
            total = dot(jnp.concatenate(weights, 1), jnp.concatenate(rows, 0), NN)
            at = pl.ds(pl.multiple_of((first + b) * BLK, BLK), BLK)
            out[pl.ds(b * BLK, BLK), :] = (own[at, :].astype(F32) + total).astype(BF16)


def aggregate(src, counts, me, arrived, tiles, features, chunk, nfeat, which):
    nblocks, per = tiles.shape[:2]
    group = nblocks // nfeat
    piece = jax.ShapeDtypeStruct((group * BLK, BLK), BF16)
    vmem = pl.BlockSpec(memory_space=pltpu.VMEM)
    return pl.pallas_call(
        functools.partial(agg_kernel, which, group, nfeat),
        grid_spec=pltpu.PrefetchScalarGridSpec(
            num_scalar_prefetch=3,
            grid=(1,),
            in_specs=[
                vmem,
                vmem,
                pl.BlockSpec((nblocks * BLK, BLK), lambda g, s, c, m: (0, chunk)),
            ],
            out_specs=[vmem] * len(which),
        ),
        out_shape=[piece] * len(which),
        compiler_params=params(12),
        cost_estimate=cost(len(which) * group * per * 2 * BLK**3, 8 * MIB),
        name="aggregate",
    )(src, counts, me, arrived, tiles, features)


def early_kernel(own, p0, p1, p2, p3, w0, w1, w2, w3, bias, pre):
    first = jnp.concatenate([p0[...], own[...]], 1)
    later = jnp.concatenate([p1[...], p2[...], p3[...]], 1)
    weights = jnp.concatenate([w1[:, :BLK], w2[:, :BLK], w3[:, :BLK]], 1)
    pre[...] = (bias[...] + dot(w0[...], first, NT)) + dot(weights, later, NT)


def early(own, pieces, weights, bias):
    nodes = own.shape[0]
    hid, width = weights[0].shape
    step = 256
    return pl.pallas_call(
        early_kernel,
        grid=(nodes // step,),
        in_specs=[pl.BlockSpec((step, BLK), lambda g: (g, 0))] * 5
        + [pl.BlockSpec((hid, width), lambda g: (0, 0))] * 4
        + [pl.BlockSpec((hid, 1), lambda g: (0, 0))],
        out_specs=pl.BlockSpec((hid, step), lambda g: (0, g)),
        out_shape=jax.ShapeDtypeStruct((hid, nodes), F32),
        compiler_params=params(20),
        cost_estimate=cost(2 * nodes * hid * 5 * BLK, 7 * MIB),
        name="early",
    )(own, *pieces, *weights, bias)


def dense_kernel(pre, p1, p2, p3, w1, w2, w3, second, hidden, proj):
    later = jnp.concatenate([p1[...], p2[...], p3[...]], 1)
    weights = jnp.concatenate([w1[:, BLK:], w2[:, BLK:], w3[:, BLK:]], 1)
    hid = jnp.maximum(pre[...] + dot(weights, later, NT), 0.0).astype(BF16)
    hidden[...] = hid
    out = dot(second[...], hid, NN)
    for b in range(proj.shape[0]):
        proj[b] = out[:, b * BLK : (b + 1) * BLK]


def dense(pre, pieces, weights, second):
    hid, nodes = pre.shape
    width = weights[0].shape[1]
    grades = second.shape[0]
    step = 256
    return pl.pallas_call(
        dense_kernel,
        grid=(nodes // step,),
        in_specs=[pl.BlockSpec((hid, step), lambda g: (0, g))]
        + [pl.BlockSpec((step, BLK), lambda g: (g, 0))] * 3
        + [pl.BlockSpec((hid, width), lambda g: (0, 0))] * 3
        + [pl.BlockSpec((grades, hid), lambda g: (0, 0))],
        out_specs=[
            pl.BlockSpec((hid, step), lambda g: (0, g)),
            pl.BlockSpec((step // BLK, grades, BLK), lambda g: (g, 0, 0)),
        ],
        out_shape=[
            jax.ShapeDtypeStruct((hid, nodes), BF16),
            jax.ShapeDtypeStruct((nodes // BLK, grades, BLK), F32),
        ],
        compiler_params=params(20),
        cost_estimate=cost(2 * nodes * hid * 3 * BLK, 9 * MIB),
        name="dense",
    )(pre, *pieces, *weights, second)


def spread_kernel(table, me, p0, p1, p2, p3, whole, out):
    nfeat, group = 4, p0.shape[0]
    for k, piece in enumerate((p0, p1, p2, p3)):
        owner = lax.rem(me[0] + nfeat - k, nfeat)
        whole[pl.ds(owner * group, group)] = piece[...]

    @pl.loop(0, out.shape[0], unroll=8)
    def _(k):
        out[k] = whole[table[k]]


def spread(table, me, pieces):
    group, grades, _ = pieces[0].shape
    slots = table.shape[0]
    vmem = pl.BlockSpec(memory_space=pltpu.VMEM)
    return pl.pallas_call(
        spread_kernel,
        grid_spec=pltpu.PrefetchScalarGridSpec(
            num_scalar_prefetch=2,
            grid=(),
            in_specs=[vmem] * 4,
            out_specs=[vmem] * 2,
        ),
        out_shape=[
            jax.ShapeDtypeStruct((group * 4, grades, BLK), F32),
            jax.ShapeDtypeStruct((slots, grades, BLK), F32),
        ],
        compiler_params=params(4),
        cost_estimate=cost(0, MIB),
        name="spread",
    )(table, me, *pieces)


def logits_kernel(
    scale, src, counts, me, arrived, own, labels, tiles, dlog_out, slots_out, parts, field, grad_b, sums
):
    nblocks, per = tiles.shape[:2]
    nslots, grades, _ = arrived.shape
    mine = dlog_out.shape[0]

    def live_of(slot):
        return jnp.where(lax.rem(slot, 2) < counts[lax.div(slot, 2)], 1.0, 0.0)

    x = arrived[...]
    for i in range(3):
        y = x.astype(BF16)
        parts[:, i * grades : (i + 1) * grades, :] = y
        x = x - y.astype(F32)

    @pl.loop(0, nblocks, unroll=8)
    def _(b):
        rows, weights = [], []
        for t in range(per):
            slot = src[b * per + t]
            rows.append(parts[slot] * live_of(slot).astype(BF16))
            weights.append(tiles[b, t])
        triple = dot(jnp.concatenate(rows, 1), jnp.concatenate(weights, 1), NT)
        field[b] = own[b] + (
            triple[:grades] + (triple[grades : 2 * grades] + triple[2 * grades :])
        )

    expo = jnp.exp(field[...])
    probs = expo / jnp.sum(expo, axis=1, keepdims=True)
    grade = lax.broadcasted_iota(jnp.int32, field.shape, 1)
    onehot = jnp.where(labels[...] == grade, 1.0, 0.0)
    dlog = (probs - onehot) * scale
    field[...] = dlog
    grad_b[...] = dlog.astype(BF16)
    dlog_out[...] = field[pl.ds(me[0] * mine, mine)]
    sums[...] = jnp.zeros_like(sums)

    @pl.loop(0, nblocks, unroll=8)
    def _(b):
        back = dot(grad_b[b], jnp.concatenate([tiles[b, t] for t in range(per)], 1), NN)
        for t in range(per):
            slot = src[b * per + t]
            sums[slot] += back[:, t * BLK : (t + 1) * BLK] * live_of(slot)

    slots_out[...] = sums[...].astype(BF16)


def logits_back(src, counts, me, arrived, own, labels, tiles, scale, nfeat):
    nblocks, per = tiles.shape[:2]
    nslots, grades, _ = arrived.shape
    vmem = pl.BlockSpec(memory_space=pltpu.VMEM)
    return pl.pallas_call(
        functools.partial(logits_kernel, scale),
        grid_spec=pltpu.PrefetchScalarGridSpec(
            num_scalar_prefetch=3,
            grid=(),
            in_specs=[vmem] * 4,
            out_specs=[vmem] * 2,
            scratch_shapes=[
                pltpu.VMEM((nslots, 3 * grades, BLK), BF16),
                pltpu.VMEM((nblocks, grades, BLK), F32),
                pltpu.VMEM((nblocks, grades, BLK), BF16),
                pltpu.VMEM(arrived.shape, F32),
            ],
        ),
        out_shape=[
            jax.ShapeDtypeStruct((nblocks // nfeat, grades, BLK), F32),
            jax.ShapeDtypeStruct(arrived.shape, BF16),
        ],
        compiler_params=params(8),
        cost_estimate=cost(nblocks * per * 2 * 64 * BLK**2, 6 * MIB),
        name="logits",
    )(src, counts, me, arrived, own, labels, tiles)


def small_kernel(table, me, returned, dlog, hidden, second, dpre_out, *refs):
    small, (total, dproj, buf) = refs[:-3], refs[-3:]
    group, grades, _ = dlog.shape
    g = pl.program_id(0)
    width = hidden.shape[0]

    @pl.when(g == 0)
    def _():
        total[pl.ds(0, group)] = dlog[...]
        buf[...] = jnp.zeros_like(buf)

        @pl.loop(0, returned.shape[0], unroll=8)
        def _(k):
            at = table[k] - me[0] * group
            at = jnp.where((at >= 0) & (at < group), at, group)
            total[at] += returned[k].astype(F32)

        for b in range(group):
            dproj[:, b * BLK : (b + 1) * BLK] = total[b].astype(BF16)

    active = hidden[...]
    dproj_b = dproj[...]
    dpre = jnp.where(active > 0, dot(second[...], dproj_b, NN), 0.0)
    dpre_out[...] = dpre.astype(BF16)
    buf[pl.ds(0, grades), :] = dot(dproj_b, active, NT)
    part = dpre[:, :BLK]
    for i in range(1, dpre.shape[1] // BLK):
        part += dpre[:, i * BLK : (i + 1) * BLK]
    buf[pl.ds(grades, 8), :] = jnp.broadcast_to(
        jnp.sum(part.T, axis=0, keepdims=True), (8, width)
    )
    for k, out in enumerate(small):

        @pl.when(g == k)
        def _():
            out[...] = buf[...]


def small_gradients(table, me, returned, dlog, hidden, second, nfeat):
    hid, nodes = hidden.shape
    group, grades, _ = dlog.shape
    width = hid // nfeat
    turn = lambda g, m: lax.rem(m[0] + nfeat - g, nfeat)
    whole3 = lambda g, t, m: (0, 0, 0)
    small = jax.ShapeDtypeStruct((32, width), F32)
    return pl.pallas_call(
        small_kernel,
        grid_spec=pltpu.PrefetchScalarGridSpec(
            num_scalar_prefetch=2,
            grid=(nfeat,),
            in_specs=[
                pl.BlockSpec(returned.shape, whole3),
                pl.BlockSpec(dlog.shape, whole3),
                pl.BlockSpec((width, nodes), lambda g, t, m: (turn(g, m), 0)),
                pl.BlockSpec((width, grades), lambda g, t, m: (turn(g, m), 0)),
            ],
            out_specs=[pl.BlockSpec((width, nodes), lambda g, t, m: (turn(g, m), 0))]
            + [pl.BlockSpec(small.shape, lambda g, t, m: (0, 0))] * nfeat,
            scratch_shapes=[
                pltpu.VMEM((group + 1, grades, BLK), F32),
                pltpu.VMEM((grades, nodes), BF16),
                pltpu.VMEM(small.shape, F32),
            ],
        ),
        out_shape=[jax.ShapeDtypeStruct((hid, nodes), BF16)] + [small] * nfeat,
        compiler_params=params(16),
        cost_estimate=cost(2 * nodes * hid * 256, 4 * MIB),
        name="small_gradients",
    )(table, me, returned, dlog, hidden, second)


def big_kernel(me, dpre, *refs):
    pieces, out = refs[:-1], refs[-1]
    nfeat = len(pieces) // 2
    for k in range(nfeat):

        @pl.when(pl.program_id(0) == k)
        def _():
            both = jnp.concatenate([pieces[k][...], pieces[nfeat + k][...]], 1)
            grad = dot(dpre[...], both, NN).astype(BF16)
            out[...] = grad.reshape(out.shape)


def big_gradient(me, dpre, pieces, parts):
    nfeat = len(pieces) // 2
    hid, nodes = dpre.shape
    whole = lambda g, m: (0, 0)
    return pl.pallas_call(
        big_kernel,
        grid_spec=pltpu.PrefetchScalarGridSpec(
            num_scalar_prefetch=1,
            grid=(nfeat,),
            in_specs=[pl.BlockSpec((hid, nodes), whole)]
            + [pl.BlockSpec((nodes, BLK), whole)] * (2 * nfeat),
            out_specs=pl.BlockSpec(
                (parts, 1, hid // parts, 2 * BLK),
                lambda g, m: (0, lax.rem(m[0] + nfeat - g, nfeat), 0, 0),
            ),
        ),
        out_shape=pltpu.HBM((parts, nfeat, hid // parts, 2 * BLK), BF16),
        compiler_params=params(24),
        cost_estimate=cost(2 * nodes * hid * hid, 6 * MIB),
        name="big_gradient",
    )(me, dpre, *pieces)


def total_kernel(arrived, out, acc):
    g = pl.program_id(0)

    @pl.when(g == 0)
    def _():
        acc[...] = jnp.zeros_like(acc)

    total = arrived[0].astype(F32)
    for i in range(1, arrived.shape[0]):
        total += arrived[i].astype(F32)
    acc[...] += total

    @pl.when(g == pl.num_programs(0) - 1)
    def _():
        out[...] = acc[...]


def total(arrived):
    n, cols, rows = arrived.shape
    step = n // 8
    return pl.pallas_call(
        total_kernel,
        grid=(n // step,),
        in_specs=[pl.BlockSpec((step, cols, rows), lambda g: (g, 0, 0))],
        out_specs=pl.BlockSpec((cols, rows), lambda g: (0, 0)),
        out_shape=jax.ShapeDtypeStruct((cols, rows), F32),
        scratch_shapes=[pltpu.VMEM((cols, rows), F32)],
        compiler_params=params(8),
        cost_estimate=cost(0, 2 * MIB),
        name="total",
    )(arrived)


def shards(features, pair_count, send_blocks, tile_src, tiles, labels, w_first, b_first, w_second):
    nblocks = tile_src.shape[0]
    parts = lax.axis_size("nodes")
    nfeat = lax.axis_size("feat")
    slots = send_blocks.shape[2]
    grades = w_second.shape[1]
    hid = w_first.shape[1]
    axis = lax.axis_index("feat").astype(jnp.int32)
    me = axis.reshape(1)
    table = send_blocks.reshape(parts * slots)
    src = tile_src.reshape(-1)
    counts = pair_count.reshape(-1)

    def ahead(x, k):
        return lax.ppermute(x, "feat", [(i, (i + k) % nfeat) for i in range(nfeat)])

    def swap(x):
        shaped = x.reshape(parts, slots, *x.shape[1:])
        moved = lax.all_to_all(shaped, "nodes", split_axis=0, concat_axis=0, tiled=True)
        return moved.reshape(x.shape)

    arrived = [swap(pick(features, table, c)) for c in range(2)]

    flat = w_first.T
    weights = [flat] + [ahead(flat, k) for k in range(1, nfeat)]
    consts = jnp.concatenate(
        [w_second.T.astype(F32), jnp.broadcast_to(b_first[None], (8, b_first.shape[0]))], 0
    )
    turned = [consts] + [ahead(consts, k) for k in range(1, nfeat)]
    ring = jnp.stack([turned[k] for k in (3, 2, 1, 0, 3, 2, 1)])
    ordered = lax.dynamic_slice_in_dim(ring, nfeat - 1 - axis, nfeat, 0)
    second_t = ordered[:, :grades].transpose(1, 0, 2).reshape(grades, hid).astype(BF16)
    bias = ordered[:, grades].reshape(hid, 1)
    second = second_t.T

    staged = stage(tiles)
    others = (2, 1, 3)
    make = functools.partial(aggregate, src, counts, me)
    first = [None] * nfeat
    *sent, first[0] = make(arrived[0], staged, features, 0, nfeat, others + (0,))
    for k, piece in zip(others, sent):
        first[k] = ahead(piece, k)
    last = [None] * nfeat
    for k, piece in zip(others, make(arrived[1], staged, features, 1, nfeat, others)):
        last[k] = ahead(piece, k)
    (last[0],) = make(arrived[1], staged, features, 1, nfeat, (0,))
    pre = early(last[0], first, weights, bias)
    hidden, proj = dense(pre, last[1:], weights[1:], second_t)

    projs = [proj] + [ahead(proj, k) for k in range(1, nfeat)]
    own, send = spread(table, me, projs)
    scale = 1.0 / math.sqrt(nblocks * BLK * parts)
    dlog, slotsum = logits_back(
        src, counts, me, swap(send), own, labels.reshape(nblocks, 1, BLK), staged, scale, nfeat
    )
    dpre, *small = small_gradients(table, me, swap(slotsum), dlog, hidden, second, nfeat)
    rest = small[0]
    for k in range(1, nfeat):
        rest = rest + ahead(small[k], nfeat - k)
    everyone = lax.all_gather(rest, "nodes", axis=0)
    big = big_gradient(me, dpre, first + last, parts)
    moved = lax.all_to_all(
        big.reshape(parts * nfeat, *big.shape[2:]),
        ("nodes", "feat"),
        split_axis=0,
        concat_axis=0,
        tiled=True,
    )
    rest = total(everyone)
    return total(moved).T, rest[grades], rest[:grades].T


def solution(mesh):
    placed = (
        P("nodes", "feat"),
        P("nodes", None),
        P("nodes", None, None),
        P("nodes", None),
        P("nodes", None, None, None),
        P("nodes"),
        P("feat", None),
        P("feat"),
        P("feat", None),
    )
    return jax.shard_map(
        shards,
        mesh=mesh,
        in_specs=placed,
        out_specs=(P("feat", "nodes"), P("feat"), P("feat", None)),
        check_vma=False,
    )
```

time: 220 us -> 244 us (1.11); the launches traced: 216 us -> 243 us
  between operations: 0.93 us -> 14.5 us
  starting transfers between devices: 52.2 us -> 41.6 us
  blocking collectives: 30.1 us -> 39.6 us
  waiting for transfers between devices: 77.5 us -> 85.7 us
  local copies, waits for them, and re-layouts: 18.2 us -> 22.7 us
    all_gather x0 -> x1, waiting for transfers between devices: none -> 43.6 us  [shards(): everyone = lax.all_gather(rest, 'nodes', axis=0)]
    ppermute x18, waiting for transfers between devices: 36.8 us -> 11.1 us  [ahead(): return lax.ppermute(x, 'feat', [(i, (i + k) % nfeat) for i in range(nfeat)])]
    ppermute x5 -> x0, starting transfers between devices: 9.66 us -> none  [shards(): lax.ppermute(rest, 'nodes', [(i, i ^ bit) for i in range(parts)])]
    all_to_all x2, blocking collectives: 30.1 us -> 39.6 us  [swap(): lax.all_to_all(shaped, 'nodes', split_axis=0, concat_axis=0, tiled=True)]
    ppermute x5 -> x0, waiting for transfers between devices: 6.26 us -> none  [shards(): lax.ppermute(rest, 'nodes', [(i, i ^ bit) for i in range(parts)])]
    pallas_call x4 -> x8, Pallas kernels: 22.7 us -> 28.3 us  [the longest x3 10.9 us: aggregate(): pl.pallas_call(functools.partial(agg_kernel, which, group, nfeat), grid_s...]
    unnamed x45 -> x56, local copies, waits for them, and re-layouts: 14.1 us -> 18.4 us
    pallas_call x1, Pallas kernels: 7.87 us -> 3.92 us  [logits_back(): pl.pallas_call(functools.partial(logits_kernel, scale), grid_spec=pltpu.P...]
  transfers between devices with their start and end apart: 26 -> 22, of which waited for: 16 -> 10; matrix products, arithmetic and copies ran while one was open for 2% -> 2% of each run, Pallas kernels for 6% -> 9%
where the time goes in v2:
time: 244 us; the launch traced here: 243 us
  waiting for transfers between devices  85.7 us (35%)
  starting transfers between devices  41.6 us (17%)
  blocking collectives  39.6 us (16%)
  Pallas kernels  38 us (16%)
  local copies, waits for them, and re-layouts  22.7 us (9%)
  between operations  14.5 us (6%)
    all_gather x1, waiting for transfers between devices, shards(): everyone = lax.all_gather(rest, 'nodes', axis=0)  43.6 us
    all_to_all x2, blocking collectives, swap(): lax.all_to_all(shaped, 'nodes', split_axis=0, concat_axis=0, tiled=True)  39.6 us
    all_to_all x2, waiting for transfers between devices, swap(): lax.all_to_all(shaped, 'nodes', split_axis=0, concat_axis=0, tiled=True)  31 us
    ppermute x18, starting transfers between devices, ahead(): return lax.ppermute(x, 'feat', [(i, (i + k) % nfeat) for i in range(nfeat)])  20.7 us
    unnamed x56, local copies, waits for them, and re-layouts  18.4 us
    all_to_all x2, starting transfers between devices, swap(): lax.all_to_all(shaped, 'nodes', split_axis=0, concat_axis=0, tiled=True)  15.2 us
    ppermute x18, waiting for transfers between devices, ahead(): return lax.ppermute(x, 'feat', [(i, (i + k) % nfeat) for i in range(nfeat)])  11.1 us
    pallas_call x3, Pallas kernels, aggregate(): pl.pallas_call(functools.partial(agg_kernel, which, group, nfeat), grid_s...  10.9 us
  transfers between devices with their start and end apart: 22, of which 10 were waited for; matrix products, arithmetic and copies ran while one was open for 2% of the time, Pallas kernels for 9%

profile of v2, /device:TPU:1, one launch (start us, length us, event | category | flops | bytes accessed | tf_op | source)
XLA Modules:
  0.0 242.7 jit_solution(1593417932402845929)
XLA Ops:
  7.2 0.8 copy.17
  7.9 0.1 reshape.52.table
  8.0 1.6 copy-done.5
  9.6 1.9 pick.3
  11.5 9.8 %all-to-all-start.1 = ((bf16[32,2,128,128]{3,2,1,0:T(8,128)(2,1)}), bf16[32,2,128,128]{3,2,1,0:T(8,128)(2,1)}, u32[]{:S(2)}, u32[]{:S(2)}) async-start(bf16[32,2,128,128]{3,2,1,0:T(8,128)(2,1)} %bitcast.50), calls=%async_computation.1 | async-start | bytes 4194304 | tf_op jit(solution)/shard_map/all_to_all | solution.py:448
  21.4 1.9 pick.2
  23.3 26.4 %all-to-all-done.1 = bf16[32,2,128,128]{3,2,1,0:T(8,128)(2,1)} async-done(((bf16[32,2,128,128]{3,2,1,0:T(8,128)(2,1)}), bf16[32,2,128,128]{3,2,1,0:T(8,128)(2,1)}, u32[]{:S(2)}, u32[]{:S(2)}) %all-to-all-start.1) | async-done | bytes 2097184 | tf_op jit(solution)/shard_map/all_to_all | solution.py:448
  49.7 5.4 %all-to-all-start = ((bf16[32,2,128,128]{3,2,1,0:T(8,128)(2,1)}), bf16[32,2,128,128]{3,2,1,0:T(8,128)(2,1)}, u32[]{:S(2)}, u32[]{:S(2)}) async-start(bf16[32,2,128,128]{3,2,1,0:T(8,128)(2,1)} %bitcast.49), calls=%async_computation | async-start | bytes 4194304 | tf_op jit(solution)/shard_map/all_to_all | solution.py:448
  55.2 2.5 %collective-permute-start.6 = (f32[24,256]{1,0:T(8,128)S(1)}, f32[24,256]{1,0:T(8,128)S(1)}, u32[]{:S(2)}, u32[]{:S(2)}) collective-permute-start(f32[24,256]{1,0:T(8,128)S(1)} %pad_maximum_fusion), channel_id=1, source_target_pairs={{0,3},{1,0},{2,1},{3,2},{4,7},{5,4},{6,5},{7,6},{8,11},{9,8},{10,9... | collective-permute-start | bytes 73736 | tf_op jit(solution)/shard_map/ppermute | solution.py:444
  57.7 1.7 collective-permute-start.7
  59.5 1.0 copy.19
  60.5 0.9 collective-permute-start.5
  61.4 2.4 collective-permute-start.4
  63.8 0.1 copy.18
  63.9 0.1 reshape.53.src
  64.0 2.2 copy-done.7
  66.2 0.3 stage.1.tiles
  66.5 2.0 copy-done
  68.6 2.2 copy-done.1
  70.8 4.3 %aggregate.4 = (bf16[1024,128]{1,0:T(8,128)(2,1)}, bf16[1024,128]{1,0:T(8,128)(2,1)}, bf16[1024,128]{1,0:T(8,128)(2,1)}, bf16[1024,128]{1,0:T(8,128)(2,1)S(1)}) custom-call(s32[128]{0:T(128)S(1)} %reshape.53.src, s32[32]{0:T(128)S(1)} %bitcast.45, s32[1]{0:T(128)} %bitcast.me, bf16[64,128,128]{2,1,0:T(8,128)(2,1)} %bitcast.5.arrived, ...), custom_call_target="tpu_custom_call" | custom-call | flops 536870912 | bytes 8388608 | tf_op jit(solution)/shard_map/aggregate/pallas_call | solution.py:102
  75.1 0.3 collective-permute-start
  75.4 3.6 %collective-permute-start.1 = (bf16[1024,128]{1,0:T(8,128)(2,1)}, bf16[1024,128]{1,0:T(8,128)(2,1)}, u32[]{:S(2)}, u32[]{:S(2)}) collective-permute-start(bf16[1024,128]{1,0:T(8,128)(2,1)} %get-tuple-element.23), channel_id=1, source_target_pairs={{0,2},{1,3},{2,0},{3,1},{4,6},{5,7},{6,4},{7,5},{8,10},{9,11},{10,... | collective-permute-start | bytes 786440 | tf_op jit(solution)/shard_map/ppermute | solution.py:444
  79.0 4.6 %all-to-all-done = bf16[32,2,128,128]{3,2,1,0:T(8,128)(2,1)} async-done(((bf16[32,2,128,128]{3,2,1,0:T(8,128)(2,1)}), bf16[32,2,128,128]{3,2,1,0:T(8,128)(2,1)}, u32[]{:S(2)}, u32[]{:S(2)}) %all-to-all-start) | async-done | bytes 2097184 | tf_op jit(solution)/shard_map/all_to_all | solution.py:448
  83.5 2.2 copy-done.2
  85.7 4.0 %aggregate.5 = (bf16[1024,128]{1,0:T(8,128)(2,1)}, bf16[1024,128]{1,0:T(8,128)(2,1)}, bf16[1024,128]{1,0:T(8,128)(2,1)}) custom-call(s32[128]{0:T(128)S(1)} %reshape.53.src, s32[32]{0:T(128)S(1)} %bitcast.46, s32[1]{0:T(128)} %bitcast.me, bf16[64,128,128]{2,1,0:T(8,128)(2,1)} %bitcast.3.arrived, bf16[32,4,128,128]{3,2,1,0:T(8,128)(2,1)S(1)} %copy-done.2, ...), custom_call_target="tpu_custom_call" | custom-call | flops 402653184 | bytes 8388608 | tf_op jit(solution)/shard_map/aggregate/pallas_call | solution.py:102
  89.7 1.2 collective-permute-start.9
  90.9 2.5 %collective-permute-start.10 = (bf16[1024,128]{1,0:T(8,128)(2,1)}, bf16[1024,128]{1,0:T(8,128)(2,1)}, u32[]{:S(2)}, u32[]{:S(2)}) collective-permute-start(bf16[1024,128]{1,0:T(8,128)(2,1)} %get-tuple-element.26), channel_id=1, source_target_pairs={{0,2},{1,3},{2,0},{3,1},{4,6},{5,7},{6,4},{7,5},{8,10},{9,11},{10,... | collective-permute-start | bytes 786440 | tf_op jit(solution)/shard_map/ppermute | solution.py:444
  93.4 2.4 %collective-permute-done.p1.refs_1_ = bf16[1024,128]{1,0:T(8,128)(2,1)} collective-permute-done((bf16[1024,128]{1,0:T(8,128)(2,1)}, bf16[1024,128]{1,0:T(8,128)(2,1)}, u32[]{:S(2)}, u32[]{:S(2)}) %collective-permute-start) | collective-permute-done | bytes 262176 | tf_op jit(solution)/shard_map/ppermute | solution.py:444
  95.8 0.8 fusion
  96.6 0.2 copy.21
  96.8 0.1 copy.22.second
  96.9 0.8 constant_dynamic-slice_fusion
  97.7 1.0 copy.20.bias
  98.7 2.2 copy-done.3
  100.9 2.6 %aggregate.3.own.refs_4_ = bf16[1024,128]{1,0:T(8,128)(2,1)S(1)} custom-call(s32[128]{0:T(128)S(1)} %reshape.53.src, s32[32]{0:T(128)S(1)} %bitcast.47, s32[1]{0:T(128)} %bitcast.me, bf16[64,128,128]{2,1,0:T(8,128)(2,1)} %bitcast.3.arrived, bf16[32,4,128,128]{3,2,1,0:T(8,128)(2,1)S(1)} %copy-done.3, bf16[4096,256]{1,0:T(8,128)(2,1)S(1)} %copy-done.6), custom_call_target="tpu_custom_call" | custom-call | flops 134217728 | bytes 8388608 | tf_op jit(solution)/shard_map/aggregate/pallas_call | solution.py:102
  103.6 4.5 %early.1.pre = f32[1024,1024]{1,0:T(8,128)S(1)} custom-call(bf16[1024,128]{1,0:T(8,128)(2,1)S(1)} %aggregate.3.own.refs_4_, bf16[1024,128]{1,0:T(8,128)(2,1)S(1)} %copy-done.13, bf16[1024,128]{1,0:T(8,128)(2,1)} %collective-permute-done.p1.refs_1_, bf16[1024,128]{1,0:T(8,128)(2,1)} %collective-permute-done.1.p2.refs_2_, ...), custom_call_target="tpu_custom_call" | custom-call | flops 1342177280 | bytes 7340032 | tf_op jit(solution)/shard_map/early/pallas_call | solution.py:132
  108.1 4.7 %dense.1 = (bf16[1024,1024]{1,0:T(8,128)(2,1)S(1)}, f32[8,16,128]{2,1,0:T(8,128)S(1)}) custom-call(f32[1024,1024]{1,0:T(8,128)S(1)} %early.1.pre, bf16[1024,128]{1,0:T(8,128)(2,1)} %collective-permute-done.9.p1.refs_5_, bf16[1024,128]{1,0:T(8,128)(2,1)} %collective-permute-done.10.p2.refs_6_, bf16[1024,128]{1,0:T(8,128)(2,1)} %collective-permute-done.11.p3.refs_7_, ...), custom_call_target="tpu_custom_call" | custom-call | flops 805306368 | bytes 9437184 | tf_op jit(solution)/shard_map/dense/pallas_call | solution.py:161
  112.8 2.7 %collective-permute-start.14 = (f32[8,16,128]{2,1,0:T(8,128)S(1)}, f32[8,16,128]{2,1,0:T(8,128)S(1)}, u32[]{:S(2)}, u32[]{:S(2)}) collective-permute-start(f32[8,16,128]{2,1,0:T(8,128)S(1)} %get-tuple-element.28.p0), channel_id=1, source_target_pairs={{0,3},{1,0},{2,1},{3,2},{4,7},{5,4},{6,5},{7,6},{8,11},{9,8},{10,9... | collective-permute-start | bytes 196616 | tf_op jit(solution)/shard_map/ppermute | solution.py:444
  115.6 0.5 collective-permute-start.13
  116.1 0.1 collective-permute-start.12
  116.2 1.2 collective-permute-done.14.p3
  117.5 2.8 %collective-permute-done.13.p2 = f32[8,16,128]{2,1,0:T(8,128)S(1)} collective-permute-done((f32[8,16,128]{2,1,0:T(8,128)S(1)}, f32[8,16,128]{2,1,0:T(8,128)S(1)}, u32[]{:S(2)}, u32[]{:S(2)}) %collective-permute-start.13) | collective-permute-done | bytes 65568 | tf_op jit(solution)/shard_map/ppermute | solution.py:444
  120.2 0.7 collective-permute-done.12.p1
  120.9 0.7 spread.1
  121.6 27.1 %all_to_all.25 = f32[32,2,16,128]{3,2,1,0:T(8,128)S(1)} all-to-all(f32[32,2,16,128]{3,2,1,0:T(8,128)S(1)} %bitcast.42), channel_id=1, replica_groups=mesh['nodes'=32,'feat'=4] {'nodes'}, dimensions={0} | all-to-all | bytes 1048576 | tf_op jit(solution)/shard_map/all_to_all | solution.py:448
  148.6 3.9 %logits.1 = (f32[8,16,128]{2,1,0:T(8,128)S(1)}, bf16[64,16,128]{2,1,0:T(8,128)(2,1)S(1)}) custom-call(s32[128]{0:T(128)S(1)} %reshape.53.src, s32[32]{0:T(128)S(1)} %bitcast.48, s32[1]{0:T(128)} %bitcast.me, f32[64,16,128]{2,1,0:T(8,128)S(1)} %bitcast.39, f32[32,16,128]{2,1,0:T(8,128)S(1)} %get-tuple-element.30.own, s32[32,1,128]{2,1,0:T(1,128)S(1)} %bitcast.44, ...), custom_call_target="tpu_custom_call" | custom-call | flops 268435456 | bytes 6291456 | tf_op jit(solution)/shard_map/logits/pallas_call | solution.py:267
  152.6 12.5 %all_to_all.26 = bf16[32,2,16,128]{3,2,1,0:T(8,128)(2,1)S(1)} all-to-all(bf16[32,2,16,128]{3,2,1,0:T(8,128)(2,1)S(1)} %bitcast.43), channel_id=1, replica_groups=mesh['nodes'=32,'feat'=4] {'nodes'}, dimensions={0} | all-to-all | bytes 524288 | tf_op jit(solution)/shard_map/all_to_all | solution.py:448
  165.1 2.7 %small_gradients.1 = (bf16[1024,1024]{1,0:T(8,128)(2,1)S(1)}, f32[32,256]{1,0:T(8,128)S(1)}, f32[32,256]{1,0:T(8,128)S(1)}, f32[32,256]{1,0:T(8,128)S(1)}, f32[32,256]{1,0:T(8,128)S(1)}) custom-call(s32[64]{0:T(128)S(1)} %reshape.52.table, s32[1]{0:T(128)} %bitcast.me, bf16[64,16,128]{2,1,0:T(8,128)(2,1)S(1)} %bitcast.40, ...), custom_call_target="tpu_custom_call" | custom-call | flops 536870912 | bytes 4194304 | tf_op jit(solution)/shard_map/small_gradients/pallas_call | solution.py:336
  167.9 1.3 copy-done.17
  169.2 1.6 collective-permute-start.15
  170.8 0.6 collective-permute-start.16
  171.4 0.6 collective-permute-done.15
  172.0 3.1 %collective-permute-done.16 = f32[32,256]{1,0:T(8,128)S(1)} collective-permute-done((f32[32,256]{1,0:T(8,128)S(1)}, f32[32,256]{1,0:T(8,128)S(1)}, u32[]{:S(2)}, u32[]{:S(2)}) %collective-permute-start.16) | collective-permute-done | bytes 32800 | tf_op jit(solution)/shard_map/ppermute | solution.py:444
  175.1 0.4 collective-permute-done.17
  175.4 0.6 add_add_fusion
  176.1 1.6 copy-done.18
  177.7 5.2 %big_gradient.1 = bf16[32,4,32,256]{3,2,1,0:T(8,128)(2,1)} custom-call(s32[1]{0:T(128)} %bitcast.me, bf16[1024,1024]{1,0:T(8,128)(2,1)S(1)} %copy-done.18, bf16[1024,128]{1,0:T(8,128)(2,1)S(1)} %copy-done.14, bf16[1024,128]{1,0:T(8,128)(2,1)} %collective-permute-done.p1.refs_1_, bf16[1024,128]{1,0:T(8,128)(2,1)} %collective-permute-done.1.p2.refs_2_, ...), custom_call_target="tpu_custom_call" | custom-call | flops 2147483648 | bytes 6291456 | tf_op jit(solution)/shard_map/big_gradient/pallas_call | solution.py:378
  182.9 5.6 %all-to-all-start.4 = ((bf16[128,32,256]{2,1,0:T(8,128)(2,1)}), bf16[128,32,256]{2,1,0:T(8,128)(2,1)S(1)}, u32[]{:S(2)}, u32[]{:S(2)}) async-start(bf16[128,32,256]{2,1,0:T(8,128)(2,1)} %bitcast.51), calls=%async_computation.4 | async-start | bytes 4194304 | tf_op jit(solution)/shard_map/all_to_all | solution.py:491
  188.6 43.6 %all-gather.3.cloned.1.call-done = f32[1024,256]{1,0:T(8,128)} async-done(((f32[32,256]{1,0:T(8,128)}), f32[1024,256]{1,0:T(8,128)}) %all-gather.3.cloned.1.call-update) | async-done | bytes 1048592 | tf_op jit(solution)/shard_map/all_gather | solution.py:489
  232.1 1.2 copy-done.11
  233.4 0.2 total.3
  233.6 0.6 slice.17
  234.1 0.6 slice_bitcast_fusion
  234.7 1.1 total.2
  (68 shorter events, 0.2 us)
Async XLA Ops:
  8.0 1.6 copy-start.5
  11.5 9.8 %copy-start.6 = (bf16[4096,256]{1,0:T(8,128)(2,1)S(1)}, bf16[4096,256]{1,0:T(8,128)(2,1)}, u32[]{:S(2)}) copy-start(bf16[4096,256]{1,0:T(8,128)(2,1)} %own.5) | copy-start | bytes 6291460
  11.5 38.2 %all-to-all-start.1 = ((bf16[32,2,128,128]{3,2,1,0:T(8,128)(2,1)}), bf16[32,2,128,128]{3,2,1,0:T(8,128)(2,1)}, u32[]{:S(2)}, u32[]{:S(2)}) async-start(bf16[32,2,128,128]{3,2,1,0:T(8,128)(2,1)} %bitcast.50), calls=%async_computation.1 | async-start | bytes 4194304 | tf_op jit(solution)/shard_map/all_to_all | solution.py:448
  49.7 5.4 %copy-start.21 = (bf16[256,16]{0,1:T(8,128)(2,1)S(1)}, bf16[256,16]{0,1:T(8,128)(2,1)}, u32[]{:S(2)}) copy-start(bf16[256,16]{0,1:T(8,128)(2,1)} %param.17) | copy-start | bytes 24580
  49.7 5.5 %copy-start.23 = (f32[256]{0:T(256)S(1)}, f32[256]{0:T(256)}, u32[]{:S(2)}) copy-start(f32[256]{0:T(256)} %param.16) | copy-start | bytes 3076
  49.7 9.8 %copy-start.19 = (bf16[256,1024]{1,0:T(8,128)(2,1)S(1)}, bf16[256,1024]{1,0:T(8,128)(2,1)}, u32[]{:S(2)}) copy-start(bf16[256,1024]{1,0:T(8,128)(2,1)} %param.15) | copy-start | bytes 1572868
  49.7 14.1 %copy-start.22 = (s32[32,4]{0,1:T(4,128)S(1)}, s32[32,4]{0,1:T(4,128)}, u32[]{:S(2)}) copy-start(s32[32,4]{0,1:T(4,128)} %param.12) | copy-start | bytes 1540
  49.7 33.8 %all-to-all-start = ((bf16[32,2,128,128]{3,2,1,0:T(8,128)(2,1)}), bf16[32,2,128,128]{3,2,1,0:T(8,128)(2,1)}, u32[]{:S(2)}, u32[]{:S(2)}) async-start(bf16[32,2,128,128]{3,2,1,0:T(8,128)(2,1)} %bitcast.49), calls=%async_computation | async-start | bytes 4194304 | tf_op jit(solution)/shard_map/all_to_all | solution.py:448
  55.1 177.1 %all-gather.3.cloned.1.call-start = ((), (), s32[]{:S(2)}) async-start(), calls=%async_computation.5 | async-start | bytes 1081344 | tf_op jit(solution)/shard_map/all_gather | solution.py:489
  55.2 13.3 %collective-permute-start.6 = (f32[24,256]{1,0:T(8,128)S(1)}, f32[24,256]{1,0:T(8,128)S(1)}, u32[]{:S(2)}, u32[]{:S(2)}) collective-permute-start(f32[24,256]{1,0:T(8,128)S(1)} %pad_maximum_fusion), channel_id=1, source_target_pairs={{0,3},{1,0},{2,1},{3,2},{4,7},{5,4},{6,5},{7,6},{8,11},{9,8},{10,9... | collective-permute-start | bytes 73736 | tf_op jit(solution)/shard_map/ppermute | solution.py:444
  57.7 10.8 %collective-permute-start.8 = (f32[24,256]{1,0:T(8,128)S(1)}, f32[24,256]{1,0:T(8,128)S(1)}, u32[]{:S(2)}, u32[]{:S(2)}) collective-permute-start(f32[24,256]{1,0:T(8,128)S(1)} %pad_maximum_fusion), channel_id=1, source_target_pairs={{0,1},{1,2},{2,3},{3,0},{4,5},{5,6},{6,7},{7,4},{8,9},{9,10},{10,1... | collective-permute-start | bytes 73736 | tf_op jit(solution)/shard_map/ppermute | solution.py:444
  57.7 10.7 %collective-permute-start.7 = (f32[24,256]{1,0:T(8,128)S(1)}, f32[24,256]{1,0:T(8,128)S(1)}, u32[]{:S(2)}, u32[]{:S(2)}) collective-permute-start(f32[24,256]{1,0:T(8,128)S(1)} %pad_maximum_fusion), channel_id=1, source_target_pairs={{0,2},{1,3},{2,0},{3,1},{4,6},{5,7},{6,4},{7,5},{8,10},{9,11},{10,... | collective-permute-start | bytes 73736 | tf_op jit(solution)/shard_map/ppermute | solution.py:444
  60.5 18.5 %collective-permute-start.5 = (bf16[1024,256]{1,0:T(8,128)(2,1)}, bf16[1024,256]{1,0:T(8,128)(2,1)S(1)}, u32[]{:S(2)}, u32[]{:S(2)}) collective-permute-start(bf16[1024,256]{1,0:T(8,128)(2,1)} %bitcast.6.w0), channel_id=1, source_target_pairs={{0,3},{1,0},{2,1},{3,2},{4,7},{5,4},{6,5},{7,6},{8,11},{9,8},{10,9... | collective-permute-start | bytes 1572872 | tf_op jit(solution)/shard_map/ppermute | solution.py:444
  61.4 28.2 %collective-permute-start.4 = (bf16[1024,256]{1,0:T(8,128)(2,1)}, bf16[1024,256]{1,0:T(8,128)(2,1)S(1)}, u32[]{:S(2)}, u32[]{:S(2)}) collective-permute-start(bf16[1024,256]{1,0:T(8,128)(2,1)} %bitcast.6.w0), channel_id=1, source_target_pairs={{0,2},{1,3},{2,0},{3,1},{4,6},{5,7},{6,4},{7,5},{8,10},{9,11},{10,... | collective-permute-start | bytes 1572872 | tf_op jit(solution)/shard_map/ppermute | solution.py:444
  64.0 2.2 copy-start.7
  66.2 2.4 copy-start.16
  66.5 2.0 copy-start
  68.5 22.4 %collective-permute-start.3 = (bf16[1024,256]{1,0:T(8,128)(2,1)}, bf16[1024,256]{1,0:T(8,128)(2,1)}, u32[]{:S(2)}, u32[]{:S(2)}) collective-permute-start(bf16[1024,256]{1,0:T(8,128)(2,1)} %bitcast.6.w0), channel_id=1, source_target_pairs={{0,1},{1,2},{2,3},{3,0},{4,5},{5,6},{6,7},{7,4},{8,9},{9,10},{10,1... | collective-permute-start | bytes 1572872 | tf_op jit(solution)/shard_map/ppermute | solution.py:444
  68.6 2.2 copy-start.1
  75.1 14.6 %copy-start.12 = (bf16[1024,128]{1,0:T(8,128)(2,1)}, bf16[1024,128]{1,0:T(8,128)(2,1)S(1)}, u32[]{:S(2)}) copy-start(bf16[1024,128]{1,0:T(8,128)(2,1)S(1)} %get-tuple-element.21.p0.refs_0_) | copy-start | bytes 786436
  75.1 20.7 %collective-permute-start = (bf16[1024,128]{1,0:T(8,128)(2,1)}, bf16[1024,128]{1,0:T(8,128)(2,1)}, u32[]{:S(2)}, u32[]{:S(2)}) collective-permute-start(bf16[1024,128]{1,0:T(8,128)(2,1)} %get-tuple-element.22), channel_id=1, source_target_pairs={{0,1},{1,2},{2,3},{3,0},{4,5},{5,6},{6,7},{7,4},{8,9},{9,10},{10,1... | collective-permute-start | bytes 786440 | tf_op jit(solution)/shard_map/ppermute | solution.py:444
  75.4 3.6 %copy-start.20 = (f32[7,24,256]{2,1,0:T(8,128)}, f32[7,24,256]{2,1,0:T(8,128)S(1)}, u32[]{:S(2)}) copy-start(f32[7,24,256]{2,1,0:T(8,128)S(1)} %bitcast_dynamic-update-slice_fusion.2) | copy-start | bytes 516100
  75.4 28.1 %collective-permute-start.1 = (bf16[1024,128]{1,0:T(8,128)(2,1)}, bf16[1024,128]{1,0:T(8,128)(2,1)}, u32[]{:S(2)}, u32[]{:S(2)}) collective-permute-start(bf16[1024,128]{1,0:T(8,128)(2,1)} %get-tuple-element.23), channel_id=1, source_target_pairs={{0,2},{1,3},{2,0},{3,1},{4,6},{5,7},{6,4},{7,5},{8,10},{9,11},{10,... | collective-permute-start | bytes 786440 | tf_op jit(solution)/shard_map/ppermute | solution.py:444
  79.0 24.6 %collective-permute-start.2 = (bf16[1024,128]{1,0:T(8,128)(2,1)}, bf16[1024,128]{1,0:T(8,128)(2,1)}, u32[]{:S(2)}, u32[]{:S(2)}) collective-permute-start(bf16[1024,128]{1,0:T(8,128)(2,1)} %get-tuple-element.24), channel_id=1, source_target_pairs={{0,3},{1,0},{2,1},{3,2},{4,7},{5,4},{6,5},{7,6},{8,11},{9,8},{10,9... | collective-permute-start | bytes 786440 | tf_op jit(solution)/shard_map/ppermute | solution.py:444
  83.5 2.2 copy-start.2
  89.7 18.4 %collective-permute-start.9 = (bf16[1024,128]{1,0:T(8,128)(2,1)}, bf16[1024,128]{1,0:T(8,128)(2,1)}, u32[]{:S(2)}, u32[]{:S(2)}) collective-permute-start(bf16[1024,128]{1,0:T(8,128)(2,1)} %get-tuple-element.25), channel_id=1, source_target_pairs={{0,1},{1,2},{2,3},{3,0},{4,5},{5,6},{6,7},{7,4},{8,9},{9,10},{10,1... | collective-permute-start | bytes 786440 | tf_op jit(solution)/shard_map/ppermute | solution.py:444
  90.9 17.2 %collective-permute-start.10 = (bf16[1024,128]{1,0:T(8,128)(2,1)}, bf16[1024,128]{1,0:T(8,128)(2,1)}, u32[]{:S(2)}, u32[]{:S(2)}) collective-permute-start(bf16[1024,128]{1,0:T(8,128)(2,1)} %get-tuple-element.26), channel_id=1, source_target_pairs={{0,2},{1,3},{2,0},{3,1},{4,6},{5,7},{6,4},{7,5},{8,10},{9,11},{10,... | collective-permute-start | bytes 786440 | tf_op jit(solution)/shard_map/ppermute | solution.py:444
  95.8 12.3 %collective-permute-start.11 = (bf16[1024,128]{1,0:T(8,128)(2,1)}, bf16[1024,128]{1,0:T(8,128)(2,1)}, u32[]{:S(2)}, u32[]{:S(2)}) collective-permute-start(bf16[1024,128]{1,0:T(8,128)(2,1)} %get-tuple-element.27), channel_id=1, source_target_pairs={{0,3},{1,0},{2,1},{3,2},{4,7},{5,4},{6,5},{7,6},{8,11},{9,8},{10,9... | collective-permute-start | bytes 786440 | tf_op jit(solution)/shard_map/ppermute | solution.py:444
  98.7 2.2 copy-start.3
  100.9 2.6 %copy-start.8 = (f32[1024,1]{1,0:T(8,128)S(1)}, f32[1024,1]{1,0:T(8,128)}, u32[]{:S(2)}) copy-start(f32[1024,1]{1,0:T(8,128)} %copy.20.bias) | copy-start | bytes 12292
  100.9 2.6 %copy-start.13 = (bf16[1024,128]{1,0:T(8,128)(2,1)S(1)}, bf16[1024,128]{1,0:T(8,128)(2,1)}, u32[]{:S(2)}) copy-start(bf16[1024,128]{1,0:T(8,128)(2,1)} %copy-done.12) | copy-start | bytes 786436
  103.5 4.5 %copy-start.9 = (bf16[1024,128]{1,0:T(8,128)(2,1)}, bf16[1024,128]{1,0:T(8,128)(2,1)S(1)}, u32[]{:S(2)}) copy-start(bf16[1024,128]{1,0:T(8,128)(2,1)S(1)} %aggregate.3.own.refs_4_) | copy-start | bytes 786436
  108.0 40.6 %copy-start.15 = (s32[4096]{0:T(1024)S(1)}, s32[4096]{0:T(1024)}, u32[]{:S(2)}) copy-start(s32[4096]{0:T(1024)} %param.14) | copy-start | bytes 49156
  108.1 40.5 %copy-start.4 = (bf16[32,4,128,128]{3,2,1,0:T(8,128)(2,1)S(1)}, bf16[32,4,128,128]{3,2,1,0:T(8,128)(2,1)}, u32[]{:S(2)}) copy-start(bf16[32,4,128,128]{3,2,1,0:T(8,128)(2,1)} %copy-done) | copy-start | bytes 12582916
  112.8 4.6 %collective-permute-start.14 = (f32[8,16,128]{2,1,0:T(8,128)S(1)}, f32[8,16,128]{2,1,0:T(8,128)S(1)}, u32[]{:S(2)}, u32[]{:S(2)}) collective-permute-start(f32[8,16,128]{2,1,0:T(8,128)S(1)} %get-tuple-element.28.p0), channel_id=1, source_target_pairs={{0,3},{1,0},{2,1},{3,2},{4,7},{5,4},{6,5},{7,6},{8,11},{9,8},{10,9... | collective-permute-start | bytes 196616 | tf_op jit(solution)/shard_map/ppermute | solution.py:444
  115.6 4.7 %collective-permute-start.13 = (f32[8,16,128]{2,1,0:T(8,128)S(1)}, f32[8,16,128]{2,1,0:T(8,128)S(1)}, u32[]{:S(2)}, u32[]{:S(2)}) collective-permute-start(f32[8,16,128]{2,1,0:T(8,128)S(1)} %get-tuple-element.28.p0), channel_id=1, source_target_pairs={{0,2},{1,3},{2,0},{3,1},{4,6},{5,7},{6,4},{7,5},{8,10},{9,11},{10,... | collective-permute-start | bytes 196616 | tf_op jit(solution)/shard_map/ppermute | solution.py:444
  116.1 4.8 %collective-permute-start.12 = (f32[8,16,128]{2,1,0:T(8,128)S(1)}, f32[8,16,128]{2,1,0:T(8,128)S(1)}, u32[]{:S(2)}, u32[]{:S(2)}) collective-permute-start(f32[8,16,128]{2,1,0:T(8,128)S(1)} %get-tuple-element.28.p0), channel_id=1, source_target_pairs={{0,1},{1,2},{2,3},{3,0},{4,5},{5,6},{6,7},{7,4},{8,9},{9,10},{10,1... | collective-permute-start | bytes 196616 | tf_op jit(solution)/shard_map/ppermute | solution.py:444
  152.5 23.6 %copy-start.10 = (bf16[1024,128]{1,0:T(8,128)(2,1)S(1)}, bf16[1024,128]{1,0:T(8,128)(2,1)}, u32[]{:S(2)}) copy-start(bf16[1024,128]{1,0:T(8,128)(2,1)} %copy-done.9) | copy-start | bytes 786436
  152.5 23.6 %copy-start.14 = (bf16[1024,128]{1,0:T(8,128)(2,1)S(1)}, bf16[1024,128]{1,0:T(8,128)(2,1)}, u32[]{:S(2)}) copy-start(bf16[1024,128]{1,0:T(8,128)(2,1)} %copy-done.12) | copy-start | bytes 786436
  167.9 1.4 copy-start.17
  169.2 2.8 %collective-permute-start.15 = (f32[32,256]{1,0:T(8,128)S(1)}, f32[32,256]{1,0:T(8,128)S(1)}, u32[]{:S(2)}, u32[]{:S(2)}) collective-permute-start(f32[32,256]{1,0:T(8,128)S(1)} %get-tuple-element.36), channel_id=1, source_target_pairs={{0,3},{1,0},{2,1},{3,2},{4,7},{5,4},{6,5},{7,6},{8,11},{9,8},{10,9... | collective-permute-start | bytes 98312 | tf_op jit(solution)/shard_map/ppermute | solution.py:444
  170.8 4.3 %collective-permute-start.16 = (f32[32,256]{1,0:T(8,128)S(1)}, f32[32,256]{1,0:T(8,128)S(1)}, u32[]{:S(2)}, u32[]{:S(2)}) collective-permute-start(f32[32,256]{1,0:T(8,128)S(1)} %get-tuple-element.37), channel_id=1, source_target_pairs={{0,2},{1,3},{2,0},{3,1},{4,6},{5,7},{6,4},{7,5},{8,10},{9,11},{10,... | collective-permute-start | bytes 98312 | tf_op jit(solution)/shard_map/ppermute | solution.py:444
  171.4 4.0 %collective-permute-start.17 = (f32[32,256]{1,0:T(8,128)S(1)}, f32[32,256]{1,0:T(8,128)S(1)}, u32[]{:S(2)}, u32[]{:S(2)}) collective-permute-start(f32[32,256]{1,0:T(8,128)S(1)} %get-tuple-element.38), channel_id=1, source_target_pairs={{0,1},{1,2},{2,3},{3,0},{4,5},{5,6},{6,7},{7,4},{8,9},{9,10},{10,1... | collective-permute-start | bytes 98312 | tf_op jit(solution)/shard_map/ppermute | solution.py:444
  176.1 1.6 copy-start.18
  182.9 51.8 %all-to-all-start.4 = ((bf16[128,32,256]{2,1,0:T(8,128)(2,1)}), bf16[128,32,256]{2,1,0:T(8,128)(2,1)S(1)}, u32[]{:S(2)}, u32[]{:S(2)}) async-start(bf16[128,32,256]{2,1,0:T(8,128)(2,1)} %bitcast.51), calls=%async_computation.4 | async-start | bytes 4194304 | tf_op jit(solution)/shard_map/all_to_all | solution.py:491
  232.1 1.2 copy-start.11
Sparse Core Ops, SparseCore 0:
  176.2 55.8 all-gather.2

commit v3 on v2

--- a/solution.py
+++ b/solution.py
@@ -26,6 +26,10 @@
 
 def dot(a, b, dims):
     return lax.dot_general(a, b, dims, preferred_element_type=F32)
+
+
+def in_hbm(x):
+    return pltpu.with_memory_space_constraint(x, pltpu.HBM)
 
 
 def pick_kernel(chunk, table, features, out, sem):
@@ -56,115 +60,93 @@
         compiler_params=params(4),
         cost_estimate=cost(0, 4 * MIB),
         name="pick",
-    )(table, features)
-
-
-def stage_kernel(x, out, sem):
-    copy = pltpu.make_async_copy(x, out, sem)
-    copy.start()
-    copy.wait()
-
-
-def stage(x):
-    return pl.pallas_call(
-        stage_kernel,
-        in_specs=[pl.BlockSpec(memory_space=pltpu.HBM)],
-        out_specs=pl.BlockSpec(memory_space=pltpu.VMEM),
-        out_shape=pltpu.VMEM(x.shape, x.dtype),
-        scratch_shapes=[pltpu.SemaphoreType.DMA],
-        compiler_params=params(4),
-        cost_estimate=cost(0, x.size * 2),
-        name="stage",
-    )(x)
-
-
-def agg_kernel(which, group, nfeat, src, counts, me, arrived, tiles, own, *outs):
-    per = tiles.shape[1]
-    for k, out in zip(which, outs):
-        first = lax.rem(me[0] + k, nfeat) * group
+    )(table, in_hbm(features))
+
+
+def agg_kernel(which, chunk, nfeat, src, counts, me, arrived_hbm, tiles_hbm, features, *refs):
+    outs, (arrived, tiles, own, sems) = refs[: len(which)], refs[len(which) :]
+    group, per = tiles.shape[1:3]
+    moves = [pltpu.make_async_copy(arrived_hbm, arrived, sems.at[0])]
+    firsts = [lax.rem(me[0] + k, nfeat) * group for k in which]
+    for i, first in enumerate(firsts):
+        rows = pl.ds(pl.multiple_of(first * BLK, BLK), group * BLK)
+        moves.append(
+            pltpu.make_async_copy(tiles_hbm.at[pl.ds(first, group)], tiles.at[i], sems.at[1 + 2 * i])
+        )
+        moves.append(
+            pltpu.make_async_copy(
+                features.at[rows, pl.ds(chunk * BLK, BLK)], own.at[i], sems.at[2 + 2 * i]
+            )
+        )
+    for move in moves:
+        move.start()
+    moves[0].wait()
+    for i, (first, out) in enumerate(zip(firsts, outs)):
+        moves[1 + 2 * i].wait()
+        moves[2 + 2 * i].wait()
         for b in range(group):
             rows, weights = [], []
             for t in range(per):
                 slot = src[(first + b) * per + t]
                 live = lax.rem(slot, 2) < counts[lax.div(slot, 2)]
                 rows.append(arrived[slot])
-                weights.append(tiles[first + b, t] * jnp.where(live, 1.0, 0.0).astype(BF16))
+                weights.append(tiles[i, b, t] * jnp.where(live, 1.0, 0.0).astype(BF16))
             total = dot(jnp.concatenate(weights, 1), jnp.concatenate(rows, 0), NN)
-            at = pl.ds(pl.multiple_of((first + b) * BLK, BLK), BLK)
-            out[pl.ds(b * BLK, BLK), :] = (own[at, :].astype(F32) + total).astype(BF16)
+            at = pl.ds(b * BLK, BLK)
+            out[at, :] = (own[i, at, :].astype(F32) + total).astype(BF16)
 
 
 def aggregate(src, counts, me, arrived, tiles, features, chunk, nfeat, which):
     nblocks, per = tiles.shape[:2]
     group = nblocks // nfeat
     piece = jax.ShapeDtypeStruct((group * BLK, BLK), BF16)
-    vmem = pl.BlockSpec(memory_space=pltpu.VMEM)
-    return pl.pallas_call(
-        functools.partial(agg_kernel, which, group, nfeat),
+    hbm = pl.BlockSpec(memory_space=pltpu.HBM)
+    return pl.pallas_call(
+        functools.partial(agg_kernel, which, chunk, nfeat),
         grid_spec=pltpu.PrefetchScalarGridSpec(
             num_scalar_prefetch=3,
-            grid=(1,),
-            in_specs=[
-                vmem,
-                vmem,
-                pl.BlockSpec((nblocks * BLK, BLK), lambda g, s, c, m: (0, chunk)),
+            grid=(),
+            in_specs=[hbm] * 3,
+            out_specs=[pl.BlockSpec(memory_space=pltpu.VMEM)] * len(which),
+            scratch_shapes=[
+                pltpu.VMEM(arrived.shape, BF16),
+                pltpu.VMEM((len(which), group, per, BLK, BLK), BF16),
+                pltpu.VMEM((len(which), group * BLK, BLK), BF16),
+                pltpu.SemaphoreType.DMA((1 + 2 * len(which),)),
             ],
-            out_specs=[vmem] * len(which),
         ),
         out_shape=[piece] * len(which),
-        compiler_params=params(12),
+        compiler_params=params(14),
         cost_estimate=cost(len(which) * group * per * 2 * BLK**3, 8 * MIB),
         name="aggregate",
-    )(src, counts, me, arrived, tiles, features)
-
-
-def early_kernel(own, p0, p1, p2, p3, w0, w1, w2, w3, bias, pre):
-    first = jnp.concatenate([p0[...], own[...]], 1)
-    later = jnp.concatenate([p1[...], p2[...], p3[...]], 1)
-    weights = jnp.concatenate([w1[:, :BLK], w2[:, :BLK], w3[:, :BLK]], 1)
-    pre[...] = (bias[...] + dot(w0[...], first, NT)) + dot(weights, later, NT)
-
-
-def early(own, pieces, weights, bias):
-    nodes = own.shape[0]
-    hid, width = weights[0].shape
-    step = 256
-    return pl.pallas_call(
-        early_kernel,
-        grid=(nodes // step,),
-        in_specs=[pl.BlockSpec((step, BLK), lambda g: (g, 0))] * 5
-        + [pl.BlockSpec((hid, width), lambda g: (0, 0))] * 4
-        + [pl.BlockSpec((hid, 1), lambda g: (0, 0))],
-        out_specs=pl.BlockSpec((hid, step), lambda g: (0, g)),
-        out_shape=jax.ShapeDtypeStruct((hid, nodes), F32),
-        compiler_params=params(20),
-        cost_estimate=cost(2 * nodes * hid * 5 * BLK, 7 * MIB),
-        name="early",
-    )(own, *pieces, *weights, bias)
-
-
-def dense_kernel(pre, p1, p2, p3, w1, w2, w3, second, hidden, proj):
-    later = jnp.concatenate([p1[...], p2[...], p3[...]], 1)
-    weights = jnp.concatenate([w1[:, BLK:], w2[:, BLK:], w3[:, BLK:]], 1)
-    hid = jnp.maximum(pre[...] + dot(weights, later, NT), 0.0).astype(BF16)
+    )(src, counts, me, in_hbm(arrived), in_hbm(tiles), in_hbm(features))
+
+
+def dense_kernel(nfeat, *refs):
+    pieces, (weights, bias, second, hidden, proj) = refs[: 2 * nfeat], refs[2 * nfeat :]
+    order = [pieces[i * nfeat + k][...] for k in range(nfeat) for i in range(2)]
+    pre = dot(weights[...], jnp.concatenate(order, 1), NT)
+    hid = jnp.maximum(pre + bias[...], 0.0).astype(BF16)
     hidden[...] = hid
     out = dot(second[...], hid, NN)
     for b in range(proj.shape[0]):
         proj[b] = out[:, b * BLK : (b + 1) * BLK]
 
 
-def dense(pre, pieces, weights, second):
-    hid, nodes = pre.shape
-    width = weights[0].shape[1]
+def dense(pieces, weights, bias, second):
+    nodes, nfeat = pieces[0].shape[0], len(pieces) // 2
+    hid, width = weights.shape
     grades = second.shape[0]
     step = 256
     return pl.pallas_call(
-        dense_kernel,
+        functools.partial(dense_kernel, nfeat),
         grid=(nodes // step,),
-        in_specs=[pl.BlockSpec((hid, step), lambda g: (0, g))]
-        + [pl.BlockSpec((step, BLK), lambda g: (g, 0))] * 3
-        + [pl.BlockSpec((hid, width), lambda g: (0, 0))] * 3
-        + [pl.BlockSpec((grades, hid), lambda g: (0, 0))],
+        in_specs=[pl.BlockSpec((step, BLK), lambda g: (g, 0))] * (2 * nfeat)
+        + [
+            pl.BlockSpec((hid, width), lambda g: (0, 0)),
+            pl.BlockSpec((hid, 1), lambda g: (0, 0)),
+            pl.BlockSpec((grades, hid), lambda g: (0, 0)),
+        ],
         out_specs=[
             pl.BlockSpec((hid, step), lambda g: (0, g)),
             pl.BlockSpec((step // BLK, grades, BLK), lambda g: (g, 0, 0)),
@@ -174,9 +156,9 @@
             jax.ShapeDtypeStruct((nodes // BLK, grades, BLK), F32),
         ],
         compiler_params=params(20),
-        cost_estimate=cost(2 * nodes * hid * 3 * BLK, 9 * MIB),
+        cost_estimate=cost(2 * nodes * hid * width, 7 * MIB),
         name="dense",
-    )(pre, *pieces, *weights, second)
+    )(*pieces, weights, bias, second)
 
 
 def spread_kernel(table, me, p0, p1, p2, p3, whole, out):
@@ -297,7 +279,6 @@
     @pl.when(g == 0)
     def _():
         total[pl.ds(0, group)] = dlog[...]
-        buf[...] = jnp.zeros_like(buf)
 
         @pl.loop(0, returned.shape[0], unroll=8)
         def _(k):
@@ -332,7 +313,7 @@
     width = hid // nfeat
     turn = lambda g, m: lax.rem(m[0] + nfeat - g, nfeat)
     whole3 = lambda g, t, m: (0, 0, 0)
-    small = jax.ShapeDtypeStruct((32, width), F32)
+    small = jax.ShapeDtypeStruct((grades + 8, width), F32)
     return pl.pallas_call(
         small_kernel,
         grid_spec=pltpu.PrefetchScalarGridSpec(
@@ -352,7 +333,7 @@
                 pltpu.VMEM(small.shape, F32),
             ],
         ),
-        out_shape=[jax.ShapeDtypeStruct((hid, nodes), BF16)] + [small] * nfeat,
+        out_shape=[pltpu.HBM((hid, nodes), BF16)] + [small] * nfeat,
         compiler_params=params(16),
         cost_estimate=cost(2 * nodes * hid * 256, 4 * MIB),
         name="small_gradients",
@@ -363,35 +344,32 @@
     pieces, out = refs[:-1], refs[-1]
     nfeat = len(pieces) // 2
     for k in range(nfeat):
-
-        @pl.when(pl.program_id(0) == k)
-        def _():
-            both = jnp.concatenate([pieces[k][...], pieces[nfeat + k][...]], 1)
-            grad = dot(dpre[...], both, NN).astype(BF16)
-            out[...] = grad.reshape(out.shape)
+        owner = lax.rem(me[0] + nfeat - k, nfeat)
+        both = jnp.concatenate([pieces[k][...], pieces[nfeat + k][...]], 1)
+        grad = dot(dpre[...], both, NN).astype(BF16)
+        out[:, owner] = grad.reshape(out.shape[0], out.shape[2], out.shape[3])
 
 
 def big_gradient(me, dpre, pieces, parts):
     nfeat = len(pieces) // 2
     hid, nodes = dpre.shape
-    whole = lambda g, m: (0, 0)
+    steps = 2
     return pl.pallas_call(
         big_kernel,
         grid_spec=pltpu.PrefetchScalarGridSpec(
             num_scalar_prefetch=1,
-            grid=(nfeat,),
-            in_specs=[pl.BlockSpec((hid, nodes), whole)]
-            + [pl.BlockSpec((nodes, BLK), whole)] * (2 * nfeat),
+            grid=(steps,),
+            in_specs=[pl.BlockSpec((hid // steps, nodes), lambda g, m: (g, 0))]
+            + [pl.BlockSpec((nodes, BLK), lambda g, m: (0, 0))] * (2 * nfeat),
             out_specs=pl.BlockSpec(
-                (parts, 1, hid // parts, 2 * BLK),
-                lambda g, m: (0, lax.rem(m[0] + nfeat - g, nfeat), 0, 0),
+                (parts // steps, nfeat, hid // parts, 2 * BLK), lambda g, m: (g, 0, 0, 0)
             ),
         ),
         out_shape=pltpu.HBM((parts, nfeat, hid // parts, 2 * BLK), BF16),
         compiler_params=params(24),
         cost_estimate=cost(2 * nodes * hid * hid, 6 * MIB),
         name="big_gradient",
-    )(me, dpre, *pieces)
+    )(me, in_hbm(dpre), *pieces)
 
 
 def total_kernel(arrived, out, acc):
@@ -448,10 +426,11 @@
         moved = lax.all_to_all(shaped, "nodes", split_axis=0, concat_axis=0, tiled=True)
         return moved.reshape(x.shape)
 
-    arrived = [swap(pick(features, table, c)) for c in range(2)]
+    arrived = [swap(pick(features, table, 0))]
+    send = pick(features, table, 1)
 
     flat = w_first.T
-    weights = [flat] + [ahead(flat, k) for k in range(1, nfeat)]
+    weights = jnp.concatenate([flat] + [ahead(flat, k) for k in range(1, nfeat)], 1)
     consts = jnp.concatenate(
         [w_second.T.astype(F32), jnp.broadcast_to(b_first[None], (8, b_first.shape[0]))], 0
     )
@@ -462,31 +441,32 @@
     bias = ordered[:, grades].reshape(hid, 1)
     second = second_t.T
 
-    staged = stage(tiles)
+    send, weights, bias, second_t, second = lax.optimization_barrier(
+        (send, weights, bias, second_t, second)
+    )
+    arrived.append(swap(send))
     others = (2, 1, 3)
     make = functools.partial(aggregate, src, counts, me)
     first = [None] * nfeat
-    *sent, first[0] = make(arrived[0], staged, features, 0, nfeat, others + (0,))
+    *sent, first[0] = make(arrived[0], tiles, features, 0, nfeat, others + (0,))
     for k, piece in zip(others, sent):
         first[k] = ahead(piece, k)
     last = [None] * nfeat
-    for k, piece in zip(others, make(arrived[1], staged, features, 1, nfeat, others)):
+    for k, piece in zip(others, make(arrived[1], tiles, features, 1, nfeat, others)):
         last[k] = ahead(piece, k)
-    (last[0],) = make(arrived[1], staged, features, 1, nfeat, (0,))
-    pre = early(last[0], first, weights, bias)
-    hidden, proj = dense(pre, last[1:], weights[1:], second_t)
+    (last[0],) = make(arrived[1], tiles, features, 1, nfeat, (0,))
+    hidden, proj = dense(first + last, weights, bias, second_t)
 
     projs = [proj] + [ahead(proj, k) for k in range(1, nfeat)]
     own, send = spread(table, me, projs)
     scale = 1.0 / math.sqrt(nblocks * BLK * parts)
     dlog, slotsum = logits_back(
-        src, counts, me, swap(send), own, labels.reshape(nblocks, 1, BLK), staged, scale, nfeat
+        src, counts, me, swap(send), own, labels.reshape(nblocks, 1, BLK), tiles, scale, nfeat
     )
     dpre, *small = small_gradients(table, me, swap(slotsum), dlog, hidden, second, nfeat)
     rest = small[0]
     for k in range(1, nfeat):
         rest = rest + ahead(small[k], nfeat - k)
-    everyone = lax.all_gather(rest, "nodes", axis=0)
     big = big_gradient(me, dpre, first + last, parts)
     moved = lax.all_to_all(
         big.reshape(parts * nfeat, *big.shape[2:]),
@@ -495,7 +475,13 @@
         concat_axis=0,
         tiled=True,
     )
-    rest = total(everyone)
+    for group in ((1, 2, 3, 4, 5, 6, 7), (8, 16, 24)):
+        terms = [rest] + [
+            lax.ppermute(rest, "nodes", [(i, i ^ d) for i in range(parts)]) for d in group
+        ]
+        while len(terms) > 1:
+            terms = [a + b for a, b in zip(terms[::2], terms[1::2])]
+        (rest,) = terms
     return total(moved).T, rest[grades], rest[:grades].T
 
 

time: 244 us -> 322 us (1.32)
  Pallas kernels: 38 us -> 163 us
  waiting for transfers between devices: 85.7 us -> 63.2 us
  local copies, waits for them, and re-layouts: 22.7 us -> 3.82 us
  starting transfers between devices: 41.6 us -> 59.8 us
  between operations: 14.5 us -> 1.02 us
  blocking collectives: 39.6 us -> 28.9 us
    pallas_call x2, Pallas kernels: 3.84 us -> 130 us  [pick(): pl.pallas_call(functools.partial(pick_kernel, chunk), grid_spec=pltpu.Pre...]
    all_gather x1 -> x0, waiting for transfers between devices: 43.6 us -> none  [shards(): everyone = lax.all_gather(rest, 'nodes', axis=0)]
    ppermute x18, waiting for transfers between devices: 11.1 us -> 37.8 us  [ahead(): return lax.ppermute(x, 'feat', [(i, (i + k) % nfeat) for i in range(nfeat)])]
    unnamed x56 -> x24, local copies, waits for them, and re-layouts: 18.4 us -> 1.9 us
    ppermute x0 -> x10, starting transfers between devices: none -> 13 us  [shards(): lax.ppermute(rest, 'nodes', [(i, i ^ d) for i in range(parts)])]
    all_to_all x2, blocking collectives: 39.6 us -> 28.9 us  [swap(): lax.all_to_all(shaped, 'nodes', split_axis=0, concat_axis=0, tiled=True)]
    all_to_all x2, waiting for transfers between devices: 31 us -> 20.3 us  [swap(): lax.all_to_all(shaped, 'nodes', split_axis=0, concat_axis=0, tiled=True)]
    ppermute x0 -> x10, waiting for transfers between devices: none -> 5.03 us  [shards(): lax.ppermute(rest, 'nodes', [(i, i ^ d) for i in range(parts)])]
  transfers between devices with their start and end apart: 22 -> 31, of which waited for: 10 -> 13; matrix products, arithmetic and copies ran while one was open for 2% -> 1% of each run, Pallas kernels for 9% -> 24%
where the time goes in v3:
time: 322 us; the launch traced here: 321 us
  Pallas kernels  163 us (51%)
  waiting for transfers between devices  63.2 us (20%)
  starting transfers between devices  59.8 us (19%)
  blocking collectives  28.9 us (9%)
  local copies, waits for them, and re-layouts  3.82 us (1%)
    pallas_call x2, Pallas kernels, pick(): pl.pallas_call(functools.partial(pick_kernel, chunk), grid_spec=pltpu.Pre...  130 us
    ppermute x18, waiting for transfers between devices, ahead(): return lax.ppermute(x, 'feat', [(i, (i + k) % nfeat) for i in range(nfeat)])  37.8 us
    all_to_all x2, blocking collectives, swap(): lax.all_to_all(shaped, 'nodes', split_axis=0, concat_axis=0, tiled=True)  28.9 us
    ppermute x18, starting transfers between devices, ahead(): return lax.ppermute(x, 'feat', [(i, (i + k) % nfeat) for i in range(nfeat)])  22.7 us
    all_to_all x2, waiting for transfers between devices, swap(): lax.all_to_all(shaped, 'nodes', split_axis=0, concat_axis=0, tiled=True)  20.3 us
    all_to_all x2, starting transfers between devices, swap(): lax.all_to_all(shaped, 'nodes', split_axis=0, concat_axis=0, tiled=True)  19.8 us
    ppermute x10, starting transfers between devices, shards(): lax.ppermute(rest, 'nodes', [(i, i ^ d) for i in range(parts)])  13 us
    pallas_call x3, Pallas kernels, aggregate(): pl.pallas_call(functools.partial(agg_kernel, which, chunk, nfeat), grid_s...  12.6 us
  transfers between devices with their start and end apart: 31, of which 13 were waited for; matrix products, arithmetic and copies ran while one was open for 1% of the time, Pallas kernels for 24%

profile of v3, /device:TPU:1, one launch (start us, length us, event | category | flops | bytes accessed | tf_op | source)
XLA Modules:
  0.0 321.4 jit_solution(377615015418617399)
XLA Ops:
  0.6 0.8 copy.17
  1.4 0.1 reshape.52.table
  1.5 65.2 %pick.2 = bf16[64,128,128]{2,1,0:T(8,128)(2,1)} custom-call(s32[64]{0:T(128)S(1)} %reshape.52.table, bf16[4096,256]{1,0:T(8,128)(2,1)} %features.9), custom_call_target="tpu_custom_call" | custom-call | bytes 4194304 | tf_op jit(solution)/shard_map/pick/pallas_call | solution.py:50
  66.7 9.8 %all-to-all-start = ((bf16[32,2,128,128]{3,2,1,0:T(8,128)(2,1)}), bf16[32,2,128,128]{3,2,1,0:T(8,128)(2,1)}, u32[]{:S(2)}, u32[]{:S(2)}) async-start(bf16[32,2,128,128]{3,2,1,0:T(8,128)(2,1)} %bitcast.47), calls=%async_computation | async-start | bytes 4194304 | tf_op jit(solution)/shard_map/all_to_all | solution.py:426
  76.6 2.5 collective-permute-start.6
  79.1 0.2 copy.19
  79.3 0.6 collective-permute-start.5
  80.0 0.2 collective-permute-start.4
  80.2 0.7 collective-permute-start.3
  80.9 3.6 %collective-permute-start.7 = (f32[24,256]{1,0:T(8,128)S(1)}, f32[24,256]{1,0:T(8,128)S(1)}, u32[]{:S(2)}, u32[]{:S(2)}) collective-permute-start(f32[24,256]{1,0:T(8,128)S(1)} %pad_maximum_fusion.1), channel_id=1, source_target_pairs={{0,2},{1,3},{2,0},{3,1},{4,6},{5,7},{6,4},{7,5},{8,10},{9,11},{10,... | collective-permute-start | bytes 73736 | tf_op jit(solution)/shard_map/ppermute | solution.py:422
  84.5 65.2 %pick.3 = bf16[64,128,128]{2,1,0:T(8,128)(2,1)} custom-call(s32[64]{0:T(128)S(1)} %reshape.52.table, bf16[4096,256]{1,0:T(8,128)(2,1)} %features.9), custom_call_target="tpu_custom_call" | custom-call | bytes 4194304 | tf_op jit(solution)/shard_map/pick/pallas_call | solution.py:50
  149.8 3.8 %collective-permute-done.8 = f32[24,256]{1,0:T(8,128)S(1)} collective-permute-done((f32[24,256]{1,0:T(8,128)S(1)}, f32[24,256]{1,0:T(8,128)S(1)}, u32[]{:S(2)}, u32[]{:S(2)}) %collective-permute-start.8) | collective-permute-done | bytes 24608 | tf_op jit(solution)/shard_map/ppermute | solution.py:422
  153.7 0.2 copy.20
  153.9 0.8 copy-done.4
  154.7 1.5 pad_maximum_fusion.refs_8_
  156.2 10.0 %all-to-all-start.1 = ((bf16[32,2,128,128]{3,2,1,0:T(8,128)(2,1)}), bf16[32,2,128,128]{3,2,1,0:T(8,128)(2,1)}, u32[]{:S(2)}, u32[]{:S(2)}) async-start(bf16[32,2,128,128]{3,2,1,0:T(8,128)(2,1)} %bitcast.48), calls=%async_computation.1 | async-start | bytes 4194304 | tf_op jit(solution)/shard_map/all_to_all | solution.py:426
  166.2 0.1 copy.18
  166.3 0.1 reshape.53.src
  166.4 5.0 %aggregate.3 = (bf16[1024,128]{1,0:T(8,128)(2,1)}, bf16[1024,128]{1,0:T(8,128)(2,1)S(1)}, bf16[1024,128]{1,0:T(8,128)(2,1)}, bf16[1024,128]{1,0:T(8,128)(2,1)S(1)}) custom-call(s32[128]{0:T(128)S(1)} %reshape.53.src, s32[32]{0:T(128)S(1)} %bitcast.43, s32[1]{0:T(128)} %bitcast.me, bf16[64,128,128]{2,1,0:T(8,128)(2,1)} %bitcast.3.arrived_hbm, ...), custom_call_target="tpu_custom_call" | custom-call | flops 536870912 | bytes 8388608 | tf_op jit(solution)/shard_map/aggregate/pallas_call | solution.py:104
  171.6 0.6 collective-permute-start.1
  172.2 2.1 collective-permute-start.2
  174.2 20.3 %all-to-all-done.1 = bf16[32,2,128,128]{3,2,1,0:T(8,128)(2,1)} async-done(((bf16[32,2,128,128]{3,2,1,0:T(8,128)(2,1)}), bf16[32,2,128,128]{3,2,1,0:T(8,128)(2,1)}, u32[]{:S(2)}, u32[]{:S(2)}) %all-to-all-start.1) | async-done | bytes 2097184 | tf_op jit(solution)/shard_map/all_to_all | solution.py:426
  194.6 4.7 %aggregate.5 = (bf16[1024,128]{1,0:T(8,128)(2,1)}, bf16[1024,128]{1,0:T(8,128)(2,1)}, bf16[1024,128]{1,0:T(8,128)(2,1)}) custom-call(s32[128]{0:T(128)S(1)} %reshape.53.src, s32[32]{0:T(128)S(1)} %bitcast.44, s32[1]{0:T(128)} %bitcast.me, bf16[64,128,128]{2,1,0:T(8,128)(2,1)} %bitcast.15.arrived_hbm, bf16[32,4,128,128]{3,2,1,0:T(8,128)(2,1)} %tiles.1, ...), custom_call_target="tpu_custom_call" | custom-call | flops 402653184 | bytes 8388608 | tf_op jit(solution)/shard_map/aggregate/pallas_call | solution.py:104
  199.2 0.1 collective-permute-start.9
  199.3 0.6 collective-permute-start.10
  199.9 2.1 collective-permute-start.11
  202.0 0.2 copy.21.refs_9_
  202.2 0.1 copy.22.refs_10_
  202.3 2.9 aggregate.4.refs_4_
  205.3 8.1 %collective-permute-done.9.refs_5_ = bf16[1024,128]{1,0:T(8,128)(2,1)} collective-permute-done((bf16[1024,128]{1,0:T(8,128)(2,1)}, bf16[1024,128]{1,0:T(8,128)(2,1)}, u32[]{:S(2)}, u32[]{:S(2)}) %collective-permute-start.9) | collective-permute-done | bytes 262176 | tf_op jit(solution)/shard_map/ppermute | solution.py:422
  213.4 0.4 collective-permute-done.11.refs_7_
  213.8 5.4 %dense.1 = (bf16[1024,1024]{1,0:T(8,128)(2,1)S(1)}, f32[8,16,128]{2,1,0:T(8,128)S(1)}) custom-call(bf16[1024,128]{1,0:T(8,128)(2,1)S(1)} %get-tuple-element.26.refs_0_, bf16[1024,128]{1,0:T(8,128)(2,1)S(1)} %collective-permute-done.refs_1_, bf16[1024,128]{1,0:T(8,128)(2,1)} %collective-permute-done.1.refs_2_, ...), custom_call_target="tpu_custom_call" | custom-call | flops 2147483648 | bytes 7340032 | tf_op jit(solution)/shard_map/dense/pallas_call | solution.py:141
  219.1 1.5 collective-permute-start.12
  220.6 2.9 collective-permute-start.13
  223.6 0.5 collective-permute-done.12.p1
  224.0 2.0 collective-permute-done.13.p2
  226.0 1.6 collective-permute-done.14.p3
  227.5 0.7 spread.1
  228.2 16.5 %all_to_all.25 = f32[32,2,16,128]{3,2,1,0:T(8,128)S(1)} all-to-all(f32[32,2,16,128]{3,2,1,0:T(8,128)S(1)} %bitcast.40), channel_id=1, replica_groups=mesh['nodes'=32,'feat'=4] {'nodes'}, dimensions={0} | all-to-all | bytes 1048576 | tf_op jit(solution)/shard_map/all_to_all | solution.py:426
  244.7 3.9 %logits.1 = (f32[8,16,128]{2,1,0:T(8,128)S(1)}, bf16[64,16,128]{2,1,0:T(8,128)(2,1)S(1)}) custom-call(s32[128]{0:T(128)S(1)} %reshape.53.src, s32[32]{0:T(128)S(1)} %bitcast.46, s32[1]{0:T(128)} %bitcast.me, f32[64,16,128]{2,1,0:T(8,128)S(1)} %bitcast.38, f32[32,16,128]{2,1,0:T(8,128)S(1)} %get-tuple-element.39.own, s32[32,1,128]{2,1,0:T(1,128)S(1)} %bitcast.42, ...), custom_call_target="tpu_custom_call" | custom-call | flops 268435456 | bytes 6291456 | tf_op jit(solution)/shard_map/logits/pallas_call | solution.py:249
  248.6 12.4 %all_to_all.26 = bf16[32,2,16,128]{3,2,1,0:T(8,128)(2,1)S(1)} all-to-all(bf16[32,2,16,128]{3,2,1,0:T(8,128)(2,1)S(1)} %bitcast.41), channel_id=1, replica_groups=mesh['nodes'=32,'feat'=4] {'nodes'}, dimensions={0} | all-to-all | bytes 524288 | tf_op jit(solution)/shard_map/all_to_all | solution.py:426
  261.1 3.9 %small_gradients.1 = (bf16[1024,1024]{1,0:T(8,128)(2,1)}, f32[24,256]{1,0:T(8,128)S(1)}, f32[24,256]{1,0:T(8,128)S(1)}, f32[24,256]{1,0:T(8,128)S(1)}, f32[24,256]{1,0:T(8,128)S(1)}) custom-call(s32[64]{0:T(128)S(1)} %reshape.52.table, s32[1]{0:T(128)} %bitcast.me, bf16[64,16,128]{2,1,0:T(8,128)(2,1)S(1)} %bitcast.39, ...), custom_call_target="tpu_custom_call" | custom-call | flops 536870912 | bytes 4194304 | tf_op jit(solution)/shard_map/small_gradients/pallas_call | solution.py:317
  265.0 5.2 %big_gradient.1 = bf16[32,4,32,256]{3,2,1,0:T(8,128)(2,1)} custom-call(s32[1]{0:T(128)} %bitcast.me, bf16[1024,1024]{1,0:T(8,128)(2,1)} %get-tuple-element.44.dpre, bf16[1024,128]{1,0:T(8,128)(2,1)S(1)} %get-tuple-element.26.refs_0_, bf16[1024,128]{1,0:T(8,128)(2,1)S(1)} %collective-permute-done.refs_1_, bf16[1024,128]{1,0:T(8,128)(2,1)} %collective-permute-done.1.refs_2_, ...), custom_call_target="tpu_custom_call" | custom-call | flops 2147483648 | bytes 6291456 | tf_op jit(solution)/shard_map/big_gradient/pallas_call | solution.py:357
  270.2 4.3 %all-to-all-start.4 = ((bf16[128,32,256]{2,1,0:T(8,128)(2,1)}), bf16[128,32,256]{2,1,0:T(8,128)(2,1)S(1)}, u32[]{:S(2)}, u32[]{:S(2)}) async-start(bf16[128,32,256]{2,1,0:T(8,128)(2,1)} %bitcast.49), calls=%async_computation.4 | async-start | bytes 4194304 | tf_op jit(solution)/shard_map/all_to_all | solution.py:471
  274.5 1.5 collective-permute-start.17
  276.0 2.4 collective-permute-start.16
  278.4 1.2 collective-permute-start.15
  279.6 20.2 %collective-permute-done.17 = f32[24,256]{1,0:T(8,128)S(1)} collective-permute-done((f32[24,256]{1,0:T(8,128)S(1)}, f32[24,256]{1,0:T(8,128)S(1)}, u32[]{:S(2)}, u32[]{:S(2)}) %collective-permute-start.17) | collective-permute-done | bytes 24608 | tf_op jit(solution)/shard_map/ppermute | solution.py:422
  299.8 1.3 collective-permute-done.16
  301.1 3.2 collective-permute-start.23
  304.2 0.8 collective-permute-start.24
  305.1 1.7 collective-permute-start.21
  306.8 1.8 collective-permute-start.22
  308.5 1.6 collective-permute-start.20
  310.1 0.3 collective-permute-start.18
  310.4 1.1 collective-permute-done.22
  311.5 0.8 collective-permute-done.20
  312.4 2.9 collective-permute-start.26
  315.3 0.8 collective-permute-start.27
  316.1 0.5 collective-permute-done.26
  316.6 2.5 collective-permute-done.27
  319.2 0.6 slice.17
  319.7 0.6 slice_bitcast_fusion
  320.3 1.1 total.1
  (53 shorter events, 0.3 us)
Async XLA Ops:
  66.7 9.8 %copy-start.5 = (bf16[256,16]{0,1:T(8,128)(2,1)S(1)}, bf16[256,16]{0,1:T(8,128)(2,1)}, u32[]{:S(2)}) copy-start(bf16[256,16]{0,1:T(8,128)(2,1)} %param.17) | copy-start | bytes 24580
  66.7 9.9 %copy-start.7 = (f32[256]{0:T(256)S(1)}, f32[256]{0:T(256)}, u32[]{:S(2)}) copy-start(f32[256]{0:T(256)} %param.16) | copy-start | bytes 3076
  66.7 12.4 %copy-start.3 = (bf16[256,1024]{1,0:T(8,128)(2,1)S(1)}, bf16[256,1024]{1,0:T(8,128)(2,1)}, u32[]{:S(2)}) copy-start(bf16[256,1024]{1,0:T(8,128)(2,1)} %param.15) | copy-start | bytes 1572868
  66.7 89.5 %all-to-all-start = ((bf16[32,2,128,128]{3,2,1,0:T(8,128)(2,1)}), bf16[32,2,128,128]{3,2,1,0:T(8,128)(2,1)}, u32[]{:S(2)}, u32[]{:S(2)}) async-start(bf16[32,2,128,128]{3,2,1,0:T(8,128)(2,1)} %bitcast.47), calls=%async_computation | async-start | bytes 4194304 | tf_op jit(solution)/shard_map/all_to_all | solution.py:426
  76.6 73.1 %collective-permute-start.6 = (f32[24,256]{1,0:T(8,128)S(1)}, f32[24,256]{1,0:T(8,128)S(1)}, u32[]{:S(2)}, u32[]{:S(2)}) collective-permute-start(f32[24,256]{1,0:T(8,128)S(1)} %pad_maximum_fusion.1), channel_id=1, source_target_pairs={{0,3},{1,0},{2,1},{3,2},{4,7},{5,4},{6,5},{7,6},{8,11},{9,8},{10,9... | collective-permute-start | bytes 73736 | tf_op jit(solution)/shard_map/ppermute | solution.py:422
  79.3 74.5 %collective-permute-start.5 = (bf16[1024,256]{1,0:T(8,128)(2,1)S(1)}, bf16[1024,256]{1,0:T(8,128)(2,1)S(1)}, u32[]{:S(2)}, u32[]{:S(2)}) collective-permute-start(bf16[1024,256]{1,0:T(8,128)(2,1)S(1)} %bitcast.50), channel_id=1, source_target_pairs={{0,3},{1,0},{2,1},{3,2},{4,7},{5,4},{6,5},{7,6},{8,11},{9,8},{10,9... | collective-permute-start | bytes 1572872 | tf_op jit(solution)/shard_map/ppermute | solution.py:422
  80.0 73.9 %collective-permute-start.4 = (bf16[1024,256]{1,0:T(8,128)(2,1)S(1)}, bf16[1024,256]{1,0:T(8,128)(2,1)S(1)}, u32[]{:S(2)}, u32[]{:S(2)}) collective-permute-start(bf16[1024,256]{1,0:T(8,128)(2,1)S(1)} %bitcast.51), channel_id=1, source_target_pairs={{0,2},{1,3},{2,0},{3,1},{4,6},{5,7},{6,4},{7,5},{8,10},{9,11},{10,... | collective-permute-start | bytes 1572872 | tf_op jit(solution)/shard_map/ppermute | solution.py:422
  80.2 74.5 %collective-permute-start.3 = (bf16[1024,256]{1,0:T(8,128)(2,1)S(1)}, bf16[1024,256]{1,0:T(8,128)(2,1)}, u32[]{:S(2)}, u32[]{:S(2)}) collective-permute-start(bf16[1024,256]{1,0:T(8,128)(2,1)S(1)} %bitcast.52), channel_id=1, source_target_pairs={{0,1},{1,2},{2,3},{3,0},{4,5},{5,6},{6,7},{7,4},{8,9},{9,10},{10,1... | collective-permute-start | bytes 1572872 | tf_op jit(solution)/shard_map/ppermute | solution.py:422
  80.9 68.9 %collective-permute-start.7 = (f32[24,256]{1,0:T(8,128)S(1)}, f32[24,256]{1,0:T(8,128)S(1)}, u32[]{:S(2)}, u32[]{:S(2)}) collective-permute-start(f32[24,256]{1,0:T(8,128)S(1)} %pad_maximum_fusion.1), channel_id=1, source_target_pairs={{0,2},{1,3},{2,0},{3,1},{4,6},{5,7},{6,4},{7,5},{8,10},{9,11},{10,... | collective-permute-start | bytes 73736 | tf_op jit(solution)/shard_map/ppermute | solution.py:422
  149.7 4.0 %collective-permute-start.8 = (f32[24,256]{1,0:T(8,128)S(1)}, f32[24,256]{1,0:T(8,128)S(1)}, u32[]{:S(2)}, u32[]{:S(2)}) collective-permute-start(f32[24,256]{1,0:T(8,128)S(1)} %pad_maximum_fusion.1), channel_id=1, source_target_pairs={{0,1},{1,2},{2,3},{3,0},{4,5},{5,6},{6,7},{7,4},{8,9},{9,10},{10,1... | collective-permute-start | bytes 73736 | tf_op jit(solution)/shard_map/ppermute | solution.py:422
  153.9 0.8 copy-start.4
  156.2 10.0 %copy-start.6 = (s32[32,4]{0,1:T(4,128)S(1)}, s32[32,4]{0,1:T(4,128)}, u32[]{:S(2)}) copy-start(s32[32,4]{0,1:T(4,128)} %param.12) | copy-start | bytes 1540
  156.2 10.2 %copy-start.2 = (s32[1,32]{1,0:T(1,128)S(1)}, s32[1,32]{1,0:T(1,128)}, u32[]{:S(2)}) copy-start(s32[1,32]{1,0:T(1,128)} %param.10) | copy-start | bytes 388
  156.2 38.4 %all-to-all-start.1 = ((bf16[32,2,128,128]{3,2,1,0:T(8,128)(2,1)}), bf16[32,2,128,128]{3,2,1,0:T(8,128)(2,1)}, u32[]{:S(2)}, u32[]{:S(2)}) async-start(bf16[32,2,128,128]{3,2,1,0:T(8,128)(2,1)} %bitcast.48), calls=%async_computation.1 | async-start | bytes 4194304 | tf_op jit(solution)/shard_map/all_to_all | solution.py:426
  171.5 28.4 %collective-permute-start = (bf16[1024,128]{1,0:T(8,128)(2,1)S(1)}, bf16[1024,128]{1,0:T(8,128)(2,1)S(1)}, u32[]{:S(2)}, u32[]{:S(2)}) collective-permute-start(bf16[1024,128]{1,0:T(8,128)(2,1)S(1)} %get-tuple-element.27), channel_id=1, source_target_pairs={{0,1},{1,2},{2,3},{3,0},{4,5},{5,6},{6,7},{7,4},{8,9},{9,10},{10,1... | collective-permute-start | bytes 786440 | tf_op jit(solution)/shard_map/ppermute | solution.py:422
  171.6 33.7 %collective-permute-start.1 = (bf16[1024,128]{1,0:T(8,128)(2,1)}, bf16[1024,128]{1,0:T(8,128)(2,1)}, u32[]{:S(2)}, u32[]{:S(2)}) collective-permute-start(bf16[1024,128]{1,0:T(8,128)(2,1)} %get-tuple-element.28), channel_id=1, source_target_pairs={{0,2},{1,3},{2,0},{3,1},{4,6},{5,7},{6,4},{7,5},{8,10},{9,11},{10,... | collective-permute-start | bytes 786440 | tf_op jit(solution)/shard_map/ppermute | solution.py:422
  172.2 33.1 %collective-permute-start.2 = (bf16[1024,128]{1,0:T(8,128)(2,1)}, bf16[1024,128]{1,0:T(8,128)(2,1)}, u32[]{:S(2)}, u32[]{:S(2)}) collective-permute-start(bf16[1024,128]{1,0:T(8,128)(2,1)} %get-tuple-element.29), channel_id=1, source_target_pairs={{0,3},{1,0},{2,1},{3,2},{4,7},{5,4},{6,5},{7,6},{8,11},{9,8},{10,9... | collective-permute-start | bytes 786440 | tf_op jit(solution)/shard_map/ppermute | solution.py:422
  199.2 14.2 %collective-permute-start.9 = (bf16[1024,128]{1,0:T(8,128)(2,1)}, bf16[1024,128]{1,0:T(8,128)(2,1)}, u32[]{:S(2)}, u32[]{:S(2)}) collective-permute-start(bf16[1024,128]{1,0:T(8,128)(2,1)} %get-tuple-element.31), channel_id=1, source_target_pairs={{0,1},{1,2},{2,3},{3,0},{4,5},{5,6},{6,7},{7,4},{8,9},{9,10},{10,1... | collective-permute-start | bytes 786440 | tf_op jit(solution)/shard_map/ppermute | solution.py:422
  199.3 14.1 %collective-permute-start.10 = (bf16[1024,128]{1,0:T(8,128)(2,1)}, bf16[1024,128]{1,0:T(8,128)(2,1)}, u32[]{:S(2)}, u32[]{:S(2)}) collective-permute-start(bf16[1024,128]{1,0:T(8,128)(2,1)} %get-tuple-element.32), channel_id=1, source_target_pairs={{0,2},{1,3},{2,0},{3,1},{4,6},{5,7},{6,4},{7,5},{8,10},{9,11},{10,... | collective-permute-start | bytes 786440 | tf_op jit(solution)/shard_map/ppermute | solution.py:422
  199.9 13.8 %collective-permute-start.11 = (bf16[1024,128]{1,0:T(8,128)(2,1)}, bf16[1024,128]{1,0:T(8,128)(2,1)}, u32[]{:S(2)}, u32[]{:S(2)}) collective-permute-start(bf16[1024,128]{1,0:T(8,128)(2,1)} %get-tuple-element.33), channel_id=1, source_target_pairs={{0,3},{1,0},{2,1},{3,2},{4,7},{5,4},{6,5},{7,6},{8,11},{9,8},{10,9... | collective-permute-start | bytes 786440 | tf_op jit(solution)/shard_map/ppermute | solution.py:422
  213.8 31.0 %copy-start = (bf16[32,4,128,128]{3,2,1,0:T(8,128)(2,1)S(1)}, bf16[32,4,128,128]{3,2,1,0:T(8,128)(2,1)}, u32[]{:S(2)}) copy-start(bf16[32,4,128,128]{3,2,1,0:T(8,128)(2,1)} %tiles.1) | copy-start | bytes 12582916
  213.8 31.0 %copy-start.1 = (s32[4096]{0:T(1024)S(1)}, s32[4096]{0:T(1024)}, u32[]{:S(2)}) copy-start(s32[4096]{0:T(1024)} %param.14) | copy-start | bytes 49156
  219.1 4.9 %collective-permute-start.12 = (f32[8,16,128]{2,1,0:T(8,128)S(1)}, f32[8,16,128]{2,1,0:T(8,128)S(1)}, u32[]{:S(2)}, u32[]{:S(2)}) collective-permute-start(f32[8,16,128]{2,1,0:T(8,128)S(1)} %get-tuple-element.37.p0), channel_id=1, source_target_pairs={{0,1},{1,2},{2,3},{3,0},{4,5},{5,6},{6,7},{7,4},{8,9},{9,10},{10,1... | collective-permute-start | bytes 196616 | tf_op jit(solution)/shard_map/ppermute | solution.py:422
  220.6 5.4 %collective-permute-start.13 = (f32[8,16,128]{2,1,0:T(8,128)S(1)}, f32[8,16,128]{2,1,0:T(8,128)S(1)}, u32[]{:S(2)}, u32[]{:S(2)}) collective-permute-start(f32[8,16,128]{2,1,0:T(8,128)S(1)} %get-tuple-element.37.p0), channel_id=1, source_target_pairs={{0,2},{1,3},{2,0},{3,1},{4,6},{5,7},{6,4},{7,5},{8,10},{9,11},{10,... | collective-permute-start | bytes 196616 | tf_op jit(solution)/shard_map/ppermute | solution.py:422
  223.6 4.0 %collective-permute-start.14 = (f32[8,16,128]{2,1,0:T(8,128)S(1)}, f32[8,16,128]{2,1,0:T(8,128)S(1)}, u32[]{:S(2)}, u32[]{:S(2)}) collective-permute-start(f32[8,16,128]{2,1,0:T(8,128)S(1)} %get-tuple-element.37.p0), channel_id=1, source_target_pairs={{0,3},{1,0},{2,1},{3,2},{4,7},{5,4},{6,5},{7,6},{8,11},{9,8},{10,9... | collective-permute-start | bytes 196616 | tf_op jit(solution)/shard_map/ppermute | solution.py:422
  270.2 50.2 %all-to-all-start.4 = ((bf16[128,32,256]{2,1,0:T(8,128)(2,1)}), bf16[128,32,256]{2,1,0:T(8,128)(2,1)S(1)}, u32[]{:S(2)}, u32[]{:S(2)}) async-start(bf16[128,32,256]{2,1,0:T(8,128)(2,1)} %bitcast.49), calls=%async_computation.4 | async-start | bytes 4194304 | tf_op jit(solution)/shard_map/all_to_all | solution.py:471
  274.5 25.2 %collective-permute-start.17 = (f32[24,256]{1,0:T(8,128)S(1)}, f32[24,256]{1,0:T(8,128)S(1)}, u32[]{:S(2)}, u32[]{:S(2)}) collective-permute-start(f32[24,256]{1,0:T(8,128)S(1)} %get-tuple-element.48), channel_id=1, source_target_pairs={{0,1},{1,2},{2,3},{3,0},{4,5},{5,6},{6,7},{7,4},{8,9},{9,10},{10,1... | collective-permute-start | bytes 73736 | tf_op jit(solution)/shard_map/ppermute | solution.py:422
  276.0 25.1 %collective-permute-start.16 = (f32[24,256]{1,0:T(8,128)S(1)}, f32[24,256]{1,0:T(8,128)S(1)}, u32[]{:S(2)}, u32[]{:S(2)}) collective-permute-start(f32[24,256]{1,0:T(8,128)S(1)} %get-tuple-element.47), channel_id=1, source_target_pairs={{0,2},{1,3},{2,0},{3,1},{4,6},{5,7},{6,4},{7,5},{8,10},{9,11},{10,... | collective-permute-start | bytes 73736 | tf_op jit(solution)/shard_map/ppermute | solution.py:422
  278.4 22.7 %collective-permute-start.15 = (f32[24,256]{1,0:T(8,128)S(1)}, f32[24,256]{1,0:T(8,128)S(1)}, u32[]{:S(2)}, u32[]{:S(2)}) collective-permute-start(f32[24,256]{1,0:T(8,128)S(1)} %get-tuple-element.46), channel_id=1, source_target_pairs={{0,3},{1,0},{2,1},{3,2},{4,7},{5,4},{6,5},{7,6},{8,11},{9,8},{10,9... | collective-permute-start | bytes 73736 | tf_op jit(solution)/shard_map/ppermute | solution.py:422
  301.1 7.5 %collective-permute-start.23 = (f32[24,256]{1,0:T(8,128)S(1)}, f32[24,256]{1,0:T(8,128)S(1)}, u32[]{:S(2)}, u32[]{:S(2)}) collective-permute-start(f32[24,256]{1,0:T(8,128)S(1)} %add_add_fusion.2), channel_id=1, source_target_pairs={{0,24},{4,28},{8,16},{12,20},{16,8},{20,12},{24,0},{28,4},{32,56},... | collective-permute-start | bytes 73736 | tf_op jit(solution)/shard_map/ppermute | solution.py:480
  304.2 5.9 %collective-permute-start.24 = (f32[24,256]{1,0:T(8,128)S(1)}, f32[24,256]{1,0:T(8,128)S(1)}, u32[]{:S(2)}, u32[]{:S(2)}) collective-permute-start(f32[24,256]{1,0:T(8,128)S(1)} %add_add_fusion.2), channel_id=1, source_target_pairs={{0,28},{4,24},{8,20},{12,16},{16,12},{20,8},{24,4},{28,0},{32,60},... | collective-permute-start | bytes 73736 | tf_op jit(solution)/shard_map/ppermute | solution.py:480
  305.1 5.3 %collective-permute-start.21 = (f32[24,256]{1,0:T(8,128)S(1)}, f32[24,256]{1,0:T(8,128)S(1)}, u32[]{:S(2)}, u32[]{:S(2)}) collective-permute-start(f32[24,256]{1,0:T(8,128)S(1)} %add_add_fusion.2), channel_id=1, source_target_pairs={{0,16},{4,20},{8,24},{12,28},{16,0},{20,4},{24,8},{28,12},{32,48},... | collective-permute-start | bytes 73736 | tf_op jit(solution)/shard_map/ppermute | solution.py:480
  306.8 4.8 %collective-permute-start.22 = (f32[24,256]{1,0:T(8,128)S(1)}, f32[24,256]{1,0:T(8,128)S(1)}, u32[]{:S(2)}, u32[]{:S(2)}) collective-permute-start(f32[24,256]{1,0:T(8,128)S(1)} %add_add_fusion.2), channel_id=1, source_target_pairs={{0,20},{4,16},{8,28},{12,24},{16,4},{20,0},{24,12},{28,8},{32,52},... | collective-permute-start | bytes 73736 | tf_op jit(solution)/shard_map/ppermute | solution.py:480
  308.5 3.0 collective-permute-start.19
  308.5 3.8 %collective-permute-start.20 = (f32[24,256]{1,0:T(8,128)S(1)}, f32[24,256]{1,0:T(8,128)S(1)}, u32[]{:S(2)}, u32[]{:S(2)}) collective-permute-start(f32[24,256]{1,0:T(8,128)S(1)} %add_add_fusion.2), channel_id=1, source_target_pairs={{0,12},{4,8},{8,4},{12,0},{16,28},{20,24},{24,20},{28,16},{32,44},... | collective-permute-start | bytes 73736 | tf_op jit(solution)/shard_map/ppermute | solution.py:480
  310.1 2.3 collective-permute-start.18
  312.4 4.3 %collective-permute-start.26 = (f32[24,256]{1,0:T(8,128)S(1)}, f32[24,256]{1,0:T(8,128)S(1)}, u32[]{:S(2)}, u32[]{:S(2)}) collective-permute-start(f32[24,256]{1,0:T(8,128)S(1)} %add_add_fusion.1), channel_id=1, source_target_pairs={{0,64},{4,68},{8,72},{12,76},{16,80},{20,84},{24,88},{28,92},{32,9... | collective-permute-start | bytes 73736 | tf_op jit(solution)/shard_map/ppermute | solution.py:480
  315.3 3.9 %collective-permute-start.27 = (f32[24,256]{1,0:T(8,128)S(1)}, f32[24,256]{1,0:T(8,128)S(1)}, u32[]{:S(2)}, u32[]{:S(2)}) collective-permute-start(f32[24,256]{1,0:T(8,128)S(1)} %add_add_fusion.1), channel_id=1, source_target_pairs={{0,96},{4,100},{8,104},{12,108},{16,112},{20,116},{24,120},{28,124... | collective-permute-start | bytes 73736 | tf_op jit(solution)/shard_map/ppermute | solution.py:480
  316.1 3.1 collective-permute-start.25

commit v4 on v3

--- a/solution.py
+++ b/solution.py
@@ -32,17 +32,18 @@
     return pltpu.with_memory_space_constraint(x, pltpu.HBM)
 
 
-def pick_kernel(chunk, table, features, out, sem):
+def pick_kernel(chunk, table, features, out, held, sems):
     slots = out.shape[0]
+    load = pltpu.make_async_copy(features.at[:, pl.ds(chunk * BLK, BLK)], held, sems.at[0])
+    load.start()
+    load.wait()
 
     @pl.loop(0, slots, unroll=8)
     def _(k):
         rows = pl.ds(pl.multiple_of(table[k] * BLK, BLK), BLK)
-        pltpu.make_async_copy(
-            features.at[rows, pl.ds(chunk * BLK, BLK)], out.at[k], sem
-        ).start()
-
-    pltpu.make_async_copy(out, out, sem).wait()
+        pltpu.make_async_copy(held.at[rows], out.at[k], sems.at[1]).start()
+
+    pltpu.make_async_copy(out, out, sems.at[1]).wait()
 
 
 def pick(features, table, chunk):
@@ -54,7 +55,10 @@
             grid=(),
             in_specs=[pl.BlockSpec(memory_space=pltpu.HBM)],
             out_specs=pl.BlockSpec(memory_space=pltpu.HBM),
-            scratch_shapes=[pltpu.SemaphoreType.DMA],
+            scratch_shapes=[
+                pltpu.VMEM((features.shape[0], BLK), BF16),
+                pltpu.SemaphoreType.DMA((2,)),
+            ],
         ),
         out_shape=pltpu.HBM((slots, BLK, BLK), BF16),
         compiler_params=params(4),
@@ -372,12 +376,19 @@
     )(me, in_hbm(dpre), *pieces)
 
 
-def total_kernel(arrived, out, acc):
+def total_kernel(nsmall, arrived, *refs):
+    small, (out, second, bias, acc) = refs[:nsmall], refs[nsmall:]
     g = pl.program_id(0)
 
     @pl.when(g == 0)
     def _():
         acc[...] = jnp.zeros_like(acc)
+        terms = [ref[...] for ref in small]
+        while len(terms) > 1:
+            terms = [a + b for a, b in zip(terms[::2], terms[1::2])]
+        grades = second.shape[0]
+        second[...] = terms[0][:grades]
+        bias[...] = terms[0][grades : grades + 1]
 
     total = arrived[0].astype(F32)
     for i in range(1, arrived.shape[0]):
@@ -389,20 +400,30 @@
         out[...] = acc[...]
 
 
-def total(arrived):
+def total(arrived, small, grades):
     n, cols, rows = arrived.shape
     step = n // 8
-    return pl.pallas_call(
-        total_kernel,
+    whole = lambda g: (0, 0)
+    return pl.pallas_call(
+        functools.partial(total_kernel, len(small)),
         grid=(n // step,),
-        in_specs=[pl.BlockSpec((step, cols, rows), lambda g: (g, 0, 0))],
-        out_specs=pl.BlockSpec((cols, rows), lambda g: (0, 0)),
-        out_shape=jax.ShapeDtypeStruct((cols, rows), F32),
+        in_specs=[pl.BlockSpec((step, cols, rows), lambda g: (g, 0, 0))]
+        + [pl.BlockSpec(small[0].shape, whole)] * len(small),
+        out_specs=[
+            pl.BlockSpec((cols, rows), whole),
+            pl.BlockSpec((grades, rows), whole),
+            pl.BlockSpec((1, rows), whole),
+        ],
+        out_shape=[
+            jax.ShapeDtypeStruct((cols, rows), F32),
+            jax.ShapeDtypeStruct((grades, rows), F32),
+            jax.ShapeDtypeStruct((1, rows), F32),
+        ],
         scratch_shapes=[pltpu.VMEM((cols, rows), F32)],
         compiler_params=params(8),
         cost_estimate=cost(0, 2 * MIB),
         name="total",
-    )(arrived)
+    )(arrived, *small)
 
 
 def shards(features, pair_count, send_blocks, tile_src, tiles, labels, w_first, b_first, w_second):
@@ -468,6 +489,7 @@
     for k in range(1, nfeat):
         rest = rest + ahead(small[k], nfeat - k)
     big = big_gradient(me, dpre, first + last, parts)
+    big, rest = lax.optimization_barrier((big, rest))
     moved = lax.all_to_all(
         big.reshape(parts * nfeat, *big.shape[2:]),
         ("nodes", "feat"),
@@ -475,14 +497,15 @@
         concat_axis=0,
         tiled=True,
     )
+    terms = [rest]
     for group in ((1, 2, 3, 4, 5, 6, 7), (8, 16, 24)):
-        terms = [rest] + [
-            lax.ppermute(rest, "nodes", [(i, i ^ d) for i in range(parts)]) for d in group
-        ]
         while len(terms) > 1:
             terms = [a + b for a, b in zip(terms[::2], terms[1::2])]
-        (rest,) = terms
-    return total(moved).T, rest[grades], rest[:grades].T
+        terms += [
+            lax.ppermute(terms[0], "nodes", [(i, i ^ d) for i in range(parts)]) for d in group
+        ]
+    grad_first, grad_second, grad_bias = total(moved, terms, grades)
+    return grad_first.T, grad_bias.reshape(-1), grad_second.T
 
 
 def solution(mesh):

time: 322 us -> 210 us (0.65)
  Pallas kernels: 163 us -> 39.1 us
  waiting for transfers between devices: 63.2 us -> 69.9 us
  starting transfers between devices: 59.8 us -> 64.6 us
    pallas_call x2, Pallas kernels: 130 us -> 6.24 us  [pick(): pl.pallas_call(functools.partial(pick_kernel, chunk), grid_spec=pltpu.Pre...]
    ppermute x10, waiting for transfers between devices: 5.03 us -> 17.2 us  [shards(): lax.ppermute(terms[0], 'nodes', [(i, i ^ d) for i in range(parts)])]
    ppermute x10, starting transfers between devices: 13 us -> 20.8 us  [shards(): lax.ppermute(terms[0], 'nodes', [(i, i ^ d) for i in range(parts)])]
    ppermute x18, waiting for transfers between devices: 37.8 us -> 32.4 us  [ahead(): return lax.ppermute(x, 'feat', [(i, (i + k) % nfeat) for i in range(nfeat)])]
  transfers between devices with their start and end apart: 31 -> 31, of which waited for: 13 -> 13; matrix products, arithmetic and copies ran while one was open for 1% -> 1% of each run, Pallas kernels for 24% -> 10%
where the time goes in v4:
time: 210 us; the launch traced here: 207 us
  waiting for transfers between devices  69.9 us (33%)
  starting transfers between devices  64.6 us (31%)
  Pallas kernels  39.1 us (19%)
  blocking collectives  28.7 us (14%)
  local copies, waits for them, and re-layouts  2.66 us (1%)
    ppermute x18, waiting for transfers between devices, ahead(): return lax.ppermute(x, 'feat', [(i, (i + k) % nfeat) for i in range(nfeat)])  32.4 us
    all_to_all x2, blocking collectives, swap(): lax.all_to_all(shaped, 'nodes', split_axis=0, concat_axis=0, tiled=True)  28.7 us
    ppermute x18, starting transfers between devices, ahead(): return lax.ppermute(x, 'feat', [(i, (i + k) % nfeat) for i in range(nfeat)])  20.9 us
    ppermute x10, starting transfers between devices, shards(): lax.ppermute(terms[0], 'nodes', [(i, i ^ d) for i in range(parts)])  20.8 us
    all_to_all x2, waiting for transfers between devices, swap(): lax.all_to_all(shaped, 'nodes', split_axis=0, concat_axis=0, tiled=True)  20.3 us
    all_to_all x2, starting transfers between devices, swap(): lax.all_to_all(shaped, 'nodes', split_axis=0, concat_axis=0, tiled=True)  17.4 us
    ppermute x10, waiting for transfers between devices, shards(): lax.ppermute(terms[0], 'nodes', [(i, i ^ d) for i in range(parts)])  17.2 us
    pallas_call x3, Pallas kernels, aggregate(): pl.pallas_call(functools.partial(agg_kernel, which, chunk, nfeat), grid_s...  12.7 us
  transfers between devices with their start and end apart: 31, of which 13 were waited for; matrix products, arithmetic and copies ran while one was open for 1% of the time, Pallas kernels for 10%

profile of v4, /device:TPU:1, one launch (start us, length us, event | category | flops | bytes accessed | tf_op | source)
XLA Modules:
  0.0 207.5 jit_solution(7541438644879823908)
XLA Ops:
  0.6 0.8 copy.17
  1.4 0.1 reshape.55.table
  1.5 3.1 %pick.2 = bf16[64,128,128]{2,1,0:T(8,128)(2,1)} custom-call(s32[64]{0:T(128)S(1)} %reshape.55.table, bf16[4096,256]{1,0:T(8,128)(2,1)} %features.9), custom_call_target="tpu_custom_call" | custom-call | bytes 4194304 | tf_op jit(solution)/shard_map/pick/pallas_call | solution.py:51
  4.7 9.8 %all-to-all-start = ((bf16[32,2,128,128]{3,2,1,0:T(8,128)(2,1)}), bf16[32,2,128,128]{3,2,1,0:T(8,128)(2,1)}, u32[]{:S(2)}, u32[]{:S(2)}) async-start(bf16[32,2,128,128]{3,2,1,0:T(8,128)(2,1)} %bitcast.46), calls=%async_computation | async-start | bytes 4194304 | tf_op jit(solution)/shard_map/all_to_all | solution.py:447
  14.5 2.5 %collective-permute-start.6 = (f32[24,256]{1,0:T(8,128)S(1)}, f32[24,256]{1,0:T(8,128)S(1)}, u32[]{:S(2)}, u32[]{:S(2)}) collective-permute-start(f32[24,256]{1,0:T(8,128)S(1)} %pad_maximum_fusion.1), channel_id=1, source_target_pairs={{0,3},{1,0},{2,1},{3,2},{4,7},{5,4},{6,5},{7,6},{8,11},{9,8},{10,9... | collective-permute-start | bytes 73736 | tf_op jit(solution)/shard_map/ppermute | solution.py:443
  17.1 0.2 copy.19
  17.3 0.6 collective-permute-start.5
  17.9 0.2 collective-permute-start.4
  18.1 0.7 collective-permute-start.3
  18.8 3.6 %collective-permute-start.7 = (f32[24,256]{1,0:T(8,128)S(1)}, f32[24,256]{1,0:T(8,128)S(1)}, u32[]{:S(2)}, u32[]{:S(2)}) collective-permute-start(f32[24,256]{1,0:T(8,128)S(1)} %pad_maximum_fusion.1), channel_id=1, source_target_pairs={{0,2},{1,3},{2,0},{3,1},{4,6},{5,7},{6,4},{7,5},{8,10},{9,11},{10,... | collective-permute-start | bytes 73736 | tf_op jit(solution)/shard_map/ppermute | solution.py:443
  22.4 3.1 %pick.3 = bf16[64,128,128]{2,1,0:T(8,128)(2,1)} custom-call(s32[64]{0:T(128)S(1)} %reshape.55.table, bf16[4096,256]{1,0:T(8,128)(2,1)} %features.9), custom_call_target="tpu_custom_call" | custom-call | bytes 4194304 | tf_op jit(solution)/shard_map/pick/pallas_call | solution.py:51
  25.5 0.1 collective-permute-start.8
  25.6 17.9 %collective-permute-done.7 = f32[24,256]{1,0:T(8,128)S(1)} collective-permute-done((f32[24,256]{1,0:T(8,128)S(1)}, f32[24,256]{1,0:T(8,128)S(1)}, u32[]{:S(2)}, u32[]{:S(2)}) %collective-permute-start.7) | collective-permute-done | bytes 24608 | tf_op jit(solution)/shard_map/ppermute | solution.py:443
  43.5 2.1 collective-permute-done.8
  45.6 0.2 copy.20
  45.8 0.8 copy-done.4
  46.6 1.5 pad_maximum_fusion.refs_8_
  48.1 7.6 %all-to-all-start.1 = ((bf16[32,2,128,128]{3,2,1,0:T(8,128)(2,1)}), bf16[32,2,128,128]{3,2,1,0:T(8,128)(2,1)}, u32[]{:S(2)}, u32[]{:S(2)}) async-start(bf16[32,2,128,128]{3,2,1,0:T(8,128)(2,1)} %bitcast.47), calls=%async_computation.1 | async-start | bytes 4194304 | tf_op jit(solution)/shard_map/all_to_all | solution.py:447
  55.7 0.1 copy.18
  55.8 0.1 reshape.56.src
  56.0 5.0 %aggregate.3 = (bf16[1024,128]{1,0:T(8,128)(2,1)}, bf16[1024,128]{1,0:T(8,128)(2,1)S(1)}, bf16[1024,128]{1,0:T(8,128)(2,1)}, bf16[1024,128]{1,0:T(8,128)(2,1)S(1)}) custom-call(s32[128]{0:T(128)S(1)} %reshape.56.src, s32[32]{0:T(128)S(1)} %bitcast.42, s32[1]{0:T(128)} %bitcast.me, bf16[64,128,128]{2,1,0:T(8,128)(2,1)} %bitcast.3.arrived_hbm, ...), custom_call_target="tpu_custom_call" | custom-call | flops 536870912 | bytes 8388608 | tf_op jit(solution)/shard_map/aggregate/pallas_call | solution.py:108
  61.0 0.1 collective-permute-start
  61.1 1.5 collective-permute-start.1
  62.6 1.2 collective-permute-start.2
  63.7 20.3 %all-to-all-done.1 = bf16[32,2,128,128]{3,2,1,0:T(8,128)(2,1)} async-done(((bf16[32,2,128,128]{3,2,1,0:T(8,128)(2,1)}), bf16[32,2,128,128]{3,2,1,0:T(8,128)(2,1)}, u32[]{:S(2)}, u32[]{:S(2)}) %all-to-all-start.1) | async-done | bytes 2097184 | tf_op jit(solution)/shard_map/all_to_all | solution.py:447
  84.1 4.7 %aggregate.5 = (bf16[1024,128]{1,0:T(8,128)(2,1)}, bf16[1024,128]{1,0:T(8,128)(2,1)}, bf16[1024,128]{1,0:T(8,128)(2,1)}) custom-call(s32[128]{0:T(128)S(1)} %reshape.56.src, s32[32]{0:T(128)S(1)} %bitcast.43, s32[1]{0:T(128)} %bitcast.me, bf16[64,128,128]{2,1,0:T(8,128)(2,1)} %bitcast.15.arrived_hbm, bf16[32,4,128,128]{3,2,1,0:T(8,128)(2,1)} %tiles.1, ...), custom_call_target="tpu_custom_call" | custom-call | flops 402653184 | bytes 8388608 | tf_op jit(solution)/shard_map/aggregate/pallas_call | solution.py:108
  88.8 0.1 collective-permute-start.9
  88.9 1.5 collective-permute-start.10
  90.4 1.2 collective-permute-start.11
  91.5 0.2 copy.21.refs_9_
  91.8 0.1 copy.22.refs_10_
  91.9 2.9 %aggregate.4.refs_4_ = bf16[1024,128]{1,0:T(8,128)(2,1)S(1)} custom-call(s32[128]{0:T(128)S(1)} %reshape.56.src, s32[32]{0:T(128)S(1)} %bitcast.44, s32[1]{0:T(128)} %bitcast.me, bf16[64,128,128]{2,1,0:T(8,128)(2,1)} %bitcast.15.arrived_hbm, bf16[32,4,128,128]{3,2,1,0:T(8,128)(2,1)} %tiles.1, bf16[4096,256]{1,0:T(8,128)(2,1)} %features.9), custom_call_target="tpu_custom_call" | custom-call | flops 134217728 | bytes 8388608 | tf_op jit(solution)/shard_map/aggregate/pallas_call | solution.py:108
  94.8 3.7 %collective-permute-done.9.refs_5_ = bf16[1024,128]{1,0:T(8,128)(2,1)} collective-permute-done((bf16[1024,128]{1,0:T(8,128)(2,1)}, bf16[1024,128]{1,0:T(8,128)(2,1)}, u32[]{:S(2)}, u32[]{:S(2)}) %collective-permute-start.9) | collective-permute-done | bytes 262176 | tf_op jit(solution)/shard_map/ppermute | solution.py:443
  98.5 3.3 %collective-permute-done.10.refs_6_ = bf16[1024,128]{1,0:T(8,128)(2,1)} collective-permute-done((bf16[1024,128]{1,0:T(8,128)(2,1)}, bf16[1024,128]{1,0:T(8,128)(2,1)}, u32[]{:S(2)}, u32[]{:S(2)}) %collective-permute-start.10) | collective-permute-done | bytes 262176 | tf_op jit(solution)/shard_map/ppermute | solution.py:443
  101.8 1.5 collective-permute-done.11.refs_7_
  103.3 5.4 %dense.1 = (bf16[1024,1024]{1,0:T(8,128)(2,1)S(1)}, f32[8,16,128]{2,1,0:T(8,128)S(1)}) custom-call(bf16[1024,128]{1,0:T(8,128)(2,1)S(1)} %get-tuple-element.31.refs_0_, bf16[1024,128]{1,0:T(8,128)(2,1)S(1)} %collective-permute-done.refs_1_, bf16[1024,128]{1,0:T(8,128)(2,1)} %collective-permute-done.1.refs_2_, ...), custom_call_target="tpu_custom_call" | custom-call | flops 2147483648 | bytes 7340032 | tf_op jit(solution)/shard_map/dense/pallas_call | solution.py:145
  108.7 1.5 collective-permute-start.12
  110.2 2.9 %collective-permute-start.13 = (f32[8,16,128]{2,1,0:T(8,128)S(1)}, f32[8,16,128]{2,1,0:T(8,128)S(1)}, u32[]{:S(2)}, u32[]{:S(2)}) collective-permute-start(f32[8,16,128]{2,1,0:T(8,128)S(1)} %get-tuple-element.42.p0), channel_id=1, source_target_pairs={{0,2},{1,3},{2,0},{3,1},{4,6},{5,7},{6,4},{7,5},{8,10},{9,11},{10,... | collective-permute-start | bytes 196616 | tf_op jit(solution)/shard_map/ppermute | solution.py:443
  113.1 0.5 collective-permute-done.12.p1
  113.6 2.0 collective-permute-done.13.p2
  115.5 1.6 collective-permute-done.14.p3
  117.1 0.7 spread.1
  117.8 16.3 %all_to_all.25 = f32[32,2,16,128]{3,2,1,0:T(8,128)S(1)} all-to-all(f32[32,2,16,128]{3,2,1,0:T(8,128)S(1)} %bitcast.39), channel_id=1, replica_groups=mesh['nodes'=32,'feat'=4] {'nodes'}, dimensions={0} | all-to-all | bytes 1048576 | tf_op jit(solution)/shard_map/all_to_all | solution.py:447
  134.1 3.9 %logits.1 = (f32[8,16,128]{2,1,0:T(8,128)S(1)}, bf16[64,16,128]{2,1,0:T(8,128)(2,1)S(1)}) custom-call(s32[128]{0:T(128)S(1)} %reshape.56.src, s32[32]{0:T(128)S(1)} %bitcast.45, s32[1]{0:T(128)} %bitcast.me, f32[64,16,128]{2,1,0:T(8,128)S(1)} %bitcast.37, f32[32,16,128]{2,1,0:T(8,128)S(1)} %get-tuple-element.44.own, s32[32,1,128]{2,1,0:T(1,128)S(1)} %bitcast.41, ...), custom_call_target="tpu_custom_call" | custom-call | flops 268435456 | bytes 6291456 | tf_op jit(solution)/shard_map/logits/pallas_call | solution.py:253
  138.0 12.4 %all_to_all.26 = bf16[32,2,16,128]{3,2,1,0:T(8,128)(2,1)S(1)} all-to-all(bf16[32,2,16,128]{3,2,1,0:T(8,128)(2,1)S(1)} %bitcast.40), channel_id=1, replica_groups=mesh['nodes'=32,'feat'=4] {'nodes'}, dimensions={0} | all-to-all | bytes 524288 | tf_op jit(solution)/shard_map/all_to_all | solution.py:447
  150.4 3.9 %small_gradients.1 = (bf16[1024,1024]{1,0:T(8,128)(2,1)}, f32[24,256]{1,0:T(8,128)S(1)}, f32[24,256]{1,0:T(8,128)S(1)}, f32[24,256]{1,0:T(8,128)S(1)}, f32[24,256]{1,0:T(8,128)S(1)}) custom-call(s32[64]{0:T(128)S(1)} %reshape.55.table, s32[1]{0:T(128)} %bitcast.me, bf16[64,16,128]{2,1,0:T(8,128)(2,1)S(1)} %bitcast.38, ...), custom_call_target="tpu_custom_call" | custom-call | flops 536870912 | bytes 4194304 | tf_op jit(solution)/shard_map/small_gradients/pallas_call | solution.py:321
  154.4 2.6 %collective-permute-start.16 = (f32[24,256]{1,0:T(8,128)S(1)}, f32[24,256]{1,0:T(8,128)S(1)}, u32[]{:S(2)}, u32[]{:S(2)}) collective-permute-start(f32[24,256]{1,0:T(8,128)S(1)} %get-tuple-element.52), channel_id=1, source_target_pairs={{0,2},{1,3},{2,0},{3,1},{4,6},{5,7},{6,4},{7,5},{8,10},{9,11},{10,... | collective-permute-start | bytes 73736 | tf_op jit(solution)/shard_map/ppermute | solution.py:443
  157.0 0.6 collective-permute-start.15
  157.6 5.2 %big_gradient.1 = bf16[32,4,32,256]{3,2,1,0:T(8,128)(2,1)} custom-call(s32[1]{0:T(128)} %bitcast.me, bf16[1024,1024]{1,0:T(8,128)(2,1)} %get-tuple-element.49.dpre, bf16[1024,128]{1,0:T(8,128)(2,1)S(1)} %get-tuple-element.31.refs_0_, bf16[1024,128]{1,0:T(8,128)(2,1)S(1)} %collective-permute-done.refs_1_, bf16[1024,128]{1,0:T(8,128)(2,1)} %collective-permute-done.1.refs_2_, ...), custom_call_target="tpu_custom_call" | custom-call | flops 2147483648 | bytes 6291456 | tf_op jit(solution)/shard_map/big_gradient/pallas_call | solution.py:361
  162.9 5.5 %all-to-all-start.4 = ((bf16[128,32,256]{2,1,0:T(8,128)(2,1)}), bf16[128,32,256]{2,1,0:T(8,128)(2,1)S(1)}, u32[]{:S(2)}, u32[]{:S(2)}) async-start(bf16[128,32,256]{2,1,0:T(8,128)(2,1)} %bitcast.48), calls=%async_computation.4 | async-start | bytes 4194304 | tf_op jit(solution)/shard_map/all_to_all | solution.py:493
  168.4 3.3 %collective-permute-start.23 = (f32[24,256]{1,0:T(8,128)S(1)}, f32[24,256]{1,0:T(8,128)S(1)}, u32[]{:S(2)}, u32[]{:S(2)}) collective-permute-start(f32[24,256]{1,0:T(8,128)S(1)} %add_add_fusion.1), channel_id=1, source_target_pairs={{0,24},{4,28},{8,16},{12,20},{16,8},{20,12},{24,0},{28,4},{32,56},... | collective-permute-start | bytes 73736 | tf_op jit(solution)/shard_map/ppermute | solution.py:505
  171.7 0.7 collective-permute-start.24
  172.4 1.4 collective-permute-start.21
  173.7 1.8 collective-permute-start.22
  175.5 1.9 collective-permute-start.20
  177.4 7.9 %collective-permute-done.24 = f32[24,256]{1,0:T(8,128)S(1)} collective-permute-done((f32[24,256]{1,0:T(8,128)S(1)}, f32[24,256]{1,0:T(8,128)S(1)}, u32[]{:S(2)}, u32[]{:S(2)}) %collective-permute-start.24) | collective-permute-done | bytes 24608 | tf_op jit(solution)/shard_map/ppermute | solution.py:505
  185.2 6.3 %collective-permute-start.18 = (f32[24,256]{1,0:T(8,128)S(1)}, f32[24,256]{1,0:T(8,128)S(1)}, u32[]{:S(2)}, u32[]{:S(2)}) collective-permute-start(f32[24,256]{1,0:T(8,128)S(1)} %add_add_fusion.1), channel_id=1, source_target_pairs={{0,4},{4,0},{8,12},{12,8},{16,20},{20,16},{24,28},{28,24},{32,36},... | collective-permute-start | bytes 73736 | tf_op jit(solution)/shard_map/ppermute | solution.py:505
  191.6 5.6 %collective-permute-done.22 = f32[24,256]{1,0:T(8,128)S(1)} collective-permute-done((f32[24,256]{1,0:T(8,128)S(1)}, f32[24,256]{1,0:T(8,128)S(1)}, u32[]{:S(2)}, u32[]{:S(2)}) %collective-permute-start.22) | collective-permute-done | bytes 24608 | tf_op jit(solution)/shard_map/ppermute | solution.py:505
  197.2 1.9 collective-permute-start.25
  199.0 3.4 %collective-permute-start.26 = (f32[24,256]{1,0:T(8,128)S(1)}, f32[24,256]{1,0:T(8,128)S(1)}, u32[]{:S(2)}, u32[]{:S(2)}) collective-permute-start(f32[24,256]{1,0:T(8,128)S(1)} %add_add_fusion.refs_0_), channel_id=1, source_target_pairs={{0,64},{4,68},{8,72},{12,76},{16,80},{20,84},{24,88},{28,92},{32,9... | collective-permute-start | bytes 73736 | tf_op jit(solution)/shard_map/ppermute | solution.py:505
  202.5 0.2 collective-permute-start.27
  202.7 1.2 collective-permute-done.26.refs_2_
  203.9 2.5 %collective-permute-done.27.refs_3_ = f32[24,256]{1,0:T(8,128)S(1)} collective-permute-done((f32[24,256]{1,0:T(8,128)S(1)}, f32[24,256]{1,0:T(8,128)S(1)}, u32[]{:S(2)}, u32[]{:S(2)}) %collective-permute-start.27) | collective-permute-done | bytes 24608 | tf_op jit(solution)/shard_map/ppermute | solution.py:505
  206.4 1.1 total.1
  (50 shorter events, 0.2 us)
Async XLA Ops:
  4.6 9.8 %copy-start.5 = (bf16[256,16]{0,1:T(8,128)(2,1)S(1)}, bf16[256,16]{0,1:T(8,128)(2,1)}, u32[]{:S(2)}) copy-start(bf16[256,16]{0,1:T(8,128)(2,1)} %param.17) | copy-start | bytes 24580
  4.6 9.9 %copy-start.7 = (f32[256]{0:T(256)S(1)}, f32[256]{0:T(256)}, u32[]{:S(2)}) copy-start(f32[256]{0:T(256)} %param.16) | copy-start | bytes 3076
  4.6 12.4 %copy-start.3 = (bf16[256,1024]{1,0:T(8,128)(2,1)S(1)}, bf16[256,1024]{1,0:T(8,128)(2,1)}, u32[]{:S(2)}) copy-start(bf16[256,1024]{1,0:T(8,128)(2,1)} %param.15) | copy-start | bytes 1572868
  4.7 43.5 %all-to-all-start = ((bf16[32,2,128,128]{3,2,1,0:T(8,128)(2,1)}), bf16[32,2,128,128]{3,2,1,0:T(8,128)(2,1)}, u32[]{:S(2)}, u32[]{:S(2)}) async-start(bf16[32,2,128,128]{3,2,1,0:T(8,128)(2,1)} %bitcast.46), calls=%async_computation | async-start | bytes 4194304 | tf_op jit(solution)/shard_map/all_to_all | solution.py:447
  14.5 11.0 %collective-permute-start.6 = (f32[24,256]{1,0:T(8,128)S(1)}, f32[24,256]{1,0:T(8,128)S(1)}, u32[]{:S(2)}, u32[]{:S(2)}) collective-permute-start(f32[24,256]{1,0:T(8,128)S(1)} %pad_maximum_fusion.1), channel_id=1, source_target_pairs={{0,3},{1,0},{2,1},{3,2},{4,7},{5,4},{6,5},{7,6},{8,11},{9,8},{10,9... | collective-permute-start | bytes 73736 | tf_op jit(solution)/shard_map/ppermute | solution.py:443
  17.3 28.5 %collective-permute-start.5 = (bf16[1024,256]{1,0:T(8,128)(2,1)S(1)}, bf16[1024,256]{1,0:T(8,128)(2,1)S(1)}, u32[]{:S(2)}, u32[]{:S(2)}) collective-permute-start(bf16[1024,256]{1,0:T(8,128)(2,1)S(1)} %bitcast.49), channel_id=1, source_target_pairs={{0,3},{1,0},{2,1},{3,2},{4,7},{5,4},{6,5},{7,6},{8,11},{9,8},{10,9... | collective-permute-start | bytes 1572872 | tf_op jit(solution)/shard_map/ppermute | solution.py:443
  17.9 27.9 %collective-permute-start.4 = (bf16[1024,256]{1,0:T(8,128)(2,1)S(1)}, bf16[1024,256]{1,0:T(8,128)(2,1)S(1)}, u32[]{:S(2)}, u32[]{:S(2)}) collective-permute-start(bf16[1024,256]{1,0:T(8,128)(2,1)S(1)} %bitcast.50), channel_id=1, source_target_pairs={{0,2},{1,3},{2,0},{3,1},{4,6},{5,7},{6,4},{7,5},{8,10},{9,11},{10,... | collective-permute-start | bytes 1572872 | tf_op jit(solution)/shard_map/ppermute | solution.py:443
  18.1 28.5 %collective-permute-start.3 = (bf16[1024,256]{1,0:T(8,128)(2,1)S(1)}, bf16[1024,256]{1,0:T(8,128)(2,1)}, u32[]{:S(2)}, u32[]{:S(2)}) collective-permute-start(bf16[1024,256]{1,0:T(8,128)(2,1)S(1)} %bitcast.51), channel_id=1, source_target_pairs={{0,1},{1,2},{2,3},{3,0},{4,5},{5,6},{6,7},{7,4},{8,9},{9,10},{10,1... | collective-permute-start | bytes 1572872 | tf_op jit(solution)/shard_map/ppermute | solution.py:443
  18.8 24.7 %collective-permute-start.7 = (f32[24,256]{1,0:T(8,128)S(1)}, f32[24,256]{1,0:T(8,128)S(1)}, u32[]{:S(2)}, u32[]{:S(2)}) collective-permute-start(f32[24,256]{1,0:T(8,128)S(1)} %pad_maximum_fusion.1), channel_id=1, source_target_pairs={{0,2},{1,3},{2,0},{3,1},{4,6},{5,7},{6,4},{7,5},{8,10},{9,11},{10,... | collective-permute-start | bytes 73736 | tf_op jit(solution)/shard_map/ppermute | solution.py:443
  25.5 20.0 %collective-permute-start.8 = (f32[24,256]{1,0:T(8,128)S(1)}, f32[24,256]{1,0:T(8,128)S(1)}, u32[]{:S(2)}, u32[]{:S(2)}) collective-permute-start(f32[24,256]{1,0:T(8,128)S(1)} %pad_maximum_fusion.1), channel_id=1, source_target_pairs={{0,1},{1,2},{2,3},{3,0},{4,5},{5,6},{6,7},{7,4},{8,9},{9,10},{10,1... | collective-permute-start | bytes 73736 | tf_op jit(solution)/shard_map/ppermute | solution.py:443
  45.8 0.8 copy-start.4
  48.1 7.6 %copy-start.6 = (s32[32,4]{0,1:T(4,128)S(1)}, s32[32,4]{0,1:T(4,128)}, u32[]{:S(2)}) copy-start(s32[32,4]{0,1:T(4,128)} %param.12) | copy-start | bytes 1540
  48.1 7.8 %copy-start.2 = (s32[1,32]{1,0:T(1,128)S(1)}, s32[1,32]{1,0:T(1,128)}, u32[]{:S(2)}) copy-start(s32[1,32]{1,0:T(1,128)} %param.10) | copy-start | bytes 388
  48.1 35.9 %all-to-all-start.1 = ((bf16[32,2,128,128]{3,2,1,0:T(8,128)(2,1)}), bf16[32,2,128,128]{3,2,1,0:T(8,128)(2,1)}, u32[]{:S(2)}, u32[]{:S(2)}) async-start(bf16[32,2,128,128]{3,2,1,0:T(8,128)(2,1)} %bitcast.47), calls=%async_computation.1 | async-start | bytes 4194304 | tf_op jit(solution)/shard_map/all_to_all | solution.py:447
  61.0 29.4 %collective-permute-start = (bf16[1024,128]{1,0:T(8,128)(2,1)S(1)}, bf16[1024,128]{1,0:T(8,128)(2,1)S(1)}, u32[]{:S(2)}, u32[]{:S(2)}) collective-permute-start(bf16[1024,128]{1,0:T(8,128)(2,1)S(1)} %get-tuple-element.32), channel_id=1, source_target_pairs={{0,1},{1,2},{2,3},{3,0},{4,5},{5,6},{6,7},{7,4},{8,9},{9,10},{10,1... | collective-permute-start | bytes 786440 | tf_op jit(solution)/shard_map/ppermute | solution.py:443
  61.1 33.8 %collective-permute-start.1 = (bf16[1024,128]{1,0:T(8,128)(2,1)}, bf16[1024,128]{1,0:T(8,128)(2,1)}, u32[]{:S(2)}, u32[]{:S(2)}) collective-permute-start(bf16[1024,128]{1,0:T(8,128)(2,1)} %get-tuple-element.33), channel_id=1, source_target_pairs={{0,2},{1,3},{2,0},{3,1},{4,6},{5,7},{6,4},{7,5},{8,10},{9,11},{10,... | collective-permute-start | bytes 786440 | tf_op jit(solution)/shard_map/ppermute | solution.py:443
  62.6 32.3 %collective-permute-start.2 = (bf16[1024,128]{1,0:T(8,128)(2,1)}, bf16[1024,128]{1,0:T(8,128)(2,1)}, u32[]{:S(2)}, u32[]{:S(2)}) collective-permute-start(bf16[1024,128]{1,0:T(8,128)(2,1)} %get-tuple-element.34), channel_id=1, source_target_pairs={{0,3},{1,0},{2,1},{3,2},{4,7},{5,4},{6,5},{7,6},{8,11},{9,8},{10,9... | collective-permute-start | bytes 786440 | tf_op jit(solution)/shard_map/ppermute | solution.py:443
  88.8 9.7 %collective-permute-start.9 = (bf16[1024,128]{1,0:T(8,128)(2,1)}, bf16[1024,128]{1,0:T(8,128)(2,1)}, u32[]{:S(2)}, u32[]{:S(2)}) collective-permute-start(bf16[1024,128]{1,0:T(8,128)(2,1)} %get-tuple-element.36), channel_id=1, source_target_pairs={{0,1},{1,2},{2,3},{3,0},{4,5},{5,6},{6,7},{7,4},{8,9},{9,10},{10,1... | collective-permute-start | bytes 786440 | tf_op jit(solution)/shard_map/ppermute | solution.py:443
  88.9 12.9 %collective-permute-start.10 = (bf16[1024,128]{1,0:T(8,128)(2,1)}, bf16[1024,128]{1,0:T(8,128)(2,1)}, u32[]{:S(2)}, u32[]{:S(2)}) collective-permute-start(bf16[1024,128]{1,0:T(8,128)(2,1)} %get-tuple-element.37), channel_id=1, source_target_pairs={{0,2},{1,3},{2,0},{3,1},{4,6},{5,7},{6,4},{7,5},{8,10},{9,11},{10,... | collective-permute-start | bytes 786440 | tf_op jit(solution)/shard_map/ppermute | solution.py:443
  90.4 13.0 %collective-permute-start.11 = (bf16[1024,128]{1,0:T(8,128)(2,1)}, bf16[1024,128]{1,0:T(8,128)(2,1)}, u32[]{:S(2)}, u32[]{:S(2)}) collective-permute-start(bf16[1024,128]{1,0:T(8,128)(2,1)} %get-tuple-element.38), channel_id=1, source_target_pairs={{0,3},{1,0},{2,1},{3,2},{4,7},{5,4},{6,5},{7,6},{8,11},{9,8},{10,9... | collective-permute-start | bytes 786440 | tf_op jit(solution)/shard_map/ppermute | solution.py:443
  103.3 30.7 %copy-start = (bf16[32,4,128,128]{3,2,1,0:T(8,128)(2,1)S(1)}, bf16[32,4,128,128]{3,2,1,0:T(8,128)(2,1)}, u32[]{:S(2)}) copy-start(bf16[32,4,128,128]{3,2,1,0:T(8,128)(2,1)} %tiles.1) | copy-start | bytes 12582916
  103.3 30.7 %copy-start.1 = (s32[4096]{0:T(1024)S(1)}, s32[4096]{0:T(1024)}, u32[]{:S(2)}) copy-start(s32[4096]{0:T(1024)} %param.14) | copy-start | bytes 49156
  108.7 4.9 %collective-permute-start.12 = (f32[8,16,128]{2,1,0:T(8,128)S(1)}, f32[8,16,128]{2,1,0:T(8,128)S(1)}, u32[]{:S(2)}, u32[]{:S(2)}) collective-permute-start(f32[8,16,128]{2,1,0:T(8,128)S(1)} %get-tuple-element.42.p0), channel_id=1, source_target_pairs={{0,1},{1,2},{2,3},{3,0},{4,5},{5,6},{6,7},{7,4},{8,9},{9,10},{10,1... | collective-permute-start | bytes 196616 | tf_op jit(solution)/shard_map/ppermute | solution.py:443
  110.2 5.4 %collective-permute-start.13 = (f32[8,16,128]{2,1,0:T(8,128)S(1)}, f32[8,16,128]{2,1,0:T(8,128)S(1)}, u32[]{:S(2)}, u32[]{:S(2)}) collective-permute-start(f32[8,16,128]{2,1,0:T(8,128)S(1)} %get-tuple-element.42.p0), channel_id=1, source_target_pairs={{0,2},{1,3},{2,0},{3,1},{4,6},{5,7},{6,4},{7,5},{8,10},{9,11},{10,... | collective-permute-start | bytes 196616 | tf_op jit(solution)/shard_map/ppermute | solution.py:443
  113.1 4.0 %collective-permute-start.14 = (f32[8,16,128]{2,1,0:T(8,128)S(1)}, f32[8,16,128]{2,1,0:T(8,128)S(1)}, u32[]{:S(2)}, u32[]{:S(2)}) collective-permute-start(f32[8,16,128]{2,1,0:T(8,128)S(1)} %get-tuple-element.42.p0), channel_id=1, source_target_pairs={{0,3},{1,0},{2,1},{3,2},{4,7},{5,4},{6,5},{7,6},{8,11},{9,8},{10,9... | collective-permute-start | bytes 196616 | tf_op jit(solution)/shard_map/ppermute | solution.py:443
  154.3 8.5 %collective-permute-start.17 = (f32[24,256]{1,0:T(8,128)S(1)}, f32[24,256]{1,0:T(8,128)S(1)}, u32[]{:S(2)}, u32[]{:S(2)}) collective-permute-start(f32[24,256]{1,0:T(8,128)S(1)} %get-tuple-element.53), channel_id=1, source_target_pairs={{0,1},{1,2},{2,3},{3,0},{4,5},{5,6},{6,7},{7,4},{8,9},{9,10},{10,1... | collective-permute-start | bytes 73736 | tf_op jit(solution)/shard_map/ppermute | solution.py:443
  154.4 8.5 %collective-permute-start.16 = (f32[24,256]{1,0:T(8,128)S(1)}, f32[24,256]{1,0:T(8,128)S(1)}, u32[]{:S(2)}, u32[]{:S(2)}) collective-permute-start(f32[24,256]{1,0:T(8,128)S(1)} %get-tuple-element.52), channel_id=1, source_target_pairs={{0,2},{1,3},{2,0},{3,1},{4,6},{5,7},{6,4},{7,5},{8,10},{9,11},{10,... | collective-permute-start | bytes 73736 | tf_op jit(solution)/shard_map/ppermute | solution.py:443
  157.0 5.8 %collective-permute-start.15 = (f32[24,256]{1,0:T(8,128)S(1)}, f32[24,256]{1,0:T(8,128)S(1)}, u32[]{:S(2)}, u32[]{:S(2)}) collective-permute-start(f32[24,256]{1,0:T(8,128)S(1)} %get-tuple-element.51), channel_id=1, source_target_pairs={{0,3},{1,0},{2,1},{3,2},{4,7},{5,4},{6,5},{7,6},{8,11},{9,8},{10,9... | collective-permute-start | bytes 73736 | tf_op jit(solution)/shard_map/ppermute | solution.py:443
  162.9 43.5 %all-to-all-start.4 = ((bf16[128,32,256]{2,1,0:T(8,128)(2,1)}), bf16[128,32,256]{2,1,0:T(8,128)(2,1)S(1)}, u32[]{:S(2)}, u32[]{:S(2)}) async-start(bf16[128,32,256]{2,1,0:T(8,128)(2,1)} %bitcast.48), calls=%async_computation.4 | async-start | bytes 4194304 | tf_op jit(solution)/shard_map/all_to_all | solution.py:493
  168.4 7.1 %collective-permute-start.23 = (f32[24,256]{1,0:T(8,128)S(1)}, f32[24,256]{1,0:T(8,128)S(1)}, u32[]{:S(2)}, u32[]{:S(2)}) collective-permute-start(f32[24,256]{1,0:T(8,128)S(1)} %add_add_fusion.1), channel_id=1, source_target_pairs={{0,24},{4,28},{8,16},{12,20},{16,8},{20,12},{24,0},{28,4},{32,56},... | collective-permute-start | bytes 73736 | tf_op jit(solution)/shard_map/ppermute | solution.py:505
  171.7 13.5 %collective-permute-start.24 = (f32[24,256]{1,0:T(8,128)S(1)}, f32[24,256]{1,0:T(8,128)S(1)}, u32[]{:S(2)}, u32[]{:S(2)}) collective-permute-start(f32[24,256]{1,0:T(8,128)S(1)} %add_add_fusion.1), channel_id=1, source_target_pairs={{0,28},{4,24},{8,20},{12,16},{16,12},{20,8},{24,4},{28,0},{32,60},... | collective-permute-start | bytes 73736 | tf_op jit(solution)/shard_map/ppermute | solution.py:505
  172.4 19.2 %collective-permute-start.21 = (f32[24,256]{1,0:T(8,128)S(1)}, f32[24,256]{1,0:T(8,128)S(1)}, u32[]{:S(2)}, u32[]{:S(2)}) collective-permute-start(f32[24,256]{1,0:T(8,128)S(1)} %add_add_fusion.1), channel_id=1, source_target_pairs={{0,16},{4,20},{8,24},{12,28},{16,0},{20,4},{24,8},{28,12},{32,48},... | collective-permute-start | bytes 73736 | tf_op jit(solution)/shard_map/ppermute | solution.py:505
  173.7 23.4 %collective-permute-start.22 = (f32[24,256]{1,0:T(8,128)S(1)}, f32[24,256]{1,0:T(8,128)S(1)}, u32[]{:S(2)}, u32[]{:S(2)}) collective-permute-start(f32[24,256]{1,0:T(8,128)S(1)} %add_add_fusion.1), channel_id=1, source_target_pairs={{0,20},{4,16},{8,28},{12,24},{16,4},{20,0},{24,12},{28,8},{32,52},... | collective-permute-start | bytes 73736 | tf_op jit(solution)/shard_map/ppermute | solution.py:505
  175.5 21.7 %collective-permute-start.19 = (f32[24,256]{1,0:T(8,128)S(1)}, f32[24,256]{1,0:T(8,128)S(1)}, u32[]{:S(2)}, u32[]{:S(2)}) collective-permute-start(f32[24,256]{1,0:T(8,128)S(1)} %add_add_fusion.1), channel_id=1, source_target_pairs={{0,8},{4,12},{8,0},{12,4},{16,24},{20,28},{24,16},{28,20},{32,40},... | collective-permute-start | bytes 73736 | tf_op jit(solution)/shard_map/ppermute | solution.py:505
  175.5 21.7 %collective-permute-start.20 = (f32[24,256]{1,0:T(8,128)S(1)}, f32[24,256]{1,0:T(8,128)S(1)}, u32[]{:S(2)}, u32[]{:S(2)}) collective-permute-start(f32[24,256]{1,0:T(8,128)S(1)} %add_add_fusion.1), channel_id=1, source_target_pairs={{0,12},{4,8},{8,4},{12,0},{16,28},{20,24},{24,20},{28,16},{32,44},... | collective-permute-start | bytes 73736 | tf_op jit(solution)/shard_map/ppermute | solution.py:505
  185.2 11.9 %collective-permute-start.18 = (f32[24,256]{1,0:T(8,128)S(1)}, f32[24,256]{1,0:T(8,128)S(1)}, u32[]{:S(2)}, u32[]{:S(2)}) collective-permute-start(f32[24,256]{1,0:T(8,128)S(1)} %add_add_fusion.1), channel_id=1, source_target_pairs={{0,4},{4,0},{8,12},{12,8},{16,20},{20,16},{24,28},{28,24},{32,36},... | collective-permute-start | bytes 73736 | tf_op jit(solution)/shard_map/ppermute | solution.py:505
  197.2 5.5 %collective-permute-start.25 = (f32[24,256]{1,0:T(8,128)S(1)}, f32[24,256]{1,0:T(8,128)S(1)}, u32[]{:S(2)}, u32[]{:S(2)}) collective-permute-start(f32[24,256]{1,0:T(8,128)S(1)} %add_add_fusion.refs_0_), channel_id=1, source_target_pairs={{0,32},{4,36},{8,40},{12,44},{16,48},{20,52},{24,56},{28,60},{32,0... | collective-permute-start | bytes 73736 | tf_op jit(solution)/shard_map/ppermute | solution.py:505
  199.0 4.8 %collective-permute-start.26 = (f32[24,256]{1,0:T(8,128)S(1)}, f32[24,256]{1,0:T(8,128)S(1)}, u32[]{:S(2)}, u32[]{:S(2)}) collective-permute-start(f32[24,256]{1,0:T(8,128)S(1)} %add_add_fusion.refs_0_), channel_id=1, source_target_pairs={{0,64},{4,68},{8,72},{12,76},{16,80},{20,84},{24,88},{28,92},{32,9... | collective-permute-start | bytes 73736 | tf_op jit(solution)/shard_map/ppermute | solution.py:505
  202.5 3.9 %collective-permute-start.27 = (f32[24,256]{1,0:T(8,128)S(1)}, f32[24,256]{1,0:T(8,128)S(1)}, u32[]{:S(2)}, u32[]{:S(2)}) collective-permute-start(f32[24,256]{1,0:T(8,128)S(1)} %add_add_fusion.refs_0_), channel_id=1, source_target_pairs={{0,96},{4,100},{8,104},{12,108},{16,112},{20,116},{24,120},{28,124... | collective-permute-start | bytes 73736 | tf_op jit(solution)/shard_map/ppermute | solution.py:505

commit v5 on v4

--- a/solution.py
+++ b/solution.py
@@ -28,13 +28,33 @@
     return lax.dot_general(a, b, dims, preferred_element_type=F32)
 
 
+def tree(terms):
+    while len(terms) > 1:
+        terms = [a + b for a, b in zip(terms[::2], terms[1::2])]
+    return terms[0]
+
+
 def in_hbm(x):
     return pltpu.with_memory_space_constraint(x, pltpu.HBM)
 
 
-def pick_kernel(chunk, table, features, out, held, sems):
+def tree(terms):
+    while len(terms) > 1:
+        terms = [a + b for a, b in zip(terms[::2], terms[1::2])]
+    return terms[0]
+
+
+def in_hbm(x):
+    return pltpu.with_memory_space_constraint(x, pltpu.HBM)
+
+
+def in_vmem(x):
+    return pltpu.with_memory_space_constraint(x, pltpu.VMEM)
+
+
+def pick_kernel(table, features, out, held, sems):
     slots = out.shape[0]
-    load = pltpu.make_async_copy(features.at[:, pl.ds(chunk * BLK, BLK)], held, sems.at[0])
+    load = pltpu.make_async_copy(features, held, sems.at[0])
     load.start()
     load.wait()
 
@@ -46,48 +66,44 @@
     pltpu.make_async_copy(out, out, sems.at[1]).wait()
 
 
-def pick(features, table, chunk):
+def pick(features, table):
     slots = table.shape[0]
     return pl.pallas_call(
-        functools.partial(pick_kernel, chunk),
+        pick_kernel,
         grid_spec=pltpu.PrefetchScalarGridSpec(
             num_scalar_prefetch=1,
             grid=(),
             in_specs=[pl.BlockSpec(memory_space=pltpu.HBM)],
             out_specs=pl.BlockSpec(memory_space=pltpu.HBM),
             scratch_shapes=[
-                pltpu.VMEM((features.shape[0], BLK), BF16),
+                pltpu.VMEM(features.shape, BF16),
                 pltpu.SemaphoreType.DMA((2,)),
             ],
         ),
-        out_shape=pltpu.HBM((slots, BLK, BLK), BF16),
-        compiler_params=params(4),
-        cost_estimate=cost(0, 4 * MIB),
+        out_shape=pltpu.HBM((slots, BLK, features.shape[1]), BF16),
+        compiler_params=params(6),
+        cost_estimate=cost(0, 6 * MIB),
         name="pick",
     )(table, in_hbm(features))
 
 
-def agg_kernel(which, chunk, nfeat, src, counts, me, arrived_hbm, tiles_hbm, features, *refs):
-    outs, (arrived, tiles, own, sems) = refs[: len(which)], refs[len(which) :]
+def agg_kernel(which, nfeat, src, counts, me, arrived, tiles_hbm, features, after, *refs):
+    outs, (tiles, own, sems) = refs[: len(which)], refs[len(which) :]
     group, per = tiles.shape[1:3]
-    moves = [pltpu.make_async_copy(arrived_hbm, arrived, sems.at[0])]
+    moves = []
     firsts = [lax.rem(me[0] + k, nfeat) * group for k in which]
     for i, first in enumerate(firsts):
         rows = pl.ds(pl.multiple_of(first * BLK, BLK), group * BLK)
-        moves.append(
-            pltpu.make_async_copy(tiles_hbm.at[pl.ds(first, group)], tiles.at[i], sems.at[1 + 2 * i])
+        pair = (
+            pltpu.make_async_copy(tiles_hbm.at[pl.ds(first, group)], tiles.at[i], sems.at[2 * i]),
+            pltpu.make_async_copy(features.at[rows], own.at[i], sems.at[2 * i + 1]),
         )
-        moves.append(
-            pltpu.make_async_copy(
-                features.at[rows, pl.ds(chunk * BLK, BLK)], own.at[i], sems.at[2 + 2 * i]
-            )
-        )
-    for move in moves:
-        move.start()
-    moves[0].wait()
+        for move in pair:
+            move.start()
+        moves.append(pair)
     for i, (first, out) in enumerate(zip(firsts, outs)):
-        moves[1 + 2 * i].wait()
-        moves[2 + 2 * i].wait()
+        for move in moves[i]:
+            move.wait()
         for b in range(group):
             rows, weights = [], []
             for t in range(per):
@@ -100,36 +116,36 @@
             out[at, :] = (own[i, at, :].astype(F32) + total).astype(BF16)
 
 
-def aggregate(src, counts, me, arrived, tiles, features, chunk, nfeat, which):
+def aggregate(src, counts, me, arrived, tiles, features, nfeat, which, after):
     nblocks, per = tiles.shape[:2]
     group = nblocks // nfeat
-    piece = jax.ShapeDtypeStruct((group * BLK, BLK), BF16)
+    width = features.shape[1]
+    piece = jax.ShapeDtypeStruct((group * BLK, width), BF16)
     hbm = pl.BlockSpec(memory_space=pltpu.HBM)
-    return pl.pallas_call(
-        functools.partial(agg_kernel, which, chunk, nfeat),
+    vmem = pl.BlockSpec(memory_space=pltpu.VMEM)
+    return pl.pallas_call(
+        functools.partial(agg_kernel, which, nfeat),
         grid_spec=pltpu.PrefetchScalarGridSpec(
             num_scalar_prefetch=3,
             grid=(),
-            in_specs=[hbm] * 3,
-            out_specs=[pl.BlockSpec(memory_space=pltpu.VMEM)] * len(which),
+            in_specs=[vmem, hbm, hbm, pl.BlockSpec(memory_space=pl.ANY)],
+            out_specs=[vmem] * len(which),
             scratch_shapes=[
-                pltpu.VMEM(arrived.shape, BF16),
                 pltpu.VMEM((len(which), group, per, BLK, BLK), BF16),
-                pltpu.VMEM((len(which), group * BLK, BLK), BF16),
-                pltpu.SemaphoreType.DMA((1 + 2 * len(which),)),
+                pltpu.VMEM((len(which), group * BLK, width), BF16),
+                pltpu.SemaphoreType.DMA((2 * len(which),)),
             ],
         ),
         out_shape=[piece] * len(which),
-        compiler_params=params(14),
-        cost_estimate=cost(len(which) * group * per * 2 * BLK**3, 8 * MIB),
+        compiler_params=params(12),
+        cost_estimate=cost(len(which) * group * per * 2 * BLK * BLK * width, 8 * MIB),
         name="aggregate",
-    )(src, counts, me, in_hbm(arrived), in_hbm(tiles), in_hbm(features))
+    )(src, counts, me, in_vmem(arrived), in_hbm(tiles), in_hbm(features), after)
 
 
 def dense_kernel(nfeat, *refs):
-    pieces, (weights, bias, second, hidden, proj) = refs[: 2 * nfeat], refs[2 * nfeat :]
-    order = [pieces[i * nfeat + k][...] for k in range(nfeat) for i in range(2)]
-    pre = dot(weights[...], jnp.concatenate(order, 1), NT)
+    pieces, (weights, bias, second, hidden, proj) = refs[:nfeat], refs[nfeat:]
+    pre = dot(weights[...], jnp.concatenate([piece[...] for piece in pieces], 1), NT)
     hid = jnp.maximum(pre + bias[...], 0.0).astype(BF16)
     hidden[...] = hid
     out = dot(second[...], hid, NN)
@@ -138,16 +154,17 @@
 
 
 def dense(pieces, weights, bias, second):
-    nodes, nfeat = pieces[0].shape[0], len(pieces) // 2
-    hid, width = weights.shape
+    nodes, width = pieces[0].shape
+    nfeat = len(pieces)
+    hid = weights.shape[0]
     grades = second.shape[0]
     step = 256
     return pl.pallas_call(
         functools.partial(dense_kernel, nfeat),
         grid=(nodes // step,),
-        in_specs=[pl.BlockSpec((step, BLK), lambda g: (g, 0))] * (2 * nfeat)
+        in_specs=[pl.BlockSpec((step, width), lambda g: (g, 0))] * nfeat
         + [
-            pl.BlockSpec((hid, width), lambda g: (0, 0)),
+            pl.BlockSpec(weights.shape, lambda g: (0, 0)),
             pl.BlockSpec((hid, 1), lambda g: (0, 0)),
             pl.BlockSpec((grades, hid), lambda g: (0, 0)),
         ],
@@ -160,7 +177,7 @@
             jax.ShapeDtypeStruct((nodes // BLK, grades, BLK), F32),
         ],
         compiler_params=params(20),
-        cost_estimate=cost(2 * nodes * hid * width, 7 * MIB),
+        cost_estimate=cost(2 * nodes * hid * width * nfeat, 7 * MIB),
         name="dense",
     )(*pieces, weights, bias, second)
 
@@ -346,17 +363,17 @@
 
 def big_kernel(me, dpre, *refs):
     pieces, out = refs[:-1], refs[-1]
-    nfeat = len(pieces) // 2
-    for k in range(nfeat):
+    nfeat = len(pieces)
+    for k, piece in enumerate(pieces):
         owner = lax.rem(me[0] + nfeat - k, nfeat)
-        both = jnp.concatenate([pieces[k][...], pieces[nfeat + k][...]], 1)
-        grad = dot(dpre[...], both, NN).astype(BF16)
+        grad = dot(dpre[...], piece[...], NN).astype(BF16)
         out[:, owner] = grad.reshape(out.shape[0], out.shape[2], out.shape[3])
 
 
 def big_gradient(me, dpre, pieces, parts):
-    nfeat = len(pieces) // 2
+    nfeat = len(pieces)
     hid, nodes = dpre.shape
+    width = pieces[0].shape[1]
     steps = 2
     return pl.pallas_call(
         big_kernel,
@@ -364,12 +381,12 @@
             num_scalar_prefetch=1,
             grid=(steps,),
             in_specs=[pl.BlockSpec((hid // steps, nodes), lambda g, m: (g, 0))]
-            + [pl.BlockSpec((nodes, BLK), lambda g, m: (0, 0))] * (2 * nfeat),
+            + [pl.BlockSpec((nodes, width), lambda g, m: (0, 0))] * nfeat,
             out_specs=pl.BlockSpec(
-                (parts // steps, nfeat, hid // parts, 2 * BLK), lambda g, m: (g, 0, 0, 0)
+                (parts // steps, nfeat, hid // parts, width), lambda g, m: (g, 0, 0, 0)
             ),
         ),
-        out_shape=pltpu.HBM((parts, nfeat, hid // parts, 2 * BLK), BF16),
+        out_shape=pltpu.HBM((parts, nfeat, hid // parts, width), BF16),
         compiler_params=params(24),
         cost_estimate=cost(2 * nodes * hid * hid, 6 * MIB),
         name="big_gradient",
@@ -383,12 +400,10 @@
     @pl.when(g == 0)
     def _():
         acc[...] = jnp.zeros_like(acc)
-        terms = [ref[...] for ref in small]
-        while len(terms) > 1:
-            terms = [a + b for a, b in zip(terms[::2], terms[1::2])]
+        whole = tree([ref[...] for ref in small])
         grades = second.shape[0]
-        second[...] = terms[0][:grades]
-        bias[...] = terms[0][grades : grades + 1]
+        second[...] = whole[:grades]
+        bias[...] = whole[grades : grades + 1]
 
     total = arrived[0].astype(F32)
     for i in range(1, arrived.shape[0]):
@@ -447,8 +462,7 @@
         moved = lax.all_to_all(shaped, "nodes", split_axis=0, concat_axis=0, tiled=True)
         return moved.reshape(x.shape)
 
-    arrived = [swap(pick(features, table, 0))]
-    send = pick(features, table, 1)
+    arrived = swap(pick(features, table))
 
     flat = w_first.T
     weights = jnp.concatenate([flat] + [ahead(flat, k) for k in range(1, nfeat)], 1)
@@ -462,21 +476,15 @@
     bias = ordered[:, grades].reshape(hid, 1)
     second = second_t.T
 
-    send, weights, bias, second_t, second = lax.optimization_barrier(
-        (send, weights, bias, second_t, second)
-    )
-    arrived.append(swap(send))
-    others = (2, 1, 3)
-    make = functools.partial(aggregate, src, counts, me)
-    first = [None] * nfeat
-    *sent, first[0] = make(arrived[0], tiles, features, 0, nfeat, others + (0,))
-    for k, piece in zip(others, sent):
-        first[k] = ahead(piece, k)
-    last = [None] * nfeat
-    for k, piece in zip(others, make(arrived[1], tiles, features, 1, nfeat, others)):
-        last[k] = ahead(piece, k)
-    (last[0],) = make(arrived[1], tiles, features, 1, nfeat, (0,))
-    hidden, proj = dense(first + last, weights, bias, second_t)
+    arrived, weights, bias, second_t, second = lax.optimization_barrier(
+        (arrived, weights, bias, second_t, second)
+    )
+    make = functools.partial(aggregate, src, counts, me, arrived, tiles, features, nfeat)
+    (two,) = make((2,), features)
+    one, three = make((1, 3), two)
+    (own,) = make((0,), three)
+    pieces = [own, ahead(one, 1), ahead(two, 2), ahead(three, 3)]
+    hidden, proj = dense(pieces, weights, bias, second_t)
 
     projs = [proj] + [ahead(proj, k) for k in range(1, nfeat)]
     own, send = spread(table, me, projs)
@@ -485,10 +493,18 @@
         src, counts, me, swap(send), own, labels.reshape(nblocks, 1, BLK), tiles, scale, nfeat
     )
     dpre, *small = small_gradients(table, me, swap(slotsum), dlog, hidden, second, nfeat)
-    rest = small[0]
-    for k in range(1, nfeat):
-        rest = rest + ahead(small[k], nfeat - k)
-    big = big_gradient(me, dpre, first + last, parts)
+    chips = []
+    for core in range(2):
+        for k in range(nfeat):
+            moves = [
+                (p * nfeat + f, (p ^ core) * nfeat + (f - k) % nfeat)
+                for p in range(parts)
+                for f in range(nfeat)
+            ]
+            here = core == 0 and k == 0
+            chips.append(small[k] if here else lax.ppermute(small[k], ("nodes", "feat"), moves))
+    rest = tree(chips)
+    big = big_gradient(me, dpre, pieces, parts)
     big, rest = lax.optimization_barrier((big, rest))
     moved = lax.all_to_all(
         big.reshape(parts * nfeat, *big.shape[2:]),
@@ -497,13 +513,10 @@
         concat_axis=0,
         tiled=True,
     )
-    terms = [rest]
-    for group in ((1, 2, 3, 4, 5, 6, 7), (8, 16, 24)):
-        while len(terms) > 1:
-            terms = [a + b for a, b in zip(terms[::2], terms[1::2])]
-        terms += [
-            lax.ppermute(terms[0], "nodes", [(i, i ^ d) for i in range(parts)]) for d in group
-        ]
+    terms = [rest] + [
+        lax.ppermute(rest, "nodes", [(i, i ^ d) for i in range(parts)])
+        for d in range(2, parts, 2)
+    ]
     grad_first, grad_second, grad_bias = total(moved, terms, grades)
     return grad_first.T, grad_bias.reshape(-1), grad_second.T
 

time: 210 us -> 233 us (1.11)
  the two profiles are of different devices: /device:TPU:1 before, /device:TPU:4 now
where the time goes in v5:
time: 233 us; the launch traced here: 232 us
  starting transfers between devices  81.5 us (35%)
  waiting for transfers between devices  75.7 us (32%)
  Pallas kernels  39.5 us (17%)
  blocking collectives  30.3 us (13%)
  local copies, waits for them, and re-layouts  2.67 us (1%)
    ppermute x15, starting transfers between devices, shards(): lax.ppermute(rest, 'nodes', [(i, i ^ d) for i in range(parts)])  44.2 us
    ppermute x12, waiting for transfers between devices, ahead(): return lax.ppermute(x, 'feat', [(i, (i + k) % nfeat) for i in range(nfeat)])  40.8 us
    all_to_all x2, blocking collectives, swap(): lax.all_to_all(shaped, 'nodes', split_axis=0, concat_axis=0, tiled=True)  30.3 us
    all_to_all x1, waiting for transfers between devices, swap(): lax.all_to_all(shaped, 'nodes', split_axis=0, concat_axis=0, tiled=True)  22.2 us
    ppermute x12, starting transfers between devices, ahead(): return lax.ppermute(x, 'feat', [(i, (i + k) % nfeat) for i in range(nfeat)])  15 us
    pallas_call x3, Pallas kernels, aggregate(): pl.pallas_call(functools.partial(agg_kernel, which, nfeat), grid_spec=plt...  15 us
    ppermute x15, waiting for transfers between devices, shards(): lax.ppermute(rest, 'nodes', [(i, i ^ d) for i in range(parts)])  12.7 us
    all_to_all x1, starting transfers between devices, swap(): lax.all_to_all(shaped, 'nodes', split_axis=0, concat_axis=0, tiled=True)  8.61 us
  transfers between devices with their start and end apart: 36, of which 9 were waited for; matrix products, arithmetic and copies ran while one was open for 1% of the time, Pallas kernels for 4%

profile of v5, /device:TPU:4, one launch (start us, length us, event | category | flops | bytes accessed | tf_op | source)
XLA Modules:
  0.0 232.2 jit_solution(14919134001394307766)
XLA Ops:
  0.6 0.8 copy.17
  1.4 0.1 reshape.49.table
  1.5 4.2 %pick.1 = bf16[64,128,256]{2,1,0:T(8,128)(2,1)} custom-call(s32[64]{0:T(128)S(1)} %reshape.49.table, bf16[4096,256]{1,0:T(8,128)(2,1)} %features.7), custom_call_target="tpu_custom_call" | custom-call | bytes 6291456 | tf_op jit(solution)/shard_map/pick/pallas_call | solution.py:71
  5.7 0.0 copy-start.5
  5.7 8.6 %all-to-all-start = ((bf16[32,2,128,256]{3,2,1,0:T(8,128)(2,1)}), bf16[32,2,128,256]{3,2,1,0:T(8,128)(2,1)}, u32[]{:S(2)}, u32[]{:S(2)}) async-start(bf16[32,2,128,256]{3,2,1,0:T(8,128)(2,1)} %bitcast.44), calls=%async_computation | async-start | bytes 8388608 | tf_op jit(solution)/shard_map/all_to_all | solution.py:462
  14.4 0.6 collective-permute-start.3
  15.0 0.2 copy.19
  15.2 0.6 collective-permute-start.2
  15.8 3.0 %collective-permute-start.1 = (bf16[1024,256]{1,0:T(8,128)(2,1)S(1)}, bf16[1024,256]{1,0:T(8,128)(2,1)}, u32[]{:S(2)}, u32[]{:S(2)}) collective-permute-start(bf16[1024,256]{1,0:T(8,128)(2,1)S(1)} %bitcast.47), channel_id=1, source_target_pairs={{0,2},{1,3},{2,0},{3,1},{4,6},{5,7},{6,4},{7,5},{8,10},{9,11},{10,... | collective-permute-start | bytes 1572872 | tf_op jit(solution)/shard_map/ppermute | solution.py:458
  18.8 1.8 collective-permute-start
  20.6 0.1 copy.18
  20.7 0.1 reshape.50.src
  20.8 2.4 %collective-permute-start.5 = (f32[24,256]{1,0:T(8,128)S(1)}, f32[24,256]{1,0:T(8,128)S(1)}, u32[]{:S(2)}, u32[]{:S(2)}) collective-permute-start(f32[24,256]{1,0:T(8,128)S(1)} %pad_maximum_fusion.1), channel_id=1, source_target_pairs={{0,1},{1,2},{2,3},{3,0},{4,5},{5,6},{6,7},{7,4},{8,9},{9,10},{10,1... | collective-permute-start | bytes 73736 | tf_op jit(solution)/shard_map/ppermute | solution.py:458
  23.2 19.7 %collective-permute-done.4 = f32[24,256]{1,0:T(8,128)S(1)} collective-permute-done((f32[24,256]{1,0:T(8,128)S(1)}, f32[24,256]{1,0:T(8,128)S(1)}, u32[]{:S(2)}, u32[]{:S(2)}) %collective-permute-start.4) | collective-permute-done | bytes 24608 | tf_op jit(solution)/shard_map/ppermute | solution.py:458
  43.0 0.1 collective-permute-done.5
  43.1 0.2 copy.20
  43.4 1.5 pad_maximum_fusion.refs_4_
  44.9 22.2 %all-to-all-done = bf16[32,2,128,256]{3,2,1,0:T(8,128)(2,1)} async-done(((bf16[32,2,128,256]{3,2,1,0:T(8,128)(2,1)}), bf16[32,2,128,256]{3,2,1,0:T(8,128)(2,1)}, u32[]{:S(2)}, u32[]{:S(2)}) %all-to-all-start) | async-done | bytes 4194336 | tf_op jit(solution)/shard_map/all_to_all | solution.py:462
  67.1 4.6 %aggregate.3.after = bf16[1024,256]{1,0:T(8,128)(2,1)S(1)} custom-call(s32[128]{0:T(128)S(1)} %reshape.50.src, s32[32]{0:T(128)S(1)} %bitcast.40, s32[1]{0:T(128)} %bitcast.me, bf16[64,128,256]{2,1,0:T(8,128)(2,1)} %bitcast.3.arrived, bf16[32,4,128,128]{3,2,1,0:T(8,128)(2,1)} %tiles.1, bf16[4096,256]{1,0:T(8,128)(2,1)} %features.7, bf16[4096,256]{1,0:T(8,128)(2,1)} %features.7), custom_call_target="tpu_custom_call" | custom-call | flops 268435456 | bytes 8388608 | tf_op jit(solution)/shard_map/aggregate/pallas_call | solution.py:126
  71.7 5.8 %aggregate.4 = (bf16[1024,256]{1,0:T(8,128)(2,1)}, bf16[1024,256]{1,0:T(8,128)(2,1)S(1)}) custom-call(s32[128]{0:T(128)S(1)} %reshape.50.src, s32[32]{0:T(128)S(1)} %bitcast.41, s32[1]{0:T(128)} %bitcast.me, bf16[64,128,256]{2,1,0:T(8,128)(2,1)} %bitcast.3.arrived, bf16[32,4,128,128]{3,2,1,0:T(8,128)(2,1)} %tiles.1, bf16[4096,256]{1,0:T(8,128)(2,1)} %features.7, ...), custom_call_target="tpu_custom_call" | custom-call | flops 536870912 | bytes 8388608 | tf_op jit(solution)/shard_map/aggregate/pallas_call | solution.py:126
  77.5 0.6 collective-permute-start.7
  78.1 2.1 collective-permute-start.6
  80.2 0.1 collective-permute-start.8
  80.2 1.0 copy.21.refs_5_
  81.3 0.1 copy.22.refs_6_
  81.4 4.6 %aggregate.5.refs_0_ = bf16[1024,256]{1,0:T(8,128)(2,1)S(1)} custom-call(s32[128]{0:T(128)S(1)} %reshape.50.src, s32[32]{0:T(128)S(1)} %bitcast.42, s32[1]{0:T(128)} %bitcast.me, bf16[64,128,256]{2,1,0:T(8,128)(2,1)} %bitcast.3.arrived, bf16[32,4,128,128]{3,2,1,0:T(8,128)(2,1)} %tiles.1, bf16[4096,256]{1,0:T(8,128)(2,1)} %features.7, ...), custom_call_target="tpu_custom_call" | custom-call | flops 268435456 | bytes 8388608 | tf_op jit(solution)/shard_map/aggregate/pallas_call | solution.py:126
  86.0 17.2 %collective-permute-done.6.refs_1_ = bf16[1024,256]{1,0:T(8,128)(2,1)} collective-permute-done((bf16[1024,256]{1,0:T(8,128)(2,1)}, bf16[1024,256]{1,0:T(8,128)(2,1)}, u32[]{:S(2)}, u32[]{:S(2)}) %collective-permute-start.6) | collective-permute-done | bytes 524320 | tf_op jit(solution)/shard_map/ppermute | solution.py:458
  103.2 5.4 %dense.1 = (bf16[1024,1024]{1,0:T(8,128)(2,1)S(1)}, f32[8,16,128]{2,1,0:T(8,128)S(1)}) custom-call(bf16[1024,256]{1,0:T(8,128)(2,1)S(1)} %aggregate.5.refs_0_, bf16[1024,256]{1,0:T(8,128)(2,1)} %collective-permute-done.6.refs_1_, bf16[1024,256]{1,0:T(8,128)(2,1)} %collective-permute-done.7.refs_2_, bf16[1024,256]{1,0:T(8,128)(2,1)} %collective-permute-done.8.refs_3_, ...), custom_call_target="tpu_custom_call" | custom-call | flops 2147483648 | bytes 7340032 | tf_op jit(solution)/shard_map/dense/pallas_call | solution.py:162
  108.7 1.8 collective-permute-start.9
  110.5 0.9 collective-permute-start.10
  111.4 1.2 collective-permute-start.11
  112.6 0.4 collective-permute-done.9.p1
  112.9 3.3 %collective-permute-done.10.p2 = f32[8,16,128]{2,1,0:T(8,128)S(1)} collective-permute-done((f32[8,16,128]{2,1,0:T(8,128)S(1)}, f32[8,16,128]{2,1,0:T(8,128)S(1)}, u32[]{:S(2)}, u32[]{:S(2)}) %collective-permute-start.10) | collective-permute-done | bytes 65568 | tf_op jit(solution)/shard_map/ppermute | solution.py:458
  116.3 0.7 spread.1
  116.9 17.5 %all_to_all.20 = f32[32,2,16,128]{3,2,1,0:T(8,128)S(1)} all-to-all(f32[32,2,16,128]{3,2,1,0:T(8,128)S(1)} %bitcast.37), channel_id=1, replica_groups=mesh['nodes'=32,'feat'=4] {'nodes'}, dimensions={0} | all-to-all | bytes 1048576 | tf_op jit(solution)/shard_map/all_to_all | solution.py:462
  134.4 3.9 %logits.1 = (f32[8,16,128]{2,1,0:T(8,128)S(1)}, bf16[64,16,128]{2,1,0:T(8,128)(2,1)S(1)}) custom-call(s32[128]{0:T(128)S(1)} %reshape.50.src, s32[32]{0:T(128)S(1)} %bitcast.43, s32[1]{0:T(128)} %bitcast.me, f32[64,16,128]{2,1,0:T(8,128)S(1)} %bitcast.35, f32[32,16,128]{2,1,0:T(8,128)S(1)} %get-tuple-element.34.own, s32[32,1,128]{2,1,0:T(1,128)S(1)} %bitcast.39, ...), custom_call_target="tpu_custom_call" | custom-call | flops 268435456 | bytes 6291456 | tf_op jit(solution)/shard_map/logits/pallas_call | solution.py:270
  138.3 12.8 %all_to_all.21 = bf16[32,2,16,128]{3,2,1,0:T(8,128)(2,1)S(1)} all-to-all(bf16[32,2,16,128]{3,2,1,0:T(8,128)(2,1)S(1)} %bitcast.38), channel_id=1, replica_groups=mesh['nodes'=32,'feat'=4] {'nodes'}, dimensions={0} | all-to-all | bytes 524288 | tf_op jit(solution)/shard_map/all_to_all | solution.py:462
  151.1 3.9 %small_gradients.1 = (bf16[1024,1024]{1,0:T(8,128)(2,1)}, f32[24,256]{1,0:T(8,128)S(1)}, f32[24,256]{1,0:T(8,128)S(1)}, f32[24,256]{1,0:T(8,128)S(1)}, f32[24,256]{1,0:T(8,128)S(1)}) custom-call(s32[64]{0:T(128)S(1)} %reshape.49.table, s32[1]{0:T(128)} %bitcast.me, bf16[64,16,128]{2,1,0:T(8,128)(2,1)S(1)} %bitcast.36, ...), custom_call_target="tpu_custom_call" | custom-call | flops 536870912 | bytes 4194304 | tf_op jit(solution)/shard_map/small_gradients/pallas_call | solution.py:338
  155.1 1.9 collective-permute-start.17
  157.0 0.8 collective-permute-start.18
  157.8 1.9 collective-permute-start.13
  159.7 1.2 collective-permute-start.14
  160.9 0.2 collective-permute-start.16
  161.1 1.2 collective-permute-start.12
  162.3 0.5 collective-permute-start.15
  162.8 5.3 %big_gradient.1 = bf16[32,4,32,256]{3,2,1,0:T(8,128)(2,1)} custom-call(s32[1]{0:T(128)} %bitcast.me, bf16[1024,1024]{1,0:T(8,128)(2,1)} %get-tuple-element.39.dpre, bf16[1024,256]{1,0:T(8,128)(2,1)S(1)} %aggregate.5.refs_0_, bf16[1024,256]{1,0:T(8,128)(2,1)} %collective-permute-done.6.refs_1_, bf16[1024,256]{1,0:T(8,128)(2,1)} %collective-permute-done.7.refs_2_, ...), custom_call_target="tpu_custom_call" | custom-call | flops 2147483648 | bytes 6291456 | tf_op jit(solution)/shard_map/big_gradient/pallas_call | solution.py:378
  168.2 6.0 %all-to-all-start.3 = ((bf16[128,32,256]{2,1,0:T(8,128)(2,1)}), bf16[128,32,256]{2,1,0:T(8,128)(2,1)S(1)}, u32[]{:S(2)}, u32[]{:S(2)}) async-start(bf16[128,32,256]{2,1,0:T(8,128)(2,1)} %bitcast.45), calls=%async_computation.3 | async-start | bytes 4194304 | tf_op jit(solution)/shard_map/all_to_all | solution.py:509
  174.1 1.7 collective-permute-start.19
  175.8 3.2 %collective-permute-start.20 = (f32[24,256]{1,0:T(8,128)S(1)}, f32[24,256]{1,0:T(8,128)S(1)}, u32[]{:S(2)}, u32[]{:S(2)}) collective-permute-start(f32[24,256]{1,0:T(8,128)S(1)} %add_add_fusion.refs_0_), channel_id=1, source_target_pairs={{0,16},{4,20},{8,24},{12,28},{16,0},{20,4},{24,8},{28,12},{32,48},... | collective-permute-start | bytes 73736 | tf_op jit(solution)/shard_map/ppermute | solution.py:517
  179.1 1.5 collective-permute-start.22
  180.6 0.2 collective-permute-start.23
  180.8 5.9 %collective-permute-done.19.refs_1_ = f32[24,256]{1,0:T(8,128)S(1)} collective-permute-done((f32[24,256]{1,0:T(8,128)S(1)}, f32[24,256]{1,0:T(8,128)S(1)}, u32[]{:S(2)}, u32[]{:S(2)}) %collective-permute-start.19) | collective-permute-done | bytes 24608 | tf_op jit(solution)/shard_map/ppermute | solution.py:517
  186.7 17.9 %collective-permute-start.24 = (f32[24,256]{1,0:T(8,128)S(1)}, f32[24,256]{1,0:T(8,128)S(1)}, u32[]{:S(2)}, u32[]{:S(2)}) collective-permute-start(f32[24,256]{1,0:T(8,128)S(1)} %add_add_fusion.refs_0_), channel_id=1, source_target_pairs={{0,48},{4,52},{8,56},{12,60},{16,32},{20,36},{24,40},{28,44},{32,1... | collective-permute-start | bytes 73736 | tf_op jit(solution)/shard_map/ppermute | solution.py:517
  204.6 2.5 %collective-permute-start.26 = (f32[24,256]{1,0:T(8,128)S(1)}, f32[24,256]{1,0:T(8,128)S(1)}, u32[]{:S(2)}, u32[]{:S(2)}) collective-permute-start(f32[24,256]{1,0:T(8,128)S(1)} %add_add_fusion.refs_0_), channel_id=1, source_target_pairs={{0,64},{4,68},{8,72},{12,76},{16,80},{20,84},{24,88},{28,92},{32,9... | collective-permute-start | bytes 73736 | tf_op jit(solution)/shard_map/ppermute | solution.py:517
  207.1 0.5 collective-permute-start.27
  207.5 5.8 %collective-permute-start.28 = (f32[24,256]{1,0:T(8,128)S(1)}, f32[24,256]{1,0:T(8,128)S(1)}, u32[]{:S(2)}, u32[]{:S(2)}) collective-permute-start(f32[24,256]{1,0:T(8,128)S(1)} %add_add_fusion.refs_0_), channel_id=1, source_target_pairs={{0,80},{4,84},{8,88},{12,92},{16,64},{20,68},{24,72},{28,76},{32,1... | collective-permute-start | bytes 73736 | tf_op jit(solution)/shard_map/ppermute | solution.py:517
  213.3 1.4 collective-permute-start.29
  214.8 1.2 collective-permute-start.30
  215.9 0.2 collective-permute-start.31
  216.1 7.8 %collective-permute-start.32 = (f32[24,256]{1,0:T(8,128)S(1)}, f32[24,256]{1,0:T(8,128)S(1)}, u32[]{:S(2)}, u32[]{:S(2)}) collective-permute-start(f32[24,256]{1,0:T(8,128)S(1)} %add_add_fusion.refs_0_), channel_id=1, source_target_pairs={{0,112},{4,116},{8,120},{12,124},{16,96},{20,100},{24,104},{28,108... | collective-permute-start | bytes 73736 | tf_op jit(solution)/shard_map/ppermute | solution.py:517
  223.9 0.4 collective-permute-start.33
  224.3 1.8 collective-permute-done.32.refs_14_
  226.1 5.0 %collective-permute-done.33.refs_15_ = f32[24,256]{1,0:T(8,128)S(1)} collective-permute-done((f32[24,256]{1,0:T(8,128)S(1)}, f32[24,256]{1,0:T(8,128)S(1)}, u32[]{:S(2)}, u32[]{:S(2)}) %collective-permute-start.33) | collective-permute-done | bytes 24608 | tf_op jit(solution)/shard_map/ppermute | solution.py:517
  231.1 1.2 total.1
  (58 shorter events, 0.2 us)
Async XLA Ops:
  5.7 8.7 %copy-start.5 = (bf16[256,16]{0,1:T(8,128)(2,1)S(1)}, bf16[256,16]{0,1:T(8,128)(2,1)}, u32[]{:S(2)}) copy-start(bf16[256,16]{0,1:T(8,128)(2,1)} %param.17) | copy-start | bytes 24580
  5.7 8.7 %copy-start.7 = (f32[256]{0:T(256)S(1)}, f32[256]{0:T(256)}, u32[]{:S(2)}) copy-start(f32[256]{0:T(256)} %param.16) | copy-start | bytes 3076
  5.7 9.3 %copy-start.4 = (bf16[256,1024]{1,0:T(8,128)(2,1)S(1)}, bf16[256,1024]{1,0:T(8,128)(2,1)}, u32[]{:S(2)}) copy-start(bf16[256,1024]{1,0:T(8,128)(2,1)} %param.15) | copy-start | bytes 1572868
  5.7 14.9 %copy-start.6 = (s32[32,4]{0,1:T(4,128)S(1)}, s32[32,4]{0,1:T(4,128)}, u32[]{:S(2)}) copy-start(s32[32,4]{0,1:T(4,128)} %param.12) | copy-start | bytes 1540
  5.7 61.4 %all-to-all-start = ((bf16[32,2,128,256]{3,2,1,0:T(8,128)(2,1)}), bf16[32,2,128,256]{3,2,1,0:T(8,128)(2,1)}, u32[]{:S(2)}, u32[]{:S(2)}) async-start(bf16[32,2,128,256]{3,2,1,0:T(8,128)(2,1)} %bitcast.44), calls=%async_computation | async-start | bytes 8388608 | tf_op jit(solution)/shard_map/all_to_all | solution.py:462
  14.4 6.4 %collective-permute-start.3 = (f32[24,256]{1,0:T(8,128)S(1)}, f32[24,256]{1,0:T(8,128)S(1)}, u32[]{:S(2)}, u32[]{:S(2)}) collective-permute-start(f32[24,256]{1,0:T(8,128)S(1)} %pad_maximum_fusion.1), channel_id=1, source_target_pairs={{0,3},{1,0},{2,1},{3,2},{4,7},{5,4},{6,5},{7,6},{8,11},{9,8},{10,9... | collective-permute-start | bytes 73736 | tf_op jit(solution)/shard_map/ppermute | solution.py:458
  15.2 28.1 %collective-permute-start.2 = (bf16[1024,256]{1,0:T(8,128)(2,1)S(1)}, bf16[1024,256]{1,0:T(8,128)(2,1)S(1)}, u32[]{:S(2)}, u32[]{:S(2)}) collective-permute-start(bf16[1024,256]{1,0:T(8,128)(2,1)S(1)} %bitcast.46), channel_id=1, source_target_pairs={{0,3},{1,0},{2,1},{3,2},{4,7},{5,4},{6,5},{7,6},{8,11},{9,8},{10,9... | collective-permute-start | bytes 1572872 | tf_op jit(solution)/shard_map/ppermute | solution.py:458
  15.8 27.6 %collective-permute-start.1 = (bf16[1024,256]{1,0:T(8,128)(2,1)S(1)}, bf16[1024,256]{1,0:T(8,128)(2,1)}, u32[]{:S(2)}, u32[]{:S(2)}) collective-permute-start(bf16[1024,256]{1,0:T(8,128)(2,1)S(1)} %bitcast.47), channel_id=1, source_target_pairs={{0,2},{1,3},{2,0},{3,1},{4,6},{5,7},{6,4},{7,5},{8,10},{9,11},{10,... | collective-permute-start | bytes 1572872 | tf_op jit(solution)/shard_map/ppermute | solution.py:458
  18.8 24.5 %collective-permute-start = (bf16[1024,256]{1,0:T(8,128)(2,1)S(1)}, bf16[1024,256]{1,0:T(8,128)(2,1)}, u32[]{:S(2)}, u32[]{:S(2)}) collective-permute-start(bf16[1024,256]{1,0:T(8,128)(2,1)S(1)} %bitcast.48), channel_id=1, source_target_pairs={{0,1},{1,2},{2,3},{3,0},{4,5},{5,6},{6,7},{7,4},{8,9},{9,10},{10,1... | collective-permute-start | bytes 1572872 | tf_op jit(solution)/shard_map/ppermute | solution.py:458
  20.6 22.3 %collective-permute-start.4 = (f32[24,256]{1,0:T(8,128)S(1)}, f32[24,256]{1,0:T(8,128)S(1)}, u32[]{:S(2)}, u32[]{:S(2)}) collective-permute-start(f32[24,256]{1,0:T(8,128)S(1)} %pad_maximum_fusion.1), channel_id=1, source_target_pairs={{0,2},{1,3},{2,0},{3,1},{4,6},{5,7},{6,4},{7,5},{8,10},{9,11},{10,... | collective-permute-start | bytes 73736 | tf_op jit(solution)/shard_map/ppermute | solution.py:458
  20.8 22.2 %collective-permute-start.5 = (f32[24,256]{1,0:T(8,128)S(1)}, f32[24,256]{1,0:T(8,128)S(1)}, u32[]{:S(2)}, u32[]{:S(2)}) collective-permute-start(f32[24,256]{1,0:T(8,128)S(1)} %pad_maximum_fusion.1), channel_id=1, source_target_pairs={{0,1},{1,2},{2,3},{3,0},{4,5},{5,6},{6,7},{7,4},{8,9},{9,10},{10,1... | collective-permute-start | bytes 73736 | tf_op jit(solution)/shard_map/ppermute | solution.py:458
  43.3 23.8 %copy-start.3 = (s32[1,32]{1,0:T(1,128)S(1)}, s32[1,32]{1,0:T(1,128)}, u32[]{:S(2)}) copy-start(s32[1,32]{1,0:T(1,128)} %param.10) | copy-start | bytes 388
  77.5 25.7 %collective-permute-start.7 = (bf16[1024,256]{1,0:T(8,128)(2,1)S(1)}, bf16[1024,256]{1,0:T(8,128)(2,1)}, u32[]{:S(2)}, u32[]{:S(2)}) collective-permute-start(bf16[1024,256]{1,0:T(8,128)(2,1)S(1)} %aggregate.3.after), channel_id=1, source_target_pairs={{0,2},{1,3},{2,0},{3,1},{4,6},{5,7},{6,4},{7,5},{8,10},{9,11},{10,... | collective-permute-start | bytes 1572872 | tf_op jit(solution)/shard_map/ppermute | solution.py:458
  78.1 25.2 %collective-permute-start.6 = (bf16[1024,256]{1,0:T(8,128)(2,1)}, bf16[1024,256]{1,0:T(8,128)(2,1)}, u32[]{:S(2)}, u32[]{:S(2)}) collective-permute-start(bf16[1024,256]{1,0:T(8,128)(2,1)} %get-tuple-element.28), channel_id=1, source_target_pairs={{0,1},{1,2},{2,3},{3,0},{4,5},{5,6},{6,7},{7,4},{8,9},{9,10},{10,1... | collective-permute-start | bytes 1572872 | tf_op jit(solution)/shard_map/ppermute | solution.py:458
  80.2 23.1 %collective-permute-start.8 = (bf16[1024,256]{1,0:T(8,128)(2,1)S(1)}, bf16[1024,256]{1,0:T(8,128)(2,1)}, u32[]{:S(2)}, u32[]{:S(2)}) collective-permute-start(bf16[1024,256]{1,0:T(8,128)(2,1)S(1)} %get-tuple-element.27.after), channel_id=1, source_target_pairs={{0,3},{1,0},{2,1},{3,2},{4,7},{5,4},{6,5},{7,6},{8,11},{9,8},{10,9... | collective-permute-start | bytes 1572872 | tf_op jit(solution)/shard_map/ppermute | solution.py:458
  81.4 21.9 %copy-start.1 = (f32[1024,1]{1,0:T(8,128)S(1)}, f32[1024,1]{1,0:T(8,128)}, u32[]{:S(2)}) copy-start(f32[1024,1]{1,0:T(8,128)} %copy.21.refs_5_) | copy-start | bytes 12292
  86.0 48.4 %copy-start.2 = (s32[4096]{0:T(1024)S(1)}, s32[4096]{0:T(1024)}, u32[]{:S(2)}) copy-start(s32[4096]{0:T(1024)} %param.14) | copy-start | bytes 49156
  103.2 31.2 %copy-start = (bf16[32,4,128,128]{3,2,1,0:T(8,128)(2,1)S(1)}, bf16[32,4,128,128]{3,2,1,0:T(8,128)(2,1)}, u32[]{:S(2)}) copy-start(bf16[32,4,128,128]{3,2,1,0:T(8,128)(2,1)} %tiles.1) | copy-start | bytes 12582916
  108.7 4.3 %collective-permute-start.9 = (f32[8,16,128]{2,1,0:T(8,128)S(1)}, f32[8,16,128]{2,1,0:T(8,128)S(1)}, u32[]{:S(2)}, u32[]{:S(2)}) collective-permute-start(f32[8,16,128]{2,1,0:T(8,128)S(1)} %get-tuple-element.32.p0), channel_id=1, source_target_pairs={{0,1},{1,2},{2,3},{3,0},{4,5},{5,6},{6,7},{7,4},{8,9},{9,10},{10,1... | collective-permute-start | bytes 196616 | tf_op jit(solution)/shard_map/ppermute | solution.py:458
  110.5 5.8 %collective-permute-start.10 = (f32[8,16,128]{2,1,0:T(8,128)S(1)}, f32[8,16,128]{2,1,0:T(8,128)S(1)}, u32[]{:S(2)}, u32[]{:S(2)}) collective-permute-start(f32[8,16,128]{2,1,0:T(8,128)S(1)} %get-tuple-element.32.p0), channel_id=1, source_target_pairs={{0,2},{1,3},{2,0},{3,1},{4,6},{5,7},{6,4},{7,5},{8,10},{9,11},{10,... | collective-permute-start | bytes 196616 | tf_op jit(solution)/shard_map/ppermute | solution.py:458
  111.4 4.9 %collective-permute-start.11 = (f32[8,16,128]{2,1,0:T(8,128)S(1)}, f32[8,16,128]{2,1,0:T(8,128)S(1)}, u32[]{:S(2)}, u32[]{:S(2)}) collective-permute-start(f32[8,16,128]{2,1,0:T(8,128)S(1)} %get-tuple-element.32.p0), channel_id=1, source_target_pairs={{0,3},{1,0},{2,1},{3,2},{4,7},{5,4},{6,5},{7,6},{8,11},{9,8},{10,9... | collective-permute-start | bytes 196616 | tf_op jit(solution)/shard_map/ppermute | solution.py:458
  155.1 6.1 %collective-permute-start.17 = (f32[24,256]{1,0:T(8,128)S(1)}, f32[24,256]{1,0:T(8,128)S(1)}, u32[]{:S(2)}, u32[]{:S(2)}) collective-permute-start(f32[24,256]{1,0:T(8,128)S(1)} %get-tuple-element.42), channel_id=1, source_target_pairs={{0,6},{1,7},{2,4},{3,5},{4,2},{5,3},{6,0},{7,1},{8,14},{9,15},{10,... | collective-permute-start | bytes 73736 | tf_op jit(solution)/shard_map/ppermute | solution.py:505
  157.0 5.4 %collective-permute-start.18 = (f32[24,256]{1,0:T(8,128)S(1)}, f32[24,256]{1,0:T(8,128)S(1)}, u32[]{:S(2)}, u32[]{:S(2)}) collective-permute-start(f32[24,256]{1,0:T(8,128)S(1)} %get-tuple-element.43), channel_id=1, source_target_pairs={{0,5},{1,6},{2,7},{3,4},{4,1},{5,2},{6,3},{7,0},{8,13},{9,14},{10,... | collective-permute-start | bytes 73736 | tf_op jit(solution)/shard_map/ppermute | solution.py:505
  157.8 10.3 %collective-permute-start.13 = (f32[24,256]{1,0:T(8,128)S(1)}, f32[24,256]{1,0:T(8,128)S(1)}, u32[]{:S(2)}, u32[]{:S(2)}) collective-permute-start(f32[24,256]{1,0:T(8,128)S(1)} %get-tuple-element.42), channel_id=1, source_target_pairs={{0,2},{1,3},{2,0},{3,1},{4,6},{5,7},{6,4},{7,5},{8,10},{9,11},{10,... | collective-permute-start | bytes 73736 | tf_op jit(solution)/shard_map/ppermute | solution.py:505
  159.7 8.4 %collective-permute-start.14 = (f32[24,256]{1,0:T(8,128)S(1)}, f32[24,256]{1,0:T(8,128)S(1)}, u32[]{:S(2)}, u32[]{:S(2)}) collective-permute-start(f32[24,256]{1,0:T(8,128)S(1)} %get-tuple-element.43), channel_id=1, source_target_pairs={{0,1},{1,2},{2,3},{3,0},{4,5},{5,6},{6,7},{7,4},{8,9},{9,10},{10,1... | collective-permute-start | bytes 73736 | tf_op jit(solution)/shard_map/ppermute | solution.py:505
  160.9 7.2 %collective-permute-start.16 = (f32[24,256]{1,0:T(8,128)S(1)}, f32[24,256]{1,0:T(8,128)S(1)}, u32[]{:S(2)}, u32[]{:S(2)}) collective-permute-start(f32[24,256]{1,0:T(8,128)S(1)} %get-tuple-element.41), channel_id=1, source_target_pairs={{0,7},{1,4},{2,5},{3,6},{4,3},{5,0},{6,1},{7,2},{8,15},{9,12},{10,... | collective-permute-start | bytes 73736 | tf_op jit(solution)/shard_map/ppermute | solution.py:505
  161.1 7.0 %collective-permute-start.12 = (f32[24,256]{1,0:T(8,128)S(1)}, f32[24,256]{1,0:T(8,128)S(1)}, u32[]{:S(2)}, u32[]{:S(2)}) collective-permute-start(f32[24,256]{1,0:T(8,128)S(1)} %get-tuple-element.41), channel_id=1, source_target_pairs={{0,3},{1,0},{2,1},{3,2},{4,7},{5,4},{6,5},{7,6},{8,11},{9,8},{10,9... | collective-permute-start | bytes 73736 | tf_op jit(solution)/shard_map/ppermute | solution.py:505
  162.3 5.8 %collective-permute-start.15 = (f32[24,256]{1,0:T(8,128)S(1)}, f32[24,256]{1,0:T(8,128)S(1)}, u32[]{:S(2)}, u32[]{:S(2)}) collective-permute-start(f32[24,256]{1,0:T(8,128)S(1)} %get-tuple-element.40), channel_id=1, source_target_pairs={{0,4},{1,5},{2,6},{3,7},{4,0},{5,1},{6,2},{7,3},{8,12},{9,13},{10,... | collective-permute-start | bytes 73736 | tf_op jit(solution)/shard_map/ppermute | solution.py:505
  168.2 62.9 %all-to-all-start.3 = ((bf16[128,32,256]{2,1,0:T(8,128)(2,1)}), bf16[128,32,256]{2,1,0:T(8,128)(2,1)S(1)}, u32[]{:S(2)}, u32[]{:S(2)}) async-start(bf16[128,32,256]{2,1,0:T(8,128)(2,1)} %bitcast.45), calls=%async_computation.3 | async-start | bytes 4194304 | tf_op jit(solution)/shard_map/all_to_all | solution.py:509
  174.1 12.5 %collective-permute-start.19 = (f32[24,256]{1,0:T(8,128)S(1)}, f32[24,256]{1,0:T(8,128)S(1)}, u32[]{:S(2)}, u32[]{:S(2)}) collective-permute-start(f32[24,256]{1,0:T(8,128)S(1)} %add_add_fusion.refs_0_), channel_id=1, source_target_pairs={{0,8},{4,12},{8,0},{12,4},{16,24},{20,28},{24,16},{28,20},{32,40},... | collective-permute-start | bytes 73736 | tf_op jit(solution)/shard_map/ppermute | solution.py:517
  175.8 28.8 %collective-permute-start.20 = (f32[24,256]{1,0:T(8,128)S(1)}, f32[24,256]{1,0:T(8,128)S(1)}, u32[]{:S(2)}, u32[]{:S(2)}) collective-permute-start(f32[24,256]{1,0:T(8,128)S(1)} %add_add_fusion.refs_0_), channel_id=1, source_target_pairs={{0,16},{4,20},{8,24},{12,28},{16,0},{20,4},{24,8},{28,12},{32,48},... | collective-permute-start | bytes 73736 | tf_op jit(solution)/shard_map/ppermute | solution.py:517
  179.1 25.6 %collective-permute-start.21 = (f32[24,256]{1,0:T(8,128)S(1)}, f32[24,256]{1,0:T(8,128)S(1)}, u32[]{:S(2)}, u32[]{:S(2)}) collective-permute-start(f32[24,256]{1,0:T(8,128)S(1)} %add_add_fusion.refs_0_), channel_id=1, source_target_pairs={{0,24},{4,28},{8,16},{12,20},{16,8},{20,12},{24,0},{28,4},{32,56},... | collective-permute-start | bytes 73736 | tf_op jit(solution)/shard_map/ppermute | solution.py:517
  179.1 28.0 %collective-permute-start.22 = (f32[24,256]{1,0:T(8,128)S(1)}, f32[24,256]{1,0:T(8,128)S(1)}, u32[]{:S(2)}, u32[]{:S(2)}) collective-permute-start(f32[24,256]{1,0:T(8,128)S(1)} %add_add_fusion.refs_0_), channel_id=1, source_target_pairs={{0,32},{4,36},{8,40},{12,44},{16,48},{20,52},{24,56},{28,60},{32,0... | collective-permute-start | bytes 73736 | tf_op jit(solution)/shard_map/ppermute | solution.py:517
  180.6 27.0 %collective-permute-start.23 = (f32[24,256]{1,0:T(8,128)S(1)}, f32[24,256]{1,0:T(8,128)S(1)}, u32[]{:S(2)}, u32[]{:S(2)}) collective-permute-start(f32[24,256]{1,0:T(8,128)S(1)} %add_add_fusion.refs_0_), channel_id=1, source_target_pairs={{0,40},{4,44},{8,32},{12,36},{16,56},{20,60},{24,48},{28,52},{32,8... | collective-permute-start | bytes 73736 | tf_op jit(solution)/shard_map/ppermute | solution.py:517
  186.7 26.6 %collective-permute-start.24 = (f32[24,256]{1,0:T(8,128)S(1)}, f32[24,256]{1,0:T(8,128)S(1)}, u32[]{:S(2)}, u32[]{:S(2)}) collective-permute-start(f32[24,256]{1,0:T(8,128)S(1)} %add_add_fusion.refs_0_), channel_id=1, source_target_pairs={{0,48},{4,52},{8,56},{12,60},{16,32},{20,36},{24,40},{28,44},{32,1... | collective-permute-start | bytes 73736 | tf_op jit(solution)/shard_map/ppermute | solution.py:517
  204.6 10.2 %collective-permute-start.25 = (f32[24,256]{1,0:T(8,128)S(1)}, f32[24,256]{1,0:T(8,128)S(1)}, u32[]{:S(2)}, u32[]{:S(2)}) collective-permute-start(f32[24,256]{1,0:T(8,128)S(1)} %add_add_fusion.refs_0_), channel_id=1, source_target_pairs={{0,56},{4,60},{8,48},{12,52},{16,40},{20,44},{24,32},{28,36},{32,2... | collective-permute-start | bytes 73736 | tf_op jit(solution)/shard_map/ppermute | solution.py:517
  204.6 11.3 %collective-permute-start.26 = (f32[24,256]{1,0:T(8,128)S(1)}, f32[24,256]{1,0:T(8,128)S(1)}, u32[]{:S(2)}, u32[]{:S(2)}) collective-permute-start(f32[24,256]{1,0:T(8,128)S(1)} %add_add_fusion.refs_0_), channel_id=1, source_target_pairs={{0,64},{4,68},{8,72},{12,76},{16,80},{20,84},{24,88},{28,92},{32,9... | collective-permute-start | bytes 73736 | tf_op jit(solution)/shard_map/ppermute | solution.py:517
  207.1 9.0 %collective-permute-start.27 = (f32[24,256]{1,0:T(8,128)S(1)}, f32[24,256]{1,0:T(8,128)S(1)}, u32[]{:S(2)}, u32[]{:S(2)}) collective-permute-start(f32[24,256]{1,0:T(8,128)S(1)} %add_add_fusion.refs_0_), channel_id=1, source_target_pairs={{0,72},{4,76},{8,64},{12,68},{16,88},{20,92},{24,80},{28,84},{32,1... | collective-permute-start | bytes 73736 | tf_op jit(solution)/shard_map/ppermute | solution.py:517
  207.5 16.4 %collective-permute-start.28 = (f32[24,256]{1,0:T(8,128)S(1)}, f32[24,256]{1,0:T(8,128)S(1)}, u32[]{:S(2)}, u32[]{:S(2)}) collective-permute-start(f32[24,256]{1,0:T(8,128)S(1)} %add_add_fusion.refs_0_), channel_id=1, source_target_pairs={{0,80},{4,84},{8,88},{12,92},{16,64},{20,68},{24,72},{28,76},{32,1... | collective-permute-start | bytes 73736 | tf_op jit(solution)/shard_map/ppermute | solution.py:517
  213.3 10.9 %collective-permute-start.29 = (f32[24,256]{1,0:T(8,128)S(1)}, f32[24,256]{1,0:T(8,128)S(1)}, u32[]{:S(2)}, u32[]{:S(2)}) collective-permute-start(f32[24,256]{1,0:T(8,128)S(1)} %add_add_fusion.refs_0_), channel_id=1, source_target_pairs={{0,88},{4,92},{8,80},{12,84},{16,72},{20,76},{24,64},{28,68},{32,1... | collective-permute-start | bytes 73736 | tf_op jit(solution)/shard_map/ppermute | solution.py:517
  214.8 9.5 %collective-permute-start.30 = (f32[24,256]{1,0:T(8,128)S(1)}, f32[24,256]{1,0:T(8,128)S(1)}, u32[]{:S(2)}, u32[]{:S(2)}) collective-permute-start(f32[24,256]{1,0:T(8,128)S(1)} %add_add_fusion.refs_0_), channel_id=1, source_target_pairs={{0,96},{4,100},{8,104},{12,108},{16,112},{20,116},{24,120},{28,124... | collective-permute-start | bytes 73736 | tf_op jit(solution)/shard_map/ppermute | solution.py:517
  215.9 8.3 %collective-permute-start.31 = (f32[24,256]{1,0:T(8,128)S(1)}, f32[24,256]{1,0:T(8,128)S(1)}, u32[]{:S(2)}, u32[]{:S(2)}) collective-permute-start(f32[24,256]{1,0:T(8,128)S(1)} %add_add_fusion.refs_0_), channel_id=1, source_target_pairs={{0,104},{4,108},{8,96},{12,100},{16,120},{20,124},{24,112},{28,116... | collective-permute-start | bytes 73736 | tf_op jit(solution)/shard_map/ppermute | solution.py:517
  216.1 10.0 %collective-permute-start.32 = (f32[24,256]{1,0:T(8,128)S(1)}, f32[24,256]{1,0:T(8,128)S(1)}, u32[]{:S(2)}, u32[]{:S(2)}) collective-permute-start(f32[24,256]{1,0:T(8,128)S(1)} %add_add_fusion.refs_0_), channel_id=1, source_target_pairs={{0,112},{4,116},{8,120},{12,124},{16,96},{20,100},{24,104},{28,108... | collective-permute-start | bytes 73736 | tf_op jit(solution)/shard_map/ppermute | solution.py:517
  223.9 7.1 %collective-permute-start.33 = (f32[24,256]{1,0:T(8,128)S(1)}, f32[24,256]{1,0:T(8,128)S(1)}, u32[]{:S(2)}, u32[]{:S(2)}) collective-permute-start(f32[24,256]{1,0:T(8,128)S(1)} %add_add_fusion.refs_0_), channel_id=1, source_target_pairs={{0,120},{4,124},{8,112},{12,116},{16,104},{20,108},{24,96},{28,100... | collective-permute-start | bytes 73736 | tf_op jit(solution)/shard_map/ppermute | solution.py:517

commit v6 on v4

--- a/solution.py
+++ b/solution.py
@@ -26,6 +26,12 @@
 
 def dot(a, b, dims):
     return lax.dot_general(a, b, dims, preferred_element_type=F32)
+
+
+def tree(terms):
+    while len(terms) > 1:
+        terms = [a + b for a, b in zip(terms[::2], terms[1::2])]
+    return terms[0]
 
 
 def in_hbm(x):
@@ -110,7 +116,7 @@
         grid_spec=pltpu.PrefetchScalarGridSpec(
             num_scalar_prefetch=3,
             grid=(),
-            in_specs=[hbm] * 3,
+            in_specs=[pl.BlockSpec(memory_space=pl.ANY), hbm, hbm],
             out_specs=[pl.BlockSpec(memory_space=pltpu.VMEM)] * len(which),
             scratch_shapes=[
                 pltpu.VMEM(arrived.shape, BF16),
@@ -123,7 +129,7 @@
         compiler_params=params(14),
         cost_estimate=cost(len(which) * group * per * 2 * BLK**3, 8 * MIB),
         name="aggregate",
-    )(src, counts, me, in_hbm(arrived), in_hbm(tiles), in_hbm(features))
+    )(src, counts, me, arrived, in_hbm(tiles), in_hbm(features))
 
 
 def dense_kernel(nfeat, *refs):
@@ -383,12 +389,10 @@
     @pl.when(g == 0)
     def _():
         acc[...] = jnp.zeros_like(acc)
-        terms = [ref[...] for ref in small]
-        while len(terms) > 1:
-            terms = [a + b for a, b in zip(terms[::2], terms[1::2])]
+        whole = tree([ref[...] for ref in small])
         grades = second.shape[0]
-        second[...] = terms[0][:grades]
-        bias[...] = terms[0][grades : grades + 1]
+        second[...] = whole[:grades]
+        bias[...] = whole[grades : grades + 1]
 
     total = arrived[0].astype(F32)
     for i in range(1, arrived.shape[0]):
@@ -442,6 +446,11 @@
     def ahead(x, k):
         return lax.ppermute(x, "feat", [(i, (i + k) % nfeat) for i in range(nfeat)])
 
+    def nearby(x, masks):
+        return [x] + [
+            lax.ppermute(x, "nodes", [(i, i ^ mask) for i in range(parts)]) for mask in masks
+        ]
+
     def swap(x):
         shaped = x.reshape(parts, slots, *x.shape[1:])
         moved = lax.all_to_all(shaped, "nodes", split_axis=0, concat_axis=0, tiled=True)
@@ -451,10 +460,13 @@
     send = pick(features, table, 1)
 
     flat = w_first.T
-    weights = jnp.concatenate([flat] + [ahead(flat, k) for k in range(1, nfeat)], 1)
+    weights = [ahead(flat, k) for k in (2, 1, 3)]
     consts = jnp.concatenate(
         [w_second.T.astype(F32), jnp.broadcast_to(b_first[None], (8, b_first.shape[0]))], 0
     )
+    send, weights = lax.optimization_barrier((send, weights))
+    consts, first_weight = lax.optimization_barrier((consts, weights[1]))
+    weights = jnp.concatenate([flat, first_weight, weights[0], weights[2]], 1)
     turned = [consts] + [ahead(consts, k) for k in range(1, nfeat)]
     ring = jnp.stack([turned[k] for k in (3, 2, 1, 0, 3, 2, 1)])
     ordered = lax.dynamic_slice_in_dim(ring, nfeat - 1 - axis, nfeat, 0)
@@ -462,9 +474,6 @@
     bias = ordered[:, grades].reshape(hid, 1)
     second = second_t.T
 
-    send, weights, bias, second_t, second = lax.optimization_barrier(
-        (send, weights, bias, second_t, second)
-    )
     arrived.append(swap(send))
     others = (2, 1, 3)
     make = functools.partial(aggregate, src, counts, me)
@@ -489,7 +498,8 @@
     for k in range(1, nfeat):
         rest = rest + ahead(small[k], nfeat - k)
     big = big_gradient(me, dpre, first + last, parts)
-    big, rest = lax.optimization_barrier((big, rest))
+    rest = nearby(rest, (1, 2, 3))
+    big, rest = lax.optimization_barrier((big, tree(rest)))
     moved = lax.all_to_all(
         big.reshape(parts * nfeat, *big.shape[2:]),
         ("nodes", "feat"),
@@ -497,13 +507,7 @@
         concat_axis=0,
         tiled=True,
     )
-    terms = [rest]
-    for group in ((1, 2, 3, 4, 5, 6, 7), (8, 16, 24)):
-        while len(terms) > 1:
-            terms = [a + b for a, b in zip(terms[::2], terms[1::2])]
-        terms += [
-            lax.ppermute(terms[0], "nodes", [(i, i ^ d) for i in range(parts)]) for d in group
-        ]
+    terms = nearby(rest, range(4, parts, 4))
     grad_first, grad_second, grad_bias = total(moved, terms, grades)
     return grad_first.T, grad_bias.reshape(-1), grad_second.T
 

time: 210 us -> 206 us (0.981)
  the two profiles are of different devices: /device:TPU:1 before, /device:TPU:6 now
where the time goes in v6:
time: 206 us
  starting transfers between devices  70.6 us (34%)
  waiting for transfers between devices  60.5 us (29%)
  Pallas kernels  37.6 us (18%)
  blocking collectives  27.6 us (13%)
  local copies, waits for them, and re-layouts  5.55 us (3%)
  other arithmetic  3.01 us (1%)
    ppermute x18, waiting for transfers between devices, ahead(): return lax.ppermute(x, 'feat', [(i, (i + k) % nfeat) for i in range(nfeat)])  37 us
    ppermute x10, starting transfers between devices, nearby(): lax.ppermute(x, 'nodes', [(i, i ^ mask) for i in range(parts)])  30.1 us
    all_to_all x2, blocking collectives, swap(): lax.all_to_all(shaped, 'nodes', split_axis=0, concat_axis=0, tiled=True)  27.6 us
    ppermute x18, starting transfers between devices, ahead(): return lax.ppermute(x, 'feat', [(i, (i + k) % nfeat) for i in range(nfeat)])  20.7 us
    all_to_all x2, waiting for transfers between devices, swap(): lax.all_to_all(shaped, 'nodes', split_axis=0, concat_axis=0, tiled=True)  14.7 us
    all_to_all x2, starting transfers between devices, swap(): lax.all_to_all(shaped, 'nodes', split_axis=0, concat_axis=0, tiled=True)  14.2 us
    pallas_call x3, Pallas kernels, aggregate(): pl.pallas_call(functools.partial(agg_kernel, which, chunk, nfeat), grid_s...  11.2 us
    ppermute x10, waiting for transfers between devices, nearby(): lax.ppermute(x, 'nodes', [(i, i ^ mask) for i in range(parts)])  8.77 us
  transfers between devices with their start and end apart: 31, of which 18 were waited for; matrix products, arithmetic and copies ran while one was open for 2% of the time, Pallas kernels for 9%

profile of v6, /device:TPU:6, one launch (start us, length us, event | category | flops | bytes accessed | tf_op | source)
XLA Modules:
  0.0 205.7 jit_solution(15564552442447054541)
XLA Ops:
  0.6 0.8 copy.17
  1.5 3.1 %pick.2 = bf16[64,128,128]{2,1,0:T(8,128)(2,1)} custom-call(s32[64]{0:T(128)S(1)} %reshape.55.table, bf16[4096,256]{1,0:T(8,128)(2,1)} %features.9), custom_call_target="tpu_custom_call" | custom-call | bytes 4194304 | tf_op jit(solution)/shard_map/pick/pallas_call | solution.py:57
  4.6 8.5 %all-to-all-start = ((bf16[32,2,128,128]{3,2,1,0:T(8,128)(2,1)}), bf16[32,2,128,128]{3,2,1,0:T(8,128)(2,1)S(1)}, u32[]{:S(2)}, u32[]{:S(2)}) async-start(bf16[32,2,128,128]{3,2,1,0:T(8,128)(2,1)} %bitcast.50), calls=%async_computation | async-start | bytes 4194304 | tf_op jit(solution)/shard_map/all_to_all | solution.py:456
  13.3 1.5 collective-permute-start.3
  14.8 2.1 %collective-permute-start.4 = (bf16[1024,256]{1,0:T(8,128)(2,1)S(1)}, bf16[1024,256]{1,0:T(8,128)(2,1)S(1)}, u32[]{:S(2)}, u32[]{:S(2)}) collective-permute-start(bf16[1024,256]{1,0:T(8,128)(2,1)S(1)} %bitcast.53), channel_id=1, source_target_pairs={{0,1},{1,2},{2,3},{3,0},{4,5},{5,6},{6,7},{7,4},{8,9},{9,10},{10,1... | collective-permute-start | bytes 1572872 | tf_op jit(solution)/shard_map/ppermute | solution.py:447
  16.9 3.1 %pick.3 = bf16[64,128,128]{2,1,0:T(8,128)(2,1)} custom-call(s32[64]{0:T(128)S(1)} %reshape.55.table, bf16[4096,256]{1,0:T(8,128)(2,1)} %features.9), custom_call_target="tpu_custom_call" | custom-call | bytes 4194304 | tf_op jit(solution)/shard_map/pick/pallas_call | solution.py:57
  20.1 9.7 %collective-permute-done.3 = bf16[1024,256]{1,0:T(8,128)(2,1)S(1)} collective-permute-done((bf16[1024,256]{1,0:T(8,128)(2,1)S(1)}, bf16[1024,256]{1,0:T(8,128)(2,1)S(1)}, u32[]{:S(2)}, u32[]{:S(2)}) %collective-permute-start.3) | collective-permute-done | bytes 524320 | tf_op jit(solution)/shard_map/ppermute | solution.py:447
  29.7 8.4 %collective-permute-done.4 = bf16[1024,256]{1,0:T(8,128)(2,1)S(1)} collective-permute-done((bf16[1024,256]{1,0:T(8,128)(2,1)S(1)}, bf16[1024,256]{1,0:T(8,128)(2,1)S(1)}, u32[]{:S(2)}, u32[]{:S(2)}) %collective-permute-start.4) | collective-permute-done | bytes 524320 | tf_op jit(solution)/shard_map/ppermute | solution.py:447
  38.1 0.8 copy-done.8
  38.9 1.4 collective-permute-done.5
  40.4 1.7 all-to-all-done
  42.0 1.4 copy-done.1
  43.4 5.7 %all-to-all-start.1 = ((bf16[32,2,128,128]{3,2,1,0:T(8,128)(2,1)}), bf16[32,2,128,128]{3,2,1,0:T(8,128)(2,1)S(1)}, u32[]{:S(2)}, u32[]{:S(2)}) async-start(bf16[32,2,128,128]{3,2,1,0:T(8,128)(2,1)} %bitcast.49), calls=%async_computation.1 | async-start | bytes 4194304 | tf_op jit(solution)/shard_map/all_to_all | solution.py:456
  49.4 0.8 collective-permute-start.9
  50.2 2.0 collective-permute-start.10
  52.2 2.2 %collective-permute-start.11 = (f32[24,256]{1,0:T(8,128)S(1)}, f32[24,256]{1,0:T(8,128)S(1)}, u32[]{:S(2)}, u32[]{:S(2)}) collective-permute-start(f32[24,256]{1,0:T(8,128)S(1)} %pad_maximum_fusion.1), channel_id=1, source_target_pairs={{0,1},{1,2},{2,3},{3,0},{4,5},{5,6},{6,7},{7,4},{8,9},{9,10},{10,1... | collective-permute-start | bytes 73736 | tf_op jit(solution)/shard_map/ppermute | solution.py:447
  54.4 3.0 %pad_maximum_fusion.refs_8_ = bf16[1024,1024]{1,0:T(8,128)(2,1)} fusion(bf16[1024,256]{1,0:T(8,128)(2,1)} %collective-permute-done.5, bf16[1024,256]{1,0:T(8,128)(2,1)} %copy-done.7, bf16[1024,256]{1,0:T(8,128)(2,1)} %copy-done.8, bf16[1024,256]{1,0:T(8,128)(2,1)S(1)} %bitcast.55), kind=kLoop, calls=%fused_computation | loop fusion | flops 8388608 | bytes 4194304 | tf_op jit(solution)/shard_map/concatenate | solution.py:469
  57.4 4.6 %aggregate.3 = (bf16[1024,128]{1,0:T(8,128)(2,1)}, bf16[1024,128]{1,0:T(8,128)(2,1)S(1)}, bf16[1024,128]{1,0:T(8,128)(2,1)}, bf16[1024,128]{1,0:T(8,128)(2,1)S(1)}) custom-call(s32[128]{0:T(128)S(1)} %reshape.56.src, s32[32]{0:T(128)S(1)} %bitcast.45, s32[1]{0:T(128)} %bitcast.me, bf16[64,128,128]{2,1,0:T(8,128)(2,1)S(1)} %bitcast.37, ...), custom_call_target="tpu_custom_call" | custom-call | flops 536870912 | bytes 8388608 | tf_op jit(solution)/shard_map/aggregate/pallas_call | solution.py:114
  62.0 2.1 %collective-permute-start = (bf16[1024,128]{1,0:T(8,128)(2,1)S(1)}, bf16[1024,128]{1,0:T(8,128)(2,1)S(1)}, u32[]{:S(2)}, u32[]{:S(2)}) collective-permute-start(bf16[1024,128]{1,0:T(8,128)(2,1)S(1)} %get-tuple-element.33), channel_id=1, source_target_pairs={{0,1},{1,2},{2,3},{3,0},{4,5},{5,6},{6,7},{7,4},{8,9},{9,10},{10,1... | collective-permute-start | bytes 786440 | tf_op jit(solution)/shard_map/ppermute | solution.py:447
  64.2 0.9 collective-permute-start.2
  65.0 13.0 %all-to-all-done.1 = bf16[32,2,128,128]{3,2,1,0:T(8,128)(2,1)S(1)} async-done(((bf16[32,2,128,128]{3,2,1,0:T(8,128)(2,1)}), bf16[32,2,128,128]{3,2,1,0:T(8,128)(2,1)S(1)}, u32[]{:S(2)}, u32[]{:S(2)}) %all-to-all-start.1) | async-done | bytes 2097184 | tf_op jit(solution)/shard_map/all_to_all | solution.py:456
  78.1 4.2 %aggregate.5 = (bf16[1024,128]{1,0:T(8,128)(2,1)}, bf16[1024,128]{1,0:T(8,128)(2,1)}, bf16[1024,128]{1,0:T(8,128)(2,1)}) custom-call(s32[128]{0:T(128)S(1)} %reshape.56.src, s32[32]{0:T(128)S(1)} %bitcast.46, s32[1]{0:T(128)} %bitcast.me, bf16[64,128,128]{2,1,0:T(8,128)(2,1)S(1)} %bitcast.35, bf16[32,4,128,128]{3,2,1,0:T(8,128)(2,1)} %tiles.1, ...), custom_call_target="tpu_custom_call" | custom-call | flops 402653184 | bytes 8388608 | tf_op jit(solution)/shard_map/aggregate/pallas_call | solution.py:114
  82.2 1.3 collective-permute-start.6
  83.5 1.5 collective-permute-start.7
  85.1 0.9 collective-permute-start.8
  86.0 0.7 copy-done.9
  86.6 0.2 copy.21.refs_9_
  86.8 0.9 fusion
  88.0 2.5 %aggregate.4.refs_4_ = bf16[1024,128]{1,0:T(8,128)(2,1)S(1)} custom-call(s32[128]{0:T(128)S(1)} %reshape.56.src, s32[32]{0:T(128)S(1)} %bitcast.47, s32[1]{0:T(128)} %bitcast.me, bf16[64,128,128]{2,1,0:T(8,128)(2,1)S(1)} %bitcast.36, bf16[32,4,128,128]{3,2,1,0:T(8,128)(2,1)} %tiles.1, bf16[4096,256]{1,0:T(8,128)(2,1)} %features.9), custom_call_target="tpu_custom_call" | custom-call | flops 134217728 | bytes 8388608 | tf_op jit(solution)/shard_map/aggregate/pallas_call | solution.py:114
  90.5 1.4 collective-permute-done.6.refs_5_
  91.8 2.8 %collective-permute-done.7.refs_6_ = bf16[1024,128]{1,0:T(8,128)(2,1)} collective-permute-done((bf16[1024,128]{1,0:T(8,128)(2,1)}, bf16[1024,128]{1,0:T(8,128)(2,1)}, u32[]{:S(2)}, u32[]{:S(2)}) %collective-permute-start.7) | collective-permute-done | bytes 262176 | tf_op jit(solution)/shard_map/ppermute | solution.py:447
  94.6 3.9 %collective-permute-done.8.refs_7_ = bf16[1024,128]{1,0:T(8,128)(2,1)} collective-permute-done((bf16[1024,128]{1,0:T(8,128)(2,1)}, bf16[1024,128]{1,0:T(8,128)(2,1)}, u32[]{:S(2)}, u32[]{:S(2)}) %collective-permute-start.8) | collective-permute-done | bytes 262176 | tf_op jit(solution)/shard_map/ppermute | solution.py:447
  98.5 5.3 %dense.1 = (bf16[1024,1024]{1,0:T(8,128)(2,1)S(1)}, f32[8,16,128]{2,1,0:T(8,128)S(1)}) custom-call(bf16[1024,128]{1,0:T(8,128)(2,1)S(1)} %get-tuple-element.32.refs_0_, bf16[1024,128]{1,0:T(8,128)(2,1)S(1)} %collective-permute-done.refs_1_, bf16[1024,128]{1,0:T(8,128)(2,1)} %collective-permute-done.1.refs_2_, ...), custom_call_target="tpu_custom_call" | custom-call | flops 2147483648 | bytes 7340032 | tf_op jit(solution)/shard_map/dense/pallas_call | solution.py:151
  103.9 0.6 collective-permute-start.12
  104.5 1.6 collective-permute-start.13
  106.0 0.8 collective-permute-start.14
  106.9 1.7 collective-permute-done.12.p1
  108.6 1.9 collective-permute-done.13.p2
  110.5 1.0 collective-permute-done.14.p3
  111.5 0.7 spread.1
  112.2 14.8 %all_to_all.25 = f32[32,2,16,128]{3,2,1,0:T(8,128)S(1)} all-to-all(f32[32,2,16,128]{3,2,1,0:T(8,128)S(1)} %bitcast.42), channel_id=1, replica_groups=mesh['nodes'=32,'feat'=4] {'nodes'}, dimensions={0} | all-to-all | bytes 1048576 | tf_op jit(solution)/shard_map/all_to_all | solution.py:456
  127.0 3.9 %logits.1 = (f32[8,16,128]{2,1,0:T(8,128)S(1)}, bf16[64,16,128]{2,1,0:T(8,128)(2,1)S(1)}) custom-call(s32[128]{0:T(128)S(1)} %reshape.56.src, s32[32]{0:T(128)S(1)} %bitcast.48, s32[1]{0:T(128)} %bitcast.me, f32[64,16,128]{2,1,0:T(8,128)S(1)} %bitcast.40, f32[32,16,128]{2,1,0:T(8,128)S(1)} %get-tuple-element.47.own, s32[32,1,128]{2,1,0:T(1,128)S(1)} %bitcast.44, ...), custom_call_target="tpu_custom_call" | custom-call | flops 268435456 | bytes 6291456 | tf_op jit(solution)/shard_map/logits/pallas_call | solution.py:259
  130.9 12.8 %all_to_all.26 = bf16[32,2,16,128]{3,2,1,0:T(8,128)(2,1)S(1)} all-to-all(bf16[32,2,16,128]{3,2,1,0:T(8,128)(2,1)S(1)} %bitcast.43), channel_id=1, replica_groups=mesh['nodes'=32,'feat'=4] {'nodes'}, dimensions={0} | all-to-all | bytes 524288 | tf_op jit(solution)/shard_map/all_to_all | solution.py:456
  143.7 3.9 %small_gradients.1 = (bf16[1024,1024]{1,0:T(8,128)(2,1)}, f32[24,256]{1,0:T(8,128)S(1)}, f32[24,256]{1,0:T(8,128)S(1)}, f32[24,256]{1,0:T(8,128)S(1)}, f32[24,256]{1,0:T(8,128)S(1)}) custom-call(s32[64]{0:T(128)S(1)} %reshape.55.table, s32[1]{0:T(128)} %bitcast.me, bf16[64,16,128]{2,1,0:T(8,128)(2,1)S(1)} %bitcast.41, ...), custom_call_target="tpu_custom_call" | custom-call | flops 536870912 | bytes 4194304 | tf_op jit(solution)/shard_map/small_gradients/pallas_call | solution.py:327
  147.6 1.3 collective-permute-start.17
  148.9 0.9 collective-permute-start.16
  149.8 0.2 collective-permute-start.15
  150.0 1.4 collective-permute-done.17
  151.4 3.0 %collective-permute-done.16 = f32[24,256]{1,0:T(8,128)S(1)} collective-permute-done((f32[24,256]{1,0:T(8,128)S(1)}, f32[24,256]{1,0:T(8,128)S(1)}, u32[]{:S(2)}, u32[]{:S(2)}) %collective-permute-start.16) | collective-permute-done | bytes 24608 | tf_op jit(solution)/shard_map/ppermute | solution.py:447
  154.4 0.4 collective-permute-done.15
  154.9 0.3 collective-permute-start.19
  155.1 2.0 collective-permute-start.18
  157.1 5.2 %big_gradient.1 = bf16[32,4,32,256]{3,2,1,0:T(8,128)(2,1)} custom-call(s32[1]{0:T(128)} %bitcast.me, bf16[1024,1024]{1,0:T(8,128)(2,1)} %get-tuple-element.51.dpre, bf16[1024,128]{1,0:T(8,128)(2,1)S(1)} %get-tuple-element.32.refs_0_, bf16[1024,128]{1,0:T(8,128)(2,1)S(1)} %collective-permute-done.refs_1_, bf16[1024,128]{1,0:T(8,128)(2,1)} %collective-permute-done.1.refs_2_, ...), custom_call_target="tpu_custom_call" | custom-call | flops 2147483648 | bytes 6291456 | tf_op jit(solution)/shard_map/big_gradient/pallas_call | solution.py:367
  162.3 5.6 %all-to-all-start.4 = ((bf16[128,32,256]{2,1,0:T(8,128)(2,1)}), bf16[128,32,256]{2,1,0:T(8,128)(2,1)S(1)}, u32[]{:S(2)}, u32[]{:S(2)}) async-start(bf16[128,32,256]{2,1,0:T(8,128)(2,1)} %bitcast.51), calls=%async_computation.4 | async-start | bytes 4194304 | tf_op jit(solution)/shard_map/all_to_all | solution.py:503
  168.0 3.5 %collective-permute-start.21 = (f32[24,256]{1,0:T(8,128)S(1)}, f32[24,256]{1,0:T(8,128)S(1)}, u32[]{:S(2)}, u32[]{:S(2)}) collective-permute-start(f32[24,256]{1,0:T(8,128)S(1)} %add_add_fusion.refs_0_), channel_id=1, source_target_pairs={{0,16},{4,20},{8,24},{12,28},{16,0},{20,4},{24,8},{28,12},{32,48},... | collective-permute-start | bytes 73736 | tf_op jit(solution)/shard_map/ppermute | solution.py:451
  171.4 1.5 collective-permute-start.22
  173.0 3.1 %collective-permute-start.24 = (f32[24,256]{1,0:T(8,128)S(1)}, f32[24,256]{1,0:T(8,128)S(1)}, u32[]{:S(2)}, u32[]{:S(2)}) collective-permute-start(f32[24,256]{1,0:T(8,128)S(1)} %add_add_fusion.refs_0_), channel_id=1, source_target_pairs={{0,64},{4,68},{8,72},{12,76},{16,80},{20,84},{24,88},{28,92},{32,9... | collective-permute-start | bytes 73736 | tf_op jit(solution)/shard_map/ppermute | solution.py:451
  176.1 3.3 %collective-permute-start.25 = (f32[24,256]{1,0:T(8,128)S(1)}, f32[24,256]{1,0:T(8,128)S(1)}, u32[]{:S(2)}, u32[]{:S(2)}) collective-permute-start(f32[24,256]{1,0:T(8,128)S(1)} %add_add_fusion.refs_0_), channel_id=1, source_target_pairs={{0,80},{4,84},{8,88},{12,92},{16,64},{20,68},{24,72},{28,76},{32,1... | collective-permute-start | bytes 73736 | tf_op jit(solution)/shard_map/ppermute | solution.py:451
  179.4 1.9 collective-permute-done.21.refs_1_
  181.3 15.8 %collective-permute-start.26 = (f32[24,256]{1,0:T(8,128)S(1)}, f32[24,256]{1,0:T(8,128)S(1)}, u32[]{:S(2)}, u32[]{:S(2)}) collective-permute-start(f32[24,256]{1,0:T(8,128)S(1)} %add_add_fusion.refs_0_), channel_id=1, source_target_pairs={{0,96},{4,100},{8,104},{12,108},{16,112},{20,116},{24,120},{28,124... | collective-permute-start | bytes 73736 | tf_op jit(solution)/shard_map/ppermute | solution.py:451
  197.1 0.6 collective-permute-start.27
  197.8 1.1 collective-permute-done.25.refs_5_
  198.9 5.6 %collective-permute-done.27.refs_7_ = f32[24,256]{1,0:T(8,128)S(1)} collective-permute-done((f32[24,256]{1,0:T(8,128)S(1)}, f32[24,256]{1,0:T(8,128)S(1)}, u32[]{:S(2)}, u32[]{:S(2)}) %collective-permute-start.27) | collective-permute-done | bytes 24608 | tf_op jit(solution)/shard_map/ppermute | solution.py:451
  204.6 1.1 total.1
  (60 shorter events, 1.2 us)
Async XLA Ops:
  4.6 8.5 %copy-start.6 = (bf16[256,1024]{1,0:T(8,128)(2,1)S(1)}, bf16[256,1024]{1,0:T(8,128)(2,1)}, u32[]{:S(2)}) copy-start(bf16[256,1024]{1,0:T(8,128)(2,1)} %param.15) | copy-start | bytes 1572868
  4.6 37.4 %all-to-all-start = ((bf16[32,2,128,128]{3,2,1,0:T(8,128)(2,1)}), bf16[32,2,128,128]{3,2,1,0:T(8,128)(2,1)S(1)}, u32[]{:S(2)}, u32[]{:S(2)}) async-start(bf16[32,2,128,128]{3,2,1,0:T(8,128)(2,1)} %bitcast.50), calls=%async_computation | async-start | bytes 4194304 | tf_op jit(solution)/shard_map/all_to_all | solution.py:456
  13.3 16.4 %collective-permute-start.3 = (bf16[1024,256]{1,0:T(8,128)(2,1)S(1)}, bf16[1024,256]{1,0:T(8,128)(2,1)S(1)}, u32[]{:S(2)}, u32[]{:S(2)}) collective-permute-start(bf16[1024,256]{1,0:T(8,128)(2,1)S(1)} %bitcast.52), channel_id=1, source_target_pairs={{0,2},{1,3},{2,0},{3,1},{4,6},{5,7},{6,4},{7,5},{8,10},{9,11},{10,... | collective-permute-start | bytes 1572872 | tf_op jit(solution)/shard_map/ppermute | solution.py:447
  14.8 23.3 %collective-permute-start.4 = (bf16[1024,256]{1,0:T(8,128)(2,1)S(1)}, bf16[1024,256]{1,0:T(8,128)(2,1)S(1)}, u32[]{:S(2)}, u32[]{:S(2)}) collective-permute-start(bf16[1024,256]{1,0:T(8,128)(2,1)S(1)} %bitcast.53), channel_id=1, source_target_pairs={{0,1},{1,2},{2,3},{3,0},{4,5},{5,6},{6,7},{7,4},{8,9},{9,10},{10,1... | collective-permute-start | bytes 1572872 | tf_op jit(solution)/shard_map/ppermute | solution.py:447
  16.9 23.4 %collective-permute-start.5 = (bf16[1024,256]{1,0:T(8,128)(2,1)S(1)}, bf16[1024,256]{1,0:T(8,128)(2,1)}, u32[]{:S(2)}, u32[]{:S(2)}) collective-permute-start(bf16[1024,256]{1,0:T(8,128)(2,1)S(1)} %bitcast.54), channel_id=1, source_target_pairs={{0,3},{1,0},{2,1},{3,2},{4,7},{5,4},{6,5},{7,6},{8,11},{9,8},{10,9... | collective-permute-start | bytes 1572872 | tf_op jit(solution)/shard_map/ppermute | solution.py:447
  29.7 13.7 %copy-start.7 = (bf16[1024,256]{1,0:T(8,128)(2,1)}, bf16[1024,256]{1,0:T(8,128)(2,1)S(1)}, u32[]{:S(2)}) copy-start(bf16[1024,256]{1,0:T(8,128)(2,1)S(1)} %collective-permute-done.3) | copy-start | bytes 1572868
  38.1 0.8 copy-start.8
  42.0 1.4 copy-start.1
  43.4 5.7 %copy-start.11 = (s32[32,4]{0,1:T(4,128)S(1)}, s32[32,4]{0,1:T(4,128)}, u32[]{:S(2)}) copy-start(s32[32,4]{0,1:T(4,128)} %param.12) | copy-start | bytes 1540
  43.4 6.0 %copy-start.10 = (bf16[256,16]{0,1:T(8,128)(2,1)S(1)}, bf16[256,16]{0,1:T(8,128)(2,1)}, u32[]{:S(2)}) copy-start(bf16[256,16]{0,1:T(8,128)(2,1)} %param.17) | copy-start | bytes 24580
  43.4 6.0 %copy-start.12 = (f32[256]{0:T(256)S(1)}, f32[256]{0:T(256)}, u32[]{:S(2)}) copy-start(f32[256]{0:T(256)} %param.16) | copy-start | bytes 3076
  43.4 34.7 %all-to-all-start.1 = ((bf16[32,2,128,128]{3,2,1,0:T(8,128)(2,1)}), bf16[32,2,128,128]{3,2,1,0:T(8,128)(2,1)S(1)}, u32[]{:S(2)}, u32[]{:S(2)}) async-start(bf16[32,2,128,128]{3,2,1,0:T(8,128)(2,1)} %bitcast.49), calls=%async_computation.1 | async-start | bytes 4194304 | tf_op jit(solution)/shard_map/all_to_all | solution.py:456
  49.4 8.0 %copy-start.2 = (bf16[32,2,128,128]{3,2,1,0:T(8,128)(2,1)S(1)}, bf16[32,2,128,128]{3,2,1,0:T(8,128)(2,1)}, u32[]{:S(2)}) copy-start(bf16[32,2,128,128]{3,2,1,0:T(8,128)(2,1)} %copy-done.1) | copy-start | bytes 6291460
  49.4 8.0 %copy-start.5 = (s32[1,32]{1,0:T(1,128)S(1)}, s32[1,32]{1,0:T(1,128)}, u32[]{:S(2)}) copy-start(s32[1,32]{1,0:T(1,128)} %param.10) | copy-start | bytes 388
  49.4 7.9 %collective-permute-start.9 = (f32[24,256]{1,0:T(8,128)S(1)}, f32[24,256]{1,0:T(8,128)S(1)}, u32[]{:S(2)}, u32[]{:S(2)}) collective-permute-start(f32[24,256]{1,0:T(8,128)S(1)} %pad_maximum_fusion.1), channel_id=1, source_target_pairs={{0,3},{1,0},{2,1},{3,2},{4,7},{5,4},{6,5},{7,6},{8,11},{9,8},{10,9... | collective-permute-start | bytes 73736 | tf_op jit(solution)/shard_map/ppermute | solution.py:447
  50.2 7.1 %collective-permute-start.10 = (f32[24,256]{1,0:T(8,128)S(1)}, f32[24,256]{1,0:T(8,128)S(1)}, u32[]{:S(2)}, u32[]{:S(2)}) collective-permute-start(f32[24,256]{1,0:T(8,128)S(1)} %pad_maximum_fusion.1), channel_id=1, source_target_pairs={{0,2},{1,3},{2,0},{3,1},{4,6},{5,7},{6,4},{7,5},{8,10},{9,11},{10,... | collective-permute-start | bytes 73736 | tf_op jit(solution)/shard_map/ppermute | solution.py:447
  52.2 5.2 %collective-permute-start.11 = (f32[24,256]{1,0:T(8,128)S(1)}, f32[24,256]{1,0:T(8,128)S(1)}, u32[]{:S(2)}, u32[]{:S(2)}) collective-permute-start(f32[24,256]{1,0:T(8,128)S(1)} %pad_maximum_fusion.1), channel_id=1, source_target_pairs={{0,1},{1,2},{2,3},{3,0},{4,5},{5,6},{6,7},{7,4},{8,9},{9,10},{10,1... | collective-permute-start | bytes 73736 | tf_op jit(solution)/shard_map/ppermute | solution.py:447
  62.0 23.1 %collective-permute-start = (bf16[1024,128]{1,0:T(8,128)(2,1)S(1)}, bf16[1024,128]{1,0:T(8,128)(2,1)S(1)}, u32[]{:S(2)}, u32[]{:S(2)}) collective-permute-start(bf16[1024,128]{1,0:T(8,128)(2,1)S(1)} %get-tuple-element.33), channel_id=1, source_target_pairs={{0,1},{1,2},{2,3},{3,0},{4,5},{5,6},{6,7},{7,4},{8,9},{9,10},{10,1... | collective-permute-start | bytes 786440 | tf_op jit(solution)/shard_map/ppermute | solution.py:447
  64.1 26.4 %collective-permute-start.1 = (bf16[1024,128]{1,0:T(8,128)(2,1)}, bf16[1024,128]{1,0:T(8,128)(2,1)}, u32[]{:S(2)}, u32[]{:S(2)}) collective-permute-start(bf16[1024,128]{1,0:T(8,128)(2,1)} %get-tuple-element.34), channel_id=1, source_target_pairs={{0,2},{1,3},{2,0},{3,1},{4,6},{5,7},{6,4},{7,5},{8,10},{9,11},{10,... | collective-permute-start | bytes 786440 | tf_op jit(solution)/shard_map/ppermute | solution.py:447
  64.2 26.3 %collective-permute-start.2 = (bf16[1024,128]{1,0:T(8,128)(2,1)}, bf16[1024,128]{1,0:T(8,128)(2,1)}, u32[]{:S(2)}, u32[]{:S(2)}) collective-permute-start(bf16[1024,128]{1,0:T(8,128)(2,1)} %get-tuple-element.35), channel_id=1, source_target_pairs={{0,3},{1,0},{2,1},{3,2},{4,7},{5,4},{6,5},{7,6},{8,11},{9,8},{10,9... | collective-permute-start | bytes 786440 | tf_op jit(solution)/shard_map/ppermute | solution.py:447
  82.2 9.6 %collective-permute-start.6 = (bf16[1024,128]{1,0:T(8,128)(2,1)}, bf16[1024,128]{1,0:T(8,128)(2,1)}, u32[]{:S(2)}, u32[]{:S(2)}) collective-permute-start(bf16[1024,128]{1,0:T(8,128)(2,1)} %get-tuple-element.37), channel_id=1, source_target_pairs={{0,1},{1,2},{2,3},{3,0},{4,5},{5,6},{6,7},{7,4},{8,9},{9,10},{10,1... | collective-permute-start | bytes 786440 | tf_op jit(solution)/shard_map/ppermute | solution.py:447
  83.5 11.1 %collective-permute-start.7 = (bf16[1024,128]{1,0:T(8,128)(2,1)}, bf16[1024,128]{1,0:T(8,128)(2,1)}, u32[]{:S(2)}, u32[]{:S(2)}) collective-permute-start(bf16[1024,128]{1,0:T(8,128)(2,1)} %get-tuple-element.38), channel_id=1, source_target_pairs={{0,2},{1,3},{2,0},{3,1},{4,6},{5,7},{6,4},{7,5},{8,10},{9,11},{10,... | collective-permute-start | bytes 786440 | tf_op jit(solution)/shard_map/ppermute | solution.py:447
  85.1 13.5 %collective-permute-start.8 = (bf16[1024,128]{1,0:T(8,128)(2,1)}, bf16[1024,128]{1,0:T(8,128)(2,1)}, u32[]{:S(2)}, u32[]{:S(2)}) collective-permute-start(bf16[1024,128]{1,0:T(8,128)(2,1)} %get-tuple-element.39), channel_id=1, source_target_pairs={{0,3},{1,0},{2,1},{3,2},{4,7},{5,4},{6,5},{7,6},{8,11},{9,8},{10,9... | collective-permute-start | bytes 786440 | tf_op jit(solution)/shard_map/ppermute | solution.py:447
  85.9 0.7 copy-start.9
  88.0 10.5 %copy-start.3 = (bf16[1024,1024]{1,0:T(8,128)(2,1)S(1)}, bf16[1024,1024]{1,0:T(8,128)(2,1)}, u32[]{:S(2)}) copy-start(bf16[1024,1024]{1,0:T(8,128)(2,1)} %pad_maximum_fusion.refs_8_) | copy-start | bytes 6291460
  98.5 28.4 %copy-start = (bf16[32,4,128,128]{3,2,1,0:T(8,128)(2,1)S(1)}, bf16[32,4,128,128]{3,2,1,0:T(8,128)(2,1)}, u32[]{:S(2)}) copy-start(bf16[32,4,128,128]{3,2,1,0:T(8,128)(2,1)} %tiles.1) | copy-start | bytes 12582916
  98.5 28.4 %copy-start.4 = (s32[4096]{0:T(1024)S(1)}, s32[4096]{0:T(1024)}, u32[]{:S(2)}) copy-start(s32[4096]{0:T(1024)} %param.14) | copy-start | bytes 49156
  103.9 4.7 %collective-permute-start.12 = (f32[8,16,128]{2,1,0:T(8,128)S(1)}, f32[8,16,128]{2,1,0:T(8,128)S(1)}, u32[]{:S(2)}, u32[]{:S(2)}) collective-permute-start(f32[8,16,128]{2,1,0:T(8,128)S(1)} %get-tuple-element.45.p0), channel_id=1, source_target_pairs={{0,1},{1,2},{2,3},{3,0},{4,5},{5,6},{6,7},{7,4},{8,9},{9,10},{10,1... | collective-permute-start | bytes 196616 | tf_op jit(solution)/shard_map/ppermute | solution.py:447
  104.5 6.0 %collective-permute-start.13 = (f32[8,16,128]{2,1,0:T(8,128)S(1)}, f32[8,16,128]{2,1,0:T(8,128)S(1)}, u32[]{:S(2)}, u32[]{:S(2)}) collective-permute-start(f32[8,16,128]{2,1,0:T(8,128)S(1)} %get-tuple-element.45.p0), channel_id=1, source_target_pairs={{0,2},{1,3},{2,0},{3,1},{4,6},{5,7},{6,4},{7,5},{8,10},{9,11},{10,... | collective-permute-start | bytes 196616 | tf_op jit(solution)/shard_map/ppermute | solution.py:447
  106.0 5.5 %collective-permute-start.14 = (f32[8,16,128]{2,1,0:T(8,128)S(1)}, f32[8,16,128]{2,1,0:T(8,128)S(1)}, u32[]{:S(2)}, u32[]{:S(2)}) collective-permute-start(f32[8,16,128]{2,1,0:T(8,128)S(1)} %get-tuple-element.45.p0), channel_id=1, source_target_pairs={{0,3},{1,0},{2,1},{3,2},{4,7},{5,4},{6,5},{7,6},{8,11},{9,8},{10,9... | collective-permute-start | bytes 196616 | tf_op jit(solution)/shard_map/ppermute | solution.py:447
  147.6 3.8 %collective-permute-start.17 = (f32[24,256]{1,0:T(8,128)S(1)}, f32[24,256]{1,0:T(8,128)S(1)}, u32[]{:S(2)}, u32[]{:S(2)}) collective-permute-start(f32[24,256]{1,0:T(8,128)S(1)} %get-tuple-element.55), channel_id=1, source_target_pairs={{0,1},{1,2},{2,3},{3,0},{4,5},{5,6},{6,7},{7,4},{8,9},{9,10},{10,1... | collective-permute-start | bytes 73736 | tf_op jit(solution)/shard_map/ppermute | solution.py:447
  148.9 5.5 %collective-permute-start.16 = (f32[24,256]{1,0:T(8,128)S(1)}, f32[24,256]{1,0:T(8,128)S(1)}, u32[]{:S(2)}, u32[]{:S(2)}) collective-permute-start(f32[24,256]{1,0:T(8,128)S(1)} %get-tuple-element.54), channel_id=1, source_target_pairs={{0,2},{1,3},{2,0},{3,1},{4,6},{5,7},{6,4},{7,5},{8,10},{9,11},{10,... | collective-permute-start | bytes 73736 | tf_op jit(solution)/shard_map/ppermute | solution.py:447
  149.8 5.0 %collective-permute-start.15 = (f32[24,256]{1,0:T(8,128)S(1)}, f32[24,256]{1,0:T(8,128)S(1)}, u32[]{:S(2)}, u32[]{:S(2)}) collective-permute-start(f32[24,256]{1,0:T(8,128)S(1)} %get-tuple-element.53), channel_id=1, source_target_pairs={{0,3},{1,0},{2,1},{3,2},{4,7},{5,4},{6,5},{7,6},{8,11},{9,8},{10,9... | collective-permute-start | bytes 73736 | tf_op jit(solution)/shard_map/ppermute | solution.py:447
  154.9 7.4 %collective-permute-start.19 = (f32[24,256]{1,0:T(8,128)S(1)}, f32[24,256]{1,0:T(8,128)S(1)}, u32[]{:S(2)}, u32[]{:S(2)}) collective-permute-start(f32[24,256]{1,0:T(8,128)S(1)} %add_add_fusion.1), channel_id=1, source_target_pairs={{0,8},{4,12},{8,0},{12,4},{16,24},{20,28},{24,16},{28,20},{32,40},... | collective-permute-start | bytes 73736 | tf_op jit(solution)/shard_map/ppermute | solution.py:451
  155.1 7.2 %collective-permute-start.20 = (f32[24,256]{1,0:T(8,128)S(1)}, f32[24,256]{1,0:T(8,128)S(1)}, u32[]{:S(2)}, u32[]{:S(2)}) collective-permute-start(f32[24,256]{1,0:T(8,128)S(1)} %add_add_fusion.1), channel_id=1, source_target_pairs={{0,12},{4,8},{8,4},{12,0},{16,28},{20,24},{24,20},{28,16},{32,44},... | collective-permute-start | bytes 73736 | tf_op jit(solution)/shard_map/ppermute | solution.py:451
  155.1 7.2 %collective-permute-start.18 = (f32[24,256]{1,0:T(8,128)S(1)}, f32[24,256]{1,0:T(8,128)S(1)}, u32[]{:S(2)}, u32[]{:S(2)}) collective-permute-start(f32[24,256]{1,0:T(8,128)S(1)} %add_add_fusion.1), channel_id=1, source_target_pairs={{0,4},{4,0},{8,12},{12,8},{16,20},{20,16},{24,28},{28,24},{32,36},... | collective-permute-start | bytes 73736 | tf_op jit(solution)/shard_map/ppermute | solution.py:451
  162.3 42.2 %all-to-all-start.4 = ((bf16[128,32,256]{2,1,0:T(8,128)(2,1)}), bf16[128,32,256]{2,1,0:T(8,128)(2,1)S(1)}, u32[]{:S(2)}, u32[]{:S(2)}) async-start(bf16[128,32,256]{2,1,0:T(8,128)(2,1)} %bitcast.51), calls=%async_computation.4 | async-start | bytes 4194304 | tf_op jit(solution)/shard_map/all_to_all | solution.py:503
  168.0 13.4 %collective-permute-start.21 = (f32[24,256]{1,0:T(8,128)S(1)}, f32[24,256]{1,0:T(8,128)S(1)}, u32[]{:S(2)}, u32[]{:S(2)}) collective-permute-start(f32[24,256]{1,0:T(8,128)S(1)} %add_add_fusion.refs_0_), channel_id=1, source_target_pairs={{0,16},{4,20},{8,24},{12,28},{16,0},{20,4},{24,8},{28,12},{32,48},... | collective-permute-start | bytes 73736 | tf_op jit(solution)/shard_map/ppermute | solution.py:451
  171.4 25.7 %collective-permute-start.22 = (f32[24,256]{1,0:T(8,128)S(1)}, f32[24,256]{1,0:T(8,128)S(1)}, u32[]{:S(2)}, u32[]{:S(2)}) collective-permute-start(f32[24,256]{1,0:T(8,128)S(1)} %add_add_fusion.refs_0_), channel_id=1, source_target_pairs={{0,32},{4,36},{8,40},{12,44},{16,48},{20,52},{24,56},{28,60},{32,0... | collective-permute-start | bytes 73736 | tf_op jit(solution)/shard_map/ppermute | solution.py:451
  173.0 24.8 %collective-permute-start.23 = (f32[24,256]{1,0:T(8,128)S(1)}, f32[24,256]{1,0:T(8,128)S(1)}, u32[]{:S(2)}, u32[]{:S(2)}) collective-permute-start(f32[24,256]{1,0:T(8,128)S(1)} %add_add_fusion.refs_0_), channel_id=1, source_target_pairs={{0,48},{4,52},{8,56},{12,60},{16,32},{20,36},{24,40},{28,44},{32,1... | collective-permute-start | bytes 73736 | tf_op jit(solution)/shard_map/ppermute | solution.py:451
  173.0 24.7 %collective-permute-start.24 = (f32[24,256]{1,0:T(8,128)S(1)}, f32[24,256]{1,0:T(8,128)S(1)}, u32[]{:S(2)}, u32[]{:S(2)}) collective-permute-start(f32[24,256]{1,0:T(8,128)S(1)} %add_add_fusion.refs_0_), channel_id=1, source_target_pairs={{0,64},{4,68},{8,72},{12,76},{16,80},{20,84},{24,88},{28,92},{32,9... | collective-permute-start | bytes 73736 | tf_op jit(solution)/shard_map/ppermute | solution.py:451
  176.1 22.7 %collective-permute-start.25 = (f32[24,256]{1,0:T(8,128)S(1)}, f32[24,256]{1,0:T(8,128)S(1)}, u32[]{:S(2)}, u32[]{:S(2)}) collective-permute-start(f32[24,256]{1,0:T(8,128)S(1)} %add_add_fusion.refs_0_), channel_id=1, source_target_pairs={{0,80},{4,84},{8,88},{12,92},{16,64},{20,68},{24,72},{28,76},{32,1... | collective-permute-start | bytes 73736 | tf_op jit(solution)/shard_map/ppermute | solution.py:451
  181.3 17.6 %collective-permute-start.26 = (f32[24,256]{1,0:T(8,128)S(1)}, f32[24,256]{1,0:T(8,128)S(1)}, u32[]{:S(2)}, u32[]{:S(2)}) collective-permute-start(f32[24,256]{1,0:T(8,128)S(1)} %add_add_fusion.refs_0_), channel_id=1, source_target_pairs={{0,96},{4,100},{8,104},{12,108},{16,112},{20,116},{24,120},{28,124... | collective-permute-start | bytes 73736 | tf_op jit(solution)/shard_map/ppermute | solution.py:451
  197.1 7.4 %collective-permute-start.27 = (f32[24,256]{1,0:T(8,128)S(1)}, f32[24,256]{1,0:T(8,128)S(1)}, u32[]{:S(2)}, u32[]{:S(2)}) collective-permute-start(f32[24,256]{1,0:T(8,128)S(1)} %add_add_fusion.refs_0_), channel_id=1, source_target_pairs={{0,112},{4,116},{8,120},{12,124},{16,96},{20,100},{24,104},{28,108... | collective-permute-start | bytes 73736 | tf_op jit(solution)/shard_map/ppermute | solution.py:451

commit v7 on v6

--- a/solution.py
+++ b/solution.py
@@ -67,7 +67,7 @@
             ],
         ),
         out_shape=pltpu.HBM((slots, BLK, BLK), BF16),
-        compiler_params=params(4),
+        compiler_params=params(63),
         cost_estimate=cost(0, 4 * MIB),
         name="pick",
     )(table, in_hbm(features))
@@ -147,7 +147,7 @@
     nodes, nfeat = pieces[0].shape[0], len(pieces) // 2
     hid, width = weights.shape
     grades = second.shape[0]
-    step = 256
+    step = 512
     return pl.pallas_call(
         functools.partial(dense_kernel, nfeat),
         grid=(nodes // step,),
@@ -350,36 +350,59 @@
     )(table, me, returned, dlog, hidden, second)
 
 
-def big_kernel(me, dpre, *refs):
+def big_kernel(me, side, dpre, *refs):
     pieces, out = refs[:-1], refs[-1]
     nfeat = len(pieces) // 2
+    rows = dpre[...].reshape(-1, dpre.shape[-1])
     for k in range(nfeat):
         owner = lax.rem(me[0] + nfeat - k, nfeat)
         both = jnp.concatenate([pieces[k][...], pieces[nfeat + k][...]], 1)
-        grad = dot(dpre[...], both, NN).astype(BF16)
+        grad = dot(rows, both, NN).astype(BF16)
         out[:, owner] = grad.reshape(out.shape[0], out.shape[2], out.shape[3])
 
 
-def big_gradient(me, dpre, pieces, parts):
+def big_gradient(me, side, dpre, pieces, parts):
     nfeat = len(pieces) // 2
     hid, nodes = dpre.shape
-    steps = 2
+    cols = hid // parts
+    vmem = pl.BlockSpec(memory_space=pltpu.VMEM)
     return pl.pallas_call(
         big_kernel,
         grid_spec=pltpu.PrefetchScalarGridSpec(
-            num_scalar_prefetch=1,
-            grid=(steps,),
-            in_specs=[pl.BlockSpec((hid // steps, nodes), lambda g, m: (g, 0))]
-            + [pl.BlockSpec((nodes, BLK), lambda g, m: (0, 0))] * (2 * nfeat),
+            num_scalar_prefetch=2,
+            grid=(1,),
+            in_specs=[
+                pl.BlockSpec((parts // 2, 1, cols, nodes), lambda g, m, s: (0, s[0], 0, 0))
+            ]
+            + [vmem] * (2 * nfeat),
             out_specs=pl.BlockSpec(
-                (parts // steps, nfeat, hid // parts, 2 * BLK), lambda g, m: (g, 0, 0, 0)
+                (parts // 2, nfeat, cols, 2 * BLK), lambda g, m, s: (0, 0, 0, 0)
             ),
         ),
-        out_shape=pltpu.HBM((parts, nfeat, hid // parts, 2 * BLK), BF16),
-        compiler_params=params(24),
-        cost_estimate=cost(2 * nodes * hid * hid, 6 * MIB),
+        out_shape=jax.ShapeDtypeStruct((parts // 2, nfeat, cols, 2 * BLK), BF16),
+        compiler_params=params(16),
+        cost_estimate=cost(nodes * hid * hid, 4 * MIB),
         name="big_gradient",
-    )(me, in_hbm(dpre), *pieces)
+    )(me, side, in_hbm(dpre.reshape(parts // 2, 2, cols, nodes)), *pieces)
+
+
+def join_kernel(a, b, out):
+    out[...] = (a[...].astype(F32) + b[...].astype(F32)).astype(BF16)
+
+
+def join(a, b):
+    lead = a.shape[0] // 4
+    spec = pl.BlockSpec((lead, *a.shape[1:]), lambda g: (g, 0, 0, 0))
+    return pl.pallas_call(
+        join_kernel,
+        grid=(4,),
+        in_specs=[spec, spec],
+        out_specs=spec,
+        out_shape=pltpu.HBM(a.shape, BF16),
+        compiler_params=params(8),
+        cost_estimate=cost(a.size, 3 * MIB),
+        name="join",
+    )(a, b)
 
 
 def total_kernel(nsmall, arrived, *refs):
@@ -464,21 +487,20 @@
     consts = jnp.concatenate(
         [w_second.T.astype(F32), jnp.broadcast_to(b_first[None], (8, b_first.shape[0]))], 0
     )
-    send, weights = lax.optimization_barrier((send, weights))
-    consts, first_weight = lax.optimization_barrier((consts, weights[1]))
-    weights = jnp.concatenate([flat, first_weight, weights[0], weights[2]], 1)
+    send, weights, arrived = lax.optimization_barrier((send, weights, arrived))
+    arrived.append(swap(send))
+    others = (2, 1, 3)
+    make = functools.partial(aggregate, src, counts, me)
+    first = [None] * nfeat
+    *sent, first[0] = make(arrived[0], tiles, features, 0, nfeat, others + (0,))
+    consts, weights, first[0] = lax.optimization_barrier((consts, weights, first[0]))
+    weights = jnp.concatenate([flat, weights[1], weights[0], weights[2]], 1)
     turned = [consts] + [ahead(consts, k) for k in range(1, nfeat)]
     ring = jnp.stack([turned[k] for k in (3, 2, 1, 0, 3, 2, 1)])
     ordered = lax.dynamic_slice_in_dim(ring, nfeat - 1 - axis, nfeat, 0)
     second_t = ordered[:, :grades].transpose(1, 0, 2).reshape(grades, hid).astype(BF16)
     bias = ordered[:, grades].reshape(hid, 1)
     second = second_t.T
-
-    arrived.append(swap(send))
-    others = (2, 1, 3)
-    make = functools.partial(aggregate, src, counts, me)
-    first = [None] * nfeat
-    *sent, first[0] = make(arrived[0], tiles, features, 0, nfeat, others + (0,))
     for k, piece in zip(others, sent):
         first[k] = ahead(piece, k)
     last = [None] * nfeat
@@ -497,14 +519,19 @@
     rest = small[0]
     for k in range(1, nfeat):
         rest = rest + ahead(small[k], nfeat - k)
-    big = big_gradient(me, dpre, first + last, parts)
     rest = nearby(rest, (1, 2, 3))
+    core = (lax.axis_index("nodes").astype(jnp.int32) % 2).reshape(1)
+    (away,) = nearby(big_gradient(me, 1 - core, dpre, first + last, parts), (1,))[1:]
+    big = join(big_gradient(me, core, dpre, first + last, parts), away)
     big, rest = lax.optimization_barrier((big, tree(rest)))
     moved = lax.all_to_all(
-        big.reshape(parts * nfeat, *big.shape[2:]),
+        big.reshape(parts // 2 * nfeat, *big.shape[2:]),
         ("nodes", "feat"),
         split_axis=0,
         concat_axis=0,
+        axis_index_groups=[
+            [p * nfeat + f for p in range(c, parts, 2) for f in range(nfeat)] for c in range(2)
+        ],
         tiled=True,
     )
     terms = nearby(rest, range(4, parts, 4))

time: 206 us -> 198 us (0.961)
  the two profiles are of different devices: /device:TPU:6 before, /device:TPU:4 now
where the time goes in v7:
time: 198 us
  starting transfers between devices  69.5 us (35%)
  waiting for transfers between devices  64.2 us (32%)
  Pallas kernels  40 us (20%)
  blocking collectives  14.5 us (7%)
  local copies, waits for them, and re-layouts  5.37 us (3%)
  other arithmetic  3.02 us (2%)
    ppermute x18, waiting for transfers between devices, ahead(): return lax.ppermute(x, 'feat', [(i, (i + k) % nfeat) for i in range(nfeat)])  32.8 us
    all_to_all x3, waiting for transfers between devices, swap(): lax.all_to_all(shaped, 'nodes', split_axis=0, concat_axis=0, tiled=True)  24.2 us
    ppermute x18, starting transfers between devices, ahead(): return lax.ppermute(x, 'feat', [(i, (i + k) % nfeat) for i in range(nfeat)])  23.7 us
    ppermute x11, starting transfers between devices, nearby(): lax.ppermute(x, 'nodes', [(i, i ^ mask) for i in range(parts)])  21 us
    all_to_all x3, starting transfers between devices, swap(): lax.all_to_all(shaped, 'nodes', split_axis=0, concat_axis=0, tiled=True)  18 us
    all_to_all x1, blocking collectives, swap(): lax.all_to_all(shaped, 'nodes', split_axis=0, concat_axis=0, tiled=True)  14.5 us
    pallas_call x3, Pallas kernels, aggregate(): pl.pallas_call(functools.partial(agg_kernel, which, chunk, nfeat), grid_s...  11.8 us
    ppermute x11, waiting for transfers between devices, nearby(): lax.ppermute(x, 'nodes', [(i, i ^ mask) for i in range(parts)])  7.19 us
  transfers between devices with their start and end apart: 33, of which 13 were waited for; matrix products, arithmetic and copies ran while one was open for 3% of the time, Pallas kernels for 9%

profile of v7, /device:TPU:4, one launch (start us, length us, event | category | flops | bytes accessed | tf_op | source)
XLA Modules:
  0.0 197.6 jit_solution(14673734525630282164)
XLA Ops:
  0.6 0.8 copy.17
  1.4 0.6 reshape.63.table
  2.0 3.3 %pick.3 = bf16[64,128,128]{2,1,0:T(8,128)(2,1)} custom-call(s32[64]{0:T(128)} %reshape.63.table, bf16[4096,256]{1,0:T(8,128)(2,1)} %features.9), custom_call_target="tpu_custom_call" | custom-call | bytes 4194304 | tf_op jit(solution)/shard_map/pick/pallas_call | solution.py:57
  5.3 8.6 %all-to-all-start = ((bf16[32,2,128,128]{3,2,1,0:T(8,128)(2,1)}), bf16[32,2,128,128]{3,2,1,0:T(8,128)(2,1)}, u32[]{:S(2)}, u32[]{:S(2)}) async-start(bf16[32,2,128,128]{3,2,1,0:T(8,128)(2,1)} %bitcast.52), calls=%async_computation | async-start | bytes 4194304 | tf_op jit(solution)/shard_map/all_to_all | solution.py:479
  13.9 0.2 copy.19
  14.1 0.6 collective-permute-start
  14.7 2.1 %collective-permute-start.1 = (bf16[1024,256]{1,0:T(8,128)(2,1)S(1)}, bf16[1024,256]{1,0:T(8,128)(2,1)}, u32[]{:S(2)}, u32[]{:S(2)}) collective-permute-start(bf16[1024,256]{1,0:T(8,128)(2,1)S(1)} %bitcast.55), channel_id=1, source_target_pairs={{0,1},{1,2},{2,3},{3,0},{4,5},{5,6},{6,7},{7,4},{8,9},{9,10},{10,1... | collective-permute-start | bytes 1572872 | tf_op jit(solution)/shard_map/ppermute | solution.py:470
  16.9 3.3 %pick.2 = bf16[64,128,128]{2,1,0:T(8,128)(2,1)} custom-call(s32[64]{0:T(128)} %reshape.63.table, bf16[4096,256]{1,0:T(8,128)(2,1)} %features.9), custom_call_target="tpu_custom_call" | custom-call | bytes 4194304 | tf_op jit(solution)/shard_map/pick/pallas_call | solution.py:57
  20.2 10.5 %collective-permute-done = bf16[1024,256]{1,0:T(8,128)(2,1)} collective-permute-done((bf16[1024,256]{1,0:T(8,128)(2,1)S(1)}, bf16[1024,256]{1,0:T(8,128)(2,1)}, u32[]{:S(2)}, u32[]{:S(2)}) %collective-permute-start) | collective-permute-done | bytes 524320 | tf_op jit(solution)/shard_map/ppermute | solution.py:470
  30.6 9.6 %collective-permute-done.1 = bf16[1024,256]{1,0:T(8,128)(2,1)} collective-permute-done((bf16[1024,256]{1,0:T(8,128)(2,1)S(1)}, bf16[1024,256]{1,0:T(8,128)(2,1)}, u32[]{:S(2)}, u32[]{:S(2)}) %collective-permute-start.1) | collective-permute-done | bytes 524320 | tf_op jit(solution)/shard_map/ppermute | solution.py:470
  40.2 2.6 %all-to-all-done = bf16[32,2,128,128]{3,2,1,0:T(8,128)(2,1)} async-done(((bf16[32,2,128,128]{3,2,1,0:T(8,128)(2,1)}), bf16[32,2,128,128]{3,2,1,0:T(8,128)(2,1)}, u32[]{:S(2)}, u32[]{:S(2)}) %all-to-all-start) | async-done | bytes 2097184 | tf_op jit(solution)/shard_map/all_to_all | solution.py:479
  42.8 4.8 %all-to-all-start.1 = ((bf16[32,2,128,128]{3,2,1,0:T(8,128)(2,1)}), bf16[32,2,128,128]{3,2,1,0:T(8,128)(2,1)S(1)}, u32[]{:S(2)}, u32[]{:S(2)}) async-start(bf16[32,2,128,128]{3,2,1,0:T(8,128)(2,1)} %bitcast.49), calls=%async_computation.1 | async-start | bytes 4194304 | tf_op jit(solution)/shard_map/all_to_all | solution.py:479
  48.0 5.1 %aggregate.3 = (bf16[1024,128]{1,0:T(8,128)(2,1)}, bf16[1024,128]{1,0:T(8,128)(2,1)S(1)}, bf16[1024,128]{1,0:T(8,128)(2,1)}, bf16[1024,128]{1,0:T(8,128)(2,1)S(1)}) custom-call(s32[128]{0:T(128)S(1)} %reshape.64.src, s32[32]{0:T(128)S(1)} %bitcast.45, s32[1]{0:T(128)} %bitcast.me, bf16[64,128,128]{2,1,0:T(8,128)(2,1)} %bitcast.6.arrived_hbm, ...), custom_call_target="tpu_custom_call" | custom-call | flops 536870912 | bytes 8388608 | tf_op jit(solution)/shard_map/aggregate/pallas_call | solution.py:114
  53.0 1.5 collective-permute-start.9
  54.6 2.6 %collective-permute-start.10 = (f32[24,256]{1,0:T(8,128)S(1)}, f32[24,256]{1,0:T(8,128)S(1)}, u32[]{:S(2)}, u32[]{:S(2)}) collective-permute-start(f32[24,256]{1,0:T(8,128)S(1)} %pad_maximum_fusion.1), channel_id=1, source_target_pairs={{0,2},{1,3},{2,0},{3,1},{4,6},{5,7},{6,4},{7,5},{8,10},{9,11},{10,... | collective-permute-start | bytes 73736 | tf_op jit(solution)/shard_map/ppermute | solution.py:470
  57.2 2.1 %collective-permute-start.3 = (bf16[1024,128]{1,0:T(8,128)(2,1)S(1)}, bf16[1024,128]{1,0:T(8,128)(2,1)S(1)}, u32[]{:S(2)}, u32[]{:S(2)}) collective-permute-start(bf16[1024,128]{1,0:T(8,128)(2,1)S(1)} %get-tuple-element.42), channel_id=1, source_target_pairs={{0,1},{1,2},{2,3},{3,0},{4,5},{5,6},{6,7},{7,4},{8,9},{9,10},{10,1... | collective-permute-start | bytes 786440 | tf_op jit(solution)/shard_map/ppermute | solution.py:470
  59.3 1.4 collective-permute-start.4
  60.7 3.0 %pad_maximum_fusion.refs_8_ = bf16[1024,1024]{1,0:T(8,128)(2,1)} fusion(bf16[1024,256]{1,0:T(8,128)(2,1)} %collective-permute-done.2, bf16[1024,256]{1,0:T(8,128)(2,1)} %collective-permute-done, bf16[1024,256]{1,0:T(8,128)(2,1)} %collective-permute-done.1, bf16[1024,256]{1,0:T(8,128)(2,1)S(1)} %bitcast.57), kind=kLoop, calls=%fused_computation | loop fusion | flops 8388608 | bytes 4194304 | tf_op jit(solution)/shard_map/concatenate | solution.py:497
  63.9 12.7 %all-to-all-done.1 = bf16[32,2,128,128]{3,2,1,0:T(8,128)(2,1)S(1)} async-done(((bf16[32,2,128,128]{3,2,1,0:T(8,128)(2,1)}), bf16[32,2,128,128]{3,2,1,0:T(8,128)(2,1)S(1)}, u32[]{:S(2)}, u32[]{:S(2)}) %all-to-all-start.1) | async-done | bytes 2097184 | tf_op jit(solution)/shard_map/all_to_all | solution.py:479
  76.6 4.1 %aggregate.5 = (bf16[1024,128]{1,0:T(8,128)(2,1)}, bf16[1024,128]{1,0:T(8,128)(2,1)}, bf16[1024,128]{1,0:T(8,128)(2,1)}) custom-call(s32[128]{0:T(128)S(1)} %reshape.64.src, s32[32]{0:T(128)S(1)} %bitcast.46, s32[1]{0:T(128)} %bitcast.me, bf16[64,128,128]{2,1,0:T(8,128)(2,1)S(1)} %bitcast.37, bf16[32,4,128,128]{3,2,1,0:T(8,128)(2,1)} %tiles.1, ...), custom_call_target="tpu_custom_call" | custom-call | flops 402653184 | bytes 8388608 | tf_op jit(solution)/shard_map/aggregate/pallas_call | solution.py:114
  80.8 2.1 %collective-permute-start.6 = (bf16[1024,128]{1,0:T(8,128)(2,1)}, bf16[1024,128]{1,0:T(8,128)(2,1)}, u32[]{:S(2)}, u32[]{:S(2)}) collective-permute-start(bf16[1024,128]{1,0:T(8,128)(2,1)} %get-tuple-element.46), channel_id=1, source_target_pairs={{0,1},{1,2},{2,3},{3,0},{4,5},{5,6},{6,7},{7,4},{8,9},{9,10},{10,1... | collective-permute-start | bytes 786440 | tf_op jit(solution)/shard_map/ppermute | solution.py:470
  82.9 0.9 collective-permute-start.7
  83.8 1.2 collective-permute-start.8
  85.0 0.7 copy-done.10
  85.6 1.0 copy.21.refs_9_
  86.6 0.8 fusion
  87.8 2.6 %aggregate.4.refs_4_ = bf16[1024,128]{1,0:T(8,128)(2,1)S(1)} custom-call(s32[128]{0:T(128)S(1)} %reshape.64.src, s32[32]{0:T(128)S(1)} %bitcast.47, s32[1]{0:T(128)} %bitcast.me, bf16[64,128,128]{2,1,0:T(8,128)(2,1)S(1)} %bitcast.38, bf16[32,4,128,128]{3,2,1,0:T(8,128)(2,1)} %tiles.1, bf16[4096,256]{1,0:T(8,128)(2,1)} %features.9), custom_call_target="tpu_custom_call" | custom-call | flops 134217728 | bytes 8388608 | tf_op jit(solution)/shard_map/aggregate/pallas_call | solution.py:114
  90.4 5.1 %collective-permute-done.7.refs_6_ = bf16[1024,128]{1,0:T(8,128)(2,1)} collective-permute-done((bf16[1024,128]{1,0:T(8,128)(2,1)}, bf16[1024,128]{1,0:T(8,128)(2,1)}, u32[]{:S(2)}, u32[]{:S(2)}) %collective-permute-start.7) | collective-permute-done | bytes 262176 | tf_op jit(solution)/shard_map/ppermute | solution.py:470
  95.5 0.9 collective-permute-done.8.refs_7_
  96.5 4.1 %dense.1 = (bf16[1024,1024]{1,0:T(8,128)(2,1)S(1)}, f32[8,16,128]{2,1,0:T(8,128)S(1)}) custom-call(bf16[1024,128]{1,0:T(8,128)(2,1)S(1)} %get-tuple-element.41.refs_0_, bf16[1024,128]{1,0:T(8,128)(2,1)S(1)} %collective-permute-done.3.refs_1_, bf16[1024,128]{1,0:T(8,128)(2,1)S(1)} %collective-permute-done.4.refs_2_, ...), custom_call_target="tpu_custom_call" | custom-call | flops 2147483648 | bytes 7340032 | tf_op jit(solution)/shard_map/dense/pallas_call | solution.py:151
  100.6 2.1 %collective-permute-start.12 = (f32[8,16,128]{2,1,0:T(8,128)S(1)}, f32[8,16,128]{2,1,0:T(8,128)S(1)}, u32[]{:S(2)}, u32[]{:S(2)}) collective-permute-start(f32[8,16,128]{2,1,0:T(8,128)S(1)} %get-tuple-element.53.p0), channel_id=1, source_target_pairs={{0,1},{1,2},{2,3},{3,0},{4,5},{5,6},{6,7},{7,4},{8,9},{9,10},{10,1... | collective-permute-start | bytes 196616 | tf_op jit(solution)/shard_map/ppermute | solution.py:470
  102.7 0.8 collective-permute-start.13
  103.5 1.5 collective-permute-start.14
  105.0 3.4 %collective-permute-done.13.p2 = f32[8,16,128]{2,1,0:T(8,128)S(1)} collective-permute-done((f32[8,16,128]{2,1,0:T(8,128)S(1)}, f32[8,16,128]{2,1,0:T(8,128)S(1)}, u32[]{:S(2)}, u32[]{:S(2)}) %collective-permute-start.13) | collective-permute-done | bytes 65568 | tf_op jit(solution)/shard_map/ppermute | solution.py:470
  108.5 0.7 spread.1
  109.2 14.5 %all_to_all.25 = f32[32,2,16,128]{3,2,1,0:T(8,128)S(1)} all-to-all(f32[32,2,16,128]{3,2,1,0:T(8,128)S(1)} %bitcast.42), channel_id=1, replica_groups=mesh['nodes'=32,'feat'=4] {'nodes'}, dimensions={0} | all-to-all | bytes 1048576 | tf_op jit(solution)/shard_map/all_to_all | solution.py:479
  123.6 3.9 %logits.1 = (f32[8,16,128]{2,1,0:T(8,128)S(1)}, bf16[64,16,128]{2,1,0:T(8,128)(2,1)S(1)}) custom-call(s32[128]{0:T(128)S(1)} %reshape.64.src, s32[32]{0:T(128)S(1)} %bitcast.48, s32[1]{0:T(128)} %bitcast.me, f32[64,16,128]{2,1,0:T(8,128)S(1)} %bitcast.41, f32[32,16,128]{2,1,0:T(8,128)S(1)} %get-tuple-element.55.own, s32[32,1,128]{2,1,0:T(1,128)S(1)} %bitcast.44, ...), custom_call_target="tpu_custom_call" | custom-call | flops 268435456 | bytes 6291456 | tf_op jit(solution)/shard_map/logits/pallas_call | solution.py:259
  127.6 0.7 copy-done.3
  128.3 4.6 %all-to-all-start.3 = ((bf16[32,2,16,128]{3,2,1,0:T(8,128)(2,1)}), bf16[32,2,16,128]{3,2,1,0:T(8,128)(2,1)}, u32[]{:S(2)}, u32[]{:S(2)}) async-start(bf16[32,2,16,128]{3,2,1,0:T(8,128)(2,1)} %bitcast.43), calls=%async_computation.3 | async-start | bytes 524288 | tf_op jit(solution)/shard_map/all_to_all | solution.py:479
  132.9 8.9 %all-to-all-done.3 = bf16[32,2,16,128]{3,2,1,0:T(8,128)(2,1)} async-done(((bf16[32,2,16,128]{3,2,1,0:T(8,128)(2,1)}), bf16[32,2,16,128]{3,2,1,0:T(8,128)(2,1)}, u32[]{:S(2)}, u32[]{:S(2)}) %all-to-all-start.3) | async-done | bytes 262176 | tf_op jit(solution)/shard_map/all_to_all | solution.py:479
  141.8 4.8 %small_gradients.1 = (bf16[1024,1024]{1,0:T(8,128)(2,1)}, f32[24,256]{1,0:T(8,128)S(1)}, f32[24,256]{1,0:T(8,128)S(1)}, f32[24,256]{1,0:T(8,128)S(1)}, f32[24,256]{1,0:T(8,128)S(1)}) custom-call(s32[64]{0:T(128)S(1)} %copy-done.5, s32[1]{0:T(128)} %bitcast.me, bf16[64,16,128]{2,1,0:T(8,128)(2,1)} %bitcast.20.returned, ...), custom_call_target="tpu_custom_call" | custom-call | flops 536870912 | bytes 4194304 | tf_op jit(solution)/shard_map/small_gradients/pallas_call | solution.py:327
  146.6 2.8 %big_gradient.3 = bf16[16,4,32,256]{3,2,1,0:T(8,128)(2,1)S(1)} custom-call(s32[1]{0:T(128)} %bitcast.me, s32[1]{0:T(128)S(6)} %sub.7.side, bf16[16,2,32,1024]{3,2,1,0:T(8,128)(2,1)} %bitcast.50, bf16[1024,128]{1,0:T(8,128)(2,1)S(1)} %get-tuple-element.41.refs_0_, bf16[1024,128]{1,0:T(8,128)(2,1)S(1)} %collective-permute-done.3.refs_1_, ...), custom_call_target="tpu_custom_call" | custom-call | flops 1073741824 | bytes 4194304 | tf_op jit(solution)/shard_map/big_gradient/pallas_call | solution.py:369
  149.4 0.4 collective-permute-start.15
  149.8 0.8 collective-permute-start.16
  150.6 3.2 %collective-permute-start.17 = (f32[24,256]{1,0:T(8,128)S(1)}, f32[24,256]{1,0:T(8,128)S(1)}, u32[]{:S(2)}, u32[]{:S(2)}) collective-permute-start(f32[24,256]{1,0:T(8,128)S(1)} %get-tuple-element.62), channel_id=1, source_target_pairs={{0,2},{1,3},{2,0},{3,1},{4,6},{5,7},{6,4},{7,5},{8,10},{9,11},{10,... | collective-permute-start | bytes 73736 | tf_op jit(solution)/shard_map/ppermute | solution.py:470
  153.8 0.6 collective-permute-start.18
  154.4 1.5 collective-permute-done.17
  155.9 1.7 collective-permute-done.18
  157.7 0.6 collective-permute-start.20
  158.3 1.3 collective-permute-start.21
  159.6 2.8 %big_gradient.2.a = bf16[16,4,32,256]{3,2,1,0:T(8,128)(2,1)S(1)} custom-call(s32[1]{0:T(128)} %bitcast.me, s32[1]{0:T(128)} %bitcast.1.side, bf16[16,2,32,1024]{3,2,1,0:T(8,128)(2,1)} %bitcast.51, bf16[1024,128]{1,0:T(8,128)(2,1)S(1)} %get-tuple-element.41.refs_0_, bf16[1024,128]{1,0:T(8,128)(2,1)S(1)} %collective-permute-done.3.refs_1_, ...), custom_call_target="tpu_custom_call" | custom-call | flops 1073741824 | bytes 4194304 | tf_op jit(solution)/shard_map/big_gradient/pallas_call | solution.py:369
  162.4 1.6 join.1
  164.0 6.7 %all-to-all-start.4 = ((bf16[64,32,256]{2,1,0:T(8,128)(2,1)}), bf16[64,32,256]{2,1,0:T(8,128)(2,1)S(1)}, u32[]{:S(2)}, u32[]{:S(2)}) async-start(bf16[64,32,256]{2,1,0:T(8,128)(2,1)} %bitcast.53), calls=%async_computation.4 | async-start | bytes 2097152 | tf_op jit(solution)/shard_map/all_to_all | solution.py:527
  170.8 3.1 %collective-permute-start.22 = (f32[24,256]{1,0:T(8,128)S(1)}, f32[24,256]{1,0:T(8,128)S(1)}, u32[]{:S(2)}, u32[]{:S(2)}) collective-permute-start(f32[24,256]{1,0:T(8,128)S(1)} %add_add_fusion.refs_0_), channel_id=1, source_target_pairs={{0,16},{4,20},{8,24},{12,28},{16,0},{20,4},{24,8},{28,12},{32,48},... | collective-permute-start | bytes 73736 | tf_op jit(solution)/shard_map/ppermute | solution.py:474
  173.8 1.5 collective-permute-start.23
  175.3 0.5 collective-permute-start.24
  175.9 3.1 %collective-permute-start.25 = (f32[24,256]{1,0:T(8,128)S(1)}, f32[24,256]{1,0:T(8,128)S(1)}, u32[]{:S(2)}, u32[]{:S(2)}) collective-permute-start(f32[24,256]{1,0:T(8,128)S(1)} %add_add_fusion.refs_0_), channel_id=1, source_target_pairs={{0,64},{4,68},{8,72},{12,76},{16,80},{20,84},{24,88},{28,92},{32,9... | collective-permute-start | bytes 73736 | tf_op jit(solution)/shard_map/ppermute | solution.py:474
  178.9 2.9 %collective-permute-start.26 = (f32[24,256]{1,0:T(8,128)S(1)}, f32[24,256]{1,0:T(8,128)S(1)}, u32[]{:S(2)}, u32[]{:S(2)}) collective-permute-start(f32[24,256]{1,0:T(8,128)S(1)} %add_add_fusion.refs_0_), channel_id=1, source_target_pairs={{0,80},{4,84},{8,88},{12,92},{16,64},{20,68},{24,72},{28,76},{32,1... | collective-permute-start | bytes 73736 | tf_op jit(solution)/shard_map/ppermute | solution.py:474
  181.8 7.4 %collective-permute-start.27 = (f32[24,256]{1,0:T(8,128)S(1)}, f32[24,256]{1,0:T(8,128)S(1)}, u32[]{:S(2)}, u32[]{:S(2)}) collective-permute-start(f32[24,256]{1,0:T(8,128)S(1)} %add_add_fusion.refs_0_), channel_id=1, source_target_pairs={{0,96},{4,100},{8,104},{12,108},{16,112},{20,116},{24,120},{28,124... | collective-permute-start | bytes 73736 | tf_op jit(solution)/shard_map/ppermute | solution.py:474
  189.2 0.3 collective-permute-start.28
  189.4 0.6 collective-permute-done.26.refs_5_
  190.1 0.9 collective-permute-done.27.refs_6_
  191.0 5.6 %collective-permute-done.28.refs_7_ = f32[24,256]{1,0:T(8,128)S(1)} collective-permute-done((f32[24,256]{1,0:T(8,128)S(1)}, f32[24,256]{1,0:T(8,128)S(1)}, u32[]{:S(2)}, u32[]{:S(2)}) %collective-permute-start.28) | collective-permute-done | bytes 24608 | tf_op jit(solution)/shard_map/ppermute | solution.py:474
  196.6 1.0 total.1
  (67 shorter events, 0.9 us)
Async XLA Ops:
  5.3 8.6 %copy-start.9 = (bf16[256,1024]{1,0:T(8,128)(2,1)S(1)}, bf16[256,1024]{1,0:T(8,128)(2,1)}, u32[]{:S(2)}) copy-start(bf16[256,1024]{1,0:T(8,128)(2,1)} %param.15) | copy-start | bytes 1572868
  5.3 37.5 %all-to-all-start = ((bf16[32,2,128,128]{3,2,1,0:T(8,128)(2,1)}), bf16[32,2,128,128]{3,2,1,0:T(8,128)(2,1)}, u32[]{:S(2)}, u32[]{:S(2)}) async-start(bf16[32,2,128,128]{3,2,1,0:T(8,128)(2,1)} %bitcast.52), calls=%async_computation | async-start | bytes 4194304 | tf_op jit(solution)/shard_map/all_to_all | solution.py:479
  14.1 6.0 %copy-start.7 = (bf16[256,1024]{0,1:T(8,128)(2,1)}, bf16[256,1024]{0,1:T(8,128)(2,1)S(1)}, u32[]{:S(2)}) copy-start(bf16[256,1024]{0,1:T(8,128)(2,1)S(1)} %copy.19) | copy-start | bytes 1572868
  14.1 16.5 %collective-permute-start = (bf16[1024,256]{1,0:T(8,128)(2,1)S(1)}, bf16[1024,256]{1,0:T(8,128)(2,1)}, u32[]{:S(2)}, u32[]{:S(2)}) collective-permute-start(bf16[1024,256]{1,0:T(8,128)(2,1)S(1)} %bitcast.54), channel_id=1, source_target_pairs={{0,2},{1,3},{2,0},{3,1},{4,6},{5,7},{6,4},{7,5},{8,10},{9,11},{10,... | collective-permute-start | bytes 1572872 | tf_op jit(solution)/shard_map/ppermute | solution.py:470
  14.7 25.5 %collective-permute-start.1 = (bf16[1024,256]{1,0:T(8,128)(2,1)S(1)}, bf16[1024,256]{1,0:T(8,128)(2,1)}, u32[]{:S(2)}, u32[]{:S(2)}) collective-permute-start(bf16[1024,256]{1,0:T(8,128)(2,1)S(1)} %bitcast.55), channel_id=1, source_target_pairs={{0,1},{1,2},{2,3},{3,0},{4,5},{5,6},{6,7},{7,4},{8,9},{9,10},{10,1... | collective-permute-start | bytes 1572872 | tf_op jit(solution)/shard_map/ppermute | solution.py:470
  16.8 23.4 %collective-permute-start.2 = (bf16[1024,256]{1,0:T(8,128)(2,1)S(1)}, bf16[1024,256]{1,0:T(8,128)(2,1)}, u32[]{:S(2)}, u32[]{:S(2)}) collective-permute-start(bf16[1024,256]{1,0:T(8,128)(2,1)S(1)} %bitcast.56), channel_id=1, source_target_pairs={{0,3},{1,0},{2,1},{3,2},{4,7},{5,4},{6,5},{7,6},{8,11},{9,8},{10,9... | collective-permute-start | bytes 1572872 | tf_op jit(solution)/shard_map/ppermute | solution.py:470
  42.8 4.9 %copy-start.12 = (s32[32,4]{0,1:T(4,128)S(1)}, s32[32,4]{0,1:T(4,128)}, u32[]{:S(2)}) copy-start(s32[32,4]{0,1:T(4,128)} %param.12) | copy-start | bytes 1540
  42.8 5.1 %copy-start.11 = (bf16[256,16]{0,1:T(8,128)(2,1)S(1)}, bf16[256,16]{0,1:T(8,128)(2,1)}, u32[]{:S(2)}) copy-start(bf16[256,16]{0,1:T(8,128)(2,1)} %param.17) | copy-start | bytes 24580
  42.8 5.1 %copy-start.13 = (f32[256]{0:T(256)S(1)}, f32[256]{0:T(256)}, u32[]{:S(2)}) copy-start(f32[256]{0:T(256)} %param.16) | copy-start | bytes 3076
  42.8 5.1 %copy-start.6 = (s32[1,32]{1,0:T(1,128)S(1)}, s32[1,32]{1,0:T(1,128)}, u32[]{:S(2)}) copy-start(s32[1,32]{1,0:T(1,128)} %param.10) | copy-start | bytes 388
  42.8 33.8 %all-to-all-start.1 = ((bf16[32,2,128,128]{3,2,1,0:T(8,128)(2,1)}), bf16[32,2,128,128]{3,2,1,0:T(8,128)(2,1)S(1)}, u32[]{:S(2)}, u32[]{:S(2)}) async-start(bf16[32,2,128,128]{3,2,1,0:T(8,128)(2,1)} %bitcast.49), calls=%async_computation.1 | async-start | bytes 4194304 | tf_op jit(solution)/shard_map/all_to_all | solution.py:479
  47.9 12.8 %copy-start.8 = (bf16[256,1024]{0,1:T(8,128)(2,1)S(1)}, bf16[256,1024]{0,1:T(8,128)(2,1)}, u32[]{:S(2)}) copy-start(bf16[256,1024]{0,1:T(8,128)(2,1)} %copy-done.7) | copy-start | bytes 1572868
  53.0 10.7 %collective-permute-start.9 = (f32[24,256]{1,0:T(8,128)S(1)}, f32[24,256]{1,0:T(8,128)S(1)}, u32[]{:S(2)}, u32[]{:S(2)}) collective-permute-start(f32[24,256]{1,0:T(8,128)S(1)} %pad_maximum_fusion.1), channel_id=1, source_target_pairs={{0,3},{1,0},{2,1},{3,2},{4,7},{5,4},{6,5},{7,6},{8,11},{9,8},{10,9... | collective-permute-start | bytes 73736 | tf_op jit(solution)/shard_map/ppermute | solution.py:470
  54.6 9.2 %collective-permute-start.10 = (f32[24,256]{1,0:T(8,128)S(1)}, f32[24,256]{1,0:T(8,128)S(1)}, u32[]{:S(2)}, u32[]{:S(2)}) collective-permute-start(f32[24,256]{1,0:T(8,128)S(1)} %pad_maximum_fusion.1), channel_id=1, source_target_pairs={{0,2},{1,3},{2,0},{3,1},{4,6},{5,7},{6,4},{7,5},{8,10},{9,11},{10,... | collective-permute-start | bytes 73736 | tf_op jit(solution)/shard_map/ppermute | solution.py:470
  57.2 6.6 %collective-permute-start.11 = (f32[24,256]{1,0:T(8,128)S(1)}, f32[24,256]{1,0:T(8,128)S(1)}, u32[]{:S(2)}, u32[]{:S(2)}) collective-permute-start(f32[24,256]{1,0:T(8,128)S(1)} %pad_maximum_fusion.1), channel_id=1, source_target_pairs={{0,1},{1,2},{2,3},{3,0},{4,5},{5,6},{6,7},{7,4},{8,9},{9,10},{10,1... | collective-permute-start | bytes 73736 | tf_op jit(solution)/shard_map/ppermute | solution.py:470
  57.2 26.6 %collective-permute-start.3 = (bf16[1024,128]{1,0:T(8,128)(2,1)S(1)}, bf16[1024,128]{1,0:T(8,128)(2,1)S(1)}, u32[]{:S(2)}, u32[]{:S(2)}) collective-permute-start(bf16[1024,128]{1,0:T(8,128)(2,1)S(1)} %get-tuple-element.42), channel_id=1, source_target_pairs={{0,1},{1,2},{2,3},{3,0},{4,5},{5,6},{6,7},{7,4},{8,9},{9,10},{10,1... | collective-permute-start | bytes 786440 | tf_op jit(solution)/shard_map/ppermute | solution.py:470
  59.3 31.1 %collective-permute-start.4 = (bf16[1024,128]{1,0:T(8,128)(2,1)}, bf16[1024,128]{1,0:T(8,128)(2,1)S(1)}, u32[]{:S(2)}, u32[]{:S(2)}) collective-permute-start(bf16[1024,128]{1,0:T(8,128)(2,1)} %get-tuple-element.43), channel_id=1, source_target_pairs={{0,2},{1,3},{2,0},{3,1},{4,6},{5,7},{6,4},{7,5},{8,10},{9,11},{10,... | collective-permute-start | bytes 786440 | tf_op jit(solution)/shard_map/ppermute | solution.py:470
  63.7 26.7 %collective-permute-start.5 = (bf16[1024,128]{1,0:T(8,128)(2,1)}, bf16[1024,128]{1,0:T(8,128)(2,1)}, u32[]{:S(2)}, u32[]{:S(2)}) collective-permute-start(bf16[1024,128]{1,0:T(8,128)(2,1)} %get-tuple-element.44), channel_id=1, source_target_pairs={{0,3},{1,0},{2,1},{3,2},{4,7},{5,4},{6,5},{7,6},{8,11},{9,8},{10,9... | collective-permute-start | bytes 786440 | tf_op jit(solution)/shard_map/ppermute | solution.py:470
  80.8 9.6 %collective-permute-start.6 = (bf16[1024,128]{1,0:T(8,128)(2,1)}, bf16[1024,128]{1,0:T(8,128)(2,1)}, u32[]{:S(2)}, u32[]{:S(2)}) collective-permute-start(bf16[1024,128]{1,0:T(8,128)(2,1)} %get-tuple-element.46), channel_id=1, source_target_pairs={{0,1},{1,2},{2,3},{3,0},{4,5},{5,6},{6,7},{7,4},{8,9},{9,10},{10,1... | collective-permute-start | bytes 786440 | tf_op jit(solution)/shard_map/ppermute | solution.py:470
  82.9 12.7 %collective-permute-start.7 = (bf16[1024,128]{1,0:T(8,128)(2,1)}, bf16[1024,128]{1,0:T(8,128)(2,1)}, u32[]{:S(2)}, u32[]{:S(2)}) collective-permute-start(bf16[1024,128]{1,0:T(8,128)(2,1)} %get-tuple-element.47), channel_id=1, source_target_pairs={{0,2},{1,3},{2,0},{3,1},{4,6},{5,7},{6,4},{7,5},{8,10},{9,11},{10,... | collective-permute-start | bytes 786440 | tf_op jit(solution)/shard_map/ppermute | solution.py:470
  83.8 12.7 %collective-permute-start.8 = (bf16[1024,128]{1,0:T(8,128)(2,1)}, bf16[1024,128]{1,0:T(8,128)(2,1)}, u32[]{:S(2)}, u32[]{:S(2)}) collective-permute-start(bf16[1024,128]{1,0:T(8,128)(2,1)} %get-tuple-element.48), channel_id=1, source_target_pairs={{0,3},{1,0},{2,1},{3,2},{4,7},{5,4},{6,5},{7,6},{8,11},{9,8},{10,9... | collective-permute-start | bytes 786440 | tf_op jit(solution)/shard_map/ppermute | solution.py:470
  84.9 0.7 copy-start.10
  87.8 8.7 %copy-start.1 = (bf16[1024,1024]{1,0:T(8,128)(2,1)S(1)}, bf16[1024,1024]{1,0:T(8,128)(2,1)}, u32[]{:S(2)}) copy-start(bf16[1024,1024]{1,0:T(8,128)(2,1)} %pad_maximum_fusion.refs_8_) | copy-start | bytes 6291460
  87.8 8.7 %copy-start.2 = (f32[1024,1]{1,0:T(8,128)S(1)}, f32[1024,1]{1,0:T(8,128)}, u32[]{:S(2)}) copy-start(f32[1024,1]{1,0:T(8,128)} %copy.21.refs_9_) | copy-start | bytes 12292
  90.4 18.1 %copy-start.5 = (s32[64]{0:T(128)S(1)}, s32[64]{0:T(128)}, u32[]{:S(2)}) copy-start(s32[64]{0:T(128)} %reshape.63.table) | copy-start | bytes 772
  90.4 33.3 %copy-start.4 = (s32[4096]{0:T(1024)S(1)}, s32[4096]{0:T(1024)}, u32[]{:S(2)}) copy-start(s32[4096]{0:T(1024)} %param.14) | copy-start | bytes 49156
  96.5 27.2 %copy-start = (bf16[32,4,128,128]{3,2,1,0:T(8,128)(2,1)S(1)}, bf16[32,4,128,128]{3,2,1,0:T(8,128)(2,1)}, u32[]{:S(2)}) copy-start(bf16[32,4,128,128]{3,2,1,0:T(8,128)(2,1)} %tiles.1) | copy-start | bytes 12582916
  100.6 4.4 %collective-permute-start.12 = (f32[8,16,128]{2,1,0:T(8,128)S(1)}, f32[8,16,128]{2,1,0:T(8,128)S(1)}, u32[]{:S(2)}, u32[]{:S(2)}) collective-permute-start(f32[8,16,128]{2,1,0:T(8,128)S(1)} %get-tuple-element.53.p0), channel_id=1, source_target_pairs={{0,1},{1,2},{2,3},{3,0},{4,5},{5,6},{6,7},{7,4},{8,9},{9,10},{10,1... | collective-permute-start | bytes 196616 | tf_op jit(solution)/shard_map/ppermute | solution.py:470
  102.7 5.8 %collective-permute-start.13 = (f32[8,16,128]{2,1,0:T(8,128)S(1)}, f32[8,16,128]{2,1,0:T(8,128)S(1)}, u32[]{:S(2)}, u32[]{:S(2)}) collective-permute-start(f32[8,16,128]{2,1,0:T(8,128)S(1)} %get-tuple-element.53.p0), channel_id=1, source_target_pairs={{0,2},{1,3},{2,0},{3,1},{4,6},{5,7},{6,4},{7,5},{8,10},{9,11},{10,... | collective-permute-start | bytes 196616 | tf_op jit(solution)/shard_map/ppermute | solution.py:470
  103.5 4.9 %collective-permute-start.14 = (f32[8,16,128]{2,1,0:T(8,128)S(1)}, f32[8,16,128]{2,1,0:T(8,128)S(1)}, u32[]{:S(2)}, u32[]{:S(2)}) collective-permute-start(f32[8,16,128]{2,1,0:T(8,128)S(1)} %get-tuple-element.53.p0), channel_id=1, source_target_pairs={{0,3},{1,0},{2,1},{3,2},{4,7},{5,4},{6,5},{7,6},{8,11},{9,8},{10,9... | collective-permute-start | bytes 196616 | tf_op jit(solution)/shard_map/ppermute | solution.py:470
  127.6 0.7 copy-start.3
  128.3 13.5 %all-to-all-start.3 = ((bf16[32,2,16,128]{3,2,1,0:T(8,128)(2,1)}), bf16[32,2,16,128]{3,2,1,0:T(8,128)(2,1)}, u32[]{:S(2)}, u32[]{:S(2)}) async-start(bf16[32,2,16,128]{3,2,1,0:T(8,128)(2,1)} %bitcast.43), calls=%async_computation.3 | async-start | bytes 524288 | tf_op jit(solution)/shard_map/all_to_all | solution.py:479
  149.4 13.0 %collective-permute-start.15 = (bf16[16,4,32,256]{3,2,1,0:T(8,128)(2,1)S(1)}, bf16[16,4,32,256]{3,2,1,0:T(8,128)(2,1)S(1)}, u32[]{:S(2)}, u32[]{:S(2)}) collective-permute-start(bf16[16,4,32,256]{3,2,1,0:T(8,128)(2,1)S(1)} %big_gradient.3), channel_id=1, source_target_pairs={{0,4},{4,0},{8,12},{12,8},{16,20},{20,16},{24,28},{28,24},{32,36},... | collective-permute-start | bytes 3145736 | tf_op jit(solution)/shard_map/ppermute | solution.py:474
  149.8 4.6 %collective-permute-start.16 = (f32[24,256]{1,0:T(8,128)S(1)}, f32[24,256]{1,0:T(8,128)S(1)}, u32[]{:S(2)}, u32[]{:S(2)}) collective-permute-start(f32[24,256]{1,0:T(8,128)S(1)} %get-tuple-element.61), channel_id=1, source_target_pairs={{0,3},{1,0},{2,1},{3,2},{4,7},{5,4},{6,5},{7,6},{8,11},{9,8},{10,9... | collective-permute-start | bytes 73736 | tf_op jit(solution)/shard_map/ppermute | solution.py:470
  150.6 5.3 %collective-permute-start.17 = (f32[24,256]{1,0:T(8,128)S(1)}, f32[24,256]{1,0:T(8,128)S(1)}, u32[]{:S(2)}, u32[]{:S(2)}) collective-permute-start(f32[24,256]{1,0:T(8,128)S(1)} %get-tuple-element.62), channel_id=1, source_target_pairs={{0,2},{1,3},{2,0},{3,1},{4,6},{5,7},{6,4},{7,5},{8,10},{9,11},{10,... | collective-permute-start | bytes 73736 | tf_op jit(solution)/shard_map/ppermute | solution.py:470
  153.8 3.8 %collective-permute-start.18 = (f32[24,256]{1,0:T(8,128)S(1)}, f32[24,256]{1,0:T(8,128)S(1)}, u32[]{:S(2)}, u32[]{:S(2)}) collective-permute-start(f32[24,256]{1,0:T(8,128)S(1)} %get-tuple-element.63), channel_id=1, source_target_pairs={{0,1},{1,2},{2,3},{3,0},{4,5},{5,6},{6,7},{7,4},{8,9},{9,10},{10,1... | collective-permute-start | bytes 73736 | tf_op jit(solution)/shard_map/ppermute | solution.py:470
  157.6 4.7 %collective-permute-start.19 = (f32[24,256]{1,0:T(8,128)S(1)}, f32[24,256]{1,0:T(8,128)S(1)}, u32[]{:S(2)}, u32[]{:S(2)}) collective-permute-start(f32[24,256]{1,0:T(8,128)S(1)} %add_add_fusion.1), channel_id=1, source_target_pairs={{0,4},{4,0},{8,12},{12,8},{16,20},{20,16},{24,28},{28,24},{32,36},... | collective-permute-start | bytes 73736 | tf_op jit(solution)/shard_map/ppermute | solution.py:474
  157.7 4.6 %collective-permute-start.20 = (f32[24,256]{1,0:T(8,128)S(1)}, f32[24,256]{1,0:T(8,128)S(1)}, u32[]{:S(2)}, u32[]{:S(2)}) collective-permute-start(f32[24,256]{1,0:T(8,128)S(1)} %add_add_fusion.1), channel_id=1, source_target_pairs={{0,8},{4,12},{8,0},{12,4},{16,24},{20,28},{24,16},{28,20},{32,40},... | collective-permute-start | bytes 73736 | tf_op jit(solution)/shard_map/ppermute | solution.py:474
  158.3 4.0 %collective-permute-start.21 = (f32[24,256]{1,0:T(8,128)S(1)}, f32[24,256]{1,0:T(8,128)S(1)}, u32[]{:S(2)}, u32[]{:S(2)}) collective-permute-start(f32[24,256]{1,0:T(8,128)S(1)} %add_add_fusion.1), channel_id=1, source_target_pairs={{0,12},{4,8},{8,4},{12,0},{16,28},{20,24},{24,20},{28,16},{32,44},... | collective-permute-start | bytes 73736 | tf_op jit(solution)/shard_map/ppermute | solution.py:474
  164.0 32.6 %all-to-all-start.4 = ((bf16[64,32,256]{2,1,0:T(8,128)(2,1)}), bf16[64,32,256]{2,1,0:T(8,128)(2,1)S(1)}, u32[]{:S(2)}, u32[]{:S(2)}) async-start(bf16[64,32,256]{2,1,0:T(8,128)(2,1)} %bitcast.53), calls=%async_computation.4 | async-start | bytes 2097152 | tf_op jit(solution)/shard_map/all_to_all | solution.py:527
  170.8 11.0 %collective-permute-start.22 = (f32[24,256]{1,0:T(8,128)S(1)}, f32[24,256]{1,0:T(8,128)S(1)}, u32[]{:S(2)}, u32[]{:S(2)}) collective-permute-start(f32[24,256]{1,0:T(8,128)S(1)} %add_add_fusion.refs_0_), channel_id=1, source_target_pairs={{0,16},{4,20},{8,24},{12,28},{16,0},{20,4},{24,8},{28,12},{32,48},... | collective-permute-start | bytes 73736 | tf_op jit(solution)/shard_map/ppermute | solution.py:474
  173.8 15.3 %collective-permute-start.23 = (f32[24,256]{1,0:T(8,128)S(1)}, f32[24,256]{1,0:T(8,128)S(1)}, u32[]{:S(2)}, u32[]{:S(2)}) collective-permute-start(f32[24,256]{1,0:T(8,128)S(1)} %add_add_fusion.refs_0_), channel_id=1, source_target_pairs={{0,32},{4,36},{8,40},{12,44},{16,48},{20,52},{24,56},{28,60},{32,0... | collective-permute-start | bytes 73736 | tf_op jit(solution)/shard_map/ppermute | solution.py:474
  175.3 14.1 %collective-permute-start.24 = (f32[24,256]{1,0:T(8,128)S(1)}, f32[24,256]{1,0:T(8,128)S(1)}, u32[]{:S(2)}, u32[]{:S(2)}) collective-permute-start(f32[24,256]{1,0:T(8,128)S(1)} %add_add_fusion.refs_0_), channel_id=1, source_target_pairs={{0,48},{4,52},{8,56},{12,60},{16,32},{20,36},{24,40},{28,44},{32,1... | collective-permute-start | bytes 73736 | tf_op jit(solution)/shard_map/ppermute | solution.py:474
  175.9 13.6 %collective-permute-start.25 = (f32[24,256]{1,0:T(8,128)S(1)}, f32[24,256]{1,0:T(8,128)S(1)}, u32[]{:S(2)}, u32[]{:S(2)}) collective-permute-start(f32[24,256]{1,0:T(8,128)S(1)} %add_add_fusion.refs_0_), channel_id=1, source_target_pairs={{0,64},{4,68},{8,72},{12,76},{16,80},{20,84},{24,88},{28,92},{32,9... | collective-permute-start | bytes 73736 | tf_op jit(solution)/shard_map/ppermute | solution.py:474
  178.9 11.1 %collective-permute-start.26 = (f32[24,256]{1,0:T(8,128)S(1)}, f32[24,256]{1,0:T(8,128)S(1)}, u32[]{:S(2)}, u32[]{:S(2)}) collective-permute-start(f32[24,256]{1,0:T(8,128)S(1)} %add_add_fusion.refs_0_), channel_id=1, source_target_pairs={{0,80},{4,84},{8,88},{12,92},{16,64},{20,68},{24,72},{28,76},{32,1... | collective-permute-start | bytes 73736 | tf_op jit(solution)/shard_map/ppermute | solution.py:474
  181.8 9.2 %collective-permute-start.27 = (f32[24,256]{1,0:T(8,128)S(1)}, f32[24,256]{1,0:T(8,128)S(1)}, u32[]{:S(2)}, u32[]{:S(2)}) collective-permute-start(f32[24,256]{1,0:T(8,128)S(1)} %add_add_fusion.refs_0_), channel_id=1, source_target_pairs={{0,96},{4,100},{8,104},{12,108},{16,112},{20,116},{24,120},{28,124... | collective-permute-start | bytes 73736 | tf_op jit(solution)/shard_map/ppermute | solution.py:474
  189.2 7.4 %collective-permute-start.28 = (f32[24,256]{1,0:T(8,128)S(1)}, f32[24,256]{1,0:T(8,128)S(1)}, u32[]{:S(2)}, u32[]{:S(2)}) collective-permute-start(f32[24,256]{1,0:T(8,128)S(1)} %add_add_fusion.refs_0_), channel_id=1, source_target_pairs={{0,112},{4,116},{8,120},{12,124},{16,96},{20,100},{24,104},{28,108... | collective-permute-start | bytes 73736 | tf_op jit(solution)/shard_map/ppermute | solution.py:474

commit v8 on v7

--- a/solution.py
+++ b/solution.py
@@ -13,6 +13,7 @@
 NT = (((1,), (1,)), ((), ()))
 NN = (((1,), (0,)), ((), ()))
 BLK = 128
+ORDER = (0, 2, 1, 3)
 MIB = 1 << 20
 
 
@@ -26,12 +27,6 @@
 
 def dot(a, b, dims):
     return lax.dot_general(a, b, dims, preferred_element_type=F32)
-
-
-def tree(terms):
-    while len(terms) > 1:
-        terms = [a + b for a, b in zip(terms[::2], terms[1::2])]
-    return terms[0]
 
 
 def in_hbm(x):
@@ -280,13 +275,11 @@
     )(src, counts, me, arrived, own, labels, tiles)
 
 
-def small_kernel(table, me, returned, dlog, hidden, second, dpre_out, *refs):
-    small, (total, dproj, buf) = refs[:-3], refs[-3:]
+def small_kernel(table, me, returned, dlog, hidden, second, dpre_out, small, total, dproj):
     group, grades, _ = dlog.shape
-    g = pl.program_id(0)
     width = hidden.shape[0]
 
-    @pl.when(g == 0)
+    @pl.when(pl.program_id(0) == 0)
     def _():
         total[pl.ds(0, group)] = dlog[...]
 
@@ -303,27 +296,20 @@
     dproj_b = dproj[...]
     dpre = jnp.where(active > 0, dot(second[...], dproj_b, NN), 0.0)
     dpre_out[...] = dpre.astype(BF16)
-    buf[pl.ds(0, grades), :] = dot(dproj_b, active, NT)
+    small[pl.ds(0, grades), :] = dot(dproj_b, active, NT)
     part = dpre[:, :BLK]
     for i in range(1, dpre.shape[1] // BLK):
         part += dpre[:, i * BLK : (i + 1) * BLK]
-    buf[pl.ds(grades, 8), :] = jnp.broadcast_to(
+    small[pl.ds(grades, 8), :] = jnp.broadcast_to(
         jnp.sum(part.T, axis=0, keepdims=True), (8, width)
     )
-    for k, out in enumerate(small):
-
-        @pl.when(g == k)
-        def _():
-            out[...] = buf[...]
 
 
 def small_gradients(table, me, returned, dlog, hidden, second, nfeat):
     hid, nodes = hidden.shape
     group, grades, _ = dlog.shape
     width = hid // nfeat
-    turn = lambda g, m: lax.rem(m[0] + nfeat - g, nfeat)
     whole3 = lambda g, t, m: (0, 0, 0)
-    small = jax.ShapeDtypeStruct((grades + 8, width), F32)
     return pl.pallas_call(
         small_kernel,
         grid_spec=pltpu.PrefetchScalarGridSpec(
@@ -332,18 +318,22 @@
             in_specs=[
                 pl.BlockSpec(returned.shape, whole3),
                 pl.BlockSpec(dlog.shape, whole3),
-                pl.BlockSpec((width, nodes), lambda g, t, m: (turn(g, m), 0)),
-                pl.BlockSpec((width, grades), lambda g, t, m: (turn(g, m), 0)),
+                pl.BlockSpec((width, nodes), lambda g, t, m: (g, 0)),
+                pl.BlockSpec((width, grades), lambda g, t, m: (g, 0)),
             ],
-            out_specs=[pl.BlockSpec((width, nodes), lambda g, t, m: (turn(g, m), 0))]
-            + [pl.BlockSpec(small.shape, lambda g, t, m: (0, 0))] * nfeat,
+            out_specs=[
+                pl.BlockSpec((width, nodes), lambda g, t, m: (g, 0)),
+                pl.BlockSpec((grades + 8, width), lambda g, t, m: (0, g)),
+            ],
             scratch_shapes=[
                 pltpu.VMEM((group + 1, grades, BLK), F32),
                 pltpu.VMEM((grades, nodes), BF16),
-                pltpu.VMEM(small.shape, F32),
             ],
         ),
-        out_shape=[pltpu.HBM((hid, nodes), BF16)] + [small] * nfeat,
+        out_shape=[
+            pltpu.HBM((hid, nodes), BF16),
+            jax.ShapeDtypeStruct((grades + 8, hid), F32),
+        ],
         compiler_params=params(16),
         cost_estimate=cost(2 * nodes * hid * 256, 4 * MIB),
         name="small_gradients",
@@ -354,9 +344,9 @@
     pieces, out = refs[:-1], refs[-1]
     nfeat = len(pieces) // 2
     rows = dpre[...].reshape(-1, dpre.shape[-1])
-    for k in range(nfeat):
+    for i, k in enumerate(ORDER):
         owner = lax.rem(me[0] + nfeat - k, nfeat)
-        both = jnp.concatenate([pieces[k][...], pieces[nfeat + k][...]], 1)
+        both = jnp.concatenate([pieces[i][...], pieces[nfeat + i][...]], 1)
         grad = dot(rows, both, NN).astype(BF16)
         out[:, owner] = grad.reshape(out.shape[0], out.shape[2], out.shape[3])
 
@@ -386,36 +376,47 @@
     )(me, side, in_hbm(dpre.reshape(parts // 2, 2, cols, nodes)), *pieces)
 
 
-def join_kernel(a, b, out):
-    out[...] = (a[...].astype(F32) + b[...].astype(F32)).astype(BF16)
-
-
-def join(a, b):
-    lead = a.shape[0] // 4
-    spec = pl.BlockSpec((lead, *a.shape[1:]), lambda g: (g, 0, 0, 0))
+def join_kernel(side, a, b, small, other, out):
+    rows, width = a.shape[2:]
+    both = small[...] + other[...]
+    near = both.astype(BF16)
+    rest = both - near.astype(F32)
+    kept = jnp.where(side[0] == 0, near.astype(F32), rest)
+    for f in range(a.shape[1]):
+        share = kept[:, f * width : (f + 1) * width]
+        for p in range(a.shape[0]):
+            grad = a[p, f].astype(F32) + b[p, f].astype(F32)
+            out[p, f] = jnp.concatenate([grad, share], 0).astype(BF16)
+
+
+def join(side, a, b, small, other):
+    steps = 4
+    lead, nfeat, rows, width = a.shape
+    more = small.shape[0]
+    spec = lambda n: pl.BlockSpec((lead // steps, nfeat, n, width), lambda g, s: (g, 0, 0, 0))
+    whole = pl.BlockSpec(small.shape, lambda g, s: (0, 0))
     return pl.pallas_call(
         join_kernel,
-        grid=(4,),
-        in_specs=[spec, spec],
-        out_specs=spec,
-        out_shape=pltpu.HBM(a.shape, BF16),
+        grid_spec=pltpu.PrefetchScalarGridSpec(
+            num_scalar_prefetch=1,
+            grid=(steps,),
+            in_specs=[spec(rows), spec(rows), whole, whole],
+            out_specs=spec(rows + more),
+        ),
+        out_shape=pltpu.HBM((lead, nfeat, rows + more, width), BF16),
         compiler_params=params(8),
-        cost_estimate=cost(a.size, 3 * MIB),
+        cost_estimate=cost(a.size, 4 * MIB),
         name="join",
-    )(a, b)
-
-
-def total_kernel(nsmall, arrived, *refs):
-    small, (out, second, bias, acc) = refs[:nsmall], refs[nsmall:]
+    )(side, a, b, small, other)
+
+
+def total_kernel(arrived, out, small, acc):
     g = pl.program_id(0)
+    rows = out.shape[0]
 
     @pl.when(g == 0)
     def _():
         acc[...] = jnp.zeros_like(acc)
-        whole = tree([ref[...] for ref in small])
-        grades = second.shape[0]
-        second[...] = whole[:grades]
-        bias[...] = whole[grades : grades + 1]
 
     total = arrived[0].astype(F32)
     for i in range(1, arrived.shape[0]):
@@ -424,33 +425,47 @@
 
     @pl.when(g == pl.num_programs(0) - 1)
     def _():
-        out[...] = acc[...]
-
-
-def total(arrived, small, grades):
-    n, cols, rows = arrived.shape
+        out[...] = acc[pl.ds(0, rows), :]
+        small[...] = acc[pl.ds(rows, small.shape[0]), :]
+
+
+def total(arrived, rows):
+    n, full, width = arrived.shape
     step = n // 8
-    whole = lambda g: (0, 0)
-    return pl.pallas_call(
-        functools.partial(total_kernel, len(small)),
+    shapes = [(rows, width), (full - rows, width)]
+    return pl.pallas_call(
+        total_kernel,
         grid=(n // step,),
-        in_specs=[pl.BlockSpec((step, cols, rows), lambda g: (g, 0, 0))]
-        + [pl.BlockSpec(small[0].shape, whole)] * len(small),
-        out_specs=[
-            pl.BlockSpec((cols, rows), whole),
-            pl.BlockSpec((grades, rows), whole),
-            pl.BlockSpec((1, rows), whole),
-        ],
-        out_shape=[
-            jax.ShapeDtypeStruct((cols, rows), F32),
-            jax.ShapeDtypeStruct((grades, rows), F32),
-            jax.ShapeDtypeStruct((1, rows), F32),
-        ],
-        scratch_shapes=[pltpu.VMEM((cols, rows), F32)],
+        in_specs=[pl.BlockSpec((step, full, width), lambda g: (g, 0, 0))],
+        out_specs=[pl.BlockSpec(shape, lambda g: (0, 0)) for shape in shapes],
+        out_shape=[jax.ShapeDtypeStruct(shape, F32) for shape in shapes],
+        scratch_shapes=[pltpu.VMEM((full, width), F32)],
         compiler_params=params(8),
         cost_estimate=cost(0, 2 * MIB),
         name="total",
-    )(arrived, *small)
+    )(arrived)
+
+
+def finish_kernel(a, b, second, bias):
+    grades = second.shape[0]
+    second[...] = a[pl.ds(0, grades), :] + b[pl.ds(0, grades), :]
+    bias[...] = a[pl.ds(grades, 1), :] + b[pl.ds(grades, 1), :]
+
+
+def finish(a, b, grades):
+    vmem = pl.BlockSpec(memory_space=pltpu.VMEM)
+    return pl.pallas_call(
+        finish_kernel,
+        in_specs=[vmem] * 2,
+        out_specs=[vmem] * 2,
+        out_shape=[
+            jax.ShapeDtypeStruct((grades, a.shape[1]), F32),
+            jax.ShapeDtypeStruct((1, a.shape[1]), F32),
+        ],
+        compiler_params=params(2),
+        cost_estimate=cost(0, MIB // 8),
+        name="finish",
+    )(a, b)
 
 
 def shards(features, pair_count, send_blocks, tile_src, tiles, labels, w_first, b_first, w_second):
@@ -469,10 +484,8 @@
     def ahead(x, k):
         return lax.ppermute(x, "feat", [(i, (i + k) % nfeat) for i in range(nfeat)])
 
-    def nearby(x, masks):
-        return [x] + [
-            lax.ppermute(x, "nodes", [(i, i ^ mask) for i in range(parts)]) for mask in masks
-        ]
+    def nearby(x):
+        return lax.ppermute(x, "nodes", [(i, i ^ 1) for i in range(parts)])
 
     def swap(x):
         shaped = x.reshape(parts, slots, *x.shape[1:])
@@ -491,22 +504,22 @@
     arrived.append(swap(send))
     others = (2, 1, 3)
     make = functools.partial(aggregate, src, counts, me)
-    first = [None] * nfeat
-    *sent, first[0] = make(arrived[0], tiles, features, 0, nfeat, others + (0,))
-    consts, weights, first[0] = lax.optimization_barrier((consts, weights, first[0]))
-    weights = jnp.concatenate([flat, weights[1], weights[0], weights[2]], 1)
+    *sent, own = make(arrived[0], tiles, features, 0, nfeat, others + (0,))
+    first = [own] + [ahead(piece, k) for k, piece in zip(others, sent)]
+    core = (lax.axis_index("nodes").astype(jnp.int32) % 2).reshape(1)
+    consts, weights, here, there, first[0] = lax.optimization_barrier(
+        (consts, weights, core, 1 - core, first[0])
+    )
+    weights = jnp.concatenate([flat] + weights, 1)
     turned = [consts] + [ahead(consts, k) for k in range(1, nfeat)]
     ring = jnp.stack([turned[k] for k in (3, 2, 1, 0, 3, 2, 1)])
     ordered = lax.dynamic_slice_in_dim(ring, nfeat - 1 - axis, nfeat, 0)
     second_t = ordered[:, :grades].transpose(1, 0, 2).reshape(grades, hid).astype(BF16)
     bias = ordered[:, grades].reshape(hid, 1)
     second = second_t.T
-    for k, piece in zip(others, sent):
-        first[k] = ahead(piece, k)
-    last = [None] * nfeat
-    for k, piece in zip(others, make(arrived[1], tiles, features, 1, nfeat, others)):
-        last[k] = ahead(piece, k)
-    (last[0],) = make(arrived[1], tiles, features, 1, nfeat, (0,))
+    sent = make(arrived[1], tiles, features, 1, nfeat, others)
+    last = list(make(arrived[1], tiles, features, 1, nfeat, (0,)))
+    last += [ahead(piece, k) for k, piece in zip(others, sent)]
     hidden, proj = dense(first + last, weights, bias, second_t)
 
     projs = [proj] + [ahead(proj, k) for k in range(1, nfeat)]
@@ -515,15 +528,10 @@
     dlog, slotsum = logits_back(
         src, counts, me, swap(send), own, labels.reshape(nblocks, 1, BLK), tiles, scale, nfeat
     )
-    dpre, *small = small_gradients(table, me, swap(slotsum), dlog, hidden, second, nfeat)
-    rest = small[0]
-    for k in range(1, nfeat):
-        rest = rest + ahead(small[k], nfeat - k)
-    rest = nearby(rest, (1, 2, 3))
-    core = (lax.axis_index("nodes").astype(jnp.int32) % 2).reshape(1)
-    (away,) = nearby(big_gradient(me, 1 - core, dpre, first + last, parts), (1,))[1:]
-    big = join(big_gradient(me, core, dpre, first + last, parts), away)
-    big, rest = lax.optimization_barrier((big, tree(rest)))
+    dpre, small = small_gradients(table, me, swap(slotsum), dlog, hidden, second, nfeat)
+    away = nearby(big_gradient(me, there, dpre, first + last, parts))
+    big = big_gradient(me, here, dpre, first + last, parts)
+    big = join(here, big, away, small, nearby(small))
     moved = lax.all_to_all(
         big.reshape(parts // 2 * nfeat, *big.shape[2:]),
         ("nodes", "feat"),
@@ -534,8 +542,8 @@
         ],
         tiled=True,
     )
-    terms = nearby(rest, range(4, parts, 4))
-    grad_first, grad_second, grad_bias = total(moved, terms, grades)
+    grad_first, rest = total(moved, hid // parts)
+    grad_second, grad_bias = finish(rest, nearby(rest), grades)
     return grad_first.T, grad_bias.reshape(-1), grad_second.T
 
 

time: 198 us -> 192 us (0.970)
  the two profiles are of different devices: /device:TPU:4 before, /device:TPU:1 now
where the time goes in v8:
time: 192 us; the launch traced here: 191 us
  blocking collectives  60.3 us (31%)
  starting transfers between devices  41.1 us (21%)
  Pallas kernels  39.8 us (21%)
  waiting for transfers between devices  36.7 us (19%)
  local copies, waits for them, and re-layouts  9.01 us (5%)
  other arithmetic  3.01 us (2%)
    all_to_all x1, blocking collectives, shards(): lax.all_to_all(big.reshape(parts // 2 * nfeat, *big.shape[2:]), ('nodes',...  31.5 us
    all_to_all x2, blocking collectives, swap(): lax.all_to_all(shaped, 'nodes', split_axis=0, concat_axis=0, tiled=True)  28.8 us
    ppermute x15, waiting for transfers between devices, ahead(): return lax.ppermute(x, 'feat', [(i, (i + k) % nfeat) for i in range(nfeat)])  26.4 us
    ppermute x15, starting transfers between devices, ahead(): return lax.ppermute(x, 'feat', [(i, (i + k) % nfeat) for i in range(nfeat)])  22 us
    all_to_all x2, starting transfers between devices, swap(): lax.all_to_all(shaped, 'nodes', split_axis=0, concat_axis=0, tiled=True)  16.3 us
    pallas_call x3, Pallas kernels, aggregate(): pl.pallas_call(functools.partial(agg_kernel, which, chunk, nfeat), grid_s...  11.9 us
    all_to_all x2, waiting for transfers between devices, swap(): lax.all_to_all(shaped, 'nodes', split_axis=0, concat_axis=0, tiled=True)  9.51 us
    pallas_call x2, Pallas kernels, pick(): pl.pallas_call(functools.partial(pick_kernel, chunk), grid_spec=pltpu.Pre...  6.52 us
  transfers between devices with their start and end apart: 20, of which 9 were waited for; matrix products, arithmetic and copies ran while one was open for 6% of the time, Pallas kernels for 9%

profile of v8, /device:TPU:1, one launch (start us, length us, event | category | flops | bytes accessed | tf_op | source)
XLA Modules:
  0.0 190.8 jit_solution(10731129868624652760)
XLA Ops:
  0.6 0.8 copy.17
  1.4 0.6 reshape.61.table
  2.0 3.3 %pick.3 = bf16[64,128,128]{2,1,0:T(8,128)(2,1)} custom-call(s32[64]{0:T(128)} %reshape.61.table, bf16[4096,256]{1,0:T(8,128)(2,1)} %features.9), custom_call_target="tpu_custom_call" | custom-call | bytes 4194304 | tf_op jit(solution)/shard_map/pick/pallas_call | solution.py:52
  5.3 9.8 %all-to-all-start = ((bf16[32,2,128,128]{3,2,1,0:T(8,128)(2,1)}), bf16[32,2,128,128]{3,2,1,0:T(8,128)(2,1)}, u32[]{:S(2)}, u32[]{:S(2)}) async-start(bf16[32,2,128,128]{3,2,1,0:T(8,128)(2,1)} %bitcast.51), calls=%async_computation | async-start | bytes 4194304 | tf_op jit(solution)/shard_map/all_to_all | solution.py:492
  15.1 0.2 copy.18
  15.3 2.8 %collective-permute-start = (bf16[1024,256]{1,0:T(8,128)(2,1)S(1)}, bf16[1024,256]{1,0:T(8,128)(2,1)}, u32[]{:S(2)}, u32[]{:S(2)}) collective-permute-start(bf16[1024,256]{1,0:T(8,128)(2,1)S(1)} %bitcast.55), channel_id=1, source_target_pairs={{0,2},{1,3},{2,0},{3,1},{4,6},{5,7},{6,4},{7,5},{8,10},{9,11},{10,... | collective-permute-start | bytes 1572872 | tf_op jit(solution)/shard_map/ppermute | solution.py:485
  18.2 0.3 collective-permute-start.1
  18.5 2.4 %collective-permute-start.2 = (bf16[1024,256]{1,0:T(8,128)(2,1)S(1)}, bf16[1024,256]{1,0:T(8,128)(2,1)}, u32[]{:S(2)}, u32[]{:S(2)}) collective-permute-start(bf16[1024,256]{1,0:T(8,128)(2,1)S(1)} %bitcast.57), channel_id=1, source_target_pairs={{0,3},{1,0},{2,1},{3,2},{4,7},{5,4},{6,5},{7,6},{8,11},{9,8},{10,9... | collective-permute-start | bytes 1572872 | tf_op jit(solution)/shard_map/ppermute | solution.py:485
  20.8 3.2 %pick.2 = bf16[64,128,128]{2,1,0:T(8,128)(2,1)} custom-call(s32[64]{0:T(128)} %reshape.61.table, bf16[4096,256]{1,0:T(8,128)(2,1)} %features.9), custom_call_target="tpu_custom_call" | custom-call | bytes 4194304 | tf_op jit(solution)/shard_map/pick/pallas_call | solution.py:52
  24.1 6.2 %collective-permute-done = bf16[1024,256]{1,0:T(8,128)(2,1)} collective-permute-done((bf16[1024,256]{1,0:T(8,128)(2,1)S(1)}, bf16[1024,256]{1,0:T(8,128)(2,1)}, u32[]{:S(2)}, u32[]{:S(2)}) %collective-permute-start) | collective-permute-done | bytes 524320 | tf_op jit(solution)/shard_map/ppermute | solution.py:485
  30.3 11.8 %collective-permute-done.1 = bf16[1024,256]{1,0:T(8,128)(2,1)} collective-permute-done((bf16[1024,256]{1,0:T(8,128)(2,1)S(1)}, bf16[1024,256]{1,0:T(8,128)(2,1)}, u32[]{:S(2)}, u32[]{:S(2)}) %collective-permute-start.1) | collective-permute-done | bytes 524320 | tf_op jit(solution)/shard_map/ppermute | solution.py:485
  42.1 1.3 all-to-all-done
  43.5 6.4 %all-to-all-start.1 = ((bf16[32,2,128,128]{3,2,1,0:T(8,128)(2,1)}), bf16[32,2,128,128]{3,2,1,0:T(8,128)(2,1)S(1)}, u32[]{:S(2)}, u32[]{:S(2)}) async-start(bf16[32,2,128,128]{3,2,1,0:T(8,128)(2,1)} %bitcast.50), calls=%async_computation.1 | async-start | bytes 4194304 | tf_op jit(solution)/shard_map/all_to_all | solution.py:492
  50.0 0.1 copy.19
  50.0 0.1 reshape.65.src
  50.2 5.1 %aggregate.3 = (bf16[1024,128]{1,0:T(8,128)(2,1)S(1)}, bf16[1024,128]{1,0:T(8,128)(2,1)}, bf16[1024,128]{1,0:T(8,128)(2,1)}, bf16[1024,128]{1,0:T(8,128)(2,1)S(1)}) custom-call(s32[128]{0:T(128)S(1)} %reshape.65.src, s32[32]{0:T(128)S(1)} %bitcast.46, s32[1]{0:T(128)} %bitcast.6.me, bf16[64,128,128]{2,1,0:T(8,128)(2,1)} %bitcast.3.arrived_hbm, ...), custom_call_target="tpu_custom_call" | custom-call | flops 536870912 | bytes 8388608 | tf_op jit(solution)/shard_map/aggregate/pallas_call | solution.py:109
  55.4 2.4 %collective-permute-start.9 = (f32[24,256]{1,0:T(8,128)S(1)}, f32[24,256]{1,0:T(8,128)S(1)}, u32[]{:S(2)}, u32[]{:S(2)}) collective-permute-start(f32[24,256]{1,0:T(8,128)S(1)} %pad_maximum_fusion.1), channel_id=1, source_target_pairs={{0,3},{1,0},{2,1},{3,2},{4,7},{5,4},{6,5},{7,6},{8,11},{9,8},{10,9... | collective-permute-start | bytes 73736 | tf_op jit(solution)/shard_map/ppermute | solution.py:485
  57.8 0.6 collective-permute-start.10
  58.4 0.1 collective-permute-start.11
  58.4 2.3 %collective-permute-start.3 = (bf16[1024,128]{1,0:T(8,128)(2,1)S(1)}, bf16[1024,128]{1,0:T(8,128)(2,1)S(1)}, u32[]{:S(2)}, u32[]{:S(2)}) collective-permute-start(bf16[1024,128]{1,0:T(8,128)(2,1)S(1)} %get-tuple-element.41), channel_id=1, source_target_pairs={{0,2},{1,3},{2,0},{3,1},{4,6},{5,7},{6,4},{7,5},{8,10},{9,11},{10,... | collective-permute-start | bytes 786440 | tf_op jit(solution)/shard_map/ppermute | solution.py:485
  60.7 0.9 collective-permute-start.4
  61.6 3.0 %pad_maximum_fusion.refs_8_ = bf16[1024,1024]{1,0:T(8,128)(2,1)} fusion(bf16[1024,256]{1,0:T(8,128)(2,1)} %collective-permute-done.2, bf16[1024,256]{1,0:T(8,128)(2,1)} %collective-permute-done.1, bf16[1024,256]{1,0:T(8,128)(2,1)} %collective-permute-done, bf16[1024,256]{1,0:T(8,128)(2,1)S(1)} %bitcast.58), kind=kLoop, calls=%fused_computation | loop fusion | flops 8388608 | bytes 4194304 | tf_op jit(solution)/shard_map/concatenate | solution.py:513
  64.7 1.8 collective-permute-start.5
  66.4 0.6 bitcast_dynamic-update-slice_fusion.5
  67.0 0.6 bitcast_dynamic-update-slice_fusion.3
  67.6 0.6 bitcast_dynamic-update-slice_fusion.1
  68.3 0.6 bitcast_dynamic-update-slice_fusion
  68.9 0.6 bitcast_dynamic-update-slice_fusion.6
  69.5 0.6 bitcast_dynamic-update-slice_fusion.4
  70.1 8.2 %all-to-all-done.1 = bf16[32,2,128,128]{3,2,1,0:T(8,128)(2,1)S(1)} async-done(((bf16[32,2,128,128]{3,2,1,0:T(8,128)(2,1)}), bf16[32,2,128,128]{3,2,1,0:T(8,128)(2,1)S(1)}, u32[]{:S(2)}, u32[]{:S(2)}) %all-to-all-start.1) | async-done | bytes 2097184 | tf_op jit(solution)/shard_map/all_to_all | solution.py:492
  78.2 4.2 %aggregate.5 = (bf16[1024,128]{1,0:T(8,128)(2,1)}, bf16[1024,128]{1,0:T(8,128)(2,1)}, bf16[1024,128]{1,0:T(8,128)(2,1)}) custom-call(s32[128]{0:T(128)S(1)} %reshape.65.src, s32[32]{0:T(128)S(1)} %bitcast.47, s32[1]{0:T(128)} %bitcast.6.me, bf16[64,128,128]{2,1,0:T(8,128)(2,1)S(1)} %bitcast.37, bf16[32,4,128,128]{3,2,1,0:T(8,128)(2,1)} %tiles.1, ...), custom_call_target="tpu_custom_call" | custom-call | flops 402653184 | bytes 8388608 | tf_op jit(solution)/shard_map/aggregate/pallas_call | solution.py:109
  82.5 1.9 collective-permute-start.6
  84.3 1.2 collective-permute-start.7
  85.5 1.5 collective-permute-start.8
  87.0 0.6 bitcast_dynamic-update-slice_fusion.2
  87.6 0.8 constant_dynamic-slice_fusion
  88.4 1.0 copy.21.refs_9_
  89.4 0.8 fusion
  90.2 0.2 copy.20
  90.4 0.1 copy.22.refs_10_
  90.6 2.6 %aggregate.4.refs_4_ = bf16[1024,128]{1,0:T(8,128)(2,1)S(1)} custom-call(s32[128]{0:T(128)S(1)} %reshape.65.src, s32[32]{0:T(128)S(1)} %bitcast.48, s32[1]{0:T(128)} %bitcast.6.me, bf16[64,128,128]{2,1,0:T(8,128)(2,1)S(1)} %bitcast.38, bf16[32,4,128,128]{3,2,1,0:T(8,128)(2,1)} %tiles.1, bf16[4096,256]{1,0:T(8,128)(2,1)} %features.9), custom_call_target="tpu_custom_call" | custom-call | flops 134217728 | bytes 8388608 | tf_op jit(solution)/shard_map/aggregate/pallas_call | solution.py:109
  93.2 5.0 %collective-permute-done.7.refs_6_ = bf16[1024,128]{1,0:T(8,128)(2,1)} collective-permute-done((bf16[1024,128]{1,0:T(8,128)(2,1)}, bf16[1024,128]{1,0:T(8,128)(2,1)}, u32[]{:S(2)}, u32[]{:S(2)}) %collective-permute-start.7) | collective-permute-done | bytes 262176 | tf_op jit(solution)/shard_map/ppermute | solution.py:485
  98.2 4.1 %dense.1 = (bf16[1024,1024]{1,0:T(8,128)(2,1)S(1)}, f32[8,16,128]{2,1,0:T(8,128)S(1)}) custom-call(bf16[1024,128]{1,0:T(8,128)(2,1)S(1)} %get-tuple-element.40.refs_0_, bf16[1024,128]{1,0:T(8,128)(2,1)S(1)} %collective-permute-done.3.refs_1_, bf16[1024,128]{1,0:T(8,128)(2,1)S(1)} %collective-permute-done.4.refs_2_, ...), custom_call_target="tpu_custom_call" | custom-call | flops 2147483648 | bytes 7340032 | tf_op jit(solution)/shard_map/dense/pallas_call | solution.py:146
  102.3 1.2 collective-permute-start.12
  103.5 2.4 %collective-permute-start.13 = (f32[8,16,128]{2,1,0:T(8,128)S(1)}, f32[8,16,128]{2,1,0:T(8,128)S(1)}, u32[]{:S(2)}, u32[]{:S(2)}) collective-permute-start(f32[8,16,128]{2,1,0:T(8,128)S(1)} %get-tuple-element.52.p0), channel_id=1, source_target_pairs={{0,2},{1,3},{2,0},{3,1},{4,6},{5,7},{6,4},{7,5},{8,10},{9,11},{10,... | collective-permute-start | bytes 196616 | tf_op jit(solution)/shard_map/ppermute | solution.py:485
  105.9 0.3 collective-permute-start.14
  106.2 0.5 collective-permute-done.12.p1
  106.7 2.0 %collective-permute-done.13.p2 = f32[8,16,128]{2,1,0:T(8,128)S(1)} collective-permute-done((f32[8,16,128]{2,1,0:T(8,128)S(1)}, f32[8,16,128]{2,1,0:T(8,128)S(1)}, u32[]{:S(2)}, u32[]{:S(2)}) %collective-permute-start.13) | collective-permute-done | bytes 65568 | tf_op jit(solution)/shard_map/ppermute | solution.py:485
  108.7 0.8 collective-permute-done.14.p3
  109.5 0.7 spread.1
  110.2 16.3 %all_to_all.25 = f32[32,2,16,128]{3,2,1,0:T(8,128)S(1)} all-to-all(f32[32,2,16,128]{3,2,1,0:T(8,128)S(1)} %bitcast.43), channel_id=1, replica_groups=mesh['nodes'=32,'feat'=4] {'nodes'}, dimensions={0} | all-to-all | bytes 1048576 | tf_op jit(solution)/shard_map/all_to_all | solution.py:492
  126.5 3.9 %logits.1 = (f32[8,16,128]{2,1,0:T(8,128)S(1)}, bf16[64,16,128]{2,1,0:T(8,128)(2,1)S(1)}) custom-call(s32[128]{0:T(128)S(1)} %reshape.65.src, s32[32]{0:T(128)S(1)} %bitcast.49, s32[1]{0:T(128)} %bitcast.6.me, f32[64,16,128]{2,1,0:T(8,128)S(1)} %bitcast.41, f32[32,16,128]{2,1,0:T(8,128)S(1)} %get-tuple-element.54.own, s32[32,1,128]{2,1,0:T(1,128)S(1)} %bitcast.45, ...), custom_call_target="tpu_custom_call" | custom-call | flops 268435456 | bytes 6291456 | tf_op jit(solution)/shard_map/logits/pallas_call | solution.py:254
  130.5 12.4 %all_to_all.26 = bf16[32,2,16,128]{3,2,1,0:T(8,128)(2,1)S(1)} all-to-all(bf16[32,2,16,128]{3,2,1,0:T(8,128)(2,1)S(1)} %bitcast.44), channel_id=1, replica_groups=mesh['nodes'=32,'feat'=4] {'nodes'}, dimensions={0} | all-to-all | bytes 524288 | tf_op jit(solution)/shard_map/all_to_all | solution.py:492
  142.9 3.7 %small_gradients.1 = (bf16[1024,1024]{1,0:T(8,128)(2,1)}, f32[24,1024]{1,0:T(8,128)S(1)}) custom-call(s32[64]{0:T(128)S(1)} %copy-done.4, s32[1]{0:T(128)} %bitcast.6.me, bf16[64,16,128]{2,1,0:T(8,128)(2,1)S(1)} %bitcast.42, f32[8,16,128]{2,1,0:T(8,128)S(1)} %get-tuple-element.56.dlog, bf16[1024,1024]{1,0:T(8,128)(2,1)S(1)} %get-tuple-element.57.hidden, ...), custom_call_target="tpu_custom_call" | custom-call | flops 536870912 | bytes 4194304 | tf_op jit(solution)/shard_map/small_gradients/pallas_call | solution.py:313
  146.6 2.7 %big_gradient.3 = bf16[16,4,32,256]{3,2,1,0:T(8,128)(2,1)S(1)} custom-call(s32[1]{0:T(128)} %bitcast.6.me, s32[1]{0:T(128)S(6)} %sub.6.side, bf16[16,2,32,1024]{3,2,1,0:T(8,128)(2,1)} %bitcast.52, bf16[1024,128]{1,0:T(8,128)(2,1)S(1)} %get-tuple-element.40.refs_0_, bf16[1024,128]{1,0:T(8,128)(2,1)S(1)} %collective-permute-done.3.refs_1_, ...), custom_call_target="tpu_custom_call" | custom-call | flops 1073741824 | bytes 4194304 | tf_op jit(solution)/shard_map/big_gradient/pallas_call | solution.py:359
  149.3 0.3 collective-permute-start.15
  149.6 0.3 collective-permute-start.16
  149.9 2.7 %big_gradient.2.a = bf16[16,4,32,256]{3,2,1,0:T(8,128)(2,1)S(1)} custom-call(s32[1]{0:T(128)} %bitcast.6.me, s32[1]{0:T(128)} %bitcast.4.side, bf16[16,2,32,1024]{3,2,1,0:T(8,128)(2,1)} %bitcast.53, bf16[1024,128]{1,0:T(8,128)(2,1)S(1)} %get-tuple-element.40.refs_0_, bf16[1024,128]{1,0:T(8,128)(2,1)S(1)} %collective-permute-done.3.refs_1_, ...), custom_call_target="tpu_custom_call" | custom-call | flops 1073741824 | bytes 4194304 | tf_op jit(solution)/shard_map/big_gradient/pallas_call | solution.py:359
  152.7 1.9 %join.1 = bf16[16,4,56,256]{3,2,1,0:T(8,128)(2,1)} custom-call(s32[1]{0:T(128)} %bitcast.4.side, bf16[16,4,32,256]{3,2,1,0:T(8,128)(2,1)S(1)} %big_gradient.2.a, bf16[16,4,32,256]{3,2,1,0:T(8,128)(2,1)S(1)} %collective-permute-done.15.b, f32[24,1024]{1,0:T(8,128)S(1)} %get-tuple-element.60.small, f32[24,1024]{1,0:T(8,128)S(1)} %collective-permute-done.16.other), custom_call_target="tpu_custom_call" | custom-call | flops 524288 | bytes 4194304 | tf_op jit(solution)/shard_map/join/pallas_call | solution.py:398
  154.6 31.5 %all_to_all.27.arrived = bf16[64,56,256]{2,1,0:T(8,128)(2,1)S(1)} all-to-all(bf16[64,56,256]{2,1,0:T(8,128)(2,1)} %bitcast.54), channel_id=1, replica_groups={{0,1,2,3,8,9,10,11,16,17,18,19,24,25,26,27,32,33,34,35,40,41,42,43,48,4..., dimensions={0} | all-to-all | bytes 3670016 | tf_op jit(solution)/shard_map/all_to_all | solution.py:535
  186.1 1.0 total.1
  187.1 2.2 %collective-permute-start.17 = (f32[24,256]{1,0:T(8,128)S(1)}, f32[24,256]{1,0:T(8,128)S(1)}, u32[]{:S(2)}, u32[]{:S(2)}) collective-permute-start(f32[24,256]{1,0:T(8,128)S(1)} %get-tuple-element.62.a), channel_id=1, source_target_pairs={{0,4},{4,0},{8,12},{12,8},{16,20},{20,16},{24,28},{28,24},{32,36},... | collective-permute-start | bytes 73736 | tf_op jit(solution)/shard_map/ppermute | solution.py:488
  189.4 0.8 collective-permute-done.17.b
  190.2 0.6 finish.1
  (38 shorter events, 0.1 us)
Async XLA Ops:
  5.3 9.8 %copy-start.8 = (bf16[256,1024]{1,0:T(8,128)(2,1)S(1)}, bf16[256,1024]{1,0:T(8,128)(2,1)}, u32[]{:S(2)}) copy-start(bf16[256,1024]{1,0:T(8,128)(2,1)} %param.15) | copy-start | bytes 1572868
  5.3 38.2 %all-to-all-start = ((bf16[32,2,128,128]{3,2,1,0:T(8,128)(2,1)}), bf16[32,2,128,128]{3,2,1,0:T(8,128)(2,1)}, u32[]{:S(2)}, u32[]{:S(2)}) async-start(bf16[32,2,128,128]{3,2,1,0:T(8,128)(2,1)} %bitcast.51), calls=%async_computation | async-start | bytes 4194304 | tf_op jit(solution)/shard_map/all_to_all | solution.py:492
  15.3 8.8 %copy-start.6 = (bf16[256,1024]{0,1:T(8,128)(2,1)}, bf16[256,1024]{0,1:T(8,128)(2,1)S(1)}, u32[]{:S(2)}) copy-start(bf16[256,1024]{0,1:T(8,128)(2,1)S(1)} %copy.18) | copy-start | bytes 1572868
  15.3 14.9 %collective-permute-start = (bf16[1024,256]{1,0:T(8,128)(2,1)S(1)}, bf16[1024,256]{1,0:T(8,128)(2,1)}, u32[]{:S(2)}, u32[]{:S(2)}) collective-permute-start(bf16[1024,256]{1,0:T(8,128)(2,1)S(1)} %bitcast.55), channel_id=1, source_target_pairs={{0,2},{1,3},{2,0},{3,1},{4,6},{5,7},{6,4},{7,5},{8,10},{9,11},{10,... | collective-permute-start | bytes 1572872 | tf_op jit(solution)/shard_map/ppermute | solution.py:485
  18.2 23.9 %collective-permute-start.1 = (bf16[1024,256]{1,0:T(8,128)(2,1)S(1)}, bf16[1024,256]{1,0:T(8,128)(2,1)}, u32[]{:S(2)}, u32[]{:S(2)}) collective-permute-start(bf16[1024,256]{1,0:T(8,128)(2,1)S(1)} %bitcast.56), channel_id=1, source_target_pairs={{0,1},{1,2},{2,3},{3,0},{4,5},{5,6},{6,7},{7,4},{8,9},{9,10},{10,1... | collective-permute-start | bytes 1572872 | tf_op jit(solution)/shard_map/ppermute | solution.py:485
  18.5 23.6 %collective-permute-start.2 = (bf16[1024,256]{1,0:T(8,128)(2,1)S(1)}, bf16[1024,256]{1,0:T(8,128)(2,1)}, u32[]{:S(2)}, u32[]{:S(2)}) collective-permute-start(bf16[1024,256]{1,0:T(8,128)(2,1)S(1)} %bitcast.57), channel_id=1, source_target_pairs={{0,3},{1,0},{2,1},{3,2},{4,7},{5,4},{6,5},{7,6},{8,11},{9,8},{10,9... | collective-permute-start | bytes 1572872 | tf_op jit(solution)/shard_map/ppermute | solution.py:485
  43.5 6.5 %copy-start.10 = (s32[32,4]{0,1:T(4,128)S(1)}, s32[32,4]{0,1:T(4,128)}, u32[]{:S(2)}) copy-start(s32[32,4]{0,1:T(4,128)} %param.12) | copy-start | bytes 1540
  43.5 6.7 %copy-start.9 = (bf16[256,16]{0,1:T(8,128)(2,1)S(1)}, bf16[256,16]{0,1:T(8,128)(2,1)}, u32[]{:S(2)}) copy-start(bf16[256,16]{0,1:T(8,128)(2,1)} %param.17) | copy-start | bytes 24580
  43.5 6.7 %copy-start.11 = (f32[256]{0:T(256)S(1)}, f32[256]{0:T(256)}, u32[]{:S(2)}) copy-start(f32[256]{0:T(256)} %param.16) | copy-start | bytes 3076
  43.5 6.7 %copy-start.5 = (s32[1,32]{1,0:T(1,128)S(1)}, s32[1,32]{1,0:T(1,128)}, u32[]{:S(2)}) copy-start(s32[1,32]{1,0:T(1,128)} %param.10) | copy-start | bytes 388
  43.5 34.8 %all-to-all-start.1 = ((bf16[32,2,128,128]{3,2,1,0:T(8,128)(2,1)}), bf16[32,2,128,128]{3,2,1,0:T(8,128)(2,1)S(1)}, u32[]{:S(2)}, u32[]{:S(2)}) async-start(bf16[32,2,128,128]{3,2,1,0:T(8,128)(2,1)} %bitcast.50), calls=%async_computation.1 | async-start | bytes 4194304 | tf_op jit(solution)/shard_map/all_to_all | solution.py:492
  50.2 11.4 %copy-start.7 = (bf16[256,1024]{0,1:T(8,128)(2,1)S(1)}, bf16[256,1024]{0,1:T(8,128)(2,1)}, u32[]{:S(2)}) copy-start(bf16[256,1024]{0,1:T(8,128)(2,1)} %copy-done.6) | copy-start | bytes 1572868
  55.4 9.3 %collective-permute-start.9 = (f32[24,256]{1,0:T(8,128)S(1)}, f32[24,256]{1,0:T(8,128)S(1)}, u32[]{:S(2)}, u32[]{:S(2)}) collective-permute-start(f32[24,256]{1,0:T(8,128)S(1)} %pad_maximum_fusion.1), channel_id=1, source_target_pairs={{0,3},{1,0},{2,1},{3,2},{4,7},{5,4},{6,5},{7,6},{8,11},{9,8},{10,9... | collective-permute-start | bytes 73736 | tf_op jit(solution)/shard_map/ppermute | solution.py:485
  57.8 9.3 %collective-permute-start.10 = (f32[24,256]{1,0:T(8,128)S(1)}, f32[24,256]{1,0:T(8,128)S(1)}, u32[]{:S(2)}, u32[]{:S(2)}) collective-permute-start(f32[24,256]{1,0:T(8,128)S(1)} %pad_maximum_fusion.1), channel_id=1, source_target_pairs={{0,2},{1,3},{2,0},{3,1},{4,6},{5,7},{6,4},{7,5},{8,10},{9,11},{10,... | collective-permute-start | bytes 73736 | tf_op jit(solution)/shard_map/ppermute | solution.py:485
  58.4 9.3 %collective-permute-start.11 = (f32[24,256]{1,0:T(8,128)S(1)}, f32[24,256]{1,0:T(8,128)S(1)}, u32[]{:S(2)}, u32[]{:S(2)}) collective-permute-start(f32[24,256]{1,0:T(8,128)S(1)} %pad_maximum_fusion.1), channel_id=1, source_target_pairs={{0,1},{1,2},{2,3},{3,0},{4,5},{5,6},{6,7},{7,4},{8,9},{9,10},{10,1... | collective-permute-start | bytes 73736 | tf_op jit(solution)/shard_map/ppermute | solution.py:485
  58.4 27.0 %collective-permute-start.3 = (bf16[1024,128]{1,0:T(8,128)(2,1)S(1)}, bf16[1024,128]{1,0:T(8,128)(2,1)S(1)}, u32[]{:S(2)}, u32[]{:S(2)}) collective-permute-start(bf16[1024,128]{1,0:T(8,128)(2,1)S(1)} %get-tuple-element.41), channel_id=1, source_target_pairs={{0,2},{1,3},{2,0},{3,1},{4,6},{5,7},{6,4},{7,5},{8,10},{9,11},{10,... | collective-permute-start | bytes 786440 | tf_op jit(solution)/shard_map/ppermute | solution.py:485
  60.7 32.4 %collective-permute-start.4 = (bf16[1024,128]{1,0:T(8,128)(2,1)}, bf16[1024,128]{1,0:T(8,128)(2,1)S(1)}, u32[]{:S(2)}, u32[]{:S(2)}) collective-permute-start(bf16[1024,128]{1,0:T(8,128)(2,1)} %get-tuple-element.42), channel_id=1, source_target_pairs={{0,1},{1,2},{2,3},{3,0},{4,5},{5,6},{6,7},{7,4},{8,9},{9,10},{10,1... | collective-permute-start | bytes 786440 | tf_op jit(solution)/shard_map/ppermute | solution.py:485
  64.7 28.5 %collective-permute-start.5 = (bf16[1024,128]{1,0:T(8,128)(2,1)}, bf16[1024,128]{1,0:T(8,128)(2,1)S(1)}, u32[]{:S(2)}, u32[]{:S(2)}) collective-permute-start(bf16[1024,128]{1,0:T(8,128)(2,1)} %get-tuple-element.43), channel_id=1, source_target_pairs={{0,3},{1,0},{2,1},{3,2},{4,7},{5,4},{6,5},{7,6},{8,11},{9,8},{10,9... | collective-permute-start | bytes 786440 | tf_op jit(solution)/shard_map/ppermute | solution.py:485
  82.5 10.7 %collective-permute-start.6 = (bf16[1024,128]{1,0:T(8,128)(2,1)}, bf16[1024,128]{1,0:T(8,128)(2,1)}, u32[]{:S(2)}, u32[]{:S(2)}) collective-permute-start(bf16[1024,128]{1,0:T(8,128)(2,1)} %get-tuple-element.45), channel_id=1, source_target_pairs={{0,2},{1,3},{2,0},{3,1},{4,6},{5,7},{6,4},{7,5},{8,10},{9,11},{10,... | collective-permute-start | bytes 786440 | tf_op jit(solution)/shard_map/ppermute | solution.py:485
  84.3 13.9 %collective-permute-start.7 = (bf16[1024,128]{1,0:T(8,128)(2,1)}, bf16[1024,128]{1,0:T(8,128)(2,1)}, u32[]{:S(2)}, u32[]{:S(2)}) collective-permute-start(bf16[1024,128]{1,0:T(8,128)(2,1)} %get-tuple-element.46), channel_id=1, source_target_pairs={{0,1},{1,2},{2,3},{3,0},{4,5},{5,6},{6,7},{7,4},{8,9},{9,10},{10,1... | collective-permute-start | bytes 786440 | tf_op jit(solution)/shard_map/ppermute | solution.py:485
  85.5 12.7 %collective-permute-start.8 = (bf16[1024,128]{1,0:T(8,128)(2,1)}, bf16[1024,128]{1,0:T(8,128)(2,1)}, u32[]{:S(2)}, u32[]{:S(2)}) collective-permute-start(bf16[1024,128]{1,0:T(8,128)(2,1)} %get-tuple-element.47), channel_id=1, source_target_pairs={{0,3},{1,0},{2,1},{3,2},{4,7},{5,4},{6,5},{7,6},{8,11},{9,8},{10,9... | collective-permute-start | bytes 786440 | tf_op jit(solution)/shard_map/ppermute | solution.py:485
  90.5 7.7 %copy-start.1 = (bf16[1024,1024]{1,0:T(8,128)(2,1)S(1)}, bf16[1024,1024]{1,0:T(8,128)(2,1)}, u32[]{:S(2)}) copy-start(bf16[1024,1024]{1,0:T(8,128)(2,1)} %pad_maximum_fusion.refs_8_) | copy-start | bytes 6291460
  90.5 7.7 %copy-start.2 = (f32[1024,1]{1,0:T(8,128)S(1)}, f32[1024,1]{1,0:T(8,128)}, u32[]{:S(2)}) copy-start(f32[1024,1]{1,0:T(8,128)} %copy.21.refs_9_) | copy-start | bytes 12292
  93.1 16.4 %copy-start.4 = (s32[64]{0:T(128)S(1)}, s32[64]{0:T(128)}, u32[]{:S(2)}) copy-start(s32[64]{0:T(128)} %reshape.61.table) | copy-start | bytes 772
  93.1 33.4 %copy-start.3 = (s32[4096]{0:T(1024)S(1)}, s32[4096]{0:T(1024)}, u32[]{:S(2)}) copy-start(s32[4096]{0:T(1024)} %param.14) | copy-start | bytes 49156
  98.2 28.3 %copy-start = (bf16[32,4,128,128]{3,2,1,0:T(8,128)(2,1)S(1)}, bf16[32,4,128,128]{3,2,1,0:T(8,128)(2,1)}, u32[]{:S(2)}) copy-start(bf16[32,4,128,128]{3,2,1,0:T(8,128)(2,1)} %tiles.1) | copy-start | bytes 12582916
  102.3 4.4 %collective-permute-start.12 = (f32[8,16,128]{2,1,0:T(8,128)S(1)}, f32[8,16,128]{2,1,0:T(8,128)S(1)}, u32[]{:S(2)}, u32[]{:S(2)}) collective-permute-start(f32[8,16,128]{2,1,0:T(8,128)S(1)} %get-tuple-element.52.p0), channel_id=1, source_target_pairs={{0,1},{1,2},{2,3},{3,0},{4,5},{5,6},{6,7},{7,4},{8,9},{9,10},{10,1... | collective-permute-start | bytes 196616 | tf_op jit(solution)/shard_map/ppermute | solution.py:485
  103.5 5.2 %collective-permute-start.13 = (f32[8,16,128]{2,1,0:T(8,128)S(1)}, f32[8,16,128]{2,1,0:T(8,128)S(1)}, u32[]{:S(2)}, u32[]{:S(2)}) collective-permute-start(f32[8,16,128]{2,1,0:T(8,128)S(1)} %get-tuple-element.52.p0), channel_id=1, source_target_pairs={{0,2},{1,3},{2,0},{3,1},{4,6},{5,7},{6,4},{7,5},{8,10},{9,11},{10,... | collective-permute-start | bytes 196616 | tf_op jit(solution)/shard_map/ppermute | solution.py:485
  105.9 3.6 %collective-permute-start.14 = (f32[8,16,128]{2,1,0:T(8,128)S(1)}, f32[8,16,128]{2,1,0:T(8,128)S(1)}, u32[]{:S(2)}, u32[]{:S(2)}) collective-permute-start(f32[8,16,128]{2,1,0:T(8,128)S(1)} %get-tuple-element.52.p0), channel_id=1, source_target_pairs={{0,3},{1,0},{2,1},{3,2},{4,7},{5,4},{6,5},{7,6},{8,11},{9,8},{10,9... | collective-permute-start | bytes 196616 | tf_op jit(solution)/shard_map/ppermute | solution.py:485
  149.3 3.3 %collective-permute-start.15 = (bf16[16,4,32,256]{3,2,1,0:T(8,128)(2,1)S(1)}, bf16[16,4,32,256]{3,2,1,0:T(8,128)(2,1)S(1)}, u32[]{:S(2)}, u32[]{:S(2)}) collective-permute-start(bf16[16,4,32,256]{3,2,1,0:T(8,128)(2,1)S(1)} %big_gradient.3), channel_id=1, source_target_pairs={{0,4},{4,0},{8,12},{12,8},{16,20},{20,16},{24,28},{28,24},{32,36},... | collective-permute-start | bytes 3145736 | tf_op jit(solution)/shard_map/ppermute | solution.py:488
  149.6 3.0 %collective-permute-start.16 = (f32[24,1024]{1,0:T(8,128)S(1)}, f32[24,1024]{1,0:T(8,128)S(1)}, u32[]{:S(2)}, u32[]{:S(2)}) collective-permute-start(f32[24,1024]{1,0:T(8,128)S(1)} %get-tuple-element.60.small), channel_id=1, source_target_pairs={{0,4},{4,0},{8,12},{12,8},{16,20},{20,16},{24,28},{28,24},{32,36},... | collective-permute-start | bytes 294920 | tf_op jit(solution)/shard_map/ppermute | solution.py:488
  187.1 3.1 %collective-permute-start.17 = (f32[24,256]{1,0:T(8,128)S(1)}, f32[24,256]{1,0:T(8,128)S(1)}, u32[]{:S(2)}, u32[]{:S(2)}) collective-permute-start(f32[24,256]{1,0:T(8,128)S(1)} %get-tuple-element.62.a), channel_id=1, source_target_pairs={{0,4},{4,0},{8,12},{12,8},{16,20},{20,16},{24,28},{28,24},{32,36},... | collective-permute-start | bytes 73736 | tf_op jit(solution)/shard_map/ppermute | solution.py:488

commit v9 on v8

--- a/solution.py
+++ b/solution.py
@@ -41,14 +41,15 @@
 
     @pl.loop(0, slots, unroll=8)
     def _(k):
-        rows = pl.ds(pl.multiple_of(table[k] * BLK, BLK), BLK)
+        block = table[0, lax.div(k, 2), lax.rem(k, 2)]
+        rows = pl.ds(pl.multiple_of(block * BLK, BLK), BLK)
         pltpu.make_async_copy(held.at[rows], out.at[k], sems.at[1]).start()
 
     pltpu.make_async_copy(out, out, sems.at[1]).wait()
 
 
 def pick(features, table, chunk):
-    slots = table.shape[0]
+    slots = table.size
     return pl.pallas_call(
         functools.partial(pick_kernel, chunk),
         grid_spec=pltpu.PrefetchScalarGridSpec(
@@ -68,27 +69,31 @@
     )(table, in_hbm(features))
 
 
-def agg_kernel(which, chunk, nfeat, src, counts, me, arrived_hbm, tiles_hbm, features, *refs):
-    outs, (arrived, tiles, own, sems) = refs[: len(which)], refs[len(which) :]
+def agg_kernel(which, chunk, nfeat, src, counts, me, arrived, tiles_hbm, features, *refs):
+    outs, (tiles, own, sems, *held) = refs[: len(which)], refs[len(which) :]
     group, per = tiles.shape[1:3]
-    moves = [pltpu.make_async_copy(arrived_hbm, arrived, sems.at[0])]
+    moves = []
+    if held:
+        moves.append(pltpu.make_async_copy(arrived, held[0], sems.at[2 * len(which)]))
+        arrived = held[0]
     firsts = [lax.rem(me[0] + k, nfeat) * group for k in which]
+    pairs = []
     for i, first in enumerate(firsts):
         rows = pl.ds(pl.multiple_of(first * BLK, BLK), group * BLK)
-        moves.append(
-            pltpu.make_async_copy(tiles_hbm.at[pl.ds(first, group)], tiles.at[i], sems.at[1 + 2 * i])
+        tiles_move = pltpu.make_async_copy(
+            tiles_hbm.at[pl.ds(first, group)], tiles.at[i], sems.at[2 * i]
         )
-        moves.append(
-            pltpu.make_async_copy(
-                features.at[rows, pl.ds(chunk * BLK, BLK)], own.at[i], sems.at[2 + 2 * i]
-            )
+        own_move = pltpu.make_async_copy(
+            features.at[rows, pl.ds(chunk * BLK, BLK)], own.at[i], sems.at[2 * i + 1]
         )
+        pairs.append((tiles_move, own_move))
+    for move in moves + [move for pair in pairs for move in pair]:
+        move.start()
     for move in moves:
-        move.start()
-    moves[0].wait()
+        move.wait()
     for i, (first, out) in enumerate(zip(firsts, outs)):
-        moves[1 + 2 * i].wait()
-        moves[2 + 2 * i].wait()
+        for move in pairs[i]:
+            move.wait()
         for b in range(group):
             rows, weights = [], []
             for t in range(per):
@@ -106,19 +111,21 @@
     group = nblocks // nfeat
     piece = jax.ShapeDtypeStruct((group * BLK, BLK), BF16)
     hbm = pl.BlockSpec(memory_space=pltpu.HBM)
+    vmem = pl.BlockSpec(memory_space=pltpu.VMEM)
+    load = chunk == 0
     return pl.pallas_call(
         functools.partial(agg_kernel, which, chunk, nfeat),
         grid_spec=pltpu.PrefetchScalarGridSpec(
             num_scalar_prefetch=3,
             grid=(),
-            in_specs=[pl.BlockSpec(memory_space=pl.ANY), hbm, hbm],
-            out_specs=[pl.BlockSpec(memory_space=pltpu.VMEM)] * len(which),
+            in_specs=[pl.BlockSpec(memory_space=pl.ANY) if load else vmem, hbm, hbm],
+            out_specs=[vmem] * len(which),
             scratch_shapes=[
-                pltpu.VMEM(arrived.shape, BF16),
                 pltpu.VMEM((len(which), group, per, BLK, BLK), BF16),
                 pltpu.VMEM((len(which), group * BLK, BLK), BF16),
                 pltpu.SemaphoreType.DMA((1 + 2 * len(which),)),
-            ],
+            ]
+            + [pltpu.VMEM(arrived.shape, BF16)] * load,
         ),
         out_shape=[piece] * len(which),
         compiler_params=params(14),
@@ -377,11 +384,15 @@
 
 
 def join_kernel(side, a, b, small, other, out):
-    rows, width = a.shape[2:]
+    width = a.shape[3]
+    more = out.shape[2] - a.shape[2]
     both = small[...] + other[...]
-    near = both.astype(BF16)
-    rest = both - near.astype(F32)
-    kept = jnp.where(side[0] == 0, near.astype(F32), rest)
+    near = both.astype(BF16).astype(F32)
+    rest = both - near
+    second = jnp.concatenate(
+        [near[more : more + 1], rest[more : more + 1], rest[: more - 2]], 0
+    )
+    kept = jnp.where(side[0] == 0, near[:more], second)
     for f in range(a.shape[1]):
         share = kept[:, f * width : (f + 1) * width]
         for p in range(a.shape[0]):
@@ -392,7 +403,7 @@
 def join(side, a, b, small, other):
     steps = 4
     lead, nfeat, rows, width = a.shape
-    more = small.shape[0]
+    more = small.shape[0] - 8
     spec = lambda n: pl.BlockSpec((lead // steps, nfeat, n, width), lambda g, s: (g, 0, 0, 0))
     whole = pl.BlockSpec(small.shape, lambda g, s: (0, 0))
     return pl.pallas_call(
@@ -446,26 +457,32 @@
     )(arrived)
 
 
-def finish_kernel(a, b, second, bias):
-    grades = second.shape[0]
-    second[...] = a[pl.ds(0, grades), :] + b[pl.ds(0, grades), :]
-    bias[...] = a[pl.ds(grades, 1), :] + b[pl.ds(grades, 1), :]
-
-
-def finish(a, b, grades):
+def finish_kernel(side, a, b, second, bias):
+    first = side[0] == 0
+    near = jnp.where(first, a[...], b[...])
+    rest = jnp.where(first, b[...], a[...])
+    second[...] = near + jnp.concatenate([rest[2:], jnp.zeros_like(rest[:2])], 0)
+    bias[...] = rest[:1] + rest[1:2]
+
+
+def finish(side, a, b):
     vmem = pl.BlockSpec(memory_space=pltpu.VMEM)
     return pl.pallas_call(
         finish_kernel,
-        in_specs=[vmem] * 2,
-        out_specs=[vmem] * 2,
+        grid_spec=pltpu.PrefetchScalarGridSpec(
+            num_scalar_prefetch=1,
+            grid=(),
+            in_specs=[vmem] * 2,
+            out_specs=[vmem] * 2,
+        ),
         out_shape=[
-            jax.ShapeDtypeStruct((grades, a.shape[1]), F32),
+            jax.ShapeDtypeStruct(a.shape, F32),
             jax.ShapeDtypeStruct((1, a.shape[1]), F32),
         ],
         compiler_params=params(2),
         cost_estimate=cost(0, MIB // 8),
         name="finish",
-    )(a, b)
+    )(side, a, b)
 
 
 def shards(features, pair_count, send_blocks, tile_src, tiles, labels, w_first, b_first, w_second):
@@ -492,8 +509,8 @@
         moved = lax.all_to_all(shaped, "nodes", split_axis=0, concat_axis=0, tiled=True)
         return moved.reshape(x.shape)
 
-    arrived = [swap(pick(features, table, 0))]
-    send = pick(features, table, 1)
+    arrived = [swap(pick(features, send_blocks, 0))]
+    send = pick(features, send_blocks, 1)
 
     flat = w_first.T
     weights = [ahead(flat, k) for k in (2, 1, 3)]
@@ -543,7 +560,7 @@
         tiled=True,
     )
     grad_first, rest = total(moved, hid // parts)
-    grad_second, grad_bias = finish(rest, nearby(rest), grades)
+    grad_second, grad_bias = finish(here, rest, nearby(rest))
     return grad_first.T, grad_bias.reshape(-1), grad_second.T
 
 

time: 192 us -> 194 us (1.010)
  local copies, waits for them, and re-layouts: 9.01 us -> 14.4 us
  blocking collectives: 60.3 us -> 57.8 us
    unnamed x33 -> x41, local copies, waits for them, and re-layouts: 4.74 us -> 9.46 us
    all_to_all x1, blocking collectives: 31.5 us -> 29 us  [shards(): lax.all_to_all(big.reshape(parts // 2 * nfeat, *big.shape[2:]), ('nodes',...]
  transfers between devices with their start and end apart: 20 -> 20, of which waited for: 9 -> 8; matrix products, arithmetic and copies ran while one was open for 6% -> 6% of each run, Pallas kernels for 9% -> 9%
where the time goes in v9:
time: 194 us; the launch traced here: 193 us
  blocking collectives  57.8 us (30%)
  Pallas kernels  40.7 us (21%)
  starting transfers between devices  40.7 us (21%)
  waiting for transfers between devices  35.3 us (18%)
  local copies, waits for them, and re-layouts  14.4 us (7%)
  other arithmetic  3.01 us (2%)
    all_to_all x1, blocking collectives, shards(): lax.all_to_all(big.reshape(parts // 2 * nfeat, *big.shape[2:]), ('nodes',...  29 us
    all_to_all x2, blocking collectives, swap(): lax.all_to_all(shaped, 'nodes', split_axis=0, concat_axis=0, tiled=True)  28.8 us
    ppermute x15, waiting for transfers between devices, ahead(): return lax.ppermute(x, 'feat', [(i, (i + k) % nfeat) for i in range(nfeat)])  24.9 us
    ppermute x15, starting transfers between devices, ahead(): return lax.ppermute(x, 'feat', [(i, (i + k) % nfeat) for i in range(nfeat)])  22 us
    all_to_all x2, starting transfers between devices, swap(): lax.all_to_all(shaped, 'nodes', split_axis=0, concat_axis=0, tiled=True)  16.3 us
    pallas_call x3, Pallas kernels, aggregate(): pl.pallas_call(functools.partial(agg_kernel, which, chunk, nfeat), grid_s...  11.6 us
    all_to_all x2, waiting for transfers between devices, swap(): lax.all_to_all(shaped, 'nodes', split_axis=0, concat_axis=0, tiled=True)  9.55 us
    unnamed x41, local copies, waits for them, and re-layouts  9.46 us
  transfers between devices with their start and end apart: 20, of which 8 were waited for; matrix products, arithmetic and copies ran while one was open for 6% of the time, Pallas kernels for 9%

profile of v9, /device:TPU:1, one launch (start us, length us, event | category | flops | bytes accessed | tf_op | source)
XLA Modules:
  0.0 192.9 jit_solution(17670854863370742171)
XLA Ops:
  0.6 1.4 copy.19.table
  2.0 3.5 %pick.3 = bf16[64,128,128]{2,1,0:T(8,128)(2,1)} custom-call(s32[1,32,2]{2,1,0:T(8,128)} %copy.19.table, bf16[4096,256]{1,0:T(8,128)(2,1)} %features.9), custom_call_target="tpu_custom_call" | custom-call | bytes 4194304 | tf_op jit(solution)/shard_map/pick/pallas_call | solution.py:53
  5.6 9.8 %all-to-all-start = ((bf16[32,2,128,128]{3,2,1,0:T(8,128)(2,1)}), bf16[32,2,128,128]{3,2,1,0:T(8,128)(2,1)}, u32[]{:S(2)}, u32[]{:S(2)}) async-start(bf16[32,2,128,128]{3,2,1,0:T(8,128)(2,1)} %bitcast.51), calls=%async_computation | async-start | bytes 4194304 | tf_op jit(solution)/shard_map/all_to_all | solution.py:509
  15.4 0.2 copy.20
  15.6 2.8 %collective-permute-start = (bf16[1024,256]{1,0:T(8,128)(2,1)S(1)}, bf16[1024,256]{1,0:T(8,128)(2,1)}, u32[]{:S(2)}, u32[]{:S(2)}) collective-permute-start(bf16[1024,256]{1,0:T(8,128)(2,1)S(1)} %bitcast.55), channel_id=1, source_target_pairs={{0,2},{1,3},{2,0},{3,1},{4,6},{5,7},{6,4},{7,5},{8,10},{9,11},{10,... | collective-permute-start | bytes 1572872 | tf_op jit(solution)/shard_map/ppermute | solution.py:502
  18.4 0.3 collective-permute-start.1
  18.7 2.4 %collective-permute-start.2 = (bf16[1024,256]{1,0:T(8,128)(2,1)S(1)}, bf16[1024,256]{1,0:T(8,128)(2,1)}, u32[]{:S(2)}, u32[]{:S(2)}) collective-permute-start(bf16[1024,256]{1,0:T(8,128)(2,1)S(1)} %bitcast.57), channel_id=1, source_target_pairs={{0,3},{1,0},{2,1},{3,2},{4,7},{5,4},{6,5},{7,6},{8,11},{9,8},{10,9... | collective-permute-start | bytes 1572872 | tf_op jit(solution)/shard_map/ppermute | solution.py:502
  21.1 3.5 %pick.2 = bf16[64,128,128]{2,1,0:T(8,128)(2,1)} custom-call(s32[1,32,2]{2,1,0:T(8,128)} %copy.19.table, bf16[4096,256]{1,0:T(8,128)(2,1)} %features.9), custom_call_target="tpu_custom_call" | custom-call | bytes 4194304 | tf_op jit(solution)/shard_map/pick/pallas_call | solution.py:53
  24.6 5.9 %collective-permute-done = bf16[1024,256]{1,0:T(8,128)(2,1)} collective-permute-done((bf16[1024,256]{1,0:T(8,128)(2,1)S(1)}, bf16[1024,256]{1,0:T(8,128)(2,1)}, u32[]{:S(2)}, u32[]{:S(2)}) %collective-permute-start) | collective-permute-done | bytes 524320 | tf_op jit(solution)/shard_map/ppermute | solution.py:502
  30.5 11.8 %collective-permute-done.1 = bf16[1024,256]{1,0:T(8,128)(2,1)} collective-permute-done((bf16[1024,256]{1,0:T(8,128)(2,1)S(1)}, bf16[1024,256]{1,0:T(8,128)(2,1)}, u32[]{:S(2)}, u32[]{:S(2)}) %collective-permute-start.1) | collective-permute-done | bytes 524320 | tf_op jit(solution)/shard_map/ppermute | solution.py:502
  42.4 1.3 all-to-all-done
  43.7 6.5 %all-to-all-start.1 = ((bf16[32,2,128,128]{3,2,1,0:T(8,128)(2,1)}), bf16[32,2,128,128]{3,2,1,0:T(8,128)(2,1)S(1)}, u32[]{:S(2)}, u32[]{:S(2)}) async-start(bf16[32,2,128,128]{3,2,1,0:T(8,128)(2,1)} %bitcast.50), calls=%async_computation.1 | async-start | bytes 4194304 | tf_op jit(solution)/shard_map/all_to_all | solution.py:509
  50.5 5.1 %aggregate.3 = (bf16[1024,128]{1,0:T(8,128)(2,1)S(1)}, bf16[1024,128]{1,0:T(8,128)(2,1)}, bf16[1024,128]{1,0:T(8,128)(2,1)}, bf16[1024,128]{1,0:T(8,128)(2,1)S(1)}) custom-call(s32[128]{0:T(128)S(1)} %reshape.64.src, s32[32]{0:T(128)S(1)} %bitcast.46, s32[1]{0:T(128)} %bitcast.6.me, bf16[64,128,128]{2,1,0:T(8,128)(2,1)} %bitcast.3.arrived, ...), custom_call_target="tpu_custom_call" | custom-call | flops 536870912 | bytes 8388608 | tf_op jit(solution)/shard_map/aggregate/pallas_call | solution.py:116
  55.6 2.4 %collective-permute-start.9 = (f32[24,256]{1,0:T(8,128)S(1)}, f32[24,256]{1,0:T(8,128)S(1)}, u32[]{:S(2)}, u32[]{:S(2)}) collective-permute-start(f32[24,256]{1,0:T(8,128)S(1)} %pad_maximum_fusion.1), channel_id=1, source_target_pairs={{0,3},{1,0},{2,1},{3,2},{4,7},{5,4},{6,5},{7,6},{8,11},{9,8},{10,9... | collective-permute-start | bytes 73736 | tf_op jit(solution)/shard_map/ppermute | solution.py:502
  58.0 0.6 collective-permute-start.10
  58.6 2.3 %collective-permute-start.3 = (bf16[1024,128]{1,0:T(8,128)(2,1)S(1)}, bf16[1024,128]{1,0:T(8,128)(2,1)S(1)}, u32[]{:S(2)}, u32[]{:S(2)}) collective-permute-start(bf16[1024,128]{1,0:T(8,128)(2,1)S(1)} %get-tuple-element.41), channel_id=1, source_target_pairs={{0,2},{1,3},{2,0},{3,1},{4,6},{5,7},{6,4},{7,5},{8,10},{9,11},{10,... | collective-permute-start | bytes 786440 | tf_op jit(solution)/shard_map/ppermute | solution.py:502
  60.9 0.9 collective-permute-start.4
  61.8 3.0 %pad_maximum_fusion.refs_8_ = bf16[1024,1024]{1,0:T(8,128)(2,1)} fusion(bf16[1024,256]{1,0:T(8,128)(2,1)} %collective-permute-done.2, bf16[1024,256]{1,0:T(8,128)(2,1)} %collective-permute-done.1, bf16[1024,256]{1,0:T(8,128)(2,1)} %collective-permute-done, bf16[1024,256]{1,0:T(8,128)(2,1)S(1)} %bitcast.58), kind=kLoop, calls=%fused_computation | loop fusion | flops 8388608 | bytes 4194304 | tf_op jit(solution)/shard_map/concatenate | solution.py:530
  64.8 1.8 collective-permute-start.5
  66.6 0.6 bitcast_dynamic-update-slice_fusion.5
  67.2 0.6 bitcast_dynamic-update-slice_fusion.3
  67.8 0.6 bitcast_dynamic-update-slice_fusion.1
  68.5 0.6 bitcast_dynamic-update-slice_fusion
  69.1 0.6 bitcast_dynamic-update-slice_fusion.6
  69.7 0.6 bitcast_dynamic-update-slice_fusion.4
  70.3 8.2 %all-to-all-done.1 = bf16[32,2,128,128]{3,2,1,0:T(8,128)(2,1)S(1)} async-done(((bf16[32,2,128,128]{3,2,1,0:T(8,128)(2,1)}), bf16[32,2,128,128]{3,2,1,0:T(8,128)(2,1)S(1)}, u32[]{:S(2)}, u32[]{:S(2)}) %all-to-all-start.1) | async-done | bytes 2097184 | tf_op jit(solution)/shard_map/all_to_all | solution.py:509
  78.5 4.0 %aggregate.5 = (bf16[1024,128]{1,0:T(8,128)(2,1)}, bf16[1024,128]{1,0:T(8,128)(2,1)}, bf16[1024,128]{1,0:T(8,128)(2,1)}) custom-call(s32[128]{0:T(128)S(1)} %reshape.64.src, s32[32]{0:T(128)S(1)} %bitcast.47, s32[1]{0:T(128)} %bitcast.6.me, bf16[64,128,128]{2,1,0:T(8,128)(2,1)S(1)} %bitcast.37, bf16[32,4,128,128]{3,2,1,0:T(8,128)(2,1)} %tiles.1, ...), custom_call_target="tpu_custom_call" | custom-call | flops 402653184 | bytes 8388608 | tf_op jit(solution)/shard_map/aggregate/pallas_call | solution.py:116
  82.5 1.8 collective-permute-start.6
  84.3 1.2 collective-permute-start.7
  85.5 1.5 collective-permute-start.8
  87.0 0.6 bitcast_dynamic-update-slice_fusion.2
  87.6 0.8 constant_dynamic-slice_fusion
  88.4 1.0 copy.25.refs_9_
  89.4 0.8 fusion
  90.3 0.2 copy.24
  90.5 0.1 copy.26.refs_10_
  90.6 2.5 %aggregate.4.refs_4_ = bf16[1024,128]{1,0:T(8,128)(2,1)S(1)} custom-call(s32[128]{0:T(128)S(1)} %reshape.64.src, s32[32]{0:T(128)S(1)} %bitcast.48, s32[1]{0:T(128)} %bitcast.6.me, bf16[64,128,128]{2,1,0:T(8,128)(2,1)S(1)} %bitcast.38, bf16[32,4,128,128]{3,2,1,0:T(8,128)(2,1)} %tiles.1, bf16[4096,256]{1,0:T(8,128)(2,1)} %features.9), custom_call_target="tpu_custom_call" | custom-call | flops 134217728 | bytes 8388608 | tf_op jit(solution)/shard_map/aggregate/pallas_call | solution.py:116
  93.2 5.1 %collective-permute-done.7.refs_6_ = bf16[1024,128]{1,0:T(8,128)(2,1)} collective-permute-done((bf16[1024,128]{1,0:T(8,128)(2,1)}, bf16[1024,128]{1,0:T(8,128)(2,1)}, u32[]{:S(2)}, u32[]{:S(2)}) %collective-permute-start.7) | collective-permute-done | bytes 262176 | tf_op jit(solution)/shard_map/ppermute | solution.py:502
  98.2 4.0 %dense.1 = (bf16[1024,1024]{1,0:T(8,128)(2,1)S(1)}, f32[8,16,128]{2,1,0:T(8,128)S(1)}) custom-call(bf16[1024,128]{1,0:T(8,128)(2,1)S(1)} %get-tuple-element.40.refs_0_, bf16[1024,128]{1,0:T(8,128)(2,1)S(1)} %collective-permute-done.3.refs_1_, bf16[1024,128]{1,0:T(8,128)(2,1)S(1)} %collective-permute-done.4.refs_2_, ...), custom_call_target="tpu_custom_call" | custom-call | flops 2147483648 | bytes 7340032 | tf_op jit(solution)/shard_map/dense/pallas_call | solution.py:153
  102.2 1.2 collective-permute-start.12
  103.5 2.4 %collective-permute-start.13 = (f32[8,16,128]{2,1,0:T(8,128)S(1)}, f32[8,16,128]{2,1,0:T(8,128)}, u32[]{:S(2)}, u32[]{:S(2)}) collective-permute-start(f32[8,16,128]{2,1,0:T(8,128)S(1)} %get-tuple-element.52.p0), channel_id=1, source_target_pairs={{0,2},{1,3},{2,0},{3,1},{4,6},{5,7},{6,4},{7,5},{8,10},{9,11},{10,... | collective-permute-start | bytes 196616 | tf_op jit(solution)/shard_map/ppermute | solution.py:502
  105.8 0.3 collective-permute-start.14
  106.1 1.3 reshape.67.table
  107.4 1.3 collective-permute-done.13.p2
  108.7 0.8 collective-permute-done.14.p3
  109.5 0.7 copy-done.8
  110.2 1.5 spread.1
  111.7 16.4 %all_to_all.25 = f32[32,2,16,128]{3,2,1,0:T(8,128)S(1)} all-to-all(f32[32,2,16,128]{3,2,1,0:T(8,128)S(1)} %bitcast.43), channel_id=1, replica_groups=mesh['nodes'=32,'feat'=4] {'nodes'}, dimensions={0} | all-to-all | bytes 1048576 | tf_op jit(solution)/shard_map/all_to_all | solution.py:509
  128.1 2.2 %copy-done = bf16[32,4,128,128]{3,2,1,0:T(8,128)(2,1)S(1)} copy-done((bf16[32,4,128,128]{3,2,1,0:T(8,128)(2,1)S(1)}, bf16[32,4,128,128]{3,2,1,0:T(8,128)(2,1)}, u32[]{:S(2)}) %copy-start) | copy-done | bytes 4194328
  130.3 0.6 copy-done.5
  130.9 0.7 copy-done.7
  131.6 3.9 %logits.1 = (f32[8,16,128]{2,1,0:T(8,128)S(1)}, bf16[64,16,128]{2,1,0:T(8,128)(2,1)S(1)}) custom-call(s32[128]{0:T(128)S(1)} %copy-done.5, s32[32]{0:T(128)S(1)} %bitcast.49, s32[1]{0:T(128)} %bitcast.6.me, f32[64,16,128]{2,1,0:T(8,128)S(1)} %bitcast.41, f32[32,16,128]{2,1,0:T(8,128)S(1)} %get-tuple-element.54.own, s32[32,1,128]{2,1,0:T(1,128)S(1)} %bitcast.45, ...), custom_call_target="tpu_custom_call" | custom-call | flops 268435456 | bytes 6291456 | tf_op jit(solution)/shard_map/logits/pallas_call | solution.py:261
  135.5 12.4 %all_to_all.26 = bf16[32,2,16,128]{3,2,1,0:T(8,128)(2,1)S(1)} all-to-all(bf16[32,2,16,128]{3,2,1,0:T(8,128)(2,1)S(1)} %bitcast.44), channel_id=1, replica_groups=mesh['nodes'=32,'feat'=4] {'nodes'}, dimensions={0} | all-to-all | bytes 524288 | tf_op jit(solution)/shard_map/all_to_all | solution.py:509
  147.9 3.7 %small_gradients.1 = (bf16[1024,1024]{1,0:T(8,128)(2,1)}, f32[24,1024]{1,0:T(8,128)S(1)}) custom-call(s32[64]{0:T(128)S(1)} %copy-done.9, s32[1]{0:T(128)} %bitcast.6.me, bf16[64,16,128]{2,1,0:T(8,128)(2,1)S(1)} %bitcast.42, f32[8,16,128]{2,1,0:T(8,128)S(1)} %get-tuple-element.56.dlog, bf16[1024,1024]{1,0:T(8,128)(2,1)S(1)} %get-tuple-element.57.hidden, ...), custom_call_target="tpu_custom_call" | custom-call | flops 536870912 | bytes 4194304 | tf_op jit(solution)/shard_map/small_gradients/pallas_call | solution.py:320
  151.6 2.8 %big_gradient.3 = bf16[16,4,32,256]{3,2,1,0:T(8,128)(2,1)S(1)} custom-call(s32[1]{0:T(128)} %bitcast.6.me, s32[1]{0:T(128)S(6)} %sub.6.side, bf16[16,2,32,1024]{3,2,1,0:T(8,128)(2,1)} %bitcast.52, bf16[1024,128]{1,0:T(8,128)(2,1)S(1)} %get-tuple-element.40.refs_0_, bf16[1024,128]{1,0:T(8,128)(2,1)S(1)} %collective-permute-done.3.refs_1_, ...), custom_call_target="tpu_custom_call" | custom-call | flops 1073741824 | bytes 4194304 | tf_op jit(solution)/shard_map/big_gradient/pallas_call | solution.py:366
  154.4 0.2 collective-permute-start.15
  154.6 0.3 collective-permute-start.16
  155.0 2.8 %big_gradient.2.a = bf16[16,4,32,256]{3,2,1,0:T(8,128)(2,1)S(1)} custom-call(s32[1]{0:T(128)} %bitcast.6.me, s32[1]{0:T(128)} %bitcast.4.side, bf16[16,2,32,1024]{3,2,1,0:T(8,128)(2,1)} %bitcast.53, bf16[1024,128]{1,0:T(8,128)(2,1)S(1)} %get-tuple-element.40.refs_0_, bf16[1024,128]{1,0:T(8,128)(2,1)S(1)} %collective-permute-done.3.refs_1_, ...), custom_call_target="tpu_custom_call" | custom-call | flops 1073741824 | bytes 4194304 | tf_op jit(solution)/shard_map/big_gradient/pallas_call | solution.py:366
  157.8 1.9 join.1
  159.6 29.0 %all_to_all.27.arrived = bf16[64,48,256]{2,1,0:T(8,128)(2,1)S(1)} all-to-all(bf16[64,48,256]{2,1,0:T(8,128)(2,1)} %bitcast.54), channel_id=1, replica_groups={{0,1,2,3,8,9,10,11,16,17,18,19,24,25,26,27,32,33,34,35,40,41,42,43,48,4..., dimensions={0} | all-to-all | bytes 3145728 | tf_op jit(solution)/shard_map/all_to_all | solution.py:552
  188.6 1.0 total.1
  189.6 1.9 collective-permute-start.17
  191.5 0.8 collective-permute-done.17.b
  192.3 0.6 finish.1
  (46 shorter events, 0.4 us)
Async XLA Ops:
  5.5 9.8 %copy-start.12 = (bf16[256,1024]{1,0:T(8,128)(2,1)S(1)}, bf16[256,1024]{1,0:T(8,128)(2,1)}, u32[]{:S(2)}) copy-start(bf16[256,1024]{1,0:T(8,128)(2,1)} %param.15) | copy-start | bytes 1572868
  5.6 38.2 %all-to-all-start = ((bf16[32,2,128,128]{3,2,1,0:T(8,128)(2,1)}), bf16[32,2,128,128]{3,2,1,0:T(8,128)(2,1)}, u32[]{:S(2)}, u32[]{:S(2)}) async-start(bf16[32,2,128,128]{3,2,1,0:T(8,128)(2,1)} %bitcast.51), calls=%async_computation | async-start | bytes 4194304 | tf_op jit(solution)/shard_map/all_to_all | solution.py:509
  15.6 9.0 %copy-start.10 = (bf16[256,1024]{0,1:T(8,128)(2,1)}, bf16[256,1024]{0,1:T(8,128)(2,1)S(1)}, u32[]{:S(2)}) copy-start(bf16[256,1024]{0,1:T(8,128)(2,1)S(1)} %copy.20) | copy-start | bytes 1572868
  15.6 14.9 %collective-permute-start = (bf16[1024,256]{1,0:T(8,128)(2,1)S(1)}, bf16[1024,256]{1,0:T(8,128)(2,1)}, u32[]{:S(2)}, u32[]{:S(2)}) collective-permute-start(bf16[1024,256]{1,0:T(8,128)(2,1)S(1)} %bitcast.55), channel_id=1, source_target_pairs={{0,2},{1,3},{2,0},{3,1},{4,6},{5,7},{6,4},{7,5},{8,10},{9,11},{10,... | collective-permute-start | bytes 1572872 | tf_op jit(solution)/shard_map/ppermute | solution.py:502
  18.4 23.9 %collective-permute-start.1 = (bf16[1024,256]{1,0:T(8,128)(2,1)S(1)}, bf16[1024,256]{1,0:T(8,128)(2,1)}, u32[]{:S(2)}, u32[]{:S(2)}) collective-permute-start(bf16[1024,256]{1,0:T(8,128)(2,1)S(1)} %bitcast.56), channel_id=1, source_target_pairs={{0,1},{1,2},{2,3},{3,0},{4,5},{5,6},{6,7},{7,4},{8,9},{9,10},{10,1... | collective-permute-start | bytes 1572872 | tf_op jit(solution)/shard_map/ppermute | solution.py:502
  18.7 23.6 %collective-permute-start.2 = (bf16[1024,256]{1,0:T(8,128)(2,1)S(1)}, bf16[1024,256]{1,0:T(8,128)(2,1)}, u32[]{:S(2)}, u32[]{:S(2)}) collective-permute-start(bf16[1024,256]{1,0:T(8,128)(2,1)S(1)} %bitcast.57), channel_id=1, source_target_pairs={{0,3},{1,0},{2,1},{3,2},{4,7},{5,4},{6,5},{7,6},{8,11},{9,8},{10,9... | collective-permute-start | bytes 1572872 | tf_op jit(solution)/shard_map/ppermute | solution.py:502
  43.7 6.5 %copy-start.14 = (s32[32,4]{0,1:T(4,128)S(1)}, s32[32,4]{0,1:T(4,128)}, u32[]{:S(2)}) copy-start(s32[32,4]{0,1:T(4,128)} %param.12) | copy-start | bytes 1540
  43.7 6.7 %copy-start.13 = (bf16[256,16]{0,1:T(8,128)(2,1)S(1)}, bf16[256,16]{0,1:T(8,128)(2,1)}, u32[]{:S(2)}) copy-start(bf16[256,16]{0,1:T(8,128)(2,1)} %param.17) | copy-start | bytes 24580
  43.7 6.7 %copy-start.15 = (f32[256]{0:T(256)S(1)}, f32[256]{0:T(256)}, u32[]{:S(2)}) copy-start(f32[256]{0:T(256)} %param.16) | copy-start | bytes 3076
  43.7 6.8 %copy-start.6 = (s32[1,32]{1,0:T(1,128)S(1)}, s32[1,32]{1,0:T(1,128)}, u32[]{:S(2)}) copy-start(s32[1,32]{1,0:T(1,128)} %param.10) | copy-start | bytes 388
  43.7 34.8 %all-to-all-start.1 = ((bf16[32,2,128,128]{3,2,1,0:T(8,128)(2,1)}), bf16[32,2,128,128]{3,2,1,0:T(8,128)(2,1)S(1)}, u32[]{:S(2)}, u32[]{:S(2)}) async-start(bf16[32,2,128,128]{3,2,1,0:T(8,128)(2,1)} %bitcast.50), calls=%async_computation.1 | async-start | bytes 4194304 | tf_op jit(solution)/shard_map/all_to_all | solution.py:509
  50.4 40.2 %copy-start.4 = (s32[128]{0:T(128)}, s32[128]{0:T(128)S(1)}, u32[]{:S(2)}) copy-start(s32[128]{0:T(128)S(1)} %reshape.64.src) | copy-start | bytes 1540
  50.5 11.4 %copy-start.11 = (bf16[256,1024]{0,1:T(8,128)(2,1)S(1)}, bf16[256,1024]{0,1:T(8,128)(2,1)}, u32[]{:S(2)}) copy-start(bf16[256,1024]{0,1:T(8,128)(2,1)} %copy-done.10) | copy-start | bytes 1572868
  55.6 9.3 %collective-permute-start.9 = (f32[24,256]{1,0:T(8,128)S(1)}, f32[24,256]{1,0:T(8,128)S(1)}, u32[]{:S(2)}, u32[]{:S(2)}) collective-permute-start(f32[24,256]{1,0:T(8,128)S(1)} %pad_maximum_fusion.1), channel_id=1, source_target_pairs={{0,3},{1,0},{2,1},{3,2},{4,7},{5,4},{6,5},{7,6},{8,11},{9,8},{10,9... | collective-permute-start | bytes 73736 | tf_op jit(solution)/shard_map/ppermute | solution.py:502
  58.0 9.3 %collective-permute-start.10 = (f32[24,256]{1,0:T(8,128)S(1)}, f32[24,256]{1,0:T(8,128)S(1)}, u32[]{:S(2)}, u32[]{:S(2)}) collective-permute-start(f32[24,256]{1,0:T(8,128)S(1)} %pad_maximum_fusion.1), channel_id=1, source_target_pairs={{0,2},{1,3},{2,0},{3,1},{4,6},{5,7},{6,4},{7,5},{8,10},{9,11},{10,... | collective-permute-start | bytes 73736 | tf_op jit(solution)/shard_map/ppermute | solution.py:502
  58.6 9.3 %collective-permute-start.11 = (f32[24,256]{1,0:T(8,128)S(1)}, f32[24,256]{1,0:T(8,128)S(1)}, u32[]{:S(2)}, u32[]{:S(2)}) collective-permute-start(f32[24,256]{1,0:T(8,128)S(1)} %pad_maximum_fusion.1), channel_id=1, source_target_pairs={{0,1},{1,2},{2,3},{3,0},{4,5},{5,6},{6,7},{7,4},{8,9},{9,10},{10,1... | collective-permute-start | bytes 73736 | tf_op jit(solution)/shard_map/ppermute | solution.py:502
  58.6 26.9 %collective-permute-start.3 = (bf16[1024,128]{1,0:T(8,128)(2,1)S(1)}, bf16[1024,128]{1,0:T(8,128)(2,1)S(1)}, u32[]{:S(2)}, u32[]{:S(2)}) collective-permute-start(bf16[1024,128]{1,0:T(8,128)(2,1)S(1)} %get-tuple-element.41), channel_id=1, source_target_pairs={{0,2},{1,3},{2,0},{3,1},{4,6},{5,7},{6,4},{7,5},{8,10},{9,11},{10,... | collective-permute-start | bytes 786440 | tf_op jit(solution)/shard_map/ppermute | solution.py:502
  60.9 32.2 %collective-permute-start.4 = (bf16[1024,128]{1,0:T(8,128)(2,1)}, bf16[1024,128]{1,0:T(8,128)(2,1)S(1)}, u32[]{:S(2)}, u32[]{:S(2)}) collective-permute-start(bf16[1024,128]{1,0:T(8,128)(2,1)} %get-tuple-element.42), channel_id=1, source_target_pairs={{0,1},{1,2},{2,3},{3,0},{4,5},{5,6},{6,7},{7,4},{8,9},{9,10},{10,1... | collective-permute-start | bytes 786440 | tf_op jit(solution)/shard_map/ppermute | solution.py:502
  64.8 28.3 %collective-permute-start.5 = (bf16[1024,128]{1,0:T(8,128)(2,1)}, bf16[1024,128]{1,0:T(8,128)(2,1)}, u32[]{:S(2)}, u32[]{:S(2)}) collective-permute-start(bf16[1024,128]{1,0:T(8,128)(2,1)} %get-tuple-element.43), channel_id=1, source_target_pairs={{0,3},{1,0},{2,1},{3,2},{4,7},{5,4},{6,5},{7,6},{8,11},{9,8},{10,9... | collective-permute-start | bytes 786440 | tf_op jit(solution)/shard_map/ppermute | solution.py:502
  82.5 10.7 %collective-permute-start.6 = (bf16[1024,128]{1,0:T(8,128)(2,1)}, bf16[1024,128]{1,0:T(8,128)(2,1)}, u32[]{:S(2)}, u32[]{:S(2)}) collective-permute-start(bf16[1024,128]{1,0:T(8,128)(2,1)} %get-tuple-element.45), channel_id=1, source_target_pairs={{0,2},{1,3},{2,0},{3,1},{4,6},{5,7},{6,4},{7,5},{8,10},{9,11},{10,... | collective-permute-start | bytes 786440 | tf_op jit(solution)/shard_map/ppermute | solution.py:502
  84.3 13.9 %collective-permute-start.7 = (bf16[1024,128]{1,0:T(8,128)(2,1)}, bf16[1024,128]{1,0:T(8,128)(2,1)}, u32[]{:S(2)}, u32[]{:S(2)}) collective-permute-start(bf16[1024,128]{1,0:T(8,128)(2,1)} %get-tuple-element.46), channel_id=1, source_target_pairs={{0,1},{1,2},{2,3},{3,0},{4,5},{5,6},{6,7},{7,4},{8,9},{9,10},{10,1... | collective-permute-start | bytes 786440 | tf_op jit(solution)/shard_map/ppermute | solution.py:502
  85.5 12.7 %collective-permute-start.8 = (bf16[1024,128]{1,0:T(8,128)(2,1)}, bf16[1024,128]{1,0:T(8,128)(2,1)}, u32[]{:S(2)}, u32[]{:S(2)}) collective-permute-start(bf16[1024,128]{1,0:T(8,128)(2,1)} %get-tuple-element.47), channel_id=1, source_target_pairs={{0,3},{1,0},{2,1},{3,2},{4,7},{5,4},{6,5},{7,6},{8,11},{9,8},{10,9... | collective-permute-start | bytes 786440 | tf_op jit(solution)/shard_map/ppermute | solution.py:502
  90.6 7.7 %copy-start.1 = (bf16[1024,1024]{1,0:T(8,128)(2,1)S(1)}, bf16[1024,1024]{1,0:T(8,128)(2,1)}, u32[]{:S(2)}) copy-start(bf16[1024,1024]{1,0:T(8,128)(2,1)} %pad_maximum_fusion.refs_8_) | copy-start | bytes 6291460
  90.6 7.7 %copy-start.2 = (f32[1024,1]{1,0:T(8,128)S(1)}, f32[1024,1]{1,0:T(8,128)}, u32[]{:S(2)}) copy-start(f32[1024,1]{1,0:T(8,128)} %copy.25.refs_9_) | copy-start | bytes 12292
  93.1 35.0 %copy-start.3 = (s32[4096]{0:T(1024)S(1)}, s32[4096]{0:T(1024)}, u32[]{:S(2)}) copy-start(s32[4096]{0:T(1024)} %param.14) | copy-start | bytes 49156
  102.2 5.2 %collective-permute-start.12 = (f32[8,16,128]{2,1,0:T(8,128)S(1)}, f32[8,16,128]{2,1,0:T(8,128)S(1)}, u32[]{:S(2)}, u32[]{:S(2)}) collective-permute-start(f32[8,16,128]{2,1,0:T(8,128)S(1)} %get-tuple-element.52.p0), channel_id=1, source_target_pairs={{0,1},{1,2},{2,3},{3,0},{4,5},{5,6},{6,7},{7,4},{8,9},{9,10},{10,1... | collective-permute-start | bytes 196616 | tf_op jit(solution)/shard_map/ppermute | solution.py:502
  103.5 5.3 %collective-permute-start.13 = (f32[8,16,128]{2,1,0:T(8,128)S(1)}, f32[8,16,128]{2,1,0:T(8,128)}, u32[]{:S(2)}, u32[]{:S(2)}) collective-permute-start(f32[8,16,128]{2,1,0:T(8,128)S(1)} %get-tuple-element.52.p0), channel_id=1, source_target_pairs={{0,2},{1,3},{2,0},{3,1},{4,6},{5,7},{6,4},{7,5},{8,10},{9,11},{10,... | collective-permute-start | bytes 196616 | tf_op jit(solution)/shard_map/ppermute | solution.py:502
  105.8 3.7 %collective-permute-start.14 = (f32[8,16,128]{2,1,0:T(8,128)S(1)}, f32[8,16,128]{2,1,0:T(8,128)}, u32[]{:S(2)}, u32[]{:S(2)}) collective-permute-start(f32[8,16,128]{2,1,0:T(8,128)S(1)} %get-tuple-element.52.p0), channel_id=1, source_target_pairs={{0,3},{1,0},{2,1},{3,2},{4,7},{5,4},{6,5},{7,6},{8,11},{9,8},{10,9... | collective-permute-start | bytes 196616 | tf_op jit(solution)/shard_map/ppermute | solution.py:502
  109.5 0.7 copy-start.8
  128.1 2.2 %copy-start = (bf16[32,4,128,128]{3,2,1,0:T(8,128)(2,1)S(1)}, bf16[32,4,128,128]{3,2,1,0:T(8,128)(2,1)}, u32[]{:S(2)}) copy-start(bf16[32,4,128,128]{3,2,1,0:T(8,128)(2,1)} %tiles.1) | copy-start | bytes 12582916
  130.3 0.6 copy-start.5
  130.9 0.7 copy-start.7
  131.6 16.3 %copy-start.9 = (s32[64]{0:T(128)S(1)}, s32[64]{0:T(128)}, u32[]{:S(2)}) copy-start(s32[64]{0:T(128)} %reshape.67.table) | copy-start | bytes 772
  154.4 3.4 %collective-permute-start.15 = (bf16[16,4,32,256]{3,2,1,0:T(8,128)(2,1)S(1)}, bf16[16,4,32,256]{3,2,1,0:T(8,128)(2,1)S(1)}, u32[]{:S(2)}, u32[]{:S(2)}) collective-permute-start(bf16[16,4,32,256]{3,2,1,0:T(8,128)(2,1)S(1)} %big_gradient.3), channel_id=1, source_target_pairs={{0,4},{4,0},{8,12},{12,8},{16,20},{20,16},{24,28},{28,24},{32,36},... | collective-permute-start | bytes 3145736 | tf_op jit(solution)/shard_map/ppermute | solution.py:505
  154.6 3.1 %collective-permute-start.16 = (f32[24,1024]{1,0:T(8,128)S(1)}, f32[24,1024]{1,0:T(8,128)S(1)}, u32[]{:S(2)}, u32[]{:S(2)}) collective-permute-start(f32[24,1024]{1,0:T(8,128)S(1)} %get-tuple-element.60.small), channel_id=1, source_target_pairs={{0,4},{4,0},{8,12},{12,8},{16,20},{20,16},{24,28},{28,24},{32,36},... | collective-permute-start | bytes 294920 | tf_op jit(solution)/shard_map/ppermute | solution.py:505
  189.6 2.7 %collective-permute-start.17 = (f32[16,256]{1,0:T(8,128)S(1)}, f32[16,256]{1,0:T(8,128)S(1)}, u32[]{:S(2)}, u32[]{:S(2)}) collective-permute-start(f32[16,256]{1,0:T(8,128)S(1)} %get-tuple-element.62.a), channel_id=1, source_target_pairs={{0,4},{4,0},{8,12},{12,8},{16,20},{20,16},{24,28},{28,24},{32,36},... | collective-permute-start | bytes 49160 | tf_op jit(solution)/shard_map/ppermute | solution.py:505

commit v10 on v9

--- a/solution.py
+++ b/solution.py
@@ -41,15 +41,14 @@
 
     @pl.loop(0, slots, unroll=8)
     def _(k):
-        block = table[0, lax.div(k, 2), lax.rem(k, 2)]
-        rows = pl.ds(pl.multiple_of(block * BLK, BLK), BLK)
+        rows = pl.ds(pl.multiple_of(table[k] * BLK, BLK), BLK)
         pltpu.make_async_copy(held.at[rows], out.at[k], sems.at[1]).start()
 
     pltpu.make_async_copy(out, out, sems.at[1]).wait()
 
 
 def pick(features, table, chunk):
-    slots = table.size
+    slots = table.shape[0]
     return pl.pallas_call(
         functools.partial(pick_kernel, chunk),
         grid_spec=pltpu.PrefetchScalarGridSpec(
@@ -509,8 +508,8 @@
         moved = lax.all_to_all(shaped, "nodes", split_axis=0, concat_axis=0, tiled=True)
         return moved.reshape(x.shape)
 
-    arrived = [swap(pick(features, send_blocks, 0))]
-    send = pick(features, send_blocks, 1)
+    arrived = [swap(pick(features, table, 0))]
+    send = pick(features, table, 1)
 
     flat = w_first.T
     weights = [ahead(flat, k) for k in (2, 1, 3)]

time: 194 us -> 188 us (0.969)
  local copies, waits for them, and re-layouts: 14.4 us -> 9.01 us
    unnamed x41 -> x33, local copies, waits for them, and re-layouts: 9.46 us -> 4.74 us
  transfers between devices with their start and end apart: 20 -> 20, of which waited for: 8 -> 9; matrix products, arithmetic and copies ran while one was open for 6% -> 6% of each run, Pallas kernels for 9% -> 9%
where the time goes in v10:
time: 188 us
  blocking collectives  57.4 us (31%)
  starting transfers between devices  40.9 us (22%)
  Pallas kernels  39.5 us (21%)
  waiting for transfers between devices  36.8 us (20%)
  local copies, waits for them, and re-layouts  9.01 us (5%)
  other arithmetic  3.01 us (2%)
    all_to_all x2, blocking collectives, swap(): lax.all_to_all(shaped, 'nodes', split_axis=0, concat_axis=0, tiled=True)  28.7 us
    all_to_all x1, blocking collectives, shards(): lax.all_to_all(big.reshape(parts // 2 * nfeat, *big.shape[2:]), ('nodes',...  28.7 us
    ppermute x15, waiting for transfers between devices, ahead(): return lax.ppermute(x, 'feat', [(i, (i + k) % nfeat) for i in range(nfeat)])  26.4 us
    ppermute x15, starting transfers between devices, ahead(): return lax.ppermute(x, 'feat', [(i, (i + k) % nfeat) for i in range(nfeat)])  22 us
    all_to_all x2, starting transfers between devices, swap(): lax.all_to_all(shaped, 'nodes', split_axis=0, concat_axis=0, tiled=True)  16.3 us
    pallas_call x3, Pallas kernels, aggregate(): pl.pallas_call(functools.partial(agg_kernel, which, chunk, nfeat), grid_s...  11.7 us
    all_to_all x2, waiting for transfers between devices, swap(): lax.all_to_all(shaped, 'nodes', split_axis=0, concat_axis=0, tiled=True)  9.51 us
    pallas_call x2, Pallas kernels, pick(): pl.pallas_call(functools.partial(pick_kernel, chunk), grid_spec=pltpu.Pre...  6.52 us
  transfers between devices with their start and end apart: 20, of which 9 were waited for; matrix products, arithmetic and copies ran while one was open for 6% of the time, Pallas kernels for 9%

profile of v10, /device:TPU:1, one launch (start us, length us, event | category | flops | bytes accessed | tf_op | source)
XLA Modules:
  0.0 187.5 jit_solution(6322507815758011559)
XLA Ops:
  0.6 0.8 copy.17
  1.4 0.6 reshape.61.table
  2.0 3.3 %pick.3 = bf16[64,128,128]{2,1,0:T(8,128)(2,1)} custom-call(s32[64]{0:T(128)} %reshape.61.table, bf16[4096,256]{1,0:T(8,128)(2,1)} %features.9), custom_call_target="tpu_custom_call" | custom-call | bytes 4194304 | tf_op jit(solution)/shard_map/pick/pallas_call | solution.py:52
  5.3 9.8 %all-to-all-start = ((bf16[32,2,128,128]{3,2,1,0:T(8,128)(2,1)}), bf16[32,2,128,128]{3,2,1,0:T(8,128)(2,1)}, u32[]{:S(2)}, u32[]{:S(2)}) async-start(bf16[32,2,128,128]{3,2,1,0:T(8,128)(2,1)} %bitcast.51), calls=%async_computation | async-start | bytes 4194304 | tf_op jit(solution)/shard_map/all_to_all | solution.py:508
  15.1 0.2 copy.18
  15.3 2.8 %collective-permute-start = (bf16[1024,256]{1,0:T(8,128)(2,1)S(1)}, bf16[1024,256]{1,0:T(8,128)(2,1)}, u32[]{:S(2)}, u32[]{:S(2)}) collective-permute-start(bf16[1024,256]{1,0:T(8,128)(2,1)S(1)} %bitcast.55), channel_id=1, source_target_pairs={{0,2},{1,3},{2,0},{3,1},{4,6},{5,7},{6,4},{7,5},{8,10},{9,11},{10,... | collective-permute-start | bytes 1572872 | tf_op jit(solution)/shard_map/ppermute | solution.py:501
  18.2 0.3 collective-permute-start.1
  18.5 2.4 %collective-permute-start.2 = (bf16[1024,256]{1,0:T(8,128)(2,1)S(1)}, bf16[1024,256]{1,0:T(8,128)(2,1)}, u32[]{:S(2)}, u32[]{:S(2)}) collective-permute-start(bf16[1024,256]{1,0:T(8,128)(2,1)S(1)} %bitcast.57), channel_id=1, source_target_pairs={{0,3},{1,0},{2,1},{3,2},{4,7},{5,4},{6,5},{7,6},{8,11},{9,8},{10,9... | collective-permute-start | bytes 1572872 | tf_op jit(solution)/shard_map/ppermute | solution.py:501
  20.8 3.2 %pick.2 = bf16[64,128,128]{2,1,0:T(8,128)(2,1)} custom-call(s32[64]{0:T(128)} %reshape.61.table, bf16[4096,256]{1,0:T(8,128)(2,1)} %features.9), custom_call_target="tpu_custom_call" | custom-call | bytes 4194304 | tf_op jit(solution)/shard_map/pick/pallas_call | solution.py:52
  24.1 6.2 %collective-permute-done = bf16[1024,256]{1,0:T(8,128)(2,1)} collective-permute-done((bf16[1024,256]{1,0:T(8,128)(2,1)S(1)}, bf16[1024,256]{1,0:T(8,128)(2,1)}, u32[]{:S(2)}, u32[]{:S(2)}) %collective-permute-start) | collective-permute-done | bytes 524320 | tf_op jit(solution)/shard_map/ppermute | solution.py:501
  30.3 11.8 %collective-permute-done.1 = bf16[1024,256]{1,0:T(8,128)(2,1)} collective-permute-done((bf16[1024,256]{1,0:T(8,128)(2,1)S(1)}, bf16[1024,256]{1,0:T(8,128)(2,1)}, u32[]{:S(2)}, u32[]{:S(2)}) %collective-permute-start.1) | collective-permute-done | bytes 524320 | tf_op jit(solution)/shard_map/ppermute | solution.py:501
  42.1 1.3 all-to-all-done
  43.5 6.5 %all-to-all-start.1 = ((bf16[32,2,128,128]{3,2,1,0:T(8,128)(2,1)}), bf16[32,2,128,128]{3,2,1,0:T(8,128)(2,1)S(1)}, u32[]{:S(2)}, u32[]{:S(2)}) async-start(bf16[32,2,128,128]{3,2,1,0:T(8,128)(2,1)} %bitcast.50), calls=%async_computation.1 | async-start | bytes 4194304 | tf_op jit(solution)/shard_map/all_to_all | solution.py:508
  50.0 0.1 copy.19
  50.0 0.1 reshape.65.src
  50.2 5.1 %aggregate.3 = (bf16[1024,128]{1,0:T(8,128)(2,1)S(1)}, bf16[1024,128]{1,0:T(8,128)(2,1)}, bf16[1024,128]{1,0:T(8,128)(2,1)}, bf16[1024,128]{1,0:T(8,128)(2,1)S(1)}) custom-call(s32[128]{0:T(128)S(1)} %reshape.65.src, s32[32]{0:T(128)S(1)} %bitcast.46, s32[1]{0:T(128)} %bitcast.6.me, bf16[64,128,128]{2,1,0:T(8,128)(2,1)} %bitcast.3.arrived, ...), custom_call_target="tpu_custom_call" | custom-call | flops 536870912 | bytes 8388608 | tf_op jit(solution)/shard_map/aggregate/pallas_call | solution.py:115
  55.4 2.4 %collective-permute-start.9 = (f32[24,256]{1,0:T(8,128)S(1)}, f32[24,256]{1,0:T(8,128)S(1)}, u32[]{:S(2)}, u32[]{:S(2)}) collective-permute-start(f32[24,256]{1,0:T(8,128)S(1)} %pad_maximum_fusion.1), channel_id=1, source_target_pairs={{0,3},{1,0},{2,1},{3,2},{4,7},{5,4},{6,5},{7,6},{8,11},{9,8},{10,9... | collective-permute-start | bytes 73736 | tf_op jit(solution)/shard_map/ppermute | solution.py:501
  57.8 0.6 collective-permute-start.10
  58.4 0.1 collective-permute-start.11
  58.4 2.3 %collective-permute-start.3 = (bf16[1024,128]{1,0:T(8,128)(2,1)S(1)}, bf16[1024,128]{1,0:T(8,128)(2,1)S(1)}, u32[]{:S(2)}, u32[]{:S(2)}) collective-permute-start(bf16[1024,128]{1,0:T(8,128)(2,1)S(1)} %get-tuple-element.41), channel_id=1, source_target_pairs={{0,2},{1,3},{2,0},{3,1},{4,6},{5,7},{6,4},{7,5},{8,10},{9,11},{10,... | collective-permute-start | bytes 786440 | tf_op jit(solution)/shard_map/ppermute | solution.py:501
  60.7 0.9 collective-permute-start.4
  61.7 3.0 %pad_maximum_fusion.refs_8_ = bf16[1024,1024]{1,0:T(8,128)(2,1)} fusion(bf16[1024,256]{1,0:T(8,128)(2,1)} %collective-permute-done.2, bf16[1024,256]{1,0:T(8,128)(2,1)} %collective-permute-done.1, bf16[1024,256]{1,0:T(8,128)(2,1)} %collective-permute-done, bf16[1024,256]{1,0:T(8,128)(2,1)S(1)} %bitcast.58), kind=kLoop, calls=%fused_computation | loop fusion | flops 8388608 | bytes 4194304 | tf_op jit(solution)/shard_map/concatenate | solution.py:529
  64.7 1.8 collective-permute-start.5
  66.4 0.6 bitcast_dynamic-update-slice_fusion.5
  67.0 0.6 bitcast_dynamic-update-slice_fusion.3
  67.7 0.6 bitcast_dynamic-update-slice_fusion.1
  68.3 0.6 bitcast_dynamic-update-slice_fusion
  68.9 0.6 bitcast_dynamic-update-slice_fusion.6
  69.5 0.6 bitcast_dynamic-update-slice_fusion.4
  70.1 8.2 %all-to-all-done.1 = bf16[32,2,128,128]{3,2,1,0:T(8,128)(2,1)S(1)} async-done(((bf16[32,2,128,128]{3,2,1,0:T(8,128)(2,1)}), bf16[32,2,128,128]{3,2,1,0:T(8,128)(2,1)S(1)}, u32[]{:S(2)}, u32[]{:S(2)}) %all-to-all-start.1) | async-done | bytes 2097184 | tf_op jit(solution)/shard_map/all_to_all | solution.py:508
  78.2 4.1 %aggregate.5 = (bf16[1024,128]{1,0:T(8,128)(2,1)}, bf16[1024,128]{1,0:T(8,128)(2,1)}, bf16[1024,128]{1,0:T(8,128)(2,1)}) custom-call(s32[128]{0:T(128)S(1)} %reshape.65.src, s32[32]{0:T(128)S(1)} %bitcast.47, s32[1]{0:T(128)} %bitcast.6.me, bf16[64,128,128]{2,1,0:T(8,128)(2,1)S(1)} %bitcast.37, bf16[32,4,128,128]{3,2,1,0:T(8,128)(2,1)} %tiles.1, ...), custom_call_target="tpu_custom_call" | custom-call | flops 402653184 | bytes 8388608 | tf_op jit(solution)/shard_map/aggregate/pallas_call | solution.py:115
  82.3 1.8 collective-permute-start.6
  84.2 1.2 collective-permute-start.7
  85.3 1.5 collective-permute-start.8
  86.8 0.6 bitcast_dynamic-update-slice_fusion.2
  87.5 0.8 constant_dynamic-slice_fusion
  88.2 1.0 copy.21.refs_9_
  89.2 0.8 fusion
  90.1 0.2 copy.20
  90.3 0.1 copy.22.refs_10_
  90.4 2.6 %aggregate.4.refs_4_ = bf16[1024,128]{1,0:T(8,128)(2,1)S(1)} custom-call(s32[128]{0:T(128)S(1)} %reshape.65.src, s32[32]{0:T(128)S(1)} %bitcast.48, s32[1]{0:T(128)} %bitcast.6.me, bf16[64,128,128]{2,1,0:T(8,128)(2,1)S(1)} %bitcast.38, bf16[32,4,128,128]{3,2,1,0:T(8,128)(2,1)} %tiles.1, bf16[4096,256]{1,0:T(8,128)(2,1)} %features.9), custom_call_target="tpu_custom_call" | custom-call | flops 134217728 | bytes 8388608 | tf_op jit(solution)/shard_map/aggregate/pallas_call | solution.py:115
  93.0 5.0 %collective-permute-done.7.refs_6_ = bf16[1024,128]{1,0:T(8,128)(2,1)} collective-permute-done((bf16[1024,128]{1,0:T(8,128)(2,1)}, bf16[1024,128]{1,0:T(8,128)(2,1)}, u32[]{:S(2)}, u32[]{:S(2)}) %collective-permute-start.7) | collective-permute-done | bytes 262176 | tf_op jit(solution)/shard_map/ppermute | solution.py:501
  98.1 4.1 %dense.1 = (bf16[1024,1024]{1,0:T(8,128)(2,1)S(1)}, f32[8,16,128]{2,1,0:T(8,128)S(1)}) custom-call(bf16[1024,128]{1,0:T(8,128)(2,1)S(1)} %get-tuple-element.40.refs_0_, bf16[1024,128]{1,0:T(8,128)(2,1)S(1)} %collective-permute-done.3.refs_1_, bf16[1024,128]{1,0:T(8,128)(2,1)S(1)} %collective-permute-done.4.refs_2_, ...), custom_call_target="tpu_custom_call" | custom-call | flops 2147483648 | bytes 7340032 | tf_op jit(solution)/shard_map/dense/pallas_call | solution.py:152
  102.1 1.2 collective-permute-start.12
  103.4 2.4 %collective-permute-start.13 = (f32[8,16,128]{2,1,0:T(8,128)S(1)}, f32[8,16,128]{2,1,0:T(8,128)S(1)}, u32[]{:S(2)}, u32[]{:S(2)}) collective-permute-start(f32[8,16,128]{2,1,0:T(8,128)S(1)} %get-tuple-element.52.p0), channel_id=1, source_target_pairs={{0,2},{1,3},{2,0},{3,1},{4,6},{5,7},{6,4},{7,5},{8,10},{9,11},{10,... | collective-permute-start | bytes 196616 | tf_op jit(solution)/shard_map/ppermute | solution.py:501
  105.7 0.3 collective-permute-start.14
  106.0 0.5 collective-permute-done.12.p1
  106.5 2.0 %collective-permute-done.13.p2 = f32[8,16,128]{2,1,0:T(8,128)S(1)} collective-permute-done((f32[8,16,128]{2,1,0:T(8,128)S(1)}, f32[8,16,128]{2,1,0:T(8,128)S(1)}, u32[]{:S(2)}, u32[]{:S(2)}) %collective-permute-start.13) | collective-permute-done | bytes 65568 | tf_op jit(solution)/shard_map/ppermute | solution.py:501
  108.5 0.8 collective-permute-done.14.p3
  109.4 0.7 spread.1
  110.0 16.3 %all_to_all.25 = f32[32,2,16,128]{3,2,1,0:T(8,128)S(1)} all-to-all(f32[32,2,16,128]{3,2,1,0:T(8,128)S(1)} %bitcast.43), channel_id=1, replica_groups=mesh['nodes'=32,'feat'=4] {'nodes'}, dimensions={0} | all-to-all | bytes 1048576 | tf_op jit(solution)/shard_map/all_to_all | solution.py:508
  126.4 3.9 %logits.1 = (f32[8,16,128]{2,1,0:T(8,128)S(1)}, bf16[64,16,128]{2,1,0:T(8,128)(2,1)S(1)}) custom-call(s32[128]{0:T(128)S(1)} %reshape.65.src, s32[32]{0:T(128)S(1)} %bitcast.49, s32[1]{0:T(128)} %bitcast.6.me, f32[64,16,128]{2,1,0:T(8,128)S(1)} %bitcast.41, f32[32,16,128]{2,1,0:T(8,128)S(1)} %get-tuple-element.54.own, s32[32,1,128]{2,1,0:T(1,128)S(1)} %bitcast.45, ...), custom_call_target="tpu_custom_call" | custom-call | flops 268435456 | bytes 6291456 | tf_op jit(solution)/shard_map/logits/pallas_call | solution.py:260
  130.3 12.4 %all_to_all.26 = bf16[32,2,16,128]{3,2,1,0:T(8,128)(2,1)S(1)} all-to-all(bf16[32,2,16,128]{3,2,1,0:T(8,128)(2,1)S(1)} %bitcast.44), channel_id=1, replica_groups=mesh['nodes'=32,'feat'=4] {'nodes'}, dimensions={0} | all-to-all | bytes 524288 | tf_op jit(solution)/shard_map/all_to_all | solution.py:508
  142.7 3.7 %small_gradients.1 = (bf16[1024,1024]{1,0:T(8,128)(2,1)}, f32[24,1024]{1,0:T(8,128)S(1)}) custom-call(s32[64]{0:T(128)S(1)} %copy-done.4, s32[1]{0:T(128)} %bitcast.6.me, bf16[64,16,128]{2,1,0:T(8,128)(2,1)S(1)} %bitcast.42, f32[8,16,128]{2,1,0:T(8,128)S(1)} %get-tuple-element.56.dlog, bf16[1024,1024]{1,0:T(8,128)(2,1)S(1)} %get-tuple-element.57.hidden, ...), custom_call_target="tpu_custom_call" | custom-call | flops 536870912 | bytes 4194304 | tf_op jit(solution)/shard_map/small_gradients/pallas_call | solution.py:319
  146.4 2.7 %big_gradient.3 = bf16[16,4,32,256]{3,2,1,0:T(8,128)(2,1)S(1)} custom-call(s32[1]{0:T(128)} %bitcast.6.me, s32[1]{0:T(128)S(6)} %sub.6.side, bf16[16,2,32,1024]{3,2,1,0:T(8,128)(2,1)} %bitcast.52, bf16[1024,128]{1,0:T(8,128)(2,1)S(1)} %get-tuple-element.40.refs_0_, bf16[1024,128]{1,0:T(8,128)(2,1)S(1)} %collective-permute-done.3.refs_1_, ...), custom_call_target="tpu_custom_call" | custom-call | flops 1073741824 | bytes 4194304 | tf_op jit(solution)/shard_map/big_gradient/pallas_call | solution.py:365
  149.1 0.3 collective-permute-start.15
  149.4 0.3 collective-permute-start.16
  149.7 2.7 %big_gradient.2.a = bf16[16,4,32,256]{3,2,1,0:T(8,128)(2,1)S(1)} custom-call(s32[1]{0:T(128)} %bitcast.6.me, s32[1]{0:T(128)} %bitcast.4.side, bf16[16,2,32,1024]{3,2,1,0:T(8,128)(2,1)} %bitcast.53, bf16[1024,128]{1,0:T(8,128)(2,1)S(1)} %get-tuple-element.40.refs_0_, bf16[1024,128]{1,0:T(8,128)(2,1)S(1)} %collective-permute-done.3.refs_1_, ...), custom_call_target="tpu_custom_call" | custom-call | flops 1073741824 | bytes 4194304 | tf_op jit(solution)/shard_map/big_gradient/pallas_call | solution.py:365
  152.5 1.8 join.1
  154.3 28.7 %all_to_all.27.arrived = bf16[64,48,256]{2,1,0:T(8,128)(2,1)S(1)} all-to-all(bf16[64,48,256]{2,1,0:T(8,128)(2,1)} %bitcast.54), channel_id=1, replica_groups={{0,1,2,3,8,9,10,11,16,17,18,19,24,25,26,27,32,33,34,35,40,41,42,43,48,4..., dimensions={0} | all-to-all | bytes 3145728 | tf_op jit(solution)/shard_map/all_to_all | solution.py:551
  183.0 1.0 total.1
  184.0 2.1 %collective-permute-start.17 = (f32[16,256]{1,0:T(8,128)S(1)}, f32[16,256]{1,0:T(8,128)S(1)}, u32[]{:S(2)}, u32[]{:S(2)}) collective-permute-start(f32[16,256]{1,0:T(8,128)S(1)} %get-tuple-element.62.a), channel_id=1, source_target_pairs={{0,4},{4,0},{8,12},{12,8},{16,20},{20,16},{24,28},{28,24},{32,36},... | collective-permute-start | bytes 49160 | tf_op jit(solution)/shard_map/ppermute | solution.py:504
  186.1 0.8 collective-permute-done.17.b
  186.9 0.6 finish.1
  (38 shorter events, 0.1 us)
Async XLA Ops:
  5.3 9.8 %copy-start.8 = (bf16[256,1024]{1,0:T(8,128)(2,1)S(1)}, bf16[256,1024]{1,0:T(8,128)(2,1)}, u32[]{:S(2)}) copy-start(bf16[256,1024]{1,0:T(8,128)(2,1)} %param.15) | copy-start | bytes 1572868
  5.3 38.2 %all-to-all-start = ((bf16[32,2,128,128]{3,2,1,0:T(8,128)(2,1)}), bf16[32,2,128,128]{3,2,1,0:T(8,128)(2,1)}, u32[]{:S(2)}, u32[]{:S(2)}) async-start(bf16[32,2,128,128]{3,2,1,0:T(8,128)(2,1)} %bitcast.51), calls=%async_computation | async-start | bytes 4194304 | tf_op jit(solution)/shard_map/all_to_all | solution.py:508
  15.3 8.8 %copy-start.6 = (bf16[256,1024]{0,1:T(8,128)(2,1)}, bf16[256,1024]{0,1:T(8,128)(2,1)S(1)}, u32[]{:S(2)}) copy-start(bf16[256,1024]{0,1:T(8,128)(2,1)S(1)} %copy.18) | copy-start | bytes 1572868
  15.3 14.9 %collective-permute-start = (bf16[1024,256]{1,0:T(8,128)(2,1)S(1)}, bf16[1024,256]{1,0:T(8,128)(2,1)}, u32[]{:S(2)}, u32[]{:S(2)}) collective-permute-start(bf16[1024,256]{1,0:T(8,128)(2,1)S(1)} %bitcast.55), channel_id=1, source_target_pairs={{0,2},{1,3},{2,0},{3,1},{4,6},{5,7},{6,4},{7,5},{8,10},{9,11},{10,... | collective-permute-start | bytes 1572872 | tf_op jit(solution)/shard_map/ppermute | solution.py:501
  18.2 23.9 %collective-permute-start.1 = (bf16[1024,256]{1,0:T(8,128)(2,1)S(1)}, bf16[1024,256]{1,0:T(8,128)(2,1)}, u32[]{:S(2)}, u32[]{:S(2)}) collective-permute-start(bf16[1024,256]{1,0:T(8,128)(2,1)S(1)} %bitcast.56), channel_id=1, source_target_pairs={{0,1},{1,2},{2,3},{3,0},{4,5},{5,6},{6,7},{7,4},{8,9},{9,10},{10,1... | collective-permute-start | bytes 1572872 | tf_op jit(solution)/shard_map/ppermute | solution.py:501
  18.5 23.6 %collective-permute-start.2 = (bf16[1024,256]{1,0:T(8,128)(2,1)S(1)}, bf16[1024,256]{1,0:T(8,128)(2,1)}, u32[]{:S(2)}, u32[]{:S(2)}) collective-permute-start(bf16[1024,256]{1,0:T(8,128)(2,1)S(1)} %bitcast.57), channel_id=1, source_target_pairs={{0,3},{1,0},{2,1},{3,2},{4,7},{5,4},{6,5},{7,6},{8,11},{9,8},{10,9... | collective-permute-start | bytes 1572872 | tf_op jit(solution)/shard_map/ppermute | solution.py:501
  43.5 6.5 %copy-start.10 = (s32[32,4]{0,1:T(4,128)S(1)}, s32[32,4]{0,1:T(4,128)}, u32[]{:S(2)}) copy-start(s32[32,4]{0,1:T(4,128)} %param.12) | copy-start | bytes 1540
  43.5 6.7 %copy-start.9 = (bf16[256,16]{0,1:T(8,128)(2,1)S(1)}, bf16[256,16]{0,1:T(8,128)(2,1)}, u32[]{:S(2)}) copy-start(bf16[256,16]{0,1:T(8,128)(2,1)} %param.17) | copy-start | bytes 24580
  43.5 6.7 %copy-start.11 = (f32[256]{0:T(256)S(1)}, f32[256]{0:T(256)}, u32[]{:S(2)}) copy-start(f32[256]{0:T(256)} %param.16) | copy-start | bytes 3076
  43.5 6.7 %copy-start.5 = (s32[1,32]{1,0:T(1,128)S(1)}, s32[1,32]{1,0:T(1,128)}, u32[]{:S(2)}) copy-start(s32[1,32]{1,0:T(1,128)} %param.10) | copy-start | bytes 388
  43.5 34.8 %all-to-all-start.1 = ((bf16[32,2,128,128]{3,2,1,0:T(8,128)(2,1)}), bf16[32,2,128,128]{3,2,1,0:T(8,128)(2,1)S(1)}, u32[]{:S(2)}, u32[]{:S(2)}) async-start(bf16[32,2,128,128]{3,2,1,0:T(8,128)(2,1)} %bitcast.50), calls=%async_computation.1 | async-start | bytes 4194304 | tf_op jit(solution)/shard_map/all_to_all | solution.py:508
  50.2 11.4 %copy-start.7 = (bf16[256,1024]{0,1:T(8,128)(2,1)S(1)}, bf16[256,1024]{0,1:T(8,128)(2,1)}, u32[]{:S(2)}) copy-start(bf16[256,1024]{0,1:T(8,128)(2,1)} %copy-done.6) | copy-start | bytes 1572868
  55.4 9.3 %collective-permute-start.9 = (f32[24,256]{1,0:T(8,128)S(1)}, f32[24,256]{1,0:T(8,128)S(1)}, u32[]{:S(2)}, u32[]{:S(2)}) collective-permute-start(f32[24,256]{1,0:T(8,128)S(1)} %pad_maximum_fusion.1), channel_id=1, source_target_pairs={{0,3},{1,0},{2,1},{3,2},{4,7},{5,4},{6,5},{7,6},{8,11},{9,8},{10,9... | collective-permute-start | bytes 73736 | tf_op jit(solution)/shard_map/ppermute | solution.py:501
  57.8 9.3 %collective-permute-start.10 = (f32[24,256]{1,0:T(8,128)S(1)}, f32[24,256]{1,0:T(8,128)S(1)}, u32[]{:S(2)}, u32[]{:S(2)}) collective-permute-start(f32[24,256]{1,0:T(8,128)S(1)} %pad_maximum_fusion.1), channel_id=1, source_target_pairs={{0,2},{1,3},{2,0},{3,1},{4,6},{5,7},{6,4},{7,5},{8,10},{9,11},{10,... | collective-permute-start | bytes 73736 | tf_op jit(solution)/shard_map/ppermute | solution.py:501
  58.4 9.3 %collective-permute-start.11 = (f32[24,256]{1,0:T(8,128)S(1)}, f32[24,256]{1,0:T(8,128)S(1)}, u32[]{:S(2)}, u32[]{:S(2)}) collective-permute-start(f32[24,256]{1,0:T(8,128)S(1)} %pad_maximum_fusion.1), channel_id=1, source_target_pairs={{0,1},{1,2},{2,3},{3,0},{4,5},{5,6},{6,7},{7,4},{8,9},{9,10},{10,1... | collective-permute-start | bytes 73736 | tf_op jit(solution)/shard_map/ppermute | solution.py:501
  58.4 26.9 %collective-permute-start.3 = (bf16[1024,128]{1,0:T(8,128)(2,1)S(1)}, bf16[1024,128]{1,0:T(8,128)(2,1)S(1)}, u32[]{:S(2)}, u32[]{:S(2)}) collective-permute-start(bf16[1024,128]{1,0:T(8,128)(2,1)S(1)} %get-tuple-element.41), channel_id=1, source_target_pairs={{0,2},{1,3},{2,0},{3,1},{4,6},{5,7},{6,4},{7,5},{8,10},{9,11},{10,... | collective-permute-start | bytes 786440 | tf_op jit(solution)/shard_map/ppermute | solution.py:501
  60.7 32.2 %collective-permute-start.4 = (bf16[1024,128]{1,0:T(8,128)(2,1)}, bf16[1024,128]{1,0:T(8,128)(2,1)S(1)}, u32[]{:S(2)}, u32[]{:S(2)}) collective-permute-start(bf16[1024,128]{1,0:T(8,128)(2,1)} %get-tuple-element.42), channel_id=1, source_target_pairs={{0,1},{1,2},{2,3},{3,0},{4,5},{5,6},{6,7},{7,4},{8,9},{9,10},{10,1... | collective-permute-start | bytes 786440 | tf_op jit(solution)/shard_map/ppermute | solution.py:501
  64.7 28.3 %collective-permute-start.5 = (bf16[1024,128]{1,0:T(8,128)(2,1)}, bf16[1024,128]{1,0:T(8,128)(2,1)S(1)}, u32[]{:S(2)}, u32[]{:S(2)}) collective-permute-start(bf16[1024,128]{1,0:T(8,128)(2,1)} %get-tuple-element.43), channel_id=1, source_target_pairs={{0,3},{1,0},{2,1},{3,2},{4,7},{5,4},{6,5},{7,6},{8,11},{9,8},{10,9... | collective-permute-start | bytes 786440 | tf_op jit(solution)/shard_map/ppermute | solution.py:501
  82.3 10.7 %collective-permute-start.6 = (bf16[1024,128]{1,0:T(8,128)(2,1)}, bf16[1024,128]{1,0:T(8,128)(2,1)}, u32[]{:S(2)}, u32[]{:S(2)}) collective-permute-start(bf16[1024,128]{1,0:T(8,128)(2,1)} %get-tuple-element.45), channel_id=1, source_target_pairs={{0,2},{1,3},{2,0},{3,1},{4,6},{5,7},{6,4},{7,5},{8,10},{9,11},{10,... | collective-permute-start | bytes 786440 | tf_op jit(solution)/shard_map/ppermute | solution.py:501
  84.2 13.9 %collective-permute-start.7 = (bf16[1024,128]{1,0:T(8,128)(2,1)}, bf16[1024,128]{1,0:T(8,128)(2,1)}, u32[]{:S(2)}, u32[]{:S(2)}) collective-permute-start(bf16[1024,128]{1,0:T(8,128)(2,1)} %get-tuple-element.46), channel_id=1, source_target_pairs={{0,1},{1,2},{2,3},{3,0},{4,5},{5,6},{6,7},{7,4},{8,9},{9,10},{10,1... | collective-permute-start | bytes 786440 | tf_op jit(solution)/shard_map/ppermute | solution.py:501
  85.3 12.7 %collective-permute-start.8 = (bf16[1024,128]{1,0:T(8,128)(2,1)}, bf16[1024,128]{1,0:T(8,128)(2,1)}, u32[]{:S(2)}, u32[]{:S(2)}) collective-permute-start(bf16[1024,128]{1,0:T(8,128)(2,1)} %get-tuple-element.47), channel_id=1, source_target_pairs={{0,3},{1,0},{2,1},{3,2},{4,7},{5,4},{6,5},{7,6},{8,11},{9,8},{10,9... | collective-permute-start | bytes 786440 | tf_op jit(solution)/shard_map/ppermute | solution.py:501
  90.4 7.7 %copy-start.1 = (bf16[1024,1024]{1,0:T(8,128)(2,1)S(1)}, bf16[1024,1024]{1,0:T(8,128)(2,1)}, u32[]{:S(2)}) copy-start(bf16[1024,1024]{1,0:T(8,128)(2,1)} %pad_maximum_fusion.refs_8_) | copy-start | bytes 6291460
  90.4 7.7 %copy-start.2 = (f32[1024,1]{1,0:T(8,128)S(1)}, f32[1024,1]{1,0:T(8,128)}, u32[]{:S(2)}) copy-start(f32[1024,1]{1,0:T(8,128)} %copy.21.refs_9_) | copy-start | bytes 12292
  93.0 16.4 %copy-start.4 = (s32[64]{0:T(128)S(1)}, s32[64]{0:T(128)}, u32[]{:S(2)}) copy-start(s32[64]{0:T(128)} %reshape.61.table) | copy-start | bytes 772
  93.0 33.4 %copy-start.3 = (s32[4096]{0:T(1024)S(1)}, s32[4096]{0:T(1024)}, u32[]{:S(2)}) copy-start(s32[4096]{0:T(1024)} %param.14) | copy-start | bytes 49156
  98.1 28.3 %copy-start = (bf16[32,4,128,128]{3,2,1,0:T(8,128)(2,1)S(1)}, bf16[32,4,128,128]{3,2,1,0:T(8,128)(2,1)}, u32[]{:S(2)}) copy-start(bf16[32,4,128,128]{3,2,1,0:T(8,128)(2,1)} %tiles.1) | copy-start | bytes 12582916
  102.1 4.4 %collective-permute-start.12 = (f32[8,16,128]{2,1,0:T(8,128)S(1)}, f32[8,16,128]{2,1,0:T(8,128)S(1)}, u32[]{:S(2)}, u32[]{:S(2)}) collective-permute-start(f32[8,16,128]{2,1,0:T(8,128)S(1)} %get-tuple-element.52.p0), channel_id=1, source_target_pairs={{0,1},{1,2},{2,3},{3,0},{4,5},{5,6},{6,7},{7,4},{8,9},{9,10},{10,1... | collective-permute-start | bytes 196616 | tf_op jit(solution)/shard_map/ppermute | solution.py:501
  103.4 5.2 %collective-permute-start.13 = (f32[8,16,128]{2,1,0:T(8,128)S(1)}, f32[8,16,128]{2,1,0:T(8,128)S(1)}, u32[]{:S(2)}, u32[]{:S(2)}) collective-permute-start(f32[8,16,128]{2,1,0:T(8,128)S(1)} %get-tuple-element.52.p0), channel_id=1, source_target_pairs={{0,2},{1,3},{2,0},{3,1},{4,6},{5,7},{6,4},{7,5},{8,10},{9,11},{10,... | collective-permute-start | bytes 196616 | tf_op jit(solution)/shard_map/ppermute | solution.py:501
  105.7 3.6 %collective-permute-start.14 = (f32[8,16,128]{2,1,0:T(8,128)S(1)}, f32[8,16,128]{2,1,0:T(8,128)S(1)}, u32[]{:S(2)}, u32[]{:S(2)}) collective-permute-start(f32[8,16,128]{2,1,0:T(8,128)S(1)} %get-tuple-element.52.p0), channel_id=1, source_target_pairs={{0,3},{1,0},{2,1},{3,2},{4,7},{5,4},{6,5},{7,6},{8,11},{9,8},{10,9... | collective-permute-start | bytes 196616 | tf_op jit(solution)/shard_map/ppermute | solution.py:501
  149.1 3.3 %collective-permute-start.15 = (bf16[16,4,32,256]{3,2,1,0:T(8,128)(2,1)S(1)}, bf16[16,4,32,256]{3,2,1,0:T(8,128)(2,1)S(1)}, u32[]{:S(2)}, u32[]{:S(2)}) collective-permute-start(bf16[16,4,32,256]{3,2,1,0:T(8,128)(2,1)S(1)} %big_gradient.3), channel_id=1, source_target_pairs={{0,4},{4,0},{8,12},{12,8},{16,20},{20,16},{24,28},{28,24},{32,36},... | collective-permute-start | bytes 3145736 | tf_op jit(solution)/shard_map/ppermute | solution.py:504
  149.4 3.0 %collective-permute-start.16 = (f32[24,1024]{1,0:T(8,128)S(1)}, f32[24,1024]{1,0:T(8,128)S(1)}, u32[]{:S(2)}, u32[]{:S(2)}) collective-permute-start(f32[24,1024]{1,0:T(8,128)S(1)} %get-tuple-element.60.small), channel_id=1, source_target_pairs={{0,4},{4,0},{8,12},{12,8},{16,20},{20,16},{24,28},{28,24},{32,36},... | collective-permute-start | bytes 294920 | tf_op jit(solution)/shard_map/ppermute | solution.py:504
  184.0 2.9 %collective-permute-start.17 = (f32[16,256]{1,0:T(8,128)S(1)}, f32[16,256]{1,0:T(8,128)S(1)}, u32[]{:S(2)}, u32[]{:S(2)}) collective-permute-start(f32[16,256]{1,0:T(8,128)S(1)} %get-tuple-element.62.a), channel_id=1, source_target_pairs={{0,4},{4,0},{8,12},{12,8},{16,20},{20,16},{24,28},{28,24},{32,36},... | collective-permute-start | bytes 49160 | tf_op jit(solution)/shard_map/ppermute | solution.py:504

commit v11 on v10

--- a/solution.py
+++ b/solution.py
@@ -133,6 +133,50 @@
     )(src, counts, me, arrived, in_hbm(tiles), in_hbm(features))
 
 
+def assemble_kernel(me, *refs):
+    flats, (weights, second_t, second, bias, consts) = refs[:4], refs[4:]
+    hid, grades = second.shape
+    width = flats[0].shape[1]
+    consts[...] = jnp.zeros_like(consts)
+    for i, k in enumerate(ORDER):
+        weights[:, i * width : (i + 1) * width] = flats[i][pl.ds(0, hid), :]
+        owner = lax.rem(me[0] + len(ORDER) - k, len(ORDER))
+        lanes = pl.ds(pl.multiple_of(owner * width, width), width)
+        tail = flats[i][pl.ds(hid, 2 * grades), :].astype(F32)
+        consts[pl.ds(0, grades), lanes] = tail[:grades]
+        b = (tail[grades : grades + 1] + tail[grades + 1 : grades + 2]) + tail[
+            grades + 2 : grades + 3
+        ]
+        consts[pl.ds(grades, 8), lanes] = jnp.broadcast_to(b, (8, width))
+    second_t[...] = consts[pl.ds(0, grades), :].astype(BF16)
+    turned = consts[...].T
+    second[...] = turned[:, :grades].astype(BF16)
+    bias[...] = turned[:, grades : grades + 1]
+
+
+def assemble(me, flats, hid, grades):
+    vmem = pl.BlockSpec(memory_space=pltpu.VMEM)
+    return pl.pallas_call(
+        assemble_kernel,
+        grid_spec=pltpu.PrefetchScalarGridSpec(
+            num_scalar_prefetch=1,
+            grid=(),
+            in_specs=[vmem] * 4,
+            out_specs=[vmem] * 4,
+            scratch_shapes=[pltpu.VMEM((BLK, hid), F32)],
+        ),
+        out_shape=[
+            jax.ShapeDtypeStruct((hid, hid), BF16),
+            jax.ShapeDtypeStruct((grades, hid), BF16),
+            jax.ShapeDtypeStruct((hid, grades), BF16),
+            jax.ShapeDtypeStruct((hid, 1), F32),
+        ],
+        compiler_params=params(16),
+        cost_estimate=cost(0, 5 * MIB),
+        name="assemble",
+    )(me, *flats)
+
+
 def dense_kernel(nfeat, *refs):
     pieces, (weights, bias, second, hidden, proj) = refs[: 2 * nfeat], refs[2 * nfeat :]
     order = [pieces[i * nfeat + k][...] for k in range(nfeat) for i in range(2)]
@@ -511,28 +555,27 @@
     arrived = [swap(pick(features, table, 0))]
     send = pick(features, table, 1)
 
-    flat = w_first.T
-    weights = [ahead(flat, k) for k in (2, 1, 3)]
-    consts = jnp.concatenate(
-        [w_second.T.astype(F32), jnp.broadcast_to(b_first[None], (8, b_first.shape[0]))], 0
-    )
-    send, weights, arrived = lax.optimization_barrier((send, weights, arrived))
+    high = lax.reduce_precision(b_first, 8, 7)
+    middle = lax.reduce_precision(b_first - high, 8, 7)
+    split = jnp.stack([high, middle, (b_first - high) - middle]).astype(BF16)
+    flat = jnp.concatenate(
+        [w_first.T, w_second.T, jnp.pad(split, ((0, grades - 3), (0, 0)))], 0
+    )
+    flats = [ahead(flat, k) for k in (2, 1, 3)]
+    send, flats, arrived = lax.optimization_barrier((send, flats, arrived))
     arrived.append(swap(send))
     others = (2, 1, 3)
     make = functools.partial(aggregate, src, counts, me)
     *sent, own = make(arrived[0], tiles, features, 0, nfeat, others + (0,))
     first = [own] + [ahead(piece, k) for k, piece in zip(others, sent)]
     core = (lax.axis_index("nodes").astype(jnp.int32) % 2).reshape(1)
-    consts, weights, here, there, first[0] = lax.optimization_barrier(
-        (consts, weights, core, 1 - core, first[0])
-    )
-    weights = jnp.concatenate([flat] + weights, 1)
-    turned = [consts] + [ahead(consts, k) for k in range(1, nfeat)]
-    ring = jnp.stack([turned[k] for k in (3, 2, 1, 0, 3, 2, 1)])
-    ordered = lax.dynamic_slice_in_dim(ring, nfeat - 1 - axis, nfeat, 0)
-    second_t = ordered[:, :grades].transpose(1, 0, 2).reshape(grades, hid).astype(BF16)
-    bias = ordered[:, grades].reshape(hid, 1)
-    second = second_t.T
+    flats, here, there, first[0] = lax.optimization_barrier(
+        (flats, core, 1 - core, first[0])
+    )
+    weights, second_t, second, bias = assemble(me, [flat] + flats, hid, grades)
+    arrived[1], weights, second_t, bias, second, first = lax.optimization_barrier(
+        (arrived[1], weights, second_t, bias, second, first)
+    )
     sent = make(arrived[1], tiles, features, 1, nfeat, others)
     last = list(make(arrived[1], tiles, features, 1, nfeat, (0,)))
     last += [ahead(piece, k) for k, piece in zip(others, sent)]

time: 188 us -> 189 us (level)
  waiting for transfers between devices: 36.8 us -> 46.5 us
  local copies, waits for them, and re-layouts: 9.01 us -> 4.67 us
  starting transfers between devices: 40.9 us -> 37.1 us
  other arithmetic: 3.01 us -> 0.06 us
    ppermute x15 -> x12, waiting for transfers between devices: 26.4 us -> 38 us  [ahead(): return lax.ppermute(x, 'feat', [(i, (i + k) % nfeat) for i in range(nfeat)])]
    ppermute x15 -> x12, starting transfers between devices: 22 us -> 18.2 us  [ahead(): return lax.ppermute(x, 'feat', [(i, (i + k) % nfeat) for i in range(nfeat)])]
    concatenate x2 -> x1, other arithmetic: 3.01 us -> 0.04 us  [shards(): jnp.concatenate([w_first.T, w_second.T, jnp.pad(split, ((0, grades - 3),...]
    pallas_call x0 -> x1, Pallas kernels: none -> 2.03 us  [assemble(): pl.pallas_call(assemble_kernel, grid_spec=pltpu.PrefetchScalarGridSpec(nu...]
    unnamed x33 -> x31, local copies, waits for them, and re-layouts: 4.74 us -> 3.94 us
  transfers between devices with their start and end apart: 20 -> 17, of which waited for: 9 -> 12; matrix products, arithmetic and copies ran while one was open for 6% -> 0% of each run, Pallas kernels for 9% -> 8%
where the time goes in v11:
time: 189 us; the launch traced here: 188 us
  blocking collectives  58.5 us (31%)
  waiting for transfers between devices  46.5 us (25%)
  Pallas kernels  40.3 us (21%)
  starting transfers between devices  37.1 us (20%)
  local copies, waits for them, and re-layouts  4.67 us (2%)
    ppermute x12, waiting for transfers between devices, ahead(): return lax.ppermute(x, 'feat', [(i, (i + k) % nfeat) for i in range(nfeat)])  38 us
    all_to_all x1, blocking collectives, shards(): lax.all_to_all(big.reshape(parts // 2 * nfeat, *big.shape[2:]), ('nodes',...  29.3 us
    all_to_all x2, blocking collectives, swap(): lax.all_to_all(shaped, 'nodes', split_axis=0, concat_axis=0, tiled=True)  29.2 us
    ppermute x12, starting transfers between devices, ahead(): return lax.ppermute(x, 'feat', [(i, (i + k) % nfeat) for i in range(nfeat)])  18.2 us
    all_to_all x2, starting transfers between devices, swap(): lax.all_to_all(shaped, 'nodes', split_axis=0, concat_axis=0, tiled=True)  17.1 us
    pallas_call x3, Pallas kernels, aggregate(): pl.pallas_call(functools.partial(agg_kernel, which, chunk, nfeat), grid_s...  10.7 us
    all_to_all x2, waiting for transfers between devices, swap(): lax.all_to_all(shaped, 'nodes', split_axis=0, concat_axis=0, tiled=True)  7.7 us
    pallas_call x2, Pallas kernels, pick(): pl.pallas_call(functools.partial(pick_kernel, chunk), grid_spec=pltpu.Pre...  6.54 us
  transfers between devices with their start and end apart: 17, of which 12 were waited for; matrix products, arithmetic and copies ran while one was open for 0% of the time, Pallas kernels for 8%

profile of v11, /device:TPU:1, one launch (start us, length us, event | category | flops | bytes accessed | tf_op | source)
XLA Modules:
  0.0 188.0 jit_solution(14342726205751417280)
XLA Ops:
  0.6 0.8 copy.15
  1.4 0.6 reshape.58.table
  2.0 3.3 %pick.3 = bf16[64,128,128]{2,1,0:T(8,128)(2,1)} custom-call(s32[64]{0:T(128)} %reshape.58.table, bf16[4096,256]{1,0:T(8,128)(2,1)} %features.9), custom_call_target="tpu_custom_call" | custom-call | bytes 4194304 | tf_op jit(solution)/shard_map/pick/pallas_call | solution.py:52
  5.3 0.0 copy-start.13
  5.3 0.0 copy-start.10
  5.3 0.0 copy-start.11
  5.3 9.8 %all-to-all-start = ((bf16[32,2,128,128]{3,2,1,0:T(8,128)(2,1)}), bf16[32,2,128,128]{3,2,1,0:T(8,128)(2,1)}, u32[]{:S(2)}, u32[]{:S(2)}) async-start(bf16[32,2,128,128]{3,2,1,0:T(8,128)(2,1)} %bitcast.31), calls=%async_computation | async-start | bytes 4194304 | tf_op jit(solution)/shard_map/all_to_all | solution.py:552
  15.2 0.2 copy.16
  15.5 2.8 %collective-permute-start = (bf16[1056,256]{1,0:T(8,128)(2,1)S(1)}, bf16[1056,256]{1,0:T(8,128)(2,1)}, u32[]{:S(2)}, u32[]{:S(2)}) collective-permute-start(bf16[1056,256]{1,0:T(8,128)(2,1)S(1)} %pad_maximum_fusion.refs_0_), channel_id=1, source_target_pairs={{0,2},{1,3},{2,0},{3,1},{4,6},{5,7},{6,4},{7,5},{8,10},{9,11},{10,... | collective-permute-start | bytes 1622024 | tf_op jit(solution)/shard_map/ppermute | solution.py:545
  18.3 0.3 collective-permute-start.1
  18.6 2.4 %collective-permute-start.2 = (bf16[1056,256]{1,0:T(8,128)(2,1)S(1)}, bf16[1056,256]{1,0:T(8,128)(2,1)}, u32[]{:S(2)}, u32[]{:S(2)}) collective-permute-start(bf16[1056,256]{1,0:T(8,128)(2,1)S(1)} %pad_maximum_fusion.refs_0_), channel_id=1, source_target_pairs={{0,3},{1,0},{2,1},{3,2},{4,7},{5,4},{6,5},{7,6},{8,11},{9,8},{10,9... | collective-permute-start | bytes 1622024 | tf_op jit(solution)/shard_map/ppermute | solution.py:545
  21.0 3.3 %pick.2 = bf16[64,128,128]{2,1,0:T(8,128)(2,1)} custom-call(s32[64]{0:T(128)} %reshape.58.table, bf16[4096,256]{1,0:T(8,128)(2,1)} %features.9), custom_call_target="tpu_custom_call" | custom-call | bytes 4194304 | tf_op jit(solution)/shard_map/pick/pallas_call | solution.py:52
  24.3 6.5 %collective-permute-done.refs_1_ = bf16[1056,256]{1,0:T(8,128)(2,1)} collective-permute-done((bf16[1056,256]{1,0:T(8,128)(2,1)S(1)}, bf16[1056,256]{1,0:T(8,128)(2,1)}, u32[]{:S(2)}, u32[]{:S(2)}) %collective-permute-start) | collective-permute-done | bytes 540704 | tf_op jit(solution)/shard_map/ppermute | solution.py:545
  30.8 12.2 %collective-permute-done.1.refs_2_ = bf16[1056,256]{1,0:T(8,128)(2,1)} collective-permute-done((bf16[1056,256]{1,0:T(8,128)(2,1)S(1)}, bf16[1056,256]{1,0:T(8,128)(2,1)}, u32[]{:S(2)}, u32[]{:S(2)}) %collective-permute-start.1) | collective-permute-done | bytes 540704 | tf_op jit(solution)/shard_map/ppermute | solution.py:545
  43.0 0.0 collective-permute-done.2.refs_3_
  43.0 0.5 all-to-all-done
  43.5 7.3 %all-to-all-start.1 = ((bf16[32,2,128,128]{3,2,1,0:T(8,128)(2,1)}), bf16[32,2,128,128]{3,2,1,0:T(8,128)(2,1)S(1)}, u32[]{:S(2)}, u32[]{:S(2)}) async-start(bf16[32,2,128,128]{3,2,1,0:T(8,128)(2,1)} %bitcast.30), calls=%async_computation.1 | async-start | bytes 4194304 | tf_op jit(solution)/shard_map/all_to_all | solution.py:552
  50.8 0.1 copy.17
  50.9 0.1 reshape.62.src
  51.0 5.1 %aggregate.3 = (bf16[1024,128]{1,0:T(8,128)(2,1)}, bf16[1024,128]{1,0:T(8,128)(2,1)}, bf16[1024,128]{1,0:T(8,128)(2,1)}, bf16[1024,128]{1,0:T(8,128)(2,1)S(1)}) custom-call(s32[128]{0:T(128)S(1)} %reshape.62.src, s32[32]{0:T(128)S(1)} %bitcast.26, s32[1]{0:T(128)} %bitcast.6.me, bf16[64,128,128]{2,1,0:T(8,128)(2,1)} %bitcast.3.arrived, ...), custom_call_target="tpu_custom_call" | custom-call | flops 536870912 | bytes 8388608 | tf_op jit(solution)/shard_map/aggregate/pallas_call | solution.py:115
  56.1 1.8 collective-permute-start.3
  58.0 1.2 collective-permute-start.4
  59.1 1.5 collective-permute-start.5
  60.6 2.0 %assemble.1 = (bf16[1024,1024]{1,0:T(8,128)(2,1)S(1)}, bf16[16,1024]{1,0:T(8,128)(2,1)S(1)}, bf16[1024,16]{1,0:T(8,128)(2,1)S(1)}, f32[1024,1]{1,0:T(8,128)S(1)}) custom-call(s32[1]{0:T(128)} %bitcast.6.me, bf16[1056,256]{1,0:T(8,128)(2,1)S(1)} %pad_maximum_fusion.refs_0_, bf16[1056,256]{1,0:T(8,128)(2,1)} %collective-permute-done.refs_1_, ...), custom_call_target="tpu_custom_call" | custom-call | bytes 5242880 | tf_op jit(solution)/shard_map/assemble/pallas_call | solution.py:159
  62.7 0.7 copy-done.1
  63.4 1.3 copy-done.6
  64.7 0.8 copy-done.8
  65.5 0.1 collective-permute-done.3.refs_1_
  65.6 6.2 %collective-permute-done.4.refs_2_ = bf16[1024,128]{1,0:T(8,128)(2,1)} collective-permute-done((bf16[1024,128]{1,0:T(8,128)(2,1)}, bf16[1024,128]{1,0:T(8,128)(2,1)}, u32[]{:S(2)}, u32[]{:S(2)}) %collective-permute-start.4) | collective-permute-done | bytes 262176 | tf_op jit(solution)/shard_map/ppermute | solution.py:545
  71.9 0.0 collective-permute-done.5.refs_3_
  71.9 7.2 %all-to-all-done.1 = bf16[32,2,128,128]{3,2,1,0:T(8,128)(2,1)S(1)} async-done(((bf16[32,2,128,128]{3,2,1,0:T(8,128)(2,1)}), bf16[32,2,128,128]{3,2,1,0:T(8,128)(2,1)S(1)}, u32[]{:S(2)}, u32[]{:S(2)}) %all-to-all-start.1) | async-done | bytes 2097184 | tf_op jit(solution)/shard_map/all_to_all | solution.py:552
  79.1 3.3 %aggregate.5 = (bf16[1024,128]{1,0:T(8,128)(2,1)S(1)}, bf16[1024,128]{1,0:T(8,128)(2,1)S(1)}, bf16[1024,128]{1,0:T(8,128)(2,1)S(1)}) custom-call(s32[128]{0:T(128)S(1)} %reshape.62.src, s32[32]{0:T(128)S(1)} %bitcast.27, s32[1]{0:T(128)} %bitcast.6.me, bf16[64,128,128]{2,1,0:T(8,128)(2,1)S(1)} %bitcast.19, bf16[32,4,128,128]{3,2,1,0:T(8,128)(2,1)} %tiles.1, ...), custom_call_target="tpu_custom_call" | custom-call | flops 402653184 | bytes 8388608 | tf_op jit(solution)/shard_map/aggregate/pallas_call | solution.py:115
  82.3 1.8 collective-permute-start.6
  84.2 1.2 collective-permute-start.7
  85.3 1.5 collective-permute-start.8
  86.9 2.3 %aggregate.4.refs_4_ = bf16[1024,128]{1,0:T(8,128)(2,1)S(1)} custom-call(s32[128]{0:T(128)S(1)} %reshape.62.src, s32[32]{0:T(128)S(1)} %bitcast.28, s32[1]{0:T(128)} %bitcast.6.me, bf16[64,128,128]{2,1,0:T(8,128)(2,1)S(1)} %bitcast.20, bf16[32,4,128,128]{3,2,1,0:T(8,128)(2,1)} %tiles.1, bf16[4096,256]{1,0:T(8,128)(2,1)} %features.9), custom_call_target="tpu_custom_call" | custom-call | flops 134217728 | bytes 8388608 | tf_op jit(solution)/shard_map/aggregate/pallas_call | solution.py:115
  89.2 0.0 copy-start.4
  89.2 0.0 copy-start.3
  89.2 1.7 collective-permute-done.6.refs_5_
  90.9 6.8 %collective-permute-done.7.refs_6_ = bf16[1024,128]{1,0:T(8,128)(2,1)S(1)} collective-permute-done((bf16[1024,128]{1,0:T(8,128)(2,1)S(1)}, bf16[1024,128]{1,0:T(8,128)(2,1)S(1)}, u32[]{:S(2)}, u32[]{:S(2)}) %collective-permute-start.7) | collective-permute-done | bytes 262176 | tf_op jit(solution)/shard_map/ppermute | solution.py:545
  97.8 0.0 copy-start
  97.8 4.0 %dense.1 = (bf16[1024,1024]{1,0:T(8,128)(2,1)S(1)}, f32[8,16,128]{2,1,0:T(8,128)S(1)}) custom-call(bf16[1024,128]{1,0:T(8,128)(2,1)S(1)} %get-tuple-element.64.refs_0_, bf16[1024,128]{1,0:T(8,128)(2,1)S(1)} %collective-permute-done.3.refs_1_, bf16[1024,128]{1,0:T(8,128)(2,1)} %collective-permute-done.4.refs_2_, ...), custom_call_target="tpu_custom_call" | custom-call | flops 2147483648 | bytes 7340032 | tf_op jit(solution)/shard_map/dense/pallas_call | solution.py:196
  101.8 1.8 collective-permute-start.10
  103.6 1.8 collective-permute-start.11
  105.4 0.0 collective-permute-start.9
  105.4 1.1 collective-permute-done.10.p2
  106.5 1.3 collective-permute-done.11.p3
  107.7 2.0 %collective-permute-done.9.p1 = f32[8,16,128]{2,1,0:T(8,128)S(1)} collective-permute-done((f32[8,16,128]{2,1,0:T(8,128)S(1)}, f32[8,16,128]{2,1,0:T(8,128)S(1)}, u32[]{:S(2)}, u32[]{:S(2)}) %collective-permute-start.9) | collective-permute-done | bytes 65568 | tf_op jit(solution)/shard_map/ppermute | solution.py:545
  109.8 0.7 spread.1
  110.4 16.8 %all_to_all.25 = f32[32,2,16,128]{3,2,1,0:T(8,128)S(1)} all-to-all(f32[32,2,16,128]{3,2,1,0:T(8,128)S(1)} %bitcast.23), channel_id=1, replica_groups=mesh['nodes'=32,'feat'=4] {'nodes'}, dimensions={0} | all-to-all | bytes 1048576 | tf_op jit(solution)/shard_map/all_to_all | solution.py:552
  127.3 3.9 %logits.1 = (f32[8,16,128]{2,1,0:T(8,128)S(1)}, bf16[64,16,128]{2,1,0:T(8,128)(2,1)S(1)}) custom-call(s32[128]{0:T(128)S(1)} %reshape.62.src, s32[32]{0:T(128)S(1)} %bitcast.29, s32[1]{0:T(128)} %bitcast.6.me, f32[64,16,128]{2,1,0:T(8,128)S(1)} %bitcast.21, f32[32,16,128]{2,1,0:T(8,128)S(1)} %get-tuple-element.77.own, s32[32,1,128]{2,1,0:T(1,128)S(1)} %bitcast.25, ...), custom_call_target="tpu_custom_call" | custom-call | flops 268435456 | bytes 6291456 | tf_op jit(solution)/shard_map/logits/pallas_call | solution.py:304
  131.2 12.4 %all_to_all.26 = bf16[32,2,16,128]{3,2,1,0:T(8,128)(2,1)S(1)} all-to-all(bf16[32,2,16,128]{3,2,1,0:T(8,128)(2,1)S(1)} %bitcast.24), channel_id=1, replica_groups=mesh['nodes'=32,'feat'=4] {'nodes'}, dimensions={0} | all-to-all | bytes 524288 | tf_op jit(solution)/shard_map/all_to_all | solution.py:552
  143.6 3.7 %small_gradients.1 = (bf16[1024,1024]{1,0:T(8,128)(2,1)}, f32[24,1024]{1,0:T(8,128)S(1)}) custom-call(s32[64]{0:T(128)S(1)} %copy-done.4, s32[1]{0:T(128)} %bitcast.6.me, bf16[64,16,128]{2,1,0:T(8,128)(2,1)S(1)} %bitcast.22, f32[8,16,128]{2,1,0:T(8,128)S(1)} %get-tuple-element.79.dlog, bf16[1024,1024]{1,0:T(8,128)(2,1)S(1)} %get-tuple-element.80.hidden, ...), custom_call_target="tpu_custom_call" | custom-call | flops 536870912 | bytes 4194304 | tf_op jit(solution)/shard_map/small_gradients/pallas_call | solution.py:363
  147.3 2.6 %big_gradient.3 = bf16[16,4,32,256]{3,2,1,0:T(8,128)(2,1)S(1)} custom-call(s32[1]{0:T(128)} %bitcast.6.me, s32[1]{0:T(128)S(6)} %sub.12.side, bf16[16,2,32,1024]{3,2,1,0:T(8,128)(2,1)} %bitcast.32, bf16[1024,128]{1,0:T(8,128)(2,1)S(1)} %get-tuple-element.64.refs_0_, bf16[1024,128]{1,0:T(8,128)(2,1)S(1)} %collective-permute-done.3.refs_1_, ...), custom_call_target="tpu_custom_call" | custom-call | flops 1073741824 | bytes 4194304 | tf_op jit(solution)/shard_map/big_gradient/pallas_call | solution.py:409
  149.9 0.3 collective-permute-start.12
  150.2 0.3 collective-permute-start.13
  150.5 2.6 %big_gradient.2.a = bf16[16,4,32,256]{3,2,1,0:T(8,128)(2,1)S(1)} custom-call(s32[1]{0:T(128)} %bitcast.6.me, s32[1]{0:T(128)} %bitcast.4.side, bf16[16,2,32,1024]{3,2,1,0:T(8,128)(2,1)} %bitcast.33, bf16[1024,128]{1,0:T(8,128)(2,1)S(1)} %get-tuple-element.64.refs_0_, bf16[1024,128]{1,0:T(8,128)(2,1)S(1)} %collective-permute-done.3.refs_1_, ...), custom_call_target="tpu_custom_call" | custom-call | flops 1073741824 | bytes 4194304 | tf_op jit(solution)/shard_map/big_gradient/pallas_call | solution.py:409
  153.1 0.0 collective-permute-done.13.other
  153.2 1.9 join.1
  155.0 29.3 %all_to_all.27.arrived = bf16[64,48,256]{2,1,0:T(8,128)(2,1)S(1)} all-to-all(bf16[64,48,256]{2,1,0:T(8,128)(2,1)} %bitcast.34), channel_id=1, replica_groups={{0,1,2,3,8,9,10,11,16,17,18,19,24,25,26,27,32,33,34,35,40,41,42,43,48,4..., dimensions={0} | all-to-all | bytes 3145728 | tf_op jit(solution)/shard_map/all_to_all | solution.py:594
  184.3 1.0 total.1
  185.3 1.3 collective-permute-start.14
  186.6 0.8 collective-permute-done.14.b
  187.4 0.6 finish.1
  (27 shorter events, 0.1 us)
Async XLA Ops:
  5.3 9.8 %copy-start.13 = (f32[256]{0:T(256)S(1)}, f32[256]{0:T(256)}, u32[]{:S(2)}) copy-start(f32[256]{0:T(256)} %param.16) | copy-start | bytes 3076
  5.3 9.9 %copy-start.10 = (bf16[256,1024]{1,0:T(8,128)(2,1)S(1)}, bf16[256,1024]{1,0:T(8,128)(2,1)}, u32[]{:S(2)}) copy-start(bf16[256,1024]{1,0:T(8,128)(2,1)} %param.15) | copy-start | bytes 1572868
  5.3 10.1 %copy-start.11 = (bf16[256,16]{0,1:T(8,128)(2,1)S(1)}, bf16[256,16]{0,1:T(8,128)(2,1)}, u32[]{:S(2)}) copy-start(bf16[256,16]{0,1:T(8,128)(2,1)} %param.17) | copy-start | bytes 24580
  5.3 38.2 %all-to-all-start = ((bf16[32,2,128,128]{3,2,1,0:T(8,128)(2,1)}), bf16[32,2,128,128]{3,2,1,0:T(8,128)(2,1)}, u32[]{:S(2)}, u32[]{:S(2)}) async-start(bf16[32,2,128,128]{3,2,1,0:T(8,128)(2,1)} %bitcast.31), calls=%async_computation | async-start | bytes 4194304 | tf_op jit(solution)/shard_map/all_to_all | solution.py:552
  15.5 15.3 %collective-permute-start = (bf16[1056,256]{1,0:T(8,128)(2,1)S(1)}, bf16[1056,256]{1,0:T(8,128)(2,1)}, u32[]{:S(2)}, u32[]{:S(2)}) collective-permute-start(bf16[1056,256]{1,0:T(8,128)(2,1)S(1)} %pad_maximum_fusion.refs_0_), channel_id=1, source_target_pairs={{0,2},{1,3},{2,0},{3,1},{4,6},{5,7},{6,4},{7,5},{8,10},{9,11},{10,... | collective-permute-start | bytes 1622024 | tf_op jit(solution)/shard_map/ppermute | solution.py:545
  18.3 24.6 %collective-permute-start.1 = (bf16[1056,256]{1,0:T(8,128)(2,1)S(1)}, bf16[1056,256]{1,0:T(8,128)(2,1)}, u32[]{:S(2)}, u32[]{:S(2)}) collective-permute-start(bf16[1056,256]{1,0:T(8,128)(2,1)S(1)} %pad_maximum_fusion.refs_0_), channel_id=1, source_target_pairs={{0,1},{1,2},{2,3},{3,0},{4,5},{5,6},{6,7},{7,4},{8,9},{9,10},{10,1... | collective-permute-start | bytes 1622024 | tf_op jit(solution)/shard_map/ppermute | solution.py:545
  18.6 24.3 %collective-permute-start.2 = (bf16[1056,256]{1,0:T(8,128)(2,1)S(1)}, bf16[1056,256]{1,0:T(8,128)(2,1)}, u32[]{:S(2)}, u32[]{:S(2)}) collective-permute-start(bf16[1056,256]{1,0:T(8,128)(2,1)S(1)} %pad_maximum_fusion.refs_0_), channel_id=1, source_target_pairs={{0,3},{1,0},{2,1},{3,2},{4,7},{5,4},{6,5},{7,6},{8,11},{9,8},{10,9... | collective-permute-start | bytes 1622024 | tf_op jit(solution)/shard_map/ppermute | solution.py:545
  43.5 7.3 %copy-start.12 = (s32[32,4]{0,1:T(4,128)S(1)}, s32[32,4]{0,1:T(4,128)}, u32[]{:S(2)}) copy-start(s32[32,4]{0,1:T(4,128)} %param.12) | copy-start | bytes 1540
  43.5 7.5 %copy-start.5 = (s32[1,32]{1,0:T(1,128)S(1)}, s32[1,32]{1,0:T(1,128)}, u32[]{:S(2)}) copy-start(s32[1,32]{1,0:T(1,128)} %param.10) | copy-start | bytes 388
  43.5 35.6 %all-to-all-start.1 = ((bf16[32,2,128,128]{3,2,1,0:T(8,128)(2,1)}), bf16[32,2,128,128]{3,2,1,0:T(8,128)(2,1)S(1)}, u32[]{:S(2)}, u32[]{:S(2)}) async-start(bf16[32,2,128,128]{3,2,1,0:T(8,128)(2,1)} %bitcast.30), calls=%async_computation.1 | async-start | bytes 4194304 | tf_op jit(solution)/shard_map/all_to_all | solution.py:552
  56.1 9.5 %collective-permute-start.3 = (bf16[1024,128]{1,0:T(8,128)(2,1)}, bf16[1024,128]{1,0:T(8,128)(2,1)S(1)}, u32[]{:S(2)}, u32[]{:S(2)}) collective-permute-start(bf16[1024,128]{1,0:T(8,128)(2,1)} %get-tuple-element.61), channel_id=1, source_target_pairs={{0,2},{1,3},{2,0},{3,1},{4,6},{5,7},{6,4},{7,5},{8,10},{9,11},{10,... | collective-permute-start | bytes 786440 | tf_op jit(solution)/shard_map/ppermute | solution.py:545
  58.0 13.9 %collective-permute-start.4 = (bf16[1024,128]{1,0:T(8,128)(2,1)}, bf16[1024,128]{1,0:T(8,128)(2,1)}, u32[]{:S(2)}, u32[]{:S(2)}) collective-permute-start(bf16[1024,128]{1,0:T(8,128)(2,1)} %get-tuple-element.62), channel_id=1, source_target_pairs={{0,1},{1,2},{2,3},{3,0},{4,5},{5,6},{6,7},{7,4},{8,9},{9,10},{10,1... | collective-permute-start | bytes 786440 | tf_op jit(solution)/shard_map/ppermute | solution.py:545
  59.1 12.8 %collective-permute-start.5 = (bf16[1024,128]{1,0:T(8,128)(2,1)}, bf16[1024,128]{1,0:T(8,128)(2,1)}, u32[]{:S(2)}, u32[]{:S(2)}) collective-permute-start(bf16[1024,128]{1,0:T(8,128)(2,1)} %get-tuple-element.63), channel_id=1, source_target_pairs={{0,3},{1,0},{2,1},{3,2},{4,7},{5,4},{6,5},{7,6},{8,11},{9,8},{10,9... | collective-permute-start | bytes 786440 | tf_op jit(solution)/shard_map/ppermute | solution.py:545
  62.7 0.7 copy-start.1
  63.4 1.3 copy-start.6
  64.7 0.8 copy-start.8
  82.3 8.6 %collective-permute-start.6 = (bf16[1024,128]{1,0:T(8,128)(2,1)S(1)}, bf16[1024,128]{1,0:T(8,128)(2,1)S(1)}, u32[]{:S(2)}, u32[]{:S(2)}) collective-permute-start(bf16[1024,128]{1,0:T(8,128)(2,1)S(1)} %get-tuple-element.69), channel_id=1, source_target_pairs={{0,2},{1,3},{2,0},{3,1},{4,6},{5,7},{6,4},{7,5},{8,10},{9,11},{10,... | collective-permute-start | bytes 786440 | tf_op jit(solution)/shard_map/ppermute | solution.py:545
  84.2 13.6 %collective-permute-start.7 = (bf16[1024,128]{1,0:T(8,128)(2,1)S(1)}, bf16[1024,128]{1,0:T(8,128)(2,1)S(1)}, u32[]{:S(2)}, u32[]{:S(2)}) collective-permute-start(bf16[1024,128]{1,0:T(8,128)(2,1)S(1)} %get-tuple-element.70), channel_id=1, source_target_pairs={{0,1},{1,2},{2,3},{3,0},{4,5},{5,6},{6,7},{7,4},{8,9},{9,10},{10,1... | collective-permute-start | bytes 786440 | tf_op jit(solution)/shard_map/ppermute | solution.py:545
  85.3 12.4 %copy-start.7 = (bf16[1024,1024]{1,0:T(8,128)(2,1)S(1)}, bf16[1024,1024]{1,0:T(8,128)(2,1)}, u32[]{:S(2)}) copy-start(bf16[1024,1024]{1,0:T(8,128)(2,1)} %copy-done.6) | copy-start | bytes 6291460
  85.3 12.4 %copy-start.9 = (f32[1024,1]{1,0:T(8,128)S(1)}, f32[1024,1]{1,0:T(8,128)}, u32[]{:S(2)}) copy-start(f32[1024,1]{1,0:T(8,128)} %copy-done.8) | copy-start | bytes 12292
  85.3 12.4 %collective-permute-start.8 = (bf16[1024,128]{1,0:T(8,128)(2,1)S(1)}, bf16[1024,128]{1,0:T(8,128)(2,1)S(1)}, u32[]{:S(2)}, u32[]{:S(2)}) collective-permute-start(bf16[1024,128]{1,0:T(8,128)(2,1)S(1)} %get-tuple-element.71), channel_id=1, source_target_pairs={{0,3},{1,0},{2,1},{3,2},{4,7},{5,4},{6,5},{7,6},{8,11},{9,8},{10,9... | collective-permute-start | bytes 786440 | tf_op jit(solution)/shard_map/ppermute | solution.py:545
  89.2 20.6 %copy-start.4 = (s32[64]{0:T(128)S(1)}, s32[64]{0:T(128)}, u32[]{:S(2)}) copy-start(s32[64]{0:T(128)} %reshape.58.table) | copy-start | bytes 772
  89.2 38.1 %copy-start.3 = (s32[4096]{0:T(1024)S(1)}, s32[4096]{0:T(1024)}, u32[]{:S(2)}) copy-start(s32[4096]{0:T(1024)} %param.14) | copy-start | bytes 49156
  97.8 29.5 %copy-start = (bf16[32,4,128,128]{3,2,1,0:T(8,128)(2,1)S(1)}, bf16[32,4,128,128]{3,2,1,0:T(8,128)(2,1)}, u32[]{:S(2)}) copy-start(bf16[32,4,128,128]{3,2,1,0:T(8,128)(2,1)} %tiles.1) | copy-start | bytes 12582916
  101.8 4.7 %collective-permute-start.10 = (f32[8,16,128]{2,1,0:T(8,128)S(1)}, f32[8,16,128]{2,1,0:T(8,128)S(1)}, u32[]{:S(2)}, u32[]{:S(2)}) collective-permute-start(f32[8,16,128]{2,1,0:T(8,128)S(1)} %get-tuple-element.75.p0), channel_id=1, source_target_pairs={{0,2},{1,3},{2,0},{3,1},{4,6},{5,7},{6,4},{7,5},{8,10},{9,11},{10,... | collective-permute-start | bytes 196616 | tf_op jit(solution)/shard_map/ppermute | solution.py:545
  103.6 4.1 %collective-permute-start.11 = (f32[8,16,128]{2,1,0:T(8,128)S(1)}, f32[8,16,128]{2,1,0:T(8,128)S(1)}, u32[]{:S(2)}, u32[]{:S(2)}) collective-permute-start(f32[8,16,128]{2,1,0:T(8,128)S(1)} %get-tuple-element.75.p0), channel_id=1, source_target_pairs={{0,3},{1,0},{2,1},{3,2},{4,7},{5,4},{6,5},{7,6},{8,11},{9,8},{10,9... | collective-permute-start | bytes 196616 | tf_op jit(solution)/shard_map/ppermute | solution.py:545
  105.4 4.3 %collective-permute-start.9 = (f32[8,16,128]{2,1,0:T(8,128)S(1)}, f32[8,16,128]{2,1,0:T(8,128)S(1)}, u32[]{:S(2)}, u32[]{:S(2)}) collective-permute-start(f32[8,16,128]{2,1,0:T(8,128)S(1)} %get-tuple-element.75.p0), channel_id=1, source_target_pairs={{0,1},{1,2},{2,3},{3,0},{4,5},{5,6},{6,7},{7,4},{8,9},{9,10},{10,1... | collective-permute-start | bytes 196616 | tf_op jit(solution)/shard_map/ppermute | solution.py:545
  127.3 16.3 %copy-start.2 = (bf16[1024,16]{1,0:T(8,128)(2,1)S(1)}, bf16[1024,16]{1,0:T(8,128)(2,1)}, u32[]{:S(2)}) copy-start(bf16[1024,16]{1,0:T(8,128)(2,1)} %copy-done.1) | copy-start | bytes 98308
  149.9 3.2 %collective-permute-start.12 = (bf16[16,4,32,256]{3,2,1,0:T(8,128)(2,1)S(1)}, bf16[16,4,32,256]{3,2,1,0:T(8,128)(2,1)S(1)}, u32[]{:S(2)}, u32[]{:S(2)}) collective-permute-start(bf16[16,4,32,256]{3,2,1,0:T(8,128)(2,1)S(1)} %big_gradient.3), channel_id=1, source_target_pairs={{0,4},{4,0},{8,12},{12,8},{16,20},{20,16},{24,28},{28,24},{32,36},... | collective-permute-start | bytes 3145736 | tf_op jit(solution)/shard_map/ppermute | solution.py:548
  150.2 2.9 %collective-permute-start.13 = (f32[24,1024]{1,0:T(8,128)S(1)}, f32[24,1024]{1,0:T(8,128)S(1)}, u32[]{:S(2)}, u32[]{:S(2)}) collective-permute-start(f32[24,1024]{1,0:T(8,128)S(1)} %get-tuple-element.84.small), channel_id=1, source_target_pairs={{0,4},{4,0},{8,12},{12,8},{16,20},{20,16},{24,28},{28,24},{32,36},... | collective-permute-start | bytes 294920 | tf_op jit(solution)/shard_map/ppermute | solution.py:548
  185.3 2.1 %collective-permute-start.14 = (f32[16,256]{1,0:T(8,128)S(1)}, f32[16,256]{1,0:T(8,128)S(1)}, u32[]{:S(2)}, u32[]{:S(2)}) collective-permute-start(f32[16,256]{1,0:T(8,128)S(1)} %get-tuple-element.86.a), channel_id=1, source_target_pairs={{0,4},{4,0},{8,12},{12,8},{16,20},{20,16},{24,28},{28,24},{32,36},... | collective-permute-start | bytes 49160 | tf_op jit(solution)/shard_map/ppermute | solution.py:548

commit v12 on v11

--- a/solution.py
+++ b/solution.py
@@ -69,46 +69,49 @@
 
 
 def agg_kernel(which, chunk, nfeat, src, counts, me, arrived, tiles_hbm, features, *refs):
-    outs, (tiles, own, sems, *held) = refs[: len(which)], refs[len(which) :]
-    group, per = tiles.shape[1:3]
+    n = len(which)
+    outs, tiles, own, (sems, *held) = refs[:n], refs[n : 2 * n], refs[2 * n : 3 * n], refs[3 * n :]
+    per = tiles[0].shape[1]
+    group = tiles_hbm.shape[0] // nfeat
     moves = []
     if held:
-        moves.append(pltpu.make_async_copy(arrived, held[0], sems.at[2 * len(which)]))
+        moves.append(pltpu.make_async_copy(arrived, held[0], sems.at[2 * n]))
         arrived = held[0]
-    firsts = [lax.rem(me[0] + k, nfeat) * group for k in which]
+    firsts = [lax.rem(me[0] + k, nfeat) * group + low for k, low, _ in which]
     pairs = []
-    for i, first in enumerate(firsts):
-        rows = pl.ds(pl.multiple_of(first * BLK, BLK), group * BLK)
+    for i, (first, (_, low, high)) in enumerate(zip(firsts, which)):
+        rows = pl.ds(pl.multiple_of(first * BLK, BLK), (high - low) * BLK)
         tiles_move = pltpu.make_async_copy(
-            tiles_hbm.at[pl.ds(first, group)], tiles.at[i], sems.at[2 * i]
+            tiles_hbm.at[pl.ds(first, high - low)], tiles[i], sems.at[2 * i]
         )
         own_move = pltpu.make_async_copy(
-            features.at[rows, pl.ds(chunk * BLK, BLK)], own.at[i], sems.at[2 * i + 1]
+            features.at[rows, pl.ds(chunk * BLK, BLK)], own[i], sems.at[2 * i + 1]
         )
         pairs.append((tiles_move, own_move))
     for move in moves + [move for pair in pairs for move in pair]:
         move.start()
     for move in moves:
         move.wait()
-    for i, (first, out) in enumerate(zip(firsts, outs)):
+    for i, (first, out, (_, low, high)) in enumerate(zip(firsts, outs, which)):
         for move in pairs[i]:
             move.wait()
-        for b in range(group):
+        for b in range(high - low):
             rows, weights = [], []
             for t in range(per):
                 slot = src[(first + b) * per + t]
                 live = lax.rem(slot, 2) < counts[lax.div(slot, 2)]
                 rows.append(arrived[slot])
-                weights.append(tiles[i, b, t] * jnp.where(live, 1.0, 0.0).astype(BF16))
+                weights.append(tiles[i][b, t] * jnp.where(live, 1.0, 0.0).astype(BF16))
             total = dot(jnp.concatenate(weights, 1), jnp.concatenate(rows, 0), NN)
             at = pl.ds(b * BLK, BLK)
-            out[at, :] = (own[i, at, :].astype(F32) + total).astype(BF16)
+            out[at, :] = (own[i][at, :].astype(F32) + total).astype(BF16)
 
 
 def aggregate(src, counts, me, arrived, tiles, features, chunk, nfeat, which):
     nblocks, per = tiles.shape[:2]
     group = nblocks // nfeat
-    piece = jax.ShapeDtypeStruct((group * BLK, BLK), BF16)
+    which = [k if isinstance(k, tuple) else (k, 0, group) for k in which]
+    sizes = [high - low for _, low, high in which]
     hbm = pl.BlockSpec(memory_space=pltpu.HBM)
     vmem = pl.BlockSpec(memory_space=pltpu.VMEM)
     load = chunk == 0
@@ -119,16 +122,14 @@
             grid=(),
             in_specs=[pl.BlockSpec(memory_space=pl.ANY) if load else vmem, hbm, hbm],
             out_specs=[vmem] * len(which),
-            scratch_shapes=[
-                pltpu.VMEM((len(which), group, per, BLK, BLK), BF16),
-                pltpu.VMEM((len(which), group * BLK, BLK), BF16),
-                pltpu.SemaphoreType.DMA((1 + 2 * len(which),)),
-            ]
+            scratch_shapes=[pltpu.VMEM((n, per, BLK, BLK), BF16) for n in sizes]
+            + [pltpu.VMEM((n * BLK, BLK), BF16) for n in sizes]
+            + [pltpu.SemaphoreType.DMA((1 + 2 * len(which),))]
             + [pltpu.VMEM(arrived.shape, BF16)] * load,
         ),
-        out_shape=[piece] * len(which),
+        out_shape=[jax.ShapeDtypeStruct((n * BLK, BLK), BF16) for n in sizes],
         compiler_params=params(14),
-        cost_estimate=cost(len(which) * group * per * 2 * BLK**3, 8 * MIB),
+        cost_estimate=cost(sum(sizes) * per * 2 * BLK**3, 8 * MIB),
         name="aggregate",
     )(src, counts, me, arrived, in_hbm(tiles), in_hbm(features))
 
@@ -178,8 +179,11 @@
 
 
 def dense_kernel(nfeat, *refs):
-    pieces, (weights, bias, second, hidden, proj) = refs[: 2 * nfeat], refs[2 * nfeat :]
-    order = [pieces[i * nfeat + k][...] for k in range(nfeat) for i in range(2)]
+    pieces, (weights, bias, second, hidden, proj) = refs[: 2 * nfeat + 1], refs[2 * nfeat + 1 :]
+    first, (own, low, high, *others) = pieces[:nfeat], pieces[nfeat:]
+    half = jnp.where(pl.program_id(0) == 0, low[...], high[...])
+    last = [own[...], half] + [piece[...] for piece in others]
+    order = [x for k in range(nfeat) for x in (first[k][...], last[k])]
     pre = dot(weights[...], jnp.concatenate(order, 1), NT)
     hid = jnp.maximum(pre + bias[...], 0.0).astype(BF16)
     hidden[...] = hid
@@ -192,11 +196,14 @@
     nodes, nfeat = pieces[0].shape[0], len(pieces) // 2
     hid, width = weights.shape
     grades = second.shape[0]
-    step = 512
+    step = nodes // 2
     return pl.pallas_call(
         functools.partial(dense_kernel, nfeat),
-        grid=(nodes // step,),
-        in_specs=[pl.BlockSpec((step, BLK), lambda g: (g, 0))] * (2 * nfeat)
+        grid=(2,),
+        in_specs=[
+            pl.BlockSpec((step, BLK), lambda g, n=piece.shape[0]: (g * (n // nodes), 0))
+            for piece in pieces
+        ]
         + [
             pl.BlockSpec((hid, width), lambda g: (0, 0)),
             pl.BlockSpec((hid, 1), lambda g: (0, 0)),
@@ -394,9 +401,12 @@
     pieces, out = refs[:-1], refs[-1]
     nfeat = len(pieces) // 2
     rows = dpre[...].reshape(-1, dpre.shape[-1])
+    first, (own, low, high, *others) = pieces[:nfeat], pieces[nfeat:]
+    middle = jnp.concatenate([low[...], high[...]], 0)
+    last = [own[...], middle] + [piece[...] for piece in others]
     for i, k in enumerate(ORDER):
         owner = lax.rem(me[0] + nfeat - k, nfeat)
-        both = jnp.concatenate([pieces[i][...], pieces[nfeat + i][...]], 1)
+        both = jnp.concatenate([first[i][...], last[i]], 1)
         grad = dot(rows, both, NN).astype(BF16)
         out[:, owner] = grad.reshape(out.shape[0], out.shape[2], out.shape[3])
 
@@ -414,7 +424,7 @@
             in_specs=[
                 pl.BlockSpec((parts // 2, 1, cols, nodes), lambda g, m, s: (0, s[0], 0, 0))
             ]
-            + [vmem] * (2 * nfeat),
+            + [vmem] * len(pieces),
             out_specs=pl.BlockSpec(
                 (parts // 2, nfeat, cols, 2 * BLK), lambda g, m, s: (0, 0, 0, 0)
             ),
@@ -576,9 +586,13 @@
     arrived[1], weights, second_t, bias, second, first = lax.optimization_barrier(
         (arrived[1], weights, second_t, bias, second, first)
     )
-    sent = make(arrived[1], tiles, features, 1, nfeat, others)
+    far = nblocks // nfeat // 2
+    high, low, one, three = make(
+        arrived[1], tiles, features, 1, nfeat, ((2, far, 2 * far), (2, 0, far), 1, 3)
+    )
+    high = ahead(high, 3)
     last = list(make(arrived[1], tiles, features, 1, nfeat, (0,)))
-    last += [ahead(piece, k) for k, piece in zip(others, sent)]
+    last += [ahead(low, 2), ahead(high, 3), ahead(one, 1), ahead(three, 3)]
     hidden, proj = dense(first + last, weights, bias, second_t)
 
     projs = [proj] + [ahead(proj, k) for k in range(1, nfeat)]

time: 189 us -> 190 us (level)
  starting transfers between devices: 37.1 us -> 42.1 us
  waiting for transfers between devices: 46.5 us -> 43 us
    ppermute x12 -> x14, starting transfers between devices: 18.2 us -> 22.4 us  [ahead(): return lax.ppermute(x, 'feat', [(i, (i + k) % nfeat) for i in range(nfeat)])]
    ppermute x12 -> x14, waiting for transfers between devices: 38 us -> 34.5 us  [ahead(): return lax.ppermute(x, 'feat', [(i, (i + k) % nfeat) for i in range(nfeat)])]
  transfers between devices with their start and end apart: 17 -> 19, of which waited for: 12 -> 12; matrix products, arithmetic and copies ran while one was open for 0% -> 0% of each run, Pallas kernels for 8% -> 8%
where the time goes in v12:
time: 190 us; the launch traced here: 189 us
  blocking collectives  58.4 us (31%)
  waiting for transfers between devices  43 us (23%)
  starting transfers between devices  42.1 us (22%)
  Pallas kernels  40.2 us (21%)
  local copies, waits for them, and re-layouts  4.65 us (2%)
    ppermute x14, waiting for transfers between devices, ahead(): return lax.ppermute(x, 'feat', [(i, (i + k) % nfeat) for i in range(nfeat)])  34.5 us
    all_to_all x2, blocking collectives, swap(): lax.all_to_all(shaped, 'nodes', split_axis=0, concat_axis=0, tiled=True)  29.9 us
    all_to_all x1, blocking collectives, shards(): lax.all_to_all(big.reshape(parts // 2 * nfeat, *big.shape[2:]), ('nodes',...  28.4 us
    ppermute x14, starting transfers between devices, ahead(): return lax.ppermute(x, 'feat', [(i, (i + k) % nfeat) for i in range(nfeat)])  22.4 us
    all_to_all x2, starting transfers between devices, swap(): lax.all_to_all(shaped, 'nodes', split_axis=0, concat_axis=0, tiled=True)  17.1 us
    pallas_call x3, Pallas kernels, aggregate(): pl.pallas_call(functools.partial(agg_kernel, which, chunk, nfeat), grid_s...  10.7 us
    all_to_all x2, waiting for transfers between devices, swap(): lax.all_to_all(shaped, 'nodes', split_axis=0, concat_axis=0, tiled=True)  7.68 us
    pallas_call x2, Pallas kernels, pick(): pl.pallas_call(functools.partial(pick_kernel, chunk), grid_spec=pltpu.Pre...  6.54 us
  transfers between devices with their start and end apart: 19, of which 12 were waited for; matrix products, arithmetic and copies ran while one was open for 0% of the time, Pallas kernels for 8%

profile of v12, /device:TPU:1, one launch (start us, length us, event | category | flops | bytes accessed | tf_op | source)
XLA Modules:
  0.0 189.3 jit_solution(2077470757611927930)
XLA Ops:
  0.6 0.8 copy.15
  1.4 0.6 reshape.58.table
  2.0 3.3 %pick.3 = bf16[64,128,128]{2,1,0:T(8,128)(2,1)} custom-call(s32[64]{0:T(128)} %reshape.58.table, bf16[4096,256]{1,0:T(8,128)(2,1)} %features.9), custom_call_target="tpu_custom_call" | custom-call | bytes 4194304 | tf_op jit(solution)/shard_map/pick/pallas_call | solution.py:52
  5.3 0.0 copy-start.13
  5.3 0.0 copy-start.10
  5.3 0.0 copy-start.11
  5.3 9.8 %all-to-all-start = ((bf16[32,2,128,128]{3,2,1,0:T(8,128)(2,1)}), bf16[32,2,128,128]{3,2,1,0:T(8,128)(2,1)}, u32[]{:S(2)}, u32[]{:S(2)}) async-start(bf16[32,2,128,128]{3,2,1,0:T(8,128)(2,1)} %bitcast.31), calls=%async_computation | async-start | bytes 4194304 | tf_op jit(solution)/shard_map/all_to_all | solution.py:562
  15.2 0.2 copy.16
  15.5 2.8 %collective-permute-start = (bf16[1056,256]{1,0:T(8,128)(2,1)S(1)}, bf16[1056,256]{1,0:T(8,128)(2,1)}, u32[]{:S(2)}, u32[]{:S(2)}) collective-permute-start(bf16[1056,256]{1,0:T(8,128)(2,1)S(1)} %pad_maximum_fusion.refs_0_), channel_id=1, source_target_pairs={{0,2},{1,3},{2,0},{3,1},{4,6},{5,7},{6,4},{7,5},{8,10},{9,11},{10,... | collective-permute-start | bytes 1622024 | tf_op jit(solution)/shard_map/ppermute | solution.py:555
  18.3 0.3 collective-permute-start.1
  18.6 2.4 %collective-permute-start.2 = (bf16[1056,256]{1,0:T(8,128)(2,1)S(1)}, bf16[1056,256]{1,0:T(8,128)(2,1)}, u32[]{:S(2)}, u32[]{:S(2)}) collective-permute-start(bf16[1056,256]{1,0:T(8,128)(2,1)S(1)} %pad_maximum_fusion.refs_0_), channel_id=1, source_target_pairs={{0,3},{1,0},{2,1},{3,2},{4,7},{5,4},{6,5},{7,6},{8,11},{9,8},{10,9... | collective-permute-start | bytes 1622024 | tf_op jit(solution)/shard_map/ppermute | solution.py:555
  21.0 3.3 %pick.2 = bf16[64,128,128]{2,1,0:T(8,128)(2,1)} custom-call(s32[64]{0:T(128)} %reshape.58.table, bf16[4096,256]{1,0:T(8,128)(2,1)} %features.9), custom_call_target="tpu_custom_call" | custom-call | bytes 4194304 | tf_op jit(solution)/shard_map/pick/pallas_call | solution.py:52
  24.3 6.5 %collective-permute-done.refs_1_ = bf16[1056,256]{1,0:T(8,128)(2,1)} collective-permute-done((bf16[1056,256]{1,0:T(8,128)(2,1)S(1)}, bf16[1056,256]{1,0:T(8,128)(2,1)}, u32[]{:S(2)}, u32[]{:S(2)}) %collective-permute-start) | collective-permute-done | bytes 540704 | tf_op jit(solution)/shard_map/ppermute | solution.py:555
  30.8 12.2 %collective-permute-done.1.refs_2_ = bf16[1056,256]{1,0:T(8,128)(2,1)} collective-permute-done((bf16[1056,256]{1,0:T(8,128)(2,1)S(1)}, bf16[1056,256]{1,0:T(8,128)(2,1)}, u32[]{:S(2)}, u32[]{:S(2)}) %collective-permute-start.1) | collective-permute-done | bytes 540704 | tf_op jit(solution)/shard_map/ppermute | solution.py:555
  43.0 0.0 collective-permute-done.2.refs_3_
  43.0 0.5 all-to-all-done
  43.5 7.3 %all-to-all-start.1 = ((bf16[32,2,128,128]{3,2,1,0:T(8,128)(2,1)}), bf16[32,2,128,128]{3,2,1,0:T(8,128)(2,1)S(1)}, u32[]{:S(2)}, u32[]{:S(2)}) async-start(bf16[32,2,128,128]{3,2,1,0:T(8,128)(2,1)} %bitcast.30), calls=%async_computation.1 | async-start | bytes 4194304 | tf_op jit(solution)/shard_map/all_to_all | solution.py:562
  50.8 0.1 copy.17
  50.9 0.1 reshape.62.src
  51.0 5.2 %aggregate.3 = (bf16[1024,128]{1,0:T(8,128)(2,1)}, bf16[1024,128]{1,0:T(8,128)(2,1)}, bf16[1024,128]{1,0:T(8,128)(2,1)}, bf16[1024,128]{1,0:T(8,128)(2,1)S(1)}) custom-call(s32[128]{0:T(128)S(1)} %reshape.62.src, s32[32]{0:T(128)S(1)} %bitcast.26, s32[1]{0:T(128)} %bitcast.6.me, bf16[64,128,128]{2,1,0:T(8,128)(2,1)} %bitcast.3.arrived, ...), custom_call_target="tpu_custom_call" | custom-call | flops 536870912 | bytes 8388608 | tf_op jit(solution)/shard_map/aggregate/pallas_call | solution.py:118
  56.1 1.8 collective-permute-start.3
  58.0 1.2 collective-permute-start.4
  59.1 1.5 collective-permute-start.5
  60.7 2.0 %assemble.1 = (bf16[1024,1024]{1,0:T(8,128)(2,1)S(1)}, bf16[16,1024]{1,0:T(8,128)(2,1)S(1)}, bf16[1024,16]{1,0:T(8,128)(2,1)S(1)}, f32[1024,1]{1,0:T(8,128)S(1)}) custom-call(s32[1]{0:T(128)} %bitcast.6.me, bf16[1056,256]{1,0:T(8,128)(2,1)S(1)} %pad_maximum_fusion.refs_0_, bf16[1056,256]{1,0:T(8,128)(2,1)} %collective-permute-done.refs_1_, ...), custom_call_target="tpu_custom_call" | custom-call | bytes 5242880 | tf_op jit(solution)/shard_map/assemble/pallas_call | solution.py:160
  62.7 0.7 copy-done.1
  63.4 1.3 copy-done.6
  64.7 0.8 copy-done.8
  65.5 0.1 collective-permute-done.3.refs_1_
  65.7 6.2 %collective-permute-done.4.refs_2_ = bf16[1024,128]{1,0:T(8,128)(2,1)} collective-permute-done((bf16[1024,128]{1,0:T(8,128)(2,1)}, bf16[1024,128]{1,0:T(8,128)(2,1)}, u32[]{:S(2)}, u32[]{:S(2)}) %collective-permute-start.4) | collective-permute-done | bytes 262176 | tf_op jit(solution)/shard_map/ppermute | solution.py:555
  71.9 0.0 collective-permute-done.5.refs_3_
  71.9 7.2 %all-to-all-done.1 = bf16[32,2,128,128]{3,2,1,0:T(8,128)(2,1)S(1)} async-done(((bf16[32,2,128,128]{3,2,1,0:T(8,128)(2,1)}), bf16[32,2,128,128]{3,2,1,0:T(8,128)(2,1)S(1)}, u32[]{:S(2)}, u32[]{:S(2)}) %all-to-all-start.1) | async-done | bytes 2097184 | tf_op jit(solution)/shard_map/all_to_all | solution.py:562
  79.1 3.3 %aggregate.5 = (bf16[512,128]{1,0:T(8,128)(2,1)S(1)}, bf16[512,128]{1,0:T(8,128)(2,1)S(1)}, bf16[1024,128]{1,0:T(8,128)(2,1)S(1)}, bf16[1024,128]{1,0:T(8,128)(2,1)S(1)}) custom-call(s32[128]{0:T(128)S(1)} %reshape.62.src, s32[32]{0:T(128)S(1)} %bitcast.27, s32[1]{0:T(128)} %bitcast.6.me, bf16[64,128,128]{2,1,0:T(8,128)(2,1)S(1)} %bitcast.19, ...), custom_call_target="tpu_custom_call" | custom-call | flops 402653184 | bytes 8388608 | tf_op jit(solution)/shard_map/aggregate/pallas_call | solution.py:118
  82.3 2.4 %collective-permute-start.7 = (bf16[512,128]{1,0:T(8,128)(2,1)S(1)}, bf16[512,128]{1,0:T(8,128)(2,1)S(1)}, u32[]{:S(2)}, u32[]{:S(2)}) collective-permute-start(bf16[512,128]{1,0:T(8,128)(2,1)S(1)} %get-tuple-element.71), channel_id=1, source_target_pairs={{0,3},{1,0},{2,1},{3,2},{4,7},{5,4},{6,5},{7,6},{8,11},{9,8},{10,9... | collective-permute-start | bytes 393224 | tf_op jit(solution)/shard_map/ppermute | solution.py:555
  84.8 0.1 collective-permute-start.10
  84.8 1.4 collective-permute-start.9
  86.2 0.6 collective-permute-start.6
  86.8 3.3 %collective-permute-start.8 = (bf16[512,128]{1,0:T(8,128)(2,1)S(1)}, bf16[512,128]{1,0:T(8,128)(2,1)S(1)}, u32[]{:S(2)}, u32[]{:S(2)}) collective-permute-start(bf16[512,128]{1,0:T(8,128)(2,1)S(1)} %collective-permute-done.7), channel_id=1, source_target_pairs={{0,3},{1,0},{2,1},{3,2},{4,7},{5,4},{6,5},{7,6},{8,11},{9,8},{10,9... | collective-permute-start | bytes 393224 | tf_op jit(solution)/shard_map/ppermute | solution.py:555
  90.1 2.3 %aggregate.4.refs_4_ = bf16[1024,128]{1,0:T(8,128)(2,1)S(1)} custom-call(s32[128]{0:T(128)S(1)} %reshape.62.src, s32[32]{0:T(128)S(1)} %bitcast.28, s32[1]{0:T(128)} %bitcast.6.me, bf16[64,128,128]{2,1,0:T(8,128)(2,1)S(1)} %bitcast.20, bf16[32,4,128,128]{3,2,1,0:T(8,128)(2,1)} %tiles.1, bf16[4096,256]{1,0:T(8,128)(2,1)} %features.9), custom_call_target="tpu_custom_call" | custom-call | flops 134217728 | bytes 8388608 | tf_op jit(solution)/shard_map/aggregate/pallas_call | solution.py:118
  92.4 0.0 copy-start.4
  92.5 0.0 copy-start.3
  92.5 1.8 collective-permute-done.6.refs_5_
  94.3 3.7 %collective-permute-done.8.refs_6_ = bf16[512,128]{1,0:T(8,128)(2,1)S(1)} collective-permute-done((bf16[512,128]{1,0:T(8,128)(2,1)S(1)}, bf16[512,128]{1,0:T(8,128)(2,1)S(1)}, u32[]{:S(2)}, u32[]{:S(2)}) %collective-permute-start.8) | collective-permute-done | bytes 131104 | tf_op jit(solution)/shard_map/ppermute | solution.py:555
  98.0 0.0 copy-start
  98.0 4.0 %dense.1 = (bf16[1024,1024]{1,0:T(8,128)(2,1)S(1)}, f32[8,16,128]{2,1,0:T(8,128)S(1)}) custom-call(bf16[1024,128]{1,0:T(8,128)(2,1)S(1)} %get-tuple-element.65.refs_0_, bf16[1024,128]{1,0:T(8,128)(2,1)S(1)} %collective-permute-done.3.refs_1_, bf16[1024,128]{1,0:T(8,128)(2,1)} %collective-permute-done.4.refs_2_, ...), custom_call_target="tpu_custom_call" | custom-call | flops 2147483648 | bytes 7340032 | tf_op jit(solution)/shard_map/dense/pallas_call | solution.py:200
  102.0 1.1 collective-permute-start.11
  103.1 3.6 %collective-permute-start.12 = (f32[8,16,128]{2,1,0:T(8,128)S(1)}, f32[8,16,128]{2,1,0:T(8,128)S(1)}, u32[]{:S(2)}, u32[]{:S(2)}) collective-permute-start(f32[8,16,128]{2,1,0:T(8,128)S(1)} %get-tuple-element.77.p0), channel_id=1, source_target_pairs={{0,2},{1,3},{2,0},{3,1},{4,6},{5,7},{6,4},{7,5},{8,10},{9,11},{10,... | collective-permute-start | bytes 196616 | tf_op jit(solution)/shard_map/ppermute | solution.py:555
  106.6 0.5 collective-permute-done.11.p1
  107.1 1.9 %collective-permute-done.12.p2 = f32[8,16,128]{2,1,0:T(8,128)S(1)} collective-permute-done((f32[8,16,128]{2,1,0:T(8,128)S(1)}, f32[8,16,128]{2,1,0:T(8,128)S(1)}, u32[]{:S(2)}, u32[]{:S(2)}) %collective-permute-start.12) | collective-permute-done | bytes 65568 | tf_op jit(solution)/shard_map/ppermute | solution.py:555
  109.1 1.4 collective-permute-done.13.p3
  110.5 0.7 spread.1
  111.2 17.5 %all_to_all.25 = f32[32,2,16,128]{3,2,1,0:T(8,128)S(1)} all-to-all(f32[32,2,16,128]{3,2,1,0:T(8,128)S(1)} %bitcast.23), channel_id=1, replica_groups=mesh['nodes'=32,'feat'=4] {'nodes'}, dimensions={0} | all-to-all | bytes 1048576 | tf_op jit(solution)/shard_map/all_to_all | solution.py:562
  128.7 3.9 %logits.1 = (f32[8,16,128]{2,1,0:T(8,128)S(1)}, bf16[64,16,128]{2,1,0:T(8,128)(2,1)S(1)}) custom-call(s32[128]{0:T(128)S(1)} %reshape.62.src, s32[32]{0:T(128)S(1)} %bitcast.29, s32[1]{0:T(128)} %bitcast.6.me, f32[64,16,128]{2,1,0:T(8,128)S(1)} %bitcast.21, f32[32,16,128]{2,1,0:T(8,128)S(1)} %get-tuple-element.79.own, s32[32,1,128]{2,1,0:T(1,128)S(1)} %bitcast.25, ...), custom_call_target="tpu_custom_call" | custom-call | flops 268435456 | bytes 6291456 | tf_op jit(solution)/shard_map/logits/pallas_call | solution.py:311
  132.6 12.4 %all_to_all.26 = bf16[32,2,16,128]{3,2,1,0:T(8,128)(2,1)S(1)} all-to-all(bf16[32,2,16,128]{3,2,1,0:T(8,128)(2,1)S(1)} %bitcast.24), channel_id=1, replica_groups=mesh['nodes'=32,'feat'=4] {'nodes'}, dimensions={0} | all-to-all | bytes 524288 | tf_op jit(solution)/shard_map/all_to_all | solution.py:562
  145.1 3.7 %small_gradients.1 = (bf16[1024,1024]{1,0:T(8,128)(2,1)}, f32[24,1024]{1,0:T(8,128)S(1)}) custom-call(s32[64]{0:T(128)S(1)} %copy-done.4, s32[1]{0:T(128)} %bitcast.6.me, bf16[64,16,128]{2,1,0:T(8,128)(2,1)S(1)} %bitcast.22, f32[8,16,128]{2,1,0:T(8,128)S(1)} %get-tuple-element.81.dlog, bf16[1024,1024]{1,0:T(8,128)(2,1)S(1)} %get-tuple-element.82.hidden, ...), custom_call_target="tpu_custom_call" | custom-call | flops 536870912 | bytes 4194304 | tf_op jit(solution)/shard_map/small_gradients/pallas_call | solution.py:370
  148.7 2.6 %big_gradient.3 = bf16[16,4,32,256]{3,2,1,0:T(8,128)(2,1)S(1)} custom-call(s32[1]{0:T(128)} %bitcast.6.me, s32[1]{0:T(128)S(6)} %sub.12.side, bf16[16,2,32,1024]{3,2,1,0:T(8,128)(2,1)} %bitcast.32, bf16[1024,128]{1,0:T(8,128)(2,1)S(1)} %get-tuple-element.65.refs_0_, bf16[1024,128]{1,0:T(8,128)(2,1)S(1)} %collective-permute-done.3.refs_1_, ...), custom_call_target="tpu_custom_call" | custom-call | flops 1073741824 | bytes 4194304 | tf_op jit(solution)/shard_map/big_gradient/pallas_call | solution.py:419
  151.3 0.3 collective-permute-start.14
  151.6 0.3 collective-permute-start.15
  151.9 2.6 %big_gradient.2.a = bf16[16,4,32,256]{3,2,1,0:T(8,128)(2,1)S(1)} custom-call(s32[1]{0:T(128)} %bitcast.6.me, s32[1]{0:T(128)} %bitcast.4.side, bf16[16,2,32,1024]{3,2,1,0:T(8,128)(2,1)} %bitcast.33, bf16[1024,128]{1,0:T(8,128)(2,1)S(1)} %get-tuple-element.65.refs_0_, bf16[1024,128]{1,0:T(8,128)(2,1)S(1)} %collective-permute-done.3.refs_1_, ...), custom_call_target="tpu_custom_call" | custom-call | flops 1073741824 | bytes 4194304 | tf_op jit(solution)/shard_map/big_gradient/pallas_call | solution.py:419
  154.6 1.9 join.1
  156.4 28.4 %all_to_all.27.arrived = bf16[64,48,256]{2,1,0:T(8,128)(2,1)S(1)} all-to-all(bf16[64,48,256]{2,1,0:T(8,128)(2,1)} %bitcast.34), channel_id=1, replica_groups={{0,1,2,3,8,9,10,11,16,17,18,19,24,25,26,27,32,33,34,35,40,41,42,43,48,4..., dimensions={0} | all-to-all | bytes 3145728 | tf_op jit(solution)/shard_map/all_to_all | solution.py:608
  184.9 1.0 total.1
  185.8 2.0 %collective-permute-start.16 = (f32[16,256]{1,0:T(8,128)S(1)}, f32[16,256]{1,0:T(8,128)S(1)}, u32[]{:S(2)}, u32[]{:S(2)}) collective-permute-start(f32[16,256]{1,0:T(8,128)S(1)} %get-tuple-element.88.a), channel_id=1, source_target_pairs={{0,4},{4,0},{8,12},{12,8},{16,20},{20,16},{24,28},{28,24},{32,36},... | collective-permute-start | bytes 49160 | tf_op jit(solution)/shard_map/ppermute | solution.py:558
  187.8 0.8 collective-permute-done.16.b
  188.7 0.6 finish.1
  (31 shorter events, 0.1 us)
Async XLA Ops:
  5.3 9.8 %copy-start.13 = (f32[256]{0:T(256)S(1)}, f32[256]{0:T(256)}, u32[]{:S(2)}) copy-start(f32[256]{0:T(256)} %param.16) | copy-start | bytes 3076
  5.3 9.9 %copy-start.10 = (bf16[256,1024]{1,0:T(8,128)(2,1)S(1)}, bf16[256,1024]{1,0:T(8,128)(2,1)}, u32[]{:S(2)}) copy-start(bf16[256,1024]{1,0:T(8,128)(2,1)} %param.15) | copy-start | bytes 1572868
  5.3 10.1 %copy-start.11 = (bf16[256,16]{0,1:T(8,128)(2,1)S(1)}, bf16[256,16]{0,1:T(8,128)(2,1)}, u32[]{:S(2)}) copy-start(bf16[256,16]{0,1:T(8,128)(2,1)} %param.17) | copy-start | bytes 24580
  5.3 38.2 %all-to-all-start = ((bf16[32,2,128,128]{3,2,1,0:T(8,128)(2,1)}), bf16[32,2,128,128]{3,2,1,0:T(8,128)(2,1)}, u32[]{:S(2)}, u32[]{:S(2)}) async-start(bf16[32,2,128,128]{3,2,1,0:T(8,128)(2,1)} %bitcast.31), calls=%async_computation | async-start | bytes 4194304 | tf_op jit(solution)/shard_map/all_to_all | solution.py:562
  15.5 15.3 %collective-permute-start = (bf16[1056,256]{1,0:T(8,128)(2,1)S(1)}, bf16[1056,256]{1,0:T(8,128)(2,1)}, u32[]{:S(2)}, u32[]{:S(2)}) collective-permute-start(bf16[1056,256]{1,0:T(8,128)(2,1)S(1)} %pad_maximum_fusion.refs_0_), channel_id=1, source_target_pairs={{0,2},{1,3},{2,0},{3,1},{4,6},{5,7},{6,4},{7,5},{8,10},{9,11},{10,... | collective-permute-start | bytes 1622024 | tf_op jit(solution)/shard_map/ppermute | solution.py:555
  18.3 24.6 %collective-permute-start.1 = (bf16[1056,256]{1,0:T(8,128)(2,1)S(1)}, bf16[1056,256]{1,0:T(8,128)(2,1)}, u32[]{:S(2)}, u32[]{:S(2)}) collective-permute-start(bf16[1056,256]{1,0:T(8,128)(2,1)S(1)} %pad_maximum_fusion.refs_0_), channel_id=1, source_target_pairs={{0,1},{1,2},{2,3},{3,0},{4,5},{5,6},{6,7},{7,4},{8,9},{9,10},{10,1... | collective-permute-start | bytes 1622024 | tf_op jit(solution)/shard_map/ppermute | solution.py:555
  18.6 24.3 %collective-permute-start.2 = (bf16[1056,256]{1,0:T(8,128)(2,1)S(1)}, bf16[1056,256]{1,0:T(8,128)(2,1)}, u32[]{:S(2)}, u32[]{:S(2)}) collective-permute-start(bf16[1056,256]{1,0:T(8,128)(2,1)S(1)} %pad_maximum_fusion.refs_0_), channel_id=1, source_target_pairs={{0,3},{1,0},{2,1},{3,2},{4,7},{5,4},{6,5},{7,6},{8,11},{9,8},{10,9... | collective-permute-start | bytes 1622024 | tf_op jit(solution)/shard_map/ppermute | solution.py:555
  43.5 7.3 %copy-start.12 = (s32[32,4]{0,1:T(4,128)S(1)}, s32[32,4]{0,1:T(4,128)}, u32[]{:S(2)}) copy-start(s32[32,4]{0,1:T(4,128)} %param.12) | copy-start | bytes 1540
  43.5 7.5 %copy-start.5 = (s32[1,32]{1,0:T(1,128)S(1)}, s32[1,32]{1,0:T(1,128)}, u32[]{:S(2)}) copy-start(s32[1,32]{1,0:T(1,128)} %param.10) | copy-start | bytes 388
  43.5 35.6 %all-to-all-start.1 = ((bf16[32,2,128,128]{3,2,1,0:T(8,128)(2,1)}), bf16[32,2,128,128]{3,2,1,0:T(8,128)(2,1)S(1)}, u32[]{:S(2)}, u32[]{:S(2)}) async-start(bf16[32,2,128,128]{3,2,1,0:T(8,128)(2,1)} %bitcast.30), calls=%async_computation.1 | async-start | bytes 4194304 | tf_op jit(solution)/shard_map/all_to_all | solution.py:562
  56.1 9.5 %collective-permute-start.3 = (bf16[1024,128]{1,0:T(8,128)(2,1)}, bf16[1024,128]{1,0:T(8,128)(2,1)S(1)}, u32[]{:S(2)}, u32[]{:S(2)}) collective-permute-start(bf16[1024,128]{1,0:T(8,128)(2,1)} %get-tuple-element.62), channel_id=1, source_target_pairs={{0,2},{1,3},{2,0},{3,1},{4,6},{5,7},{6,4},{7,5},{8,10},{9,11},{10,... | collective-permute-start | bytes 786440 | tf_op jit(solution)/shard_map/ppermute | solution.py:555
  58.0 13.9 %collective-permute-start.4 = (bf16[1024,128]{1,0:T(8,128)(2,1)}, bf16[1024,128]{1,0:T(8,128)(2,1)}, u32[]{:S(2)}, u32[]{:S(2)}) collective-permute-start(bf16[1024,128]{1,0:T(8,128)(2,1)} %get-tuple-element.63), channel_id=1, source_target_pairs={{0,1},{1,2},{2,3},{3,0},{4,5},{5,6},{6,7},{7,4},{8,9},{9,10},{10,1... | collective-permute-start | bytes 786440 | tf_op jit(solution)/shard_map/ppermute | solution.py:555
  59.1 12.8 %collective-permute-start.5 = (bf16[1024,128]{1,0:T(8,128)(2,1)}, bf16[1024,128]{1,0:T(8,128)(2,1)}, u32[]{:S(2)}, u32[]{:S(2)}) collective-permute-start(bf16[1024,128]{1,0:T(8,128)(2,1)} %get-tuple-element.64), channel_id=1, source_target_pairs={{0,3},{1,0},{2,1},{3,2},{4,7},{5,4},{6,5},{7,6},{8,11},{9,8},{10,9... | collective-permute-start | bytes 786440 | tf_op jit(solution)/shard_map/ppermute | solution.py:555
  62.7 0.7 copy-start.1
  63.4 1.3 copy-start.6
  64.7 0.8 copy-start.8
  82.3 4.5 %collective-permute-start.7 = (bf16[512,128]{1,0:T(8,128)(2,1)S(1)}, bf16[512,128]{1,0:T(8,128)(2,1)S(1)}, u32[]{:S(2)}, u32[]{:S(2)}) collective-permute-start(bf16[512,128]{1,0:T(8,128)(2,1)S(1)} %get-tuple-element.71), channel_id=1, source_target_pairs={{0,3},{1,0},{2,1},{3,2},{4,7},{5,4},{6,5},{7,6},{8,11},{9,8},{10,9... | collective-permute-start | bytes 393224 | tf_op jit(solution)/shard_map/ppermute | solution.py:555
  84.8 13.2 %collective-permute-start.10 = (bf16[1024,128]{1,0:T(8,128)(2,1)S(1)}, bf16[1024,128]{1,0:T(8,128)(2,1)S(1)}, u32[]{:S(2)}, u32[]{:S(2)}) collective-permute-start(bf16[1024,128]{1,0:T(8,128)(2,1)S(1)} %get-tuple-element.73), channel_id=1, source_target_pairs={{0,3},{1,0},{2,1},{3,2},{4,7},{5,4},{6,5},{7,6},{8,11},{9,8},{10,9... | collective-permute-start | bytes 786440 | tf_op jit(solution)/shard_map/ppermute | solution.py:555
  84.8 13.1 %collective-permute-start.9 = (bf16[1024,128]{1,0:T(8,128)(2,1)S(1)}, bf16[1024,128]{1,0:T(8,128)(2,1)S(1)}, u32[]{:S(2)}, u32[]{:S(2)}) collective-permute-start(bf16[1024,128]{1,0:T(8,128)(2,1)S(1)} %get-tuple-element.72), channel_id=1, source_target_pairs={{0,1},{1,2},{2,3},{3,0},{4,5},{5,6},{6,7},{7,4},{8,9},{9,10},{10,1... | collective-permute-start | bytes 786440 | tf_op jit(solution)/shard_map/ppermute | solution.py:555
  86.2 11.7 %copy-start.7 = (bf16[1024,1024]{1,0:T(8,128)(2,1)S(1)}, bf16[1024,1024]{1,0:T(8,128)(2,1)}, u32[]{:S(2)}) copy-start(bf16[1024,1024]{1,0:T(8,128)(2,1)} %copy-done.6) | copy-start | bytes 6291460
  86.2 11.7 %copy-start.9 = (f32[1024,1]{1,0:T(8,128)S(1)}, f32[1024,1]{1,0:T(8,128)}, u32[]{:S(2)}) copy-start(f32[1024,1]{1,0:T(8,128)} %copy-done.8) | copy-start | bytes 12292
  86.2 8.0 %collective-permute-start.6 = (bf16[512,128]{1,0:T(8,128)(2,1)S(1)}, bf16[512,128]{1,0:T(8,128)(2,1)S(1)}, u32[]{:S(2)}, u32[]{:S(2)}) collective-permute-start(bf16[512,128]{1,0:T(8,128)(2,1)S(1)} %get-tuple-element.70), channel_id=1, source_target_pairs={{0,2},{1,3},{2,0},{3,1},{4,6},{5,7},{6,4},{7,5},{8,10},{9,11},{10,... | collective-permute-start | bytes 393224 | tf_op jit(solution)/shard_map/ppermute | solution.py:555
  86.8 11.1 %collective-permute-start.8 = (bf16[512,128]{1,0:T(8,128)(2,1)S(1)}, bf16[512,128]{1,0:T(8,128)(2,1)S(1)}, u32[]{:S(2)}, u32[]{:S(2)}) collective-permute-start(bf16[512,128]{1,0:T(8,128)(2,1)S(1)} %collective-permute-done.7), channel_id=1, source_target_pairs={{0,3},{1,0},{2,1},{3,2},{4,7},{5,4},{6,5},{7,6},{8,11},{9,8},{10,9... | collective-permute-start | bytes 393224 | tf_op jit(solution)/shard_map/ppermute | solution.py:555
  92.4 18.1 %copy-start.4 = (s32[64]{0:T(128)S(1)}, s32[64]{0:T(128)}, u32[]{:S(2)}) copy-start(s32[64]{0:T(128)} %reshape.58.table) | copy-start | bytes 772
  92.5 36.3 %copy-start.3 = (s32[4096]{0:T(1024)S(1)}, s32[4096]{0:T(1024)}, u32[]{:S(2)}) copy-start(s32[4096]{0:T(1024)} %param.14) | copy-start | bytes 49156
  98.0 30.7 %copy-start = (bf16[32,4,128,128]{3,2,1,0:T(8,128)(2,1)S(1)}, bf16[32,4,128,128]{3,2,1,0:T(8,128)(2,1)}, u32[]{:S(2)}) copy-start(bf16[32,4,128,128]{3,2,1,0:T(8,128)(2,1)} %tiles.1) | copy-start | bytes 12582916
  102.0 5.1 %collective-permute-start.11 = (f32[8,16,128]{2,1,0:T(8,128)S(1)}, f32[8,16,128]{2,1,0:T(8,128)S(1)}, u32[]{:S(2)}, u32[]{:S(2)}) collective-permute-start(f32[8,16,128]{2,1,0:T(8,128)S(1)} %get-tuple-element.77.p0), channel_id=1, source_target_pairs={{0,1},{1,2},{2,3},{3,0},{4,5},{5,6},{6,7},{7,4},{8,9},{9,10},{10,1... | collective-permute-start | bytes 196616 | tf_op jit(solution)/shard_map/ppermute | solution.py:555
  103.1 6.0 %collective-permute-start.12 = (f32[8,16,128]{2,1,0:T(8,128)S(1)}, f32[8,16,128]{2,1,0:T(8,128)S(1)}, u32[]{:S(2)}, u32[]{:S(2)}) collective-permute-start(f32[8,16,128]{2,1,0:T(8,128)S(1)} %get-tuple-element.77.p0), channel_id=1, source_target_pairs={{0,2},{1,3},{2,0},{3,1},{4,6},{5,7},{6,4},{7,5},{8,10},{9,11},{10,... | collective-permute-start | bytes 196616 | tf_op jit(solution)/shard_map/ppermute | solution.py:555
  106.6 3.9 %collective-permute-start.13 = (f32[8,16,128]{2,1,0:T(8,128)S(1)}, f32[8,16,128]{2,1,0:T(8,128)S(1)}, u32[]{:S(2)}, u32[]{:S(2)}) collective-permute-start(f32[8,16,128]{2,1,0:T(8,128)S(1)} %get-tuple-element.77.p0), channel_id=1, source_target_pairs={{0,3},{1,0},{2,1},{3,2},{4,7},{5,4},{6,5},{7,6},{8,11},{9,8},{10,9... | collective-permute-start | bytes 196616 | tf_op jit(solution)/shard_map/ppermute | solution.py:555
  128.7 16.3 %copy-start.2 = (bf16[1024,16]{1,0:T(8,128)(2,1)S(1)}, bf16[1024,16]{1,0:T(8,128)(2,1)}, u32[]{:S(2)}) copy-start(bf16[1024,16]{1,0:T(8,128)(2,1)} %copy-done.1) | copy-start | bytes 98308
  151.3 3.2 %collective-permute-start.14 = (bf16[16,4,32,256]{3,2,1,0:T(8,128)(2,1)S(1)}, bf16[16,4,32,256]{3,2,1,0:T(8,128)(2,1)S(1)}, u32[]{:S(2)}, u32[]{:S(2)}) collective-permute-start(bf16[16,4,32,256]{3,2,1,0:T(8,128)(2,1)S(1)} %big_gradient.3), channel_id=1, source_target_pairs={{0,4},{4,0},{8,12},{12,8},{16,20},{20,16},{24,28},{28,24},{32,36},... | collective-permute-start | bytes 3145736 | tf_op jit(solution)/shard_map/ppermute | solution.py:558
  151.6 2.9 %collective-permute-start.15 = (f32[24,1024]{1,0:T(8,128)S(1)}, f32[24,1024]{1,0:T(8,128)S(1)}, u32[]{:S(2)}, u32[]{:S(2)}) collective-permute-start(f32[24,1024]{1,0:T(8,128)S(1)} %get-tuple-element.86.small), channel_id=1, source_target_pairs={{0,4},{4,0},{8,12},{12,8},{16,20},{20,16},{24,28},{28,24},{32,36},... | collective-permute-start | bytes 294920 | tf_op jit(solution)/shard_map/ppermute | solution.py:558
  185.8 2.8 %collective-permute-start.16 = (f32[16,256]{1,0:T(8,128)S(1)}, f32[16,256]{1,0:T(8,128)S(1)}, u32[]{:S(2)}, u32[]{:S(2)}) collective-permute-start(f32[16,256]{1,0:T(8,128)S(1)} %get-tuple-element.88.a), channel_id=1, source_target_pairs={{0,4},{4,0},{8,12},{12,8},{16,20},{20,16},{24,28},{28,24},{32,36},... | collective-permute-start | bytes 49160 | tf_op jit(solution)/shard_map/ppermute | solution.py:558

commit v13 on v11

--- a/solution.py
+++ b/solution.py
@@ -224,7 +224,7 @@
 
     @pl.loop(0, out.shape[0], unroll=8)
     def _(k):
-        out[k] = whole[table[k]]
+        out[k] = whole[table[k]].astype(BF16)
 
 
 def spread(table, me, pieces):
@@ -241,7 +241,7 @@
         ),
         out_shape=[
             jax.ShapeDtypeStruct((group * 4, grades, BLK), F32),
-            jax.ShapeDtypeStruct((slots, grades, BLK), F32),
+            jax.ShapeDtypeStruct((slots, grades, BLK), BF16),
         ],
         compiler_params=params(4),
         cost_estimate=cost(0, MIB),
@@ -250,31 +250,24 @@
 
 
 def logits_kernel(
-    scale, src, counts, me, arrived, own, labels, tiles, dlog_out, slots_out, parts, field, grad_b, sums
+    scale, src, counts, me, arrived, own, labels, tiles, dlog_out, slots_out, field, grad_b, sums
 ):
     nblocks, per = tiles.shape[:2]
-    nslots, grades, _ = arrived.shape
+    grades = arrived.shape[1]
     mine = dlog_out.shape[0]
 
     def live_of(slot):
         return jnp.where(lax.rem(slot, 2) < counts[lax.div(slot, 2)], 1.0, 0.0)
-
-    x = arrived[...]
-    for i in range(3):
-        y = x.astype(BF16)
-        parts[:, i * grades : (i + 1) * grades, :] = y
-        x = x - y.astype(F32)
 
     @pl.loop(0, nblocks, unroll=8)
     def _(b):
         rows, weights = [], []
         for t in range(per):
             slot = src[b * per + t]
-            rows.append(parts[slot] * live_of(slot).astype(BF16))
+            rows.append(arrived[slot] * live_of(slot).astype(BF16))
             weights.append(tiles[b, t])
-        triple = dot(jnp.concatenate(rows, 1), jnp.concatenate(weights, 1), NT)
-        field[b] = own[b] + (
-            triple[:grades] + (triple[grades : 2 * grades] + triple[2 * grades :])
+        field[b] = own[b] + dot(
+            jnp.concatenate(rows, 1), jnp.concatenate(weights, 1), NT
         )
 
     expo = jnp.exp(field[...])
@@ -299,7 +292,7 @@
 
 def logits_back(src, counts, me, arrived, own, labels, tiles, scale, nfeat):
     nblocks, per = tiles.shape[:2]
-    nslots, grades, _ = arrived.shape
+    grades = arrived.shape[1]
     vmem = pl.BlockSpec(memory_space=pltpu.VMEM)
     return pl.pallas_call(
         functools.partial(logits_kernel, scale),
@@ -309,7 +302,6 @@
             in_specs=[vmem] * 4,
             out_specs=[vmem] * 2,
             scratch_shapes=[
-                pltpu.VMEM((nslots, 3 * grades, BLK), BF16),
                 pltpu.VMEM((nblocks, grades, BLK), F32),
                 pltpu.VMEM((nblocks, grades, BLK), BF16),
                 pltpu.VMEM(arrived.shape, F32),
@@ -355,16 +347,16 @@
     )
 
 
-def small_gradients(table, me, returned, dlog, hidden, second, nfeat):
+def small_gradients(table, me, returned, dlog, hidden, second, steps):
     hid, nodes = hidden.shape
     group, grades, _ = dlog.shape
-    width = hid // nfeat
+    width = hid // steps
     whole3 = lambda g, t, m: (0, 0, 0)
     return pl.pallas_call(
         small_kernel,
         grid_spec=pltpu.PrefetchScalarGridSpec(
             num_scalar_prefetch=2,
-            grid=(nfeat,),
+            grid=(steps,),
             in_specs=[
                 pl.BlockSpec(returned.shape, whole3),
                 pl.BlockSpec(dlog.shape, whole3),
@@ -587,7 +579,7 @@
     dlog, slotsum = logits_back(
         src, counts, me, swap(send), own, labels.reshape(nblocks, 1, BLK), tiles, scale, nfeat
     )
-    dpre, small = small_gradients(table, me, swap(slotsum), dlog, hidden, second, nfeat)
+    dpre, small = small_gradients(table, me, swap(slotsum), dlog, hidden, second, 2)
     away = nearby(big_gradient(me, there, dpre, first + last, parts))
     big = big_gradient(me, here, dpre, first + last, parts)
     big = join(here, big, away, small, nearby(small))

time: 189 us -> 185 us (0.979)
  blocking collectives: 58.5 us -> 55.8 us
    all_to_all x2, blocking collectives: 29.2 us -> 26.6 us  [swap(): lax.all_to_all(shaped, 'nodes', split_axis=0, concat_axis=0, tiled=True)]
where the time goes in v13:
time: 185 us; the launch traced here: 184 us
  blocking collectives  55.8 us (30%)
  waiting for transfers between devices  46.5 us (25%)
  Pallas kernels  39.2 us (21%)
  starting transfers between devices  37.2 us (20%)
  local copies, waits for them, and re-layouts  4.67 us (3%)
    ppermute x12, waiting for transfers between devices, ahead(): return lax.ppermute(x, 'feat', [(i, (i + k) % nfeat) for i in range(nfeat)])  38 us
    all_to_all x1, blocking collectives, shards(): lax.all_to_all(big.reshape(parts // 2 * nfeat, *big.shape[2:]), ('nodes',...  29.2 us
    all_to_all x2, blocking collectives, swap(): lax.all_to_all(shaped, 'nodes', split_axis=0, concat_axis=0, tiled=True)  26.6 us
    ppermute x12, starting transfers between devices, ahead(): return lax.ppermute(x, 'feat', [(i, (i + k) % nfeat) for i in range(nfeat)])  18.2 us
    all_to_all x2, starting transfers between devices, swap(): lax.all_to_all(shaped, 'nodes', split_axis=0, concat_axis=0, tiled=True)  17.1 us
    pallas_call x3, Pallas kernels, aggregate(): pl.pallas_call(functools.partial(agg_kernel, which, chunk, nfeat), grid_s...  10.7 us
    all_to_all x2, waiting for transfers between devices, swap(): lax.all_to_all(shaped, 'nodes', split_axis=0, concat_axis=0, tiled=True)  7.7 us
    pallas_call x2, Pallas kernels, pick(): pl.pallas_call(functools.partial(pick_kernel, chunk), grid_spec=pltpu.Pre...  6.54 us
  transfers between devices with their start and end apart: 17, of which 12 were waited for; matrix products, arithmetic and copies ran while one was open for 0% of the time, Pallas kernels for 8%

profile of v13, /device:TPU:1, one launch (start us, length us, event | category | flops | bytes accessed | tf_op | source)
XLA Modules:
  0.0 184.4 jit_solution(15756642645736708872)
XLA Ops:
  0.6 0.8 copy.15
  1.4 0.6 reshape.58.table
  2.0 3.3 %pick.3 = bf16[64,128,128]{2,1,0:T(8,128)(2,1)} custom-call(s32[64]{0:T(128)} %reshape.58.table, bf16[4096,256]{1,0:T(8,128)(2,1)} %features.9), custom_call_target="tpu_custom_call" | custom-call | bytes 4194304 | tf_op jit(solution)/shard_map/pick/pallas_call | solution.py:52
  5.3 0.0 copy-start.13
  5.3 0.0 copy-start.10
  5.3 0.0 copy-start.11
  5.3 9.8 %all-to-all-start = ((bf16[32,2,128,128]{3,2,1,0:T(8,128)(2,1)}), bf16[32,2,128,128]{3,2,1,0:T(8,128)(2,1)}, u32[]{:S(2)}, u32[]{:S(2)}) async-start(bf16[32,2,128,128]{3,2,1,0:T(8,128)(2,1)} %bitcast.31), calls=%async_computation | async-start | bytes 4194304 | tf_op jit(solution)/shard_map/all_to_all | solution.py:544
  15.2 0.2 copy.16
  15.5 2.8 %collective-permute-start = (bf16[1056,256]{1,0:T(8,128)(2,1)S(1)}, bf16[1056,256]{1,0:T(8,128)(2,1)}, u32[]{:S(2)}, u32[]{:S(2)}) collective-permute-start(bf16[1056,256]{1,0:T(8,128)(2,1)S(1)} %pad_maximum_fusion.refs_0_), channel_id=1, source_target_pairs={{0,2},{1,3},{2,0},{3,1},{4,6},{5,7},{6,4},{7,5},{8,10},{9,11},{10,... | collective-permute-start | bytes 1622024 | tf_op jit(solution)/shard_map/ppermute | solution.py:537
  18.3 0.3 collective-permute-start.1
  18.6 2.4 %collective-permute-start.2 = (bf16[1056,256]{1,0:T(8,128)(2,1)S(1)}, bf16[1056,256]{1,0:T(8,128)(2,1)}, u32[]{:S(2)}, u32[]{:S(2)}) collective-permute-start(bf16[1056,256]{1,0:T(8,128)(2,1)S(1)} %pad_maximum_fusion.refs_0_), channel_id=1, source_target_pairs={{0,3},{1,0},{2,1},{3,2},{4,7},{5,4},{6,5},{7,6},{8,11},{9,8},{10,9... | collective-permute-start | bytes 1622024 | tf_op jit(solution)/shard_map/ppermute | solution.py:537
  21.0 3.3 %pick.2 = bf16[64,128,128]{2,1,0:T(8,128)(2,1)} custom-call(s32[64]{0:T(128)} %reshape.58.table, bf16[4096,256]{1,0:T(8,128)(2,1)} %features.9), custom_call_target="tpu_custom_call" | custom-call | bytes 4194304 | tf_op jit(solution)/shard_map/pick/pallas_call | solution.py:52
  24.3 6.5 %collective-permute-done.refs_1_ = bf16[1056,256]{1,0:T(8,128)(2,1)} collective-permute-done((bf16[1056,256]{1,0:T(8,128)(2,1)S(1)}, bf16[1056,256]{1,0:T(8,128)(2,1)}, u32[]{:S(2)}, u32[]{:S(2)}) %collective-permute-start) | collective-permute-done | bytes 540704 | tf_op jit(solution)/shard_map/ppermute | solution.py:537
  30.8 12.2 %collective-permute-done.1.refs_2_ = bf16[1056,256]{1,0:T(8,128)(2,1)} collective-permute-done((bf16[1056,256]{1,0:T(8,128)(2,1)S(1)}, bf16[1056,256]{1,0:T(8,128)(2,1)}, u32[]{:S(2)}, u32[]{:S(2)}) %collective-permute-start.1) | collective-permute-done | bytes 540704 | tf_op jit(solution)/shard_map/ppermute | solution.py:537
  43.0 0.0 collective-permute-done.2.refs_3_
  43.0 0.5 all-to-all-done
  43.5 7.3 %all-to-all-start.1 = ((bf16[32,2,128,128]{3,2,1,0:T(8,128)(2,1)}), bf16[32,2,128,128]{3,2,1,0:T(8,128)(2,1)S(1)}, u32[]{:S(2)}, u32[]{:S(2)}) async-start(bf16[32,2,128,128]{3,2,1,0:T(8,128)(2,1)} %bitcast.30), calls=%async_computation.1 | async-start | bytes 4194304 | tf_op jit(solution)/shard_map/all_to_all | solution.py:544
  50.8 0.1 copy.17
  50.9 0.1 reshape.62.src
  51.0 5.1 %aggregate.3 = (bf16[1024,128]{1,0:T(8,128)(2,1)}, bf16[1024,128]{1,0:T(8,128)(2,1)}, bf16[1024,128]{1,0:T(8,128)(2,1)}, bf16[1024,128]{1,0:T(8,128)(2,1)S(1)}) custom-call(s32[128]{0:T(128)S(1)} %reshape.62.src, s32[32]{0:T(128)S(1)} %bitcast.26, s32[1]{0:T(128)} %bitcast.6.me, bf16[64,128,128]{2,1,0:T(8,128)(2,1)} %bitcast.3.arrived, ...), custom_call_target="tpu_custom_call" | custom-call | flops 536870912 | bytes 8388608 | tf_op jit(solution)/shard_map/aggregate/pallas_call | solution.py:115
  56.1 1.8 collective-permute-start.3
  58.0 1.2 collective-permute-start.4
  59.1 1.5 collective-permute-start.5
  60.6 2.0 %assemble.1 = (bf16[1024,1024]{1,0:T(8,128)(2,1)S(1)}, bf16[16,1024]{1,0:T(8,128)(2,1)S(1)}, bf16[1024,16]{1,0:T(8,128)(2,1)S(1)}, f32[1024,1]{1,0:T(8,128)S(1)}) custom-call(s32[1]{0:T(128)} %bitcast.6.me, bf16[1056,256]{1,0:T(8,128)(2,1)S(1)} %pad_maximum_fusion.refs_0_, bf16[1056,256]{1,0:T(8,128)(2,1)} %collective-permute-done.refs_1_, ...), custom_call_target="tpu_custom_call" | custom-call | bytes 5242880 | tf_op jit(solution)/shard_map/assemble/pallas_call | solution.py:159
  62.7 0.7 copy-done.1
  63.4 1.3 copy-done.6
  64.7 0.8 copy-done.8
  65.5 0.1 collective-permute-done.3.refs_1_
  65.6 6.2 %collective-permute-done.4.refs_2_ = bf16[1024,128]{1,0:T(8,128)(2,1)} collective-permute-done((bf16[1024,128]{1,0:T(8,128)(2,1)}, bf16[1024,128]{1,0:T(8,128)(2,1)}, u32[]{:S(2)}, u32[]{:S(2)}) %collective-permute-start.4) | collective-permute-done | bytes 262176 | tf_op jit(solution)/shard_map/ppermute | solution.py:537
  71.9 7.2 %all-to-all-done.1 = bf16[32,2,128,128]{3,2,1,0:T(8,128)(2,1)S(1)} async-done(((bf16[32,2,128,128]{3,2,1,0:T(8,128)(2,1)}), bf16[32,2,128,128]{3,2,1,0:T(8,128)(2,1)S(1)}, u32[]{:S(2)}, u32[]{:S(2)}) %all-to-all-start.1) | async-done | bytes 2097184 | tf_op jit(solution)/shard_map/all_to_all | solution.py:544
  79.1 3.3 %aggregate.5 = (bf16[1024,128]{1,0:T(8,128)(2,1)S(1)}, bf16[1024,128]{1,0:T(8,128)(2,1)S(1)}, bf16[1024,128]{1,0:T(8,128)(2,1)S(1)}) custom-call(s32[128]{0:T(128)S(1)} %reshape.62.src, s32[32]{0:T(128)S(1)} %bitcast.27, s32[1]{0:T(128)} %bitcast.6.me, bf16[64,128,128]{2,1,0:T(8,128)(2,1)S(1)} %bitcast.19, bf16[32,4,128,128]{3,2,1,0:T(8,128)(2,1)} %tiles.1, ...), custom_call_target="tpu_custom_call" | custom-call | flops 402653184 | bytes 8388608 | tf_op jit(solution)/shard_map/aggregate/pallas_call | solution.py:115
  82.3 1.8 %collective-permute-start.6 = (bf16[1024,128]{1,0:T(8,128)(2,1)S(1)}, bf16[1024,128]{1,0:T(8,128)(2,1)S(1)}, u32[]{:S(2)}, u32[]{:S(2)}) collective-permute-start(bf16[1024,128]{1,0:T(8,128)(2,1)S(1)} %get-tuple-element.69), channel_id=1, source_target_pairs={{0,2},{1,3},{2,0},{3,1},{4,6},{5,7},{6,4},{7,5},{8,10},{9,11},{10,... | collective-permute-start | bytes 786440 | tf_op jit(solution)/shard_map/ppermute | solution.py:537
  84.2 1.2 collective-permute-start.7
  85.3 1.5 collective-permute-start.8
  86.9 2.3 %aggregate.4.refs_4_ = bf16[1024,128]{1,0:T(8,128)(2,1)S(1)} custom-call(s32[128]{0:T(128)S(1)} %reshape.62.src, s32[32]{0:T(128)S(1)} %bitcast.28, s32[1]{0:T(128)} %bitcast.6.me, bf16[64,128,128]{2,1,0:T(8,128)(2,1)S(1)} %bitcast.20, bf16[32,4,128,128]{3,2,1,0:T(8,128)(2,1)} %tiles.1, bf16[4096,256]{1,0:T(8,128)(2,1)} %features.9), custom_call_target="tpu_custom_call" | custom-call | flops 134217728 | bytes 8388608 | tf_op jit(solution)/shard_map/aggregate/pallas_call | solution.py:115
  89.2 0.0 copy-start.4
  89.2 0.0 copy-start.3
  89.2 1.7 collective-permute-done.6.refs_5_
  90.9 6.8 %collective-permute-done.7.refs_6_ = bf16[1024,128]{1,0:T(8,128)(2,1)S(1)} collective-permute-done((bf16[1024,128]{1,0:T(8,128)(2,1)S(1)}, bf16[1024,128]{1,0:T(8,128)(2,1)S(1)}, u32[]{:S(2)}, u32[]{:S(2)}) %collective-permute-start.7) | collective-permute-done | bytes 262176 | tf_op jit(solution)/shard_map/ppermute | solution.py:537
  97.8 0.0 copy-start
  97.8 4.0 %dense.1 = (bf16[1024,1024]{1,0:T(8,128)(2,1)S(1)}, f32[8,16,128]{2,1,0:T(8,128)S(1)}) custom-call(bf16[1024,128]{1,0:T(8,128)(2,1)S(1)} %get-tuple-element.64.refs_0_, bf16[1024,128]{1,0:T(8,128)(2,1)S(1)} %collective-permute-done.3.refs_1_, bf16[1024,128]{1,0:T(8,128)(2,1)} %collective-permute-done.4.refs_2_, ...), custom_call_target="tpu_custom_call" | custom-call | flops 2147483648 | bytes 7340032 | tf_op jit(solution)/shard_map/dense/pallas_call | solution.py:196
  101.8 1.8 collective-permute-start.10
  103.6 1.8 collective-permute-start.11
  105.4 0.0 collective-permute-start.9
  105.4 1.1 collective-permute-done.10.p2
  106.5 1.3 collective-permute-done.11.p3
  107.7 2.0 %collective-permute-done.9.p1 = f32[8,16,128]{2,1,0:T(8,128)S(1)} collective-permute-done((f32[8,16,128]{2,1,0:T(8,128)S(1)}, f32[8,16,128]{2,1,0:T(8,128)S(1)}, u32[]{:S(2)}, u32[]{:S(2)}) %collective-permute-start.9) | collective-permute-done | bytes 65568 | tf_op jit(solution)/shard_map/ppermute | solution.py:537
  109.8 0.7 spread.1
  110.4 14.2 %all_to_all.25 = bf16[32,2,16,128]{3,2,1,0:T(8,128)(2,1)S(1)} all-to-all(bf16[32,2,16,128]{3,2,1,0:T(8,128)(2,1)S(1)} %bitcast.23), channel_id=1, replica_groups=mesh['nodes'=32,'feat'=4] {'nodes'}, dimensions={0} | all-to-all | bytes 524288 | tf_op jit(solution)/shard_map/all_to_all | solution.py:544
  124.6 3.4 %logits.1 = (f32[8,16,128]{2,1,0:T(8,128)S(1)}, bf16[64,16,128]{2,1,0:T(8,128)(2,1)S(1)}) custom-call(s32[128]{0:T(128)S(1)} %reshape.62.src, s32[32]{0:T(128)S(1)} %bitcast.29, s32[1]{0:T(128)} %bitcast.6.me, bf16[64,16,128]{2,1,0:T(8,128)(2,1)S(1)} %bitcast.22, f32[32,16,128]{2,1,0:T(8,128)S(1)} %get-tuple-element.77.own, s32[32,1,128]{2,1,0:T(1,128)S(1)} %bitcast.25, ...), custom_call_target="tpu_custom_call" | custom-call | flops 268435456 | bytes 6291456 | tf_op jit(solution)/shard_map/logits/pallas_call | solution.py:297
  128.0 12.5 %all_to_all.26 = bf16[32,2,16,128]{3,2,1,0:T(8,128)(2,1)S(1)} all-to-all(bf16[32,2,16,128]{3,2,1,0:T(8,128)(2,1)S(1)} %bitcast.24), channel_id=1, replica_groups=mesh['nodes'=32,'feat'=4] {'nodes'}, dimensions={0} | all-to-all | bytes 524288 | tf_op jit(solution)/shard_map/all_to_all | solution.py:544
  140.5 3.2 %small_gradients.1 = (bf16[1024,1024]{1,0:T(8,128)(2,1)}, f32[24,1024]{1,0:T(8,128)S(1)}) custom-call(s32[64]{0:T(128)S(1)} %copy-done.4, s32[1]{0:T(128)} %bitcast.6.me, bf16[64,16,128]{2,1,0:T(8,128)(2,1)S(1)} %bitcast.21, f32[8,16,128]{2,1,0:T(8,128)S(1)} %get-tuple-element.79.dlog, bf16[1024,1024]{1,0:T(8,128)(2,1)S(1)} %get-tuple-element.80.hidden, ...), custom_call_target="tpu_custom_call" | custom-call | flops 536870912 | bytes 4194304 | tf_op jit(solution)/shard_map/small_gradients/pallas_call | solution.py:355
  143.7 2.6 %big_gradient.3 = bf16[16,4,32,256]{3,2,1,0:T(8,128)(2,1)S(1)} custom-call(s32[1]{0:T(128)} %bitcast.6.me, s32[1]{0:T(128)S(6)} %sub.12.side, bf16[16,2,32,1024]{3,2,1,0:T(8,128)(2,1)} %bitcast.32, bf16[1024,128]{1,0:T(8,128)(2,1)S(1)} %get-tuple-element.64.refs_0_, bf16[1024,128]{1,0:T(8,128)(2,1)S(1)} %collective-permute-done.3.refs_1_, ...), custom_call_target="tpu_custom_call" | custom-call | flops 1073741824 | bytes 4194304 | tf_op jit(solution)/shard_map/big_gradient/pallas_call | solution.py:401
  146.3 0.3 collective-permute-start.12
  146.6 0.3 collective-permute-start.13
  146.9 2.6 %big_gradient.2.a = bf16[16,4,32,256]{3,2,1,0:T(8,128)(2,1)S(1)} custom-call(s32[1]{0:T(128)} %bitcast.6.me, s32[1]{0:T(128)} %bitcast.4.side, bf16[16,2,32,1024]{3,2,1,0:T(8,128)(2,1)} %bitcast.33, bf16[1024,128]{1,0:T(8,128)(2,1)S(1)} %get-tuple-element.64.refs_0_, bf16[1024,128]{1,0:T(8,128)(2,1)S(1)} %collective-permute-done.3.refs_1_, ...), custom_call_target="tpu_custom_call" | custom-call | flops 1073741824 | bytes 4194304 | tf_op jit(solution)/shard_map/big_gradient/pallas_call | solution.py:401
  149.5 0.0 collective-permute-done.13.other
  149.5 0.0 collective-permute-done.12.b
  149.5 1.9 %join.1 = bf16[16,4,48,256]{3,2,1,0:T(8,128)(2,1)} custom-call(s32[1]{0:T(128)} %bitcast.4.side, bf16[16,4,32,256]{3,2,1,0:T(8,128)(2,1)S(1)} %big_gradient.2.a, bf16[16,4,32,256]{3,2,1,0:T(8,128)(2,1)S(1)} %collective-permute-done.12.b, f32[24,1024]{1,0:T(8,128)S(1)} %get-tuple-element.84.small, f32[24,1024]{1,0:T(8,128)S(1)} %collective-permute-done.13.other), custom_call_target="tpu_custom_call" | custom-call | flops 524288 | bytes 4194304 | tf_op jit(solution)/shard_map/join/pallas_call | solution.py:444
  151.4 29.2 %all_to_all.27.arrived = bf16[64,48,256]{2,1,0:T(8,128)(2,1)S(1)} all-to-all(bf16[64,48,256]{2,1,0:T(8,128)(2,1)} %bitcast.34), channel_id=1, replica_groups={{0,1,2,3,8,9,10,11,16,17,18,19,24,25,26,27,32,33,34,35,40,41,42,43,48,4..., dimensions={0} | all-to-all | bytes 3145728 | tf_op jit(solution)/shard_map/all_to_all | solution.py:586
  180.5 1.0 total.1
  181.5 1.4 collective-permute-start.14
  182.9 0.8 collective-permute-done.14.b
  183.8 0.6 finish.1
  (27 shorter events, 0.1 us)
Async XLA Ops:
  5.3 9.8 %copy-start.13 = (f32[256]{0:T(256)S(1)}, f32[256]{0:T(256)}, u32[]{:S(2)}) copy-start(f32[256]{0:T(256)} %param.16) | copy-start | bytes 3076
  5.3 9.9 %copy-start.10 = (bf16[256,1024]{1,0:T(8,128)(2,1)S(1)}, bf16[256,1024]{1,0:T(8,128)(2,1)}, u32[]{:S(2)}) copy-start(bf16[256,1024]{1,0:T(8,128)(2,1)} %param.15) | copy-start | bytes 1572868
  5.3 10.1 %copy-start.11 = (bf16[256,16]{0,1:T(8,128)(2,1)S(1)}, bf16[256,16]{0,1:T(8,128)(2,1)}, u32[]{:S(2)}) copy-start(bf16[256,16]{0,1:T(8,128)(2,1)} %param.17) | copy-start | bytes 24580
  5.3 38.2 %all-to-all-start = ((bf16[32,2,128,128]{3,2,1,0:T(8,128)(2,1)}), bf16[32,2,128,128]{3,2,1,0:T(8,128)(2,1)}, u32[]{:S(2)}, u32[]{:S(2)}) async-start(bf16[32,2,128,128]{3,2,1,0:T(8,128)(2,1)} %bitcast.31), calls=%async_computation | async-start | bytes 4194304 | tf_op jit(solution)/shard_map/all_to_all | solution.py:544
  15.5 15.3 %collective-permute-start = (bf16[1056,256]{1,0:T(8,128)(2,1)S(1)}, bf16[1056,256]{1,0:T(8,128)(2,1)}, u32[]{:S(2)}, u32[]{:S(2)}) collective-permute-start(bf16[1056,256]{1,0:T(8,128)(2,1)S(1)} %pad_maximum_fusion.refs_0_), channel_id=1, source_target_pairs={{0,2},{1,3},{2,0},{3,1},{4,6},{5,7},{6,4},{7,5},{8,10},{9,11},{10,... | collective-permute-start | bytes 1622024 | tf_op jit(solution)/shard_map/ppermute | solution.py:537
  18.3 24.6 %collective-permute-start.1 = (bf16[1056,256]{1,0:T(8,128)(2,1)S(1)}, bf16[1056,256]{1,0:T(8,128)(2,1)}, u32[]{:S(2)}, u32[]{:S(2)}) collective-permute-start(bf16[1056,256]{1,0:T(8,128)(2,1)S(1)} %pad_maximum_fusion.refs_0_), channel_id=1, source_target_pairs={{0,1},{1,2},{2,3},{3,0},{4,5},{5,6},{6,7},{7,4},{8,9},{9,10},{10,1... | collective-permute-start | bytes 1622024 | tf_op jit(solution)/shard_map/ppermute | solution.py:537
  18.6 24.3 %collective-permute-start.2 = (bf16[1056,256]{1,0:T(8,128)(2,1)S(1)}, bf16[1056,256]{1,0:T(8,128)(2,1)}, u32[]{:S(2)}, u32[]{:S(2)}) collective-permute-start(bf16[1056,256]{1,0:T(8,128)(2,1)S(1)} %pad_maximum_fusion.refs_0_), channel_id=1, source_target_pairs={{0,3},{1,0},{2,1},{3,2},{4,7},{5,4},{6,5},{7,6},{8,11},{9,8},{10,9... | collective-permute-start | bytes 1622024 | tf_op jit(solution)/shard_map/ppermute | solution.py:537
  43.5 7.3 %copy-start.12 = (s32[32,4]{0,1:T(4,128)S(1)}, s32[32,4]{0,1:T(4,128)}, u32[]{:S(2)}) copy-start(s32[32,4]{0,1:T(4,128)} %param.12) | copy-start | bytes 1540
  43.5 7.5 %copy-start.5 = (s32[1,32]{1,0:T(1,128)S(1)}, s32[1,32]{1,0:T(1,128)}, u32[]{:S(2)}) copy-start(s32[1,32]{1,0:T(1,128)} %param.10) | copy-start | bytes 388
  43.5 35.6 %all-to-all-start.1 = ((bf16[32,2,128,128]{3,2,1,0:T(8,128)(2,1)}), bf16[32,2,128,128]{3,2,1,0:T(8,128)(2,1)S(1)}, u32[]{:S(2)}, u32[]{:S(2)}) async-start(bf16[32,2,128,128]{3,2,1,0:T(8,128)(2,1)} %bitcast.30), calls=%async_computation.1 | async-start | bytes 4194304 | tf_op jit(solution)/shard_map/all_to_all | solution.py:544
  56.1 9.5 %collective-permute-start.3 = (bf16[1024,128]{1,0:T(8,128)(2,1)}, bf16[1024,128]{1,0:T(8,128)(2,1)S(1)}, u32[]{:S(2)}, u32[]{:S(2)}) collective-permute-start(bf16[1024,128]{1,0:T(8,128)(2,1)} %get-tuple-element.61), channel_id=1, source_target_pairs={{0,2},{1,3},{2,0},{3,1},{4,6},{5,7},{6,4},{7,5},{8,10},{9,11},{10,... | collective-permute-start | bytes 786440 | tf_op jit(solution)/shard_map/ppermute | solution.py:537
  58.0 13.9 %collective-permute-start.4 = (bf16[1024,128]{1,0:T(8,128)(2,1)}, bf16[1024,128]{1,0:T(8,128)(2,1)}, u32[]{:S(2)}, u32[]{:S(2)}) collective-permute-start(bf16[1024,128]{1,0:T(8,128)(2,1)} %get-tuple-element.62), channel_id=1, source_target_pairs={{0,1},{1,2},{2,3},{3,0},{4,5},{5,6},{6,7},{7,4},{8,9},{9,10},{10,1... | collective-permute-start | bytes 786440 | tf_op jit(solution)/shard_map/ppermute | solution.py:537
  59.1 12.8 %collective-permute-start.5 = (bf16[1024,128]{1,0:T(8,128)(2,1)}, bf16[1024,128]{1,0:T(8,128)(2,1)}, u32[]{:S(2)}, u32[]{:S(2)}) collective-permute-start(bf16[1024,128]{1,0:T(8,128)(2,1)} %get-tuple-element.63), channel_id=1, source_target_pairs={{0,3},{1,0},{2,1},{3,2},{4,7},{5,4},{6,5},{7,6},{8,11},{9,8},{10,9... | collective-permute-start | bytes 786440 | tf_op jit(solution)/shard_map/ppermute | solution.py:537
  62.7 0.7 copy-start.1
  63.4 1.3 copy-start.6
  64.7 0.8 copy-start.8
  82.3 8.6 %collective-permute-start.6 = (bf16[1024,128]{1,0:T(8,128)(2,1)S(1)}, bf16[1024,128]{1,0:T(8,128)(2,1)S(1)}, u32[]{:S(2)}, u32[]{:S(2)}) collective-permute-start(bf16[1024,128]{1,0:T(8,128)(2,1)S(1)} %get-tuple-element.69), channel_id=1, source_target_pairs={{0,2},{1,3},{2,0},{3,1},{4,6},{5,7},{6,4},{7,5},{8,10},{9,11},{10,... | collective-permute-start | bytes 786440 | tf_op jit(solution)/shard_map/ppermute | solution.py:537
  84.2 13.6 %collective-permute-start.7 = (bf16[1024,128]{1,0:T(8,128)(2,1)S(1)}, bf16[1024,128]{1,0:T(8,128)(2,1)S(1)}, u32[]{:S(2)}, u32[]{:S(2)}) collective-permute-start(bf16[1024,128]{1,0:T(8,128)(2,1)S(1)} %get-tuple-element.70), channel_id=1, source_target_pairs={{0,1},{1,2},{2,3},{3,0},{4,5},{5,6},{6,7},{7,4},{8,9},{9,10},{10,1... | collective-permute-start | bytes 786440 | tf_op jit(solution)/shard_map/ppermute | solution.py:537
  85.3 12.4 %copy-start.7 = (bf16[1024,1024]{1,0:T(8,128)(2,1)S(1)}, bf16[1024,1024]{1,0:T(8,128)(2,1)}, u32[]{:S(2)}) copy-start(bf16[1024,1024]{1,0:T(8,128)(2,1)} %copy-done.6) | copy-start | bytes 6291460
  85.3 12.4 %copy-start.9 = (f32[1024,1]{1,0:T(8,128)S(1)}, f32[1024,1]{1,0:T(8,128)}, u32[]{:S(2)}) copy-start(f32[1024,1]{1,0:T(8,128)} %copy-done.8) | copy-start | bytes 12292
  85.3 12.4 %collective-permute-start.8 = (bf16[1024,128]{1,0:T(8,128)(2,1)S(1)}, bf16[1024,128]{1,0:T(8,128)(2,1)S(1)}, u32[]{:S(2)}, u32[]{:S(2)}) collective-permute-start(bf16[1024,128]{1,0:T(8,128)(2,1)S(1)} %get-tuple-element.71), channel_id=1, source_target_pairs={{0,3},{1,0},{2,1},{3,2},{4,7},{5,4},{6,5},{7,6},{8,11},{9,8},{10,9... | collective-permute-start | bytes 786440 | tf_op jit(solution)/shard_map/ppermute | solution.py:537
  89.2 20.6 %copy-start.4 = (s32[64]{0:T(128)S(1)}, s32[64]{0:T(128)}, u32[]{:S(2)}) copy-start(s32[64]{0:T(128)} %reshape.58.table) | copy-start | bytes 772
  89.2 35.4 %copy-start.3 = (s32[4096]{0:T(1024)S(1)}, s32[4096]{0:T(1024)}, u32[]{:S(2)}) copy-start(s32[4096]{0:T(1024)} %param.14) | copy-start | bytes 49156
  97.8 26.9 %copy-start = (bf16[32,4,128,128]{3,2,1,0:T(8,128)(2,1)S(1)}, bf16[32,4,128,128]{3,2,1,0:T(8,128)(2,1)}, u32[]{:S(2)}) copy-start(bf16[32,4,128,128]{3,2,1,0:T(8,128)(2,1)} %tiles.1) | copy-start | bytes 12582916
  101.8 4.7 %collective-permute-start.10 = (f32[8,16,128]{2,1,0:T(8,128)S(1)}, f32[8,16,128]{2,1,0:T(8,128)S(1)}, u32[]{:S(2)}, u32[]{:S(2)}) collective-permute-start(f32[8,16,128]{2,1,0:T(8,128)S(1)} %get-tuple-element.75.p0), channel_id=1, source_target_pairs={{0,2},{1,3},{2,0},{3,1},{4,6},{5,7},{6,4},{7,5},{8,10},{9,11},{10,... | collective-permute-start | bytes 196616 | tf_op jit(solution)/shard_map/ppermute | solution.py:537
  103.6 4.1 %collective-permute-start.11 = (f32[8,16,128]{2,1,0:T(8,128)S(1)}, f32[8,16,128]{2,1,0:T(8,128)S(1)}, u32[]{:S(2)}, u32[]{:S(2)}) collective-permute-start(f32[8,16,128]{2,1,0:T(8,128)S(1)} %get-tuple-element.75.p0), channel_id=1, source_target_pairs={{0,3},{1,0},{2,1},{3,2},{4,7},{5,4},{6,5},{7,6},{8,11},{9,8},{10,9... | collective-permute-start | bytes 196616 | tf_op jit(solution)/shard_map/ppermute | solution.py:537
  105.4 4.3 %collective-permute-start.9 = (f32[8,16,128]{2,1,0:T(8,128)S(1)}, f32[8,16,128]{2,1,0:T(8,128)S(1)}, u32[]{:S(2)}, u32[]{:S(2)}) collective-permute-start(f32[8,16,128]{2,1,0:T(8,128)S(1)} %get-tuple-element.75.p0), channel_id=1, source_target_pairs={{0,1},{1,2},{2,3},{3,0},{4,5},{5,6},{6,7},{7,4},{8,9},{9,10},{10,1... | collective-permute-start | bytes 196616 | tf_op jit(solution)/shard_map/ppermute | solution.py:537
  124.6 15.9 %copy-start.2 = (bf16[1024,16]{1,0:T(8,128)(2,1)S(1)}, bf16[1024,16]{1,0:T(8,128)(2,1)}, u32[]{:S(2)}) copy-start(bf16[1024,16]{1,0:T(8,128)(2,1)} %copy-done.1) | copy-start | bytes 98308
  146.3 3.2 %collective-permute-start.12 = (bf16[16,4,32,256]{3,2,1,0:T(8,128)(2,1)S(1)}, bf16[16,4,32,256]{3,2,1,0:T(8,128)(2,1)S(1)}, u32[]{:S(2)}, u32[]{:S(2)}) collective-permute-start(bf16[16,4,32,256]{3,2,1,0:T(8,128)(2,1)S(1)} %big_gradient.3), channel_id=1, source_target_pairs={{0,4},{4,0},{8,12},{12,8},{16,20},{20,16},{24,28},{28,24},{32,36},... | collective-permute-start | bytes 3145736 | tf_op jit(solution)/shard_map/ppermute | solution.py:540
  146.6 2.9 %collective-permute-start.13 = (f32[24,1024]{1,0:T(8,128)S(1)}, f32[24,1024]{1,0:T(8,128)S(1)}, u32[]{:S(2)}, u32[]{:S(2)}) collective-permute-start(f32[24,1024]{1,0:T(8,128)S(1)} %get-tuple-element.84.small), channel_id=1, source_target_pairs={{0,4},{4,0},{8,12},{12,8},{16,20},{20,16},{24,28},{28,24},{32,36},... | collective-permute-start | bytes 294920 | tf_op jit(solution)/shard_map/ppermute | solution.py:540
  181.5 2.2 %collective-permute-start.14 = (f32[16,256]{1,0:T(8,128)S(1)}, f32[16,256]{1,0:T(8,128)S(1)}, u32[]{:S(2)}, u32[]{:S(2)}) collective-permute-start(f32[16,256]{1,0:T(8,128)S(1)} %get-tuple-element.86.a), channel_id=1, source_target_pairs={{0,4},{4,0},{8,12},{12,8},{16,20},{20,16},{24,28},{28,24},{32,36},... | collective-permute-start | bytes 49160 | tf_op jit(solution)/shard_map/ppermute | solution.py:540

commit v14 on v13

--- a/solution.py
+++ b/solution.py
@@ -179,33 +179,27 @@
 
 def dense_kernel(nfeat, *refs):
     pieces, (weights, bias, second, hidden, proj) = refs[: 2 * nfeat], refs[2 * nfeat :]
-    order = [pieces[i * nfeat + k][...] for k in range(nfeat) for i in range(2)]
-    pre = dot(weights[...], jnp.concatenate(order, 1), NT)
-    hid = jnp.maximum(pre + bias[...], 0.0).astype(BF16)
-    hidden[...] = hid
-    out = dot(second[...], hid, NN)
-    for b in range(proj.shape[0]):
-        proj[b] = out[:, b * BLK : (b + 1) * BLK]
+    step = hidden.shape[1] // 2
+    for half in range(2):
+        rows = slice(half * step, (half + 1) * step)
+        order = [pieces[i * nfeat + k][rows, :] for k in range(nfeat) for i in range(2)]
+        pre = dot(weights[...], jnp.concatenate(order, 1), NT)
+        hid = jnp.maximum(pre + bias[...], 0.0).astype(BF16)
+        hidden[:, rows] = hid
+        out = dot(second[...], hid, NN)
+        for b in range(step // BLK):
+            proj[half * (step // BLK) + b] = out[:, b * BLK : (b + 1) * BLK]
 
 
 def dense(pieces, weights, bias, second):
     nodes, nfeat = pieces[0].shape[0], len(pieces) // 2
     hid, width = weights.shape
     grades = second.shape[0]
-    step = 512
+    vmem = pl.BlockSpec(memory_space=pltpu.VMEM)
     return pl.pallas_call(
         functools.partial(dense_kernel, nfeat),
-        grid=(nodes // step,),
-        in_specs=[pl.BlockSpec((step, BLK), lambda g: (g, 0))] * (2 * nfeat)
-        + [
-            pl.BlockSpec((hid, width), lambda g: (0, 0)),
-            pl.BlockSpec((hid, 1), lambda g: (0, 0)),
-            pl.BlockSpec((grades, hid), lambda g: (0, 0)),
-        ],
-        out_specs=[
-            pl.BlockSpec((hid, step), lambda g: (0, g)),
-            pl.BlockSpec((step // BLK, grades, BLK), lambda g: (g, 0, 0)),
-        ],
+        in_specs=[vmem] * (2 * nfeat + 3),
+        out_specs=[vmem] * 2,
         out_shape=[
             jax.ShapeDtypeStruct((hid, nodes), BF16),
             jax.ShapeDtypeStruct((nodes // BLK, grades, BLK), F32),

time: 185 us -> 185 us (level)
  no operation moved by 1% of the time
where the time goes in v14:
time: 185 us; the launch traced here: 184 us
  blocking collectives  56 us (30%)
  waiting for transfers between devices  46.5 us (25%)
  Pallas kernels  39.1 us (21%)
  starting transfers between devices  37 us (20%)
  local copies, waits for them, and re-layouts  4.67 us (3%)
    ppermute x12, waiting for transfers between devices, ahead(): return lax.ppermute(x, 'feat', [(i, (i + k) % nfeat) for i in range(nfeat)])  38 us
    all_to_all x1, blocking collectives, shards(): lax.all_to_all(big.reshape(parts // 2 * nfeat, *big.shape[2:]), ('nodes',...  29.3 us
    all_to_all x2, blocking collectives, swap(): lax.all_to_all(shaped, 'nodes', split_axis=0, concat_axis=0, tiled=True)  26.6 us
    ppermute x12, starting transfers between devices, ahead(): return lax.ppermute(x, 'feat', [(i, (i + k) % nfeat) for i in range(nfeat)])  18.1 us
    all_to_all x2, starting transfers between devices, swap(): lax.all_to_all(shaped, 'nodes', split_axis=0, concat_axis=0, tiled=True)  17.1 us
    pallas_call x3, Pallas kernels, aggregate(): pl.pallas_call(functools.partial(agg_kernel, which, chunk, nfeat), grid_s...  10.7 us
    all_to_all x2, waiting for transfers between devices, swap(): lax.all_to_all(shaped, 'nodes', split_axis=0, concat_axis=0, tiled=True)  7.7 us
    pallas_call x2, Pallas kernels, pick(): pl.pallas_call(functools.partial(pick_kernel, chunk), grid_spec=pltpu.Pre...  6.54 us
  transfers between devices with their start and end apart: 17, of which 12 were waited for; matrix products, arithmetic and copies ran while one was open for 0% of the time, Pallas kernels for 8%

profile of v14, /device:TPU:1, one launch (start us, length us, event | category | flops | bytes accessed | tf_op | source)
XLA Modules:
  0.0 184.2 jit_solution(11404234836853730395)
XLA Ops:
  0.6 0.8 copy.15
  1.4 0.6 reshape.58.table
  2.0 3.3 %pick.3 = bf16[64,128,128]{2,1,0:T(8,128)(2,1)} custom-call(s32[64]{0:T(128)} %reshape.58.table, bf16[4096,256]{1,0:T(8,128)(2,1)} %features.9), custom_call_target="tpu_custom_call" | custom-call | bytes 4194304 | tf_op jit(solution)/shard_map/pick/pallas_call | solution.py:52
  5.3 0.0 copy-start.13
  5.3 0.0 copy-start.10
  5.3 0.0 copy-start.11
  5.3 9.8 %all-to-all-start = ((bf16[32,2,128,128]{3,2,1,0:T(8,128)(2,1)}), bf16[32,2,128,128]{3,2,1,0:T(8,128)(2,1)}, u32[]{:S(2)}, u32[]{:S(2)}) async-start(bf16[32,2,128,128]{3,2,1,0:T(8,128)(2,1)} %bitcast.31), calls=%async_computation | async-start | bytes 4194304 | tf_op jit(solution)/shard_map/all_to_all | solution.py:538
  15.2 0.2 copy.16
  15.5 2.8 %collective-permute-start = (bf16[1056,256]{1,0:T(8,128)(2,1)S(1)}, bf16[1056,256]{1,0:T(8,128)(2,1)}, u32[]{:S(2)}, u32[]{:S(2)}) collective-permute-start(bf16[1056,256]{1,0:T(8,128)(2,1)S(1)} %pad_maximum_fusion.refs_0_), channel_id=1, source_target_pairs={{0,2},{1,3},{2,0},{3,1},{4,6},{5,7},{6,4},{7,5},{8,10},{9,11},{10,... | collective-permute-start | bytes 1622024 | tf_op jit(solution)/shard_map/ppermute | solution.py:531
  18.3 0.3 collective-permute-start.1
  18.6 2.4 %collective-permute-start.2 = (bf16[1056,256]{1,0:T(8,128)(2,1)S(1)}, bf16[1056,256]{1,0:T(8,128)(2,1)}, u32[]{:S(2)}, u32[]{:S(2)}) collective-permute-start(bf16[1056,256]{1,0:T(8,128)(2,1)S(1)} %pad_maximum_fusion.refs_0_), channel_id=1, source_target_pairs={{0,3},{1,0},{2,1},{3,2},{4,7},{5,4},{6,5},{7,6},{8,11},{9,8},{10,9... | collective-permute-start | bytes 1622024 | tf_op jit(solution)/shard_map/ppermute | solution.py:531
  21.0 3.3 %pick.2 = bf16[64,128,128]{2,1,0:T(8,128)(2,1)} custom-call(s32[64]{0:T(128)} %reshape.58.table, bf16[4096,256]{1,0:T(8,128)(2,1)} %features.9), custom_call_target="tpu_custom_call" | custom-call | bytes 4194304 | tf_op jit(solution)/shard_map/pick/pallas_call | solution.py:52
  24.3 6.5 %collective-permute-done.refs_1_ = bf16[1056,256]{1,0:T(8,128)(2,1)} collective-permute-done((bf16[1056,256]{1,0:T(8,128)(2,1)S(1)}, bf16[1056,256]{1,0:T(8,128)(2,1)}, u32[]{:S(2)}, u32[]{:S(2)}) %collective-permute-start) | collective-permute-done | bytes 540704 | tf_op jit(solution)/shard_map/ppermute | solution.py:531
  30.8 12.2 %collective-permute-done.1.refs_2_ = bf16[1056,256]{1,0:T(8,128)(2,1)} collective-permute-done((bf16[1056,256]{1,0:T(8,128)(2,1)S(1)}, bf16[1056,256]{1,0:T(8,128)(2,1)}, u32[]{:S(2)}, u32[]{:S(2)}) %collective-permute-start.1) | collective-permute-done | bytes 540704 | tf_op jit(solution)/shard_map/ppermute | solution.py:531
  43.0 0.0 collective-permute-done.2.refs_3_
  43.0 0.5 all-to-all-done
  43.5 7.3 %all-to-all-start.1 = ((bf16[32,2,128,128]{3,2,1,0:T(8,128)(2,1)}), bf16[32,2,128,128]{3,2,1,0:T(8,128)(2,1)S(1)}, u32[]{:S(2)}, u32[]{:S(2)}) async-start(bf16[32,2,128,128]{3,2,1,0:T(8,128)(2,1)} %bitcast.30), calls=%async_computation.1 | async-start | bytes 4194304 | tf_op jit(solution)/shard_map/all_to_all | solution.py:538
  50.8 0.1 copy.17
  50.9 0.1 reshape.62.src
  51.0 5.1 %aggregate.3 = (bf16[1024,128]{1,0:T(8,128)(2,1)}, bf16[1024,128]{1,0:T(8,128)(2,1)}, bf16[1024,128]{1,0:T(8,128)(2,1)}, bf16[1024,128]{1,0:T(8,128)(2,1)S(1)}) custom-call(s32[128]{0:T(128)S(1)} %reshape.62.src, s32[32]{0:T(128)S(1)} %bitcast.26, s32[1]{0:T(128)} %bitcast.6.me, bf16[64,128,128]{2,1,0:T(8,128)(2,1)} %bitcast.3.arrived, ...), custom_call_target="tpu_custom_call" | custom-call | flops 536870912 | bytes 8388608 | tf_op jit(solution)/shard_map/aggregate/pallas_call | solution.py:115
  56.1 1.8 collective-permute-start.3
  58.0 1.2 collective-permute-start.4
  59.1 1.5 collective-permute-start.5
  60.6 2.0 %assemble.1 = (bf16[1024,1024]{1,0:T(8,128)(2,1)S(1)}, bf16[16,1024]{1,0:T(8,128)(2,1)S(1)}, bf16[1024,16]{1,0:T(8,128)(2,1)S(1)}, f32[1024,1]{1,0:T(8,128)S(1)}) custom-call(s32[1]{0:T(128)} %bitcast.6.me, bf16[1056,256]{1,0:T(8,128)(2,1)S(1)} %pad_maximum_fusion.refs_0_, bf16[1056,256]{1,0:T(8,128)(2,1)} %collective-permute-done.refs_1_, ...), custom_call_target="tpu_custom_call" | custom-call | bytes 5242880 | tf_op jit(solution)/shard_map/assemble/pallas_call | solution.py:159
  62.7 0.7 copy-done.1
  63.4 1.3 copy-done.6
  64.7 0.8 copy-done.8
  65.5 0.1 collective-permute-done.3.refs_1_
  65.6 6.2 %collective-permute-done.4.refs_2_ = bf16[1024,128]{1,0:T(8,128)(2,1)} collective-permute-done((bf16[1024,128]{1,0:T(8,128)(2,1)}, bf16[1024,128]{1,0:T(8,128)(2,1)}, u32[]{:S(2)}, u32[]{:S(2)}) %collective-permute-start.4) | collective-permute-done | bytes 262176 | tf_op jit(solution)/shard_map/ppermute | solution.py:531
  71.9 7.2 %all-to-all-done.1 = bf16[32,2,128,128]{3,2,1,0:T(8,128)(2,1)S(1)} async-done(((bf16[32,2,128,128]{3,2,1,0:T(8,128)(2,1)}), bf16[32,2,128,128]{3,2,1,0:T(8,128)(2,1)S(1)}, u32[]{:S(2)}, u32[]{:S(2)}) %all-to-all-start.1) | async-done | bytes 2097184 | tf_op jit(solution)/shard_map/all_to_all | solution.py:538
  79.1 3.3 %aggregate.5 = (bf16[1024,128]{1,0:T(8,128)(2,1)S(1)}, bf16[1024,128]{1,0:T(8,128)(2,1)S(1)}, bf16[1024,128]{1,0:T(8,128)(2,1)S(1)}) custom-call(s32[128]{0:T(128)S(1)} %reshape.62.src, s32[32]{0:T(128)S(1)} %bitcast.27, s32[1]{0:T(128)} %bitcast.6.me, bf16[64,128,128]{2,1,0:T(8,128)(2,1)S(1)} %bitcast.19, bf16[32,4,128,128]{3,2,1,0:T(8,128)(2,1)} %tiles.1, ...), custom_call_target="tpu_custom_call" | custom-call | flops 402653184 | bytes 8388608 | tf_op jit(solution)/shard_map/aggregate/pallas_call | solution.py:115
  82.3 1.8 %collective-permute-start.6 = (bf16[1024,128]{1,0:T(8,128)(2,1)S(1)}, bf16[1024,128]{1,0:T(8,128)(2,1)S(1)}, u32[]{:S(2)}, u32[]{:S(2)}) collective-permute-start(bf16[1024,128]{1,0:T(8,128)(2,1)S(1)} %get-tuple-element.69), channel_id=1, source_target_pairs={{0,2},{1,3},{2,0},{3,1},{4,6},{5,7},{6,4},{7,5},{8,10},{9,11},{10,... | collective-permute-start | bytes 786440 | tf_op jit(solution)/shard_map/ppermute | solution.py:531
  84.2 1.2 collective-permute-start.7
  85.3 1.5 collective-permute-start.8
  86.9 2.3 %aggregate.4.refs_4_ = bf16[1024,128]{1,0:T(8,128)(2,1)S(1)} custom-call(s32[128]{0:T(128)S(1)} %reshape.62.src, s32[32]{0:T(128)S(1)} %bitcast.28, s32[1]{0:T(128)} %bitcast.6.me, bf16[64,128,128]{2,1,0:T(8,128)(2,1)S(1)} %bitcast.20, bf16[32,4,128,128]{3,2,1,0:T(8,128)(2,1)} %tiles.1, bf16[4096,256]{1,0:T(8,128)(2,1)} %features.9), custom_call_target="tpu_custom_call" | custom-call | flops 134217728 | bytes 8388608 | tf_op jit(solution)/shard_map/aggregate/pallas_call | solution.py:115
  89.2 0.0 copy-start.4
  89.2 0.0 copy-start.3
  89.2 1.7 collective-permute-done.6.refs_5_
  90.9 6.8 %collective-permute-done.7.refs_6_ = bf16[1024,128]{1,0:T(8,128)(2,1)S(1)} collective-permute-done((bf16[1024,128]{1,0:T(8,128)(2,1)S(1)}, bf16[1024,128]{1,0:T(8,128)(2,1)S(1)}, u32[]{:S(2)}, u32[]{:S(2)}) %collective-permute-start.7) | collective-permute-done | bytes 262176 | tf_op jit(solution)/shard_map/ppermute | solution.py:531
  97.8 0.0 copy-start
  97.8 3.9 %dense.1 = (bf16[1024,1024]{1,0:T(8,128)(2,1)S(1)}, f32[8,16,128]{2,1,0:T(8,128)S(1)}) custom-call(bf16[1024,128]{1,0:T(8,128)(2,1)S(1)} %get-tuple-element.64.refs_0_, bf16[1024,128]{1,0:T(8,128)(2,1)S(1)} %collective-permute-done.3.refs_1_, bf16[1024,128]{1,0:T(8,128)(2,1)} %collective-permute-done.4.refs_2_, ...), custom_call_target="tpu_custom_call" | custom-call | flops 2147483648 | bytes 7340032 | tf_op jit(solution)/shard_map/dense/pallas_call | solution.py:199
  101.7 1.7 collective-permute-start.10
  103.4 1.8 collective-permute-start.11
  105.2 0.0 collective-permute-start.9
  105.2 1.1 collective-permute-done.10.p2
  106.3 1.2 collective-permute-done.11.p3
  107.5 2.0 %collective-permute-done.9.p1 = f32[8,16,128]{2,1,0:T(8,128)S(1)} collective-permute-done((f32[8,16,128]{2,1,0:T(8,128)S(1)}, f32[8,16,128]{2,1,0:T(8,128)S(1)}, u32[]{:S(2)}, u32[]{:S(2)}) %collective-permute-start.9) | collective-permute-done | bytes 65568 | tf_op jit(solution)/shard_map/ppermute | solution.py:531
  109.5 0.7 spread.1
  110.2 14.2 %all_to_all.25 = bf16[32,2,16,128]{3,2,1,0:T(8,128)(2,1)S(1)} all-to-all(bf16[32,2,16,128]{3,2,1,0:T(8,128)(2,1)S(1)} %bitcast.23), channel_id=1, replica_groups=mesh['nodes'=32,'feat'=4] {'nodes'}, dimensions={0} | all-to-all | bytes 524288 | tf_op jit(solution)/shard_map/all_to_all | solution.py:538
  124.4 3.4 %logits.1 = (f32[8,16,128]{2,1,0:T(8,128)S(1)}, bf16[64,16,128]{2,1,0:T(8,128)(2,1)S(1)}) custom-call(s32[128]{0:T(128)S(1)} %reshape.62.src, s32[32]{0:T(128)S(1)} %bitcast.29, s32[1]{0:T(128)} %bitcast.6.me, bf16[64,16,128]{2,1,0:T(8,128)(2,1)S(1)} %bitcast.22, f32[32,16,128]{2,1,0:T(8,128)S(1)} %get-tuple-element.77.own, s32[32,1,128]{2,1,0:T(1,128)S(1)} %bitcast.25, ...), custom_call_target="tpu_custom_call" | custom-call | flops 268435456 | bytes 6291456 | tf_op jit(solution)/shard_map/logits/pallas_call | solution.py:291
  127.8 12.5 %all_to_all.26 = bf16[32,2,16,128]{3,2,1,0:T(8,128)(2,1)S(1)} all-to-all(bf16[32,2,16,128]{3,2,1,0:T(8,128)(2,1)S(1)} %bitcast.24), channel_id=1, replica_groups=mesh['nodes'=32,'feat'=4] {'nodes'}, dimensions={0} | all-to-all | bytes 524288 | tf_op jit(solution)/shard_map/all_to_all | solution.py:538
  140.3 3.2 %small_gradients.1 = (bf16[1024,1024]{1,0:T(8,128)(2,1)}, f32[24,1024]{1,0:T(8,128)S(1)}) custom-call(s32[64]{0:T(128)S(1)} %copy-done.4, s32[1]{0:T(128)} %bitcast.6.me, bf16[64,16,128]{2,1,0:T(8,128)(2,1)S(1)} %bitcast.21, f32[8,16,128]{2,1,0:T(8,128)S(1)} %get-tuple-element.79.dlog, bf16[1024,1024]{1,0:T(8,128)(2,1)S(1)} %get-tuple-element.80.hidden, ...), custom_call_target="tpu_custom_call" | custom-call | flops 536870912 | bytes 4194304 | tf_op jit(solution)/shard_map/small_gradients/pallas_call | solution.py:349
  143.5 2.6 %big_gradient.3 = bf16[16,4,32,256]{3,2,1,0:T(8,128)(2,1)S(1)} custom-call(s32[1]{0:T(128)} %bitcast.6.me, s32[1]{0:T(128)S(6)} %sub.12.side, bf16[16,2,32,1024]{3,2,1,0:T(8,128)(2,1)} %bitcast.32, bf16[1024,128]{1,0:T(8,128)(2,1)S(1)} %get-tuple-element.64.refs_0_, bf16[1024,128]{1,0:T(8,128)(2,1)S(1)} %collective-permute-done.3.refs_1_, ...), custom_call_target="tpu_custom_call" | custom-call | flops 1073741824 | bytes 4194304 | tf_op jit(solution)/shard_map/big_gradient/pallas_call | solution.py:395
  146.1 0.2 collective-permute-start.12
  146.4 0.3 collective-permute-start.13
  146.7 2.6 %big_gradient.2.a = bf16[16,4,32,256]{3,2,1,0:T(8,128)(2,1)S(1)} custom-call(s32[1]{0:T(128)} %bitcast.6.me, s32[1]{0:T(128)} %bitcast.4.side, bf16[16,2,32,1024]{3,2,1,0:T(8,128)(2,1)} %bitcast.33, bf16[1024,128]{1,0:T(8,128)(2,1)S(1)} %get-tuple-element.64.refs_0_, bf16[1024,128]{1,0:T(8,128)(2,1)S(1)} %collective-permute-done.3.refs_1_, ...), custom_call_target="tpu_custom_call" | custom-call | flops 1073741824 | bytes 4194304 | tf_op jit(solution)/shard_map/big_gradient/pallas_call | solution.py:395
  149.3 0.0 collective-permute-done.13.other
  149.3 0.0 collective-permute-done.12.b
  149.3 1.9 %join.1 = bf16[16,4,48,256]{3,2,1,0:T(8,128)(2,1)} custom-call(s32[1]{0:T(128)} %bitcast.4.side, bf16[16,4,32,256]{3,2,1,0:T(8,128)(2,1)S(1)} %big_gradient.2.a, bf16[16,4,32,256]{3,2,1,0:T(8,128)(2,1)S(1)} %collective-permute-done.12.b, f32[24,1024]{1,0:T(8,128)S(1)} %get-tuple-element.84.small, f32[24,1024]{1,0:T(8,128)S(1)} %collective-permute-done.13.other), custom_call_target="tpu_custom_call" | custom-call | flops 524288 | bytes 4194304 | tf_op jit(solution)/shard_map/join/pallas_call | solution.py:438
  151.2 29.3 %all_to_all.27.arrived = bf16[64,48,256]{2,1,0:T(8,128)(2,1)S(1)} all-to-all(bf16[64,48,256]{2,1,0:T(8,128)(2,1)} %bitcast.34), channel_id=1, replica_groups={{0,1,2,3,8,9,10,11,16,17,18,19,24,25,26,27,32,33,34,35,40,41,42,43,48,4..., dimensions={0} | all-to-all | bytes 3145728 | tf_op jit(solution)/shard_map/all_to_all | solution.py:580
  180.5 1.0 total.1
  181.5 1.3 collective-permute-start.14
  182.8 0.8 collective-permute-done.14.b
  183.6 0.6 finish.1
  (27 shorter events, 0.1 us)
Async XLA Ops:
  5.3 9.8 %copy-start.13 = (f32[256]{0:T(256)S(1)}, f32[256]{0:T(256)}, u32[]{:S(2)}) copy-start(f32[256]{0:T(256)} %param.16) | copy-start | bytes 3076
  5.3 9.9 %copy-start.10 = (bf16[256,1024]{1,0:T(8,128)(2,1)S(1)}, bf16[256,1024]{1,0:T(8,128)(2,1)}, u32[]{:S(2)}) copy-start(bf16[256,1024]{1,0:T(8,128)(2,1)} %param.15) | copy-start | bytes 1572868
  5.3 10.1 %copy-start.11 = (bf16[256,16]{0,1:T(8,128)(2,1)S(1)}, bf16[256,16]{0,1:T(8,128)(2,1)}, u32[]{:S(2)}) copy-start(bf16[256,16]{0,1:T(8,128)(2,1)} %param.17) | copy-start | bytes 24580
  5.3 38.2 %all-to-all-start = ((bf16[32,2,128,128]{3,2,1,0:T(8,128)(2,1)}), bf16[32,2,128,128]{3,2,1,0:T(8,128)(2,1)}, u32[]{:S(2)}, u32[]{:S(2)}) async-start(bf16[32,2,128,128]{3,2,1,0:T(8,128)(2,1)} %bitcast.31), calls=%async_computation | async-start | bytes 4194304 | tf_op jit(solution)/shard_map/all_to_all | solution.py:538
  15.5 15.3 %collective-permute-start = (bf16[1056,256]{1,0:T(8,128)(2,1)S(1)}, bf16[1056,256]{1,0:T(8,128)(2,1)}, u32[]{:S(2)}, u32[]{:S(2)}) collective-permute-start(bf16[1056,256]{1,0:T(8,128)(2,1)S(1)} %pad_maximum_fusion.refs_0_), channel_id=1, source_target_pairs={{0,2},{1,3},{2,0},{3,1},{4,6},{5,7},{6,4},{7,5},{8,10},{9,11},{10,... | collective-permute-start | bytes 1622024 | tf_op jit(solution)/shard_map/ppermute | solution.py:531
  18.3 24.6 %collective-permute-start.1 = (bf16[1056,256]{1,0:T(8,128)(2,1)S(1)}, bf16[1056,256]{1,0:T(8,128)(2,1)}, u32[]{:S(2)}, u32[]{:S(2)}) collective-permute-start(bf16[1056,256]{1,0:T(8,128)(2,1)S(1)} %pad_maximum_fusion.refs_0_), channel_id=1, source_target_pairs={{0,1},{1,2},{2,3},{3,0},{4,5},{5,6},{6,7},{7,4},{8,9},{9,10},{10,1... | collective-permute-start | bytes 1622024 | tf_op jit(solution)/shard_map/ppermute | solution.py:531
  18.6 24.3 %collective-permute-start.2 = (bf16[1056,256]{1,0:T(8,128)(2,1)S(1)}, bf16[1056,256]{1,0:T(8,128)(2,1)}, u32[]{:S(2)}, u32[]{:S(2)}) collective-permute-start(bf16[1056,256]{1,0:T(8,128)(2,1)S(1)} %pad_maximum_fusion.refs_0_), channel_id=1, source_target_pairs={{0,3},{1,0},{2,1},{3,2},{4,7},{5,4},{6,5},{7,6},{8,11},{9,8},{10,9... | collective-permute-start | bytes 1622024 | tf_op jit(solution)/shard_map/ppermute | solution.py:531
  43.5 7.3 %copy-start.12 = (s32[32,4]{0,1:T(4,128)S(1)}, s32[32,4]{0,1:T(4,128)}, u32[]{:S(2)}) copy-start(s32[32,4]{0,1:T(4,128)} %param.12) | copy-start | bytes 1540
  43.5 7.5 %copy-start.5 = (s32[1,32]{1,0:T(1,128)S(1)}, s32[1,32]{1,0:T(1,128)}, u32[]{:S(2)}) copy-start(s32[1,32]{1,0:T(1,128)} %param.10) | copy-start | bytes 388
  43.5 35.6 %all-to-all-start.1 = ((bf16[32,2,128,128]{3,2,1,0:T(8,128)(2,1)}), bf16[32,2,128,128]{3,2,1,0:T(8,128)(2,1)S(1)}, u32[]{:S(2)}, u32[]{:S(2)}) async-start(bf16[32,2,128,128]{3,2,1,0:T(8,128)(2,1)} %bitcast.30), calls=%async_computation.1 | async-start | bytes 4194304 | tf_op jit(solution)/shard_map/all_to_all | solution.py:538
  56.1 9.5 %collective-permute-start.3 = (bf16[1024,128]{1,0:T(8,128)(2,1)}, bf16[1024,128]{1,0:T(8,128)(2,1)S(1)}, u32[]{:S(2)}, u32[]{:S(2)}) collective-permute-start(bf16[1024,128]{1,0:T(8,128)(2,1)} %get-tuple-element.61), channel_id=1, source_target_pairs={{0,2},{1,3},{2,0},{3,1},{4,6},{5,7},{6,4},{7,5},{8,10},{9,11},{10,... | collective-permute-start | bytes 786440 | tf_op jit(solution)/shard_map/ppermute | solution.py:531
  58.0 13.9 %collective-permute-start.4 = (bf16[1024,128]{1,0:T(8,128)(2,1)}, bf16[1024,128]{1,0:T(8,128)(2,1)}, u32[]{:S(2)}, u32[]{:S(2)}) collective-permute-start(bf16[1024,128]{1,0:T(8,128)(2,1)} %get-tuple-element.62), channel_id=1, source_target_pairs={{0,1},{1,2},{2,3},{3,0},{4,5},{5,6},{6,7},{7,4},{8,9},{9,10},{10,1... | collective-permute-start | bytes 786440 | tf_op jit(solution)/shard_map/ppermute | solution.py:531
  59.1 12.8 %collective-permute-start.5 = (bf16[1024,128]{1,0:T(8,128)(2,1)}, bf16[1024,128]{1,0:T(8,128)(2,1)}, u32[]{:S(2)}, u32[]{:S(2)}) collective-permute-start(bf16[1024,128]{1,0:T(8,128)(2,1)} %get-tuple-element.63), channel_id=1, source_target_pairs={{0,3},{1,0},{2,1},{3,2},{4,7},{5,4},{6,5},{7,6},{8,11},{9,8},{10,9... | collective-permute-start | bytes 786440 | tf_op jit(solution)/shard_map/ppermute | solution.py:531
  62.7 0.7 copy-start.1
  63.4 1.3 copy-start.6
  64.7 0.8 copy-start.8
  82.3 8.6 %collective-permute-start.6 = (bf16[1024,128]{1,0:T(8,128)(2,1)S(1)}, bf16[1024,128]{1,0:T(8,128)(2,1)S(1)}, u32[]{:S(2)}, u32[]{:S(2)}) collective-permute-start(bf16[1024,128]{1,0:T(8,128)(2,1)S(1)} %get-tuple-element.69), channel_id=1, source_target_pairs={{0,2},{1,3},{2,0},{3,1},{4,6},{5,7},{6,4},{7,5},{8,10},{9,11},{10,... | collective-permute-start | bytes 786440 | tf_op jit(solution)/shard_map/ppermute | solution.py:531
  84.2 13.6 %collective-permute-start.7 = (bf16[1024,128]{1,0:T(8,128)(2,1)S(1)}, bf16[1024,128]{1,0:T(8,128)(2,1)S(1)}, u32[]{:S(2)}, u32[]{:S(2)}) collective-permute-start(bf16[1024,128]{1,0:T(8,128)(2,1)S(1)} %get-tuple-element.70), channel_id=1, source_target_pairs={{0,1},{1,2},{2,3},{3,0},{4,5},{5,6},{6,7},{7,4},{8,9},{9,10},{10,1... | collective-permute-start | bytes 786440 | tf_op jit(solution)/shard_map/ppermute | solution.py:531
  85.3 12.4 %copy-start.7 = (bf16[1024,1024]{1,0:T(8,128)(2,1)S(1)}, bf16[1024,1024]{1,0:T(8,128)(2,1)}, u32[]{:S(2)}) copy-start(bf16[1024,1024]{1,0:T(8,128)(2,1)} %copy-done.6) | copy-start | bytes 6291460
  85.3 12.4 %copy-start.9 = (f32[1024,1]{1,0:T(8,128)S(1)}, f32[1024,1]{1,0:T(8,128)}, u32[]{:S(2)}) copy-start(f32[1024,1]{1,0:T(8,128)} %copy-done.8) | copy-start | bytes 12292
  85.3 12.4 %collective-permute-start.8 = (bf16[1024,128]{1,0:T(8,128)(2,1)S(1)}, bf16[1024,128]{1,0:T(8,128)(2,1)S(1)}, u32[]{:S(2)}, u32[]{:S(2)}) collective-permute-start(bf16[1024,128]{1,0:T(8,128)(2,1)S(1)} %get-tuple-element.71), channel_id=1, source_target_pairs={{0,3},{1,0},{2,1},{3,2},{4,7},{5,4},{6,5},{7,6},{8,11},{9,8},{10,9... | collective-permute-start | bytes 786440 | tf_op jit(solution)/shard_map/ppermute | solution.py:531
  89.2 20.4 %copy-start.4 = (s32[64]{0:T(128)S(1)}, s32[64]{0:T(128)}, u32[]{:S(2)}) copy-start(s32[64]{0:T(128)} %reshape.58.table) | copy-start | bytes 772
  89.2 35.2 %copy-start.3 = (s32[4096]{0:T(1024)S(1)}, s32[4096]{0:T(1024)}, u32[]{:S(2)}) copy-start(s32[4096]{0:T(1024)} %param.14) | copy-start | bytes 49156
  97.8 26.6 %copy-start = (bf16[32,4,128,128]{3,2,1,0:T(8,128)(2,1)S(1)}, bf16[32,4,128,128]{3,2,1,0:T(8,128)(2,1)}, u32[]{:S(2)}) copy-start(bf16[32,4,128,128]{3,2,1,0:T(8,128)(2,1)} %tiles.1) | copy-start | bytes 12582916
  101.7 4.6 %collective-permute-start.10 = (f32[8,16,128]{2,1,0:T(8,128)S(1)}, f32[8,16,128]{2,1,0:T(8,128)S(1)}, u32[]{:S(2)}, u32[]{:S(2)}) collective-permute-start(f32[8,16,128]{2,1,0:T(8,128)S(1)} %get-tuple-element.75.p0), channel_id=1, source_target_pairs={{0,2},{1,3},{2,0},{3,1},{4,6},{5,7},{6,4},{7,5},{8,10},{9,11},{10,... | collective-permute-start | bytes 196616 | tf_op jit(solution)/shard_map/ppermute | solution.py:531
  103.4 4.1 %collective-permute-start.11 = (f32[8,16,128]{2,1,0:T(8,128)S(1)}, f32[8,16,128]{2,1,0:T(8,128)S(1)}, u32[]{:S(2)}, u32[]{:S(2)}) collective-permute-start(f32[8,16,128]{2,1,0:T(8,128)S(1)} %get-tuple-element.75.p0), channel_id=1, source_target_pairs={{0,3},{1,0},{2,1},{3,2},{4,7},{5,4},{6,5},{7,6},{8,11},{9,8},{10,9... | collective-permute-start | bytes 196616 | tf_op jit(solution)/shard_map/ppermute | solution.py:531
  105.2 4.3 %collective-permute-start.9 = (f32[8,16,128]{2,1,0:T(8,128)S(1)}, f32[8,16,128]{2,1,0:T(8,128)S(1)}, u32[]{:S(2)}, u32[]{:S(2)}) collective-permute-start(f32[8,16,128]{2,1,0:T(8,128)S(1)} %get-tuple-element.75.p0), channel_id=1, source_target_pairs={{0,1},{1,2},{2,3},{3,0},{4,5},{5,6},{6,7},{7,4},{8,9},{9,10},{10,1... | collective-permute-start | bytes 196616 | tf_op jit(solution)/shard_map/ppermute | solution.py:531
  124.4 15.9 %copy-start.2 = (bf16[1024,16]{1,0:T(8,128)(2,1)S(1)}, bf16[1024,16]{1,0:T(8,128)(2,1)}, u32[]{:S(2)}) copy-start(bf16[1024,16]{1,0:T(8,128)(2,1)} %copy-done.1) | copy-start | bytes 98308
  146.1 3.2 %collective-permute-start.12 = (bf16[16,4,32,256]{3,2,1,0:T(8,128)(2,1)S(1)}, bf16[16,4,32,256]{3,2,1,0:T(8,128)(2,1)S(1)}, u32[]{:S(2)}, u32[]{:S(2)}) collective-permute-start(bf16[16,4,32,256]{3,2,1,0:T(8,128)(2,1)S(1)} %big_gradient.3), channel_id=1, source_target_pairs={{0,4},{4,0},{8,12},{12,8},{16,20},{20,16},{24,28},{28,24},{32,36},... | collective-permute-start | bytes 3145736 | tf_op jit(solution)/shard_map/ppermute | solution.py:534
  146.4 2.9 %collective-permute-start.13 = (f32[24,1024]{1,0:T(8,128)S(1)}, f32[24,1024]{1,0:T(8,128)S(1)}, u32[]{:S(2)}, u32[]{:S(2)}) collective-permute-start(f32[24,1024]{1,0:T(8,128)S(1)} %get-tuple-element.84.small), channel_id=1, source_target_pairs={{0,4},{4,0},{8,12},{12,8},{16,20},{20,16},{24,28},{28,24},{32,36},... | collective-permute-start | bytes 294920 | tf_op jit(solution)/shard_map/ppermute | solution.py:534
  181.5 2.1 %collective-permute-start.14 = (f32[16,256]{1,0:T(8,128)S(1)}, f32[16,256]{1,0:T(8,128)S(1)}, u32[]{:S(2)}, u32[]{:S(2)}) collective-permute-start(f32[16,256]{1,0:T(8,128)S(1)} %get-tuple-element.86.a), channel_id=1, source_target_pairs={{0,4},{4,0},{8,12},{12,8},{16,20},{20,16},{24,28},{28,24},{32,36},... | collective-permute-start | bytes 49160 | tf_op jit(solution)/shard_map/ppermute | solution.py:534

commit v15 on v13

--- a/solution.py
+++ b/solution.py
@@ -259,7 +259,7 @@
     def live_of(slot):
         return jnp.where(lax.rem(slot, 2) < counts[lax.div(slot, 2)], 1.0, 0.0)
 
-    @pl.loop(0, nblocks, unroll=8)
+    @pl.loop(0, nblocks, unroll=16)
     def _(b):
         rows, weights = [], []
         for t in range(per):
@@ -280,7 +280,7 @@
     dlog_out[...] = field[pl.ds(me[0] * mine, mine)]
     sums[...] = jnp.zeros_like(sums)
 
-    @pl.loop(0, nblocks, unroll=8)
+    @pl.loop(0, nblocks, unroll=16)
     def _(b):
         back = dot(grad_b[b], jnp.concatenate([tiles[b, t] for t in range(per)], 1), NN)
         for t in range(per):
@@ -436,7 +436,7 @@
 
 
 def join(side, a, b, small, other):
-    steps = 4
+    steps = 2
     lead, nfeat, rows, width = a.shape
     more = small.shape[0] - 8
     spec = lambda n: pl.BlockSpec((lead // steps, nfeat, n, width), lambda g, s: (g, 0, 0, 0))
@@ -450,7 +450,7 @@
             out_specs=spec(rows + more),
         ),
         out_shape=pltpu.HBM((lead, nfeat, rows + more, width), BF16),
-        compiler_params=params(8),
+        compiler_params=params(12),
         cost_estimate=cost(a.size, 4 * MIB),
         name="join",
     )(side, a, b, small, other)
@@ -477,7 +477,7 @@
 
 def total(arrived, rows):
     n, full, width = arrived.shape
-    step = n // 8
+    step = n // 4
     shapes = [(rows, width), (full - rows, width)]
     return pl.pallas_call(
         total_kernel,

time: 185 us -> 184 us (level)
  no operation moved by 1% of the time
where the time goes in v15:
time: 184 us; the launch traced here: 183 us
  blocking collectives  55.9 us (30%)
  waiting for transfers between devices  46.5 us (25%)
  Pallas kernels  38.2 us (21%)
  starting transfers between devices  37.1 us (20%)
  local copies, waits for them, and re-layouts  4.67 us (3%)
    ppermute x12, waiting for transfers between devices, ahead(): return lax.ppermute(x, 'feat', [(i, (i + k) % nfeat) for i in range(nfeat)])  38 us
    all_to_all x1, blocking collectives, shards(): lax.all_to_all(big.reshape(parts // 2 * nfeat, *big.shape[2:]), ('nodes',...  29.2 us
    all_to_all x2, blocking collectives, swap(): lax.all_to_all(shaped, 'nodes', split_axis=0, concat_axis=0, tiled=True)  26.6 us
    ppermute x12, starting transfers between devices, ahead(): return lax.ppermute(x, 'feat', [(i, (i + k) % nfeat) for i in range(nfeat)])  18.2 us
    all_to_all x2, starting transfers between devices, swap(): lax.all_to_all(shaped, 'nodes', split_axis=0, concat_axis=0, tiled=True)  17.1 us
    pallas_call x3, Pallas kernels, aggregate(): pl.pallas_call(functools.partial(agg_kernel, which, chunk, nfeat), grid_s...  10.7 us
    all_to_all x2, waiting for transfers between devices, swap(): lax.all_to_all(shaped, 'nodes', split_axis=0, concat_axis=0, tiled=True)  7.7 us
    pallas_call x2, Pallas kernels, pick(): pl.pallas_call(functools.partial(pick_kernel, chunk), grid_spec=pltpu.Pre...  6.54 us
  transfers between devices with their start and end apart: 17, of which 12 were waited for; matrix products, arithmetic and copies ran while one was open for 0% of the time, Pallas kernels for 8%

profile of v15, /device:TPU:1, one launch (start us, length us, event | category | flops | bytes accessed | tf_op | source)
XLA Modules:
  0.0 183.4 jit_solution(1492425012229490380)
XLA Ops:
  0.6 0.8 copy.15
  1.4 0.6 reshape.58.table
  2.0 3.3 %pick.3 = bf16[64,128,128]{2,1,0:T(8,128)(2,1)} custom-call(s32[64]{0:T(128)} %reshape.58.table, bf16[4096,256]{1,0:T(8,128)(2,1)} %features.9), custom_call_target="tpu_custom_call" | custom-call | bytes 4194304 | tf_op jit(solution)/shard_map/pick/pallas_call | solution.py:52
  5.3 0.0 copy-start.13
  5.3 0.0 copy-start.10
  5.3 0.0 copy-start.11
  5.3 9.8 %all-to-all-start = ((bf16[32,2,128,128]{3,2,1,0:T(8,128)(2,1)}), bf16[32,2,128,128]{3,2,1,0:T(8,128)(2,1)}, u32[]{:S(2)}, u32[]{:S(2)}) async-start(bf16[32,2,128,128]{3,2,1,0:T(8,128)(2,1)} %bitcast.31), calls=%async_computation | async-start | bytes 4194304 | tf_op jit(solution)/shard_map/all_to_all | solution.py:544
  15.2 0.2 copy.16
  15.5 2.8 %collective-permute-start = (bf16[1056,256]{1,0:T(8,128)(2,1)S(1)}, bf16[1056,256]{1,0:T(8,128)(2,1)}, u32[]{:S(2)}, u32[]{:S(2)}) collective-permute-start(bf16[1056,256]{1,0:T(8,128)(2,1)S(1)} %pad_maximum_fusion.refs_0_), channel_id=1, source_target_pairs={{0,2},{1,3},{2,0},{3,1},{4,6},{5,7},{6,4},{7,5},{8,10},{9,11},{10,... | collective-permute-start | bytes 1622024 | tf_op jit(solution)/shard_map/ppermute | solution.py:537
  18.3 0.3 collective-permute-start.1
  18.6 2.4 %collective-permute-start.2 = (bf16[1056,256]{1,0:T(8,128)(2,1)S(1)}, bf16[1056,256]{1,0:T(8,128)(2,1)}, u32[]{:S(2)}, u32[]{:S(2)}) collective-permute-start(bf16[1056,256]{1,0:T(8,128)(2,1)S(1)} %pad_maximum_fusion.refs_0_), channel_id=1, source_target_pairs={{0,3},{1,0},{2,1},{3,2},{4,7},{5,4},{6,5},{7,6},{8,11},{9,8},{10,9... | collective-permute-start | bytes 1622024 | tf_op jit(solution)/shard_map/ppermute | solution.py:537
  21.0 3.3 %pick.2 = bf16[64,128,128]{2,1,0:T(8,128)(2,1)} custom-call(s32[64]{0:T(128)} %reshape.58.table, bf16[4096,256]{1,0:T(8,128)(2,1)} %features.9), custom_call_target="tpu_custom_call" | custom-call | bytes 4194304 | tf_op jit(solution)/shard_map/pick/pallas_call | solution.py:52
  24.3 6.5 %collective-permute-done.refs_1_ = bf16[1056,256]{1,0:T(8,128)(2,1)} collective-permute-done((bf16[1056,256]{1,0:T(8,128)(2,1)S(1)}, bf16[1056,256]{1,0:T(8,128)(2,1)}, u32[]{:S(2)}, u32[]{:S(2)}) %collective-permute-start) | collective-permute-done | bytes 540704 | tf_op jit(solution)/shard_map/ppermute | solution.py:537
  30.8 12.2 %collective-permute-done.1.refs_2_ = bf16[1056,256]{1,0:T(8,128)(2,1)} collective-permute-done((bf16[1056,256]{1,0:T(8,128)(2,1)S(1)}, bf16[1056,256]{1,0:T(8,128)(2,1)}, u32[]{:S(2)}, u32[]{:S(2)}) %collective-permute-start.1) | collective-permute-done | bytes 540704 | tf_op jit(solution)/shard_map/ppermute | solution.py:537
  43.0 0.0 collective-permute-done.2.refs_3_
  43.0 0.5 all-to-all-done
  43.5 7.3 %all-to-all-start.1 = ((bf16[32,2,128,128]{3,2,1,0:T(8,128)(2,1)}), bf16[32,2,128,128]{3,2,1,0:T(8,128)(2,1)S(1)}, u32[]{:S(2)}, u32[]{:S(2)}) async-start(bf16[32,2,128,128]{3,2,1,0:T(8,128)(2,1)} %bitcast.30), calls=%async_computation.1 | async-start | bytes 4194304 | tf_op jit(solution)/shard_map/all_to_all | solution.py:544
  50.8 0.1 copy.17
  50.9 0.1 reshape.62.src
  51.0 5.1 %aggregate.3 = (bf16[1024,128]{1,0:T(8,128)(2,1)}, bf16[1024,128]{1,0:T(8,128)(2,1)}, bf16[1024,128]{1,0:T(8,128)(2,1)}, bf16[1024,128]{1,0:T(8,128)(2,1)S(1)}) custom-call(s32[128]{0:T(128)S(1)} %reshape.62.src, s32[32]{0:T(128)S(1)} %bitcast.26, s32[1]{0:T(128)} %bitcast.6.me, bf16[64,128,128]{2,1,0:T(8,128)(2,1)} %bitcast.3.arrived, ...), custom_call_target="tpu_custom_call" | custom-call | flops 536870912 | bytes 8388608 | tf_op jit(solution)/shard_map/aggregate/pallas_call | solution.py:115
  56.1 1.8 %collective-permute-start.3 = (bf16[1024,128]{1,0:T(8,128)(2,1)}, bf16[1024,128]{1,0:T(8,128)(2,1)S(1)}, u32[]{:S(2)}, u32[]{:S(2)}) collective-permute-start(bf16[1024,128]{1,0:T(8,128)(2,1)} %get-tuple-element.61), channel_id=1, source_target_pairs={{0,2},{1,3},{2,0},{3,1},{4,6},{5,7},{6,4},{7,5},{8,10},{9,11},{10,... | collective-permute-start | bytes 786440 | tf_op jit(solution)/shard_map/ppermute | solution.py:537
  58.0 1.2 collective-permute-start.4
  59.1 1.5 collective-permute-start.5
  60.6 2.0 %assemble.1 = (bf16[1024,1024]{1,0:T(8,128)(2,1)S(1)}, bf16[16,1024]{1,0:T(8,128)(2,1)S(1)}, bf16[1024,16]{1,0:T(8,128)(2,1)S(1)}, f32[1024,1]{1,0:T(8,128)S(1)}) custom-call(s32[1]{0:T(128)} %bitcast.6.me, bf16[1056,256]{1,0:T(8,128)(2,1)S(1)} %pad_maximum_fusion.refs_0_, bf16[1056,256]{1,0:T(8,128)(2,1)} %collective-permute-done.refs_1_, ...), custom_call_target="tpu_custom_call" | custom-call | bytes 5242880 | tf_op jit(solution)/shard_map/assemble/pallas_call | solution.py:159
  62.7 0.7 copy-done.1
  63.4 1.3 copy-done.6
  64.7 0.8 copy-done.8
  65.5 0.1 collective-permute-done.3.refs_1_
  65.6 6.2 %collective-permute-done.4.refs_2_ = bf16[1024,128]{1,0:T(8,128)(2,1)} collective-permute-done((bf16[1024,128]{1,0:T(8,128)(2,1)}, bf16[1024,128]{1,0:T(8,128)(2,1)}, u32[]{:S(2)}, u32[]{:S(2)}) %collective-permute-start.4) | collective-permute-done | bytes 262176 | tf_op jit(solution)/shard_map/ppermute | solution.py:537
  71.9 0.0 collective-permute-done.5.refs_3_
  71.9 7.2 %all-to-all-done.1 = bf16[32,2,128,128]{3,2,1,0:T(8,128)(2,1)S(1)} async-done(((bf16[32,2,128,128]{3,2,1,0:T(8,128)(2,1)}), bf16[32,2,128,128]{3,2,1,0:T(8,128)(2,1)S(1)}, u32[]{:S(2)}, u32[]{:S(2)}) %all-to-all-start.1) | async-done | bytes 2097184 | tf_op jit(solution)/shard_map/all_to_all | solution.py:544
  79.1 3.3 %aggregate.5 = (bf16[1024,128]{1,0:T(8,128)(2,1)S(1)}, bf16[1024,128]{1,0:T(8,128)(2,1)S(1)}, bf16[1024,128]{1,0:T(8,128)(2,1)S(1)}) custom-call(s32[128]{0:T(128)S(1)} %reshape.62.src, s32[32]{0:T(128)S(1)} %bitcast.27, s32[1]{0:T(128)} %bitcast.6.me, bf16[64,128,128]{2,1,0:T(8,128)(2,1)S(1)} %bitcast.19, bf16[32,4,128,128]{3,2,1,0:T(8,128)(2,1)} %tiles.1, ...), custom_call_target="tpu_custom_call" | custom-call | flops 402653184 | bytes 8388608 | tf_op jit(solution)/shard_map/aggregate/pallas_call | solution.py:115
  82.3 1.8 %collective-permute-start.6 = (bf16[1024,128]{1,0:T(8,128)(2,1)S(1)}, bf16[1024,128]{1,0:T(8,128)(2,1)S(1)}, u32[]{:S(2)}, u32[]{:S(2)}) collective-permute-start(bf16[1024,128]{1,0:T(8,128)(2,1)S(1)} %get-tuple-element.69), channel_id=1, source_target_pairs={{0,2},{1,3},{2,0},{3,1},{4,6},{5,7},{6,4},{7,5},{8,10},{9,11},{10,... | collective-permute-start | bytes 786440 | tf_op jit(solution)/shard_map/ppermute | solution.py:537
  84.2 1.2 collective-permute-start.7
  85.3 1.5 collective-permute-start.8
  86.9 2.3 %aggregate.4.refs_4_ = bf16[1024,128]{1,0:T(8,128)(2,1)S(1)} custom-call(s32[128]{0:T(128)S(1)} %reshape.62.src, s32[32]{0:T(128)S(1)} %bitcast.28, s32[1]{0:T(128)} %bitcast.6.me, bf16[64,128,128]{2,1,0:T(8,128)(2,1)S(1)} %bitcast.20, bf16[32,4,128,128]{3,2,1,0:T(8,128)(2,1)} %tiles.1, bf16[4096,256]{1,0:T(8,128)(2,1)} %features.9), custom_call_target="tpu_custom_call" | custom-call | flops 134217728 | bytes 8388608 | tf_op jit(solution)/shard_map/aggregate/pallas_call | solution.py:115
  89.2 0.0 copy-start.4
  89.2 0.0 copy-start.3
  89.2 1.7 collective-permute-done.6.refs_5_
  90.9 6.8 %collective-permute-done.7.refs_6_ = bf16[1024,128]{1,0:T(8,128)(2,1)S(1)} collective-permute-done((bf16[1024,128]{1,0:T(8,128)(2,1)S(1)}, bf16[1024,128]{1,0:T(8,128)(2,1)S(1)}, u32[]{:S(2)}, u32[]{:S(2)}) %collective-permute-start.7) | collective-permute-done | bytes 262176 | tf_op jit(solution)/shard_map/ppermute | solution.py:537
  97.8 0.0 copy-start
  97.8 4.0 %dense.1 = (bf16[1024,1024]{1,0:T(8,128)(2,1)S(1)}, f32[8,16,128]{2,1,0:T(8,128)S(1)}) custom-call(bf16[1024,128]{1,0:T(8,128)(2,1)S(1)} %get-tuple-element.64.refs_0_, bf16[1024,128]{1,0:T(8,128)(2,1)S(1)} %collective-permute-done.3.refs_1_, bf16[1024,128]{1,0:T(8,128)(2,1)} %collective-permute-done.4.refs_2_, ...), custom_call_target="tpu_custom_call" | custom-call | flops 2147483648 | bytes 7340032 | tf_op jit(solution)/shard_map/dense/pallas_call | solution.py:196
  101.8 1.8 collective-permute-start.10
  103.6 1.8 collective-permute-start.11
  105.4 0.0 collective-permute-start.9
  105.4 1.1 collective-permute-done.10.p2
  106.5 1.3 collective-permute-done.11.p3
  107.7 2.0 %collective-permute-done.9.p1 = f32[8,16,128]{2,1,0:T(8,128)S(1)} collective-permute-done((f32[8,16,128]{2,1,0:T(8,128)S(1)}, f32[8,16,128]{2,1,0:T(8,128)S(1)}, u32[]{:S(2)}, u32[]{:S(2)}) %collective-permute-start.9) | collective-permute-done | bytes 65568 | tf_op jit(solution)/shard_map/ppermute | solution.py:537
  109.8 0.7 spread.1
  110.4 14.2 %all_to_all.25 = bf16[32,2,16,128]{3,2,1,0:T(8,128)(2,1)S(1)} all-to-all(bf16[32,2,16,128]{3,2,1,0:T(8,128)(2,1)S(1)} %bitcast.23), channel_id=1, replica_groups=mesh['nodes'=32,'feat'=4] {'nodes'}, dimensions={0} | all-to-all | bytes 524288 | tf_op jit(solution)/shard_map/all_to_all | solution.py:544
  124.6 2.9 %logits.1 = (f32[8,16,128]{2,1,0:T(8,128)S(1)}, bf16[64,16,128]{2,1,0:T(8,128)(2,1)S(1)}) custom-call(s32[128]{0:T(128)S(1)} %reshape.62.src, s32[32]{0:T(128)S(1)} %bitcast.29, s32[1]{0:T(128)} %bitcast.6.me, bf16[64,16,128]{2,1,0:T(8,128)(2,1)S(1)} %bitcast.22, f32[32,16,128]{2,1,0:T(8,128)S(1)} %get-tuple-element.77.own, s32[32,1,128]{2,1,0:T(1,128)S(1)} %bitcast.25, ...), custom_call_target="tpu_custom_call" | custom-call | flops 268435456 | bytes 6291456 | tf_op jit(solution)/shard_map/logits/pallas_call | solution.py:297
  127.6 12.5 %all_to_all.26 = bf16[32,2,16,128]{3,2,1,0:T(8,128)(2,1)S(1)} all-to-all(bf16[32,2,16,128]{3,2,1,0:T(8,128)(2,1)S(1)} %bitcast.24), channel_id=1, replica_groups=mesh['nodes'=32,'feat'=4] {'nodes'}, dimensions={0} | all-to-all | bytes 524288 | tf_op jit(solution)/shard_map/all_to_all | solution.py:544
  140.0 3.2 %small_gradients.1 = (bf16[1024,1024]{1,0:T(8,128)(2,1)}, f32[24,1024]{1,0:T(8,128)S(1)}) custom-call(s32[64]{0:T(128)S(1)} %copy-done.4, s32[1]{0:T(128)} %bitcast.6.me, bf16[64,16,128]{2,1,0:T(8,128)(2,1)S(1)} %bitcast.21, f32[8,16,128]{2,1,0:T(8,128)S(1)} %get-tuple-element.79.dlog, bf16[1024,1024]{1,0:T(8,128)(2,1)S(1)} %get-tuple-element.80.hidden, ...), custom_call_target="tpu_custom_call" | custom-call | flops 536870912 | bytes 4194304 | tf_op jit(solution)/shard_map/small_gradients/pallas_call | solution.py:355
  143.3 2.6 %big_gradient.3 = bf16[16,4,32,256]{3,2,1,0:T(8,128)(2,1)S(1)} custom-call(s32[1]{0:T(128)} %bitcast.6.me, s32[1]{0:T(128)S(6)} %sub.12.side, bf16[16,2,32,1024]{3,2,1,0:T(8,128)(2,1)} %bitcast.32, bf16[1024,128]{1,0:T(8,128)(2,1)S(1)} %get-tuple-element.64.refs_0_, bf16[1024,128]{1,0:T(8,128)(2,1)S(1)} %collective-permute-done.3.refs_1_, ...), custom_call_target="tpu_custom_call" | custom-call | flops 1073741824 | bytes 4194304 | tf_op jit(solution)/shard_map/big_gradient/pallas_call | solution.py:401
  145.9 0.3 collective-permute-start.12
  146.1 0.3 collective-permute-start.13
  146.4 2.6 %big_gradient.2.a = bf16[16,4,32,256]{3,2,1,0:T(8,128)(2,1)S(1)} custom-call(s32[1]{0:T(128)} %bitcast.6.me, s32[1]{0:T(128)} %bitcast.4.side, bf16[16,2,32,1024]{3,2,1,0:T(8,128)(2,1)} %bitcast.33, bf16[1024,128]{1,0:T(8,128)(2,1)S(1)} %get-tuple-element.64.refs_0_, bf16[1024,128]{1,0:T(8,128)(2,1)S(1)} %collective-permute-done.3.refs_1_, ...), custom_call_target="tpu_custom_call" | custom-call | flops 1073741824 | bytes 4194304 | tf_op jit(solution)/shard_map/big_gradient/pallas_call | solution.py:401
  149.1 0.0 collective-permute-done.12.b
  149.1 1.4 join.1
  150.4 29.2 %all_to_all.27.arrived = bf16[64,48,256]{2,1,0:T(8,128)(2,1)S(1)} all-to-all(bf16[64,48,256]{2,1,0:T(8,128)(2,1)} %bitcast.34), channel_id=1, replica_groups={{0,1,2,3,8,9,10,11,16,17,18,19,24,25,26,27,32,33,34,35,40,41,42,43,48,4..., dimensions={0} | all-to-all | bytes 3145728 | tf_op jit(solution)/shard_map/all_to_all | solution.py:586
  179.7 0.9 total.1
  180.6 1.3 collective-permute-start.14
  181.9 0.8 collective-permute-done.14.b
  182.7 0.6 finish.1
  (27 shorter events, 0.1 us)
Async XLA Ops:
  5.3 9.8 %copy-start.13 = (f32[256]{0:T(256)S(1)}, f32[256]{0:T(256)}, u32[]{:S(2)}) copy-start(f32[256]{0:T(256)} %param.16) | copy-start | bytes 3076
  5.3 9.9 %copy-start.10 = (bf16[256,1024]{1,0:T(8,128)(2,1)S(1)}, bf16[256,1024]{1,0:T(8,128)(2,1)}, u32[]{:S(2)}) copy-start(bf16[256,1024]{1,0:T(8,128)(2,1)} %param.15) | copy-start | bytes 1572868
  5.3 10.1 %copy-start.11 = (bf16[256,16]{0,1:T(8,128)(2,1)S(1)}, bf16[256,16]{0,1:T(8,128)(2,1)}, u32[]{:S(2)}) copy-start(bf16[256,16]{0,1:T(8,128)(2,1)} %param.17) | copy-start | bytes 24580
  5.3 38.2 %all-to-all-start = ((bf16[32,2,128,128]{3,2,1,0:T(8,128)(2,1)}), bf16[32,2,128,128]{3,2,1,0:T(8,128)(2,1)}, u32[]{:S(2)}, u32[]{:S(2)}) async-start(bf16[32,2,128,128]{3,2,1,0:T(8,128)(2,1)} %bitcast.31), calls=%async_computation | async-start | bytes 4194304 | tf_op jit(solution)/shard_map/all_to_all | solution.py:544
  15.5 15.3 %collective-permute-start = (bf16[1056,256]{1,0:T(8,128)(2,1)S(1)}, bf16[1056,256]{1,0:T(8,128)(2,1)}, u32[]{:S(2)}, u32[]{:S(2)}) collective-permute-start(bf16[1056,256]{1,0:T(8,128)(2,1)S(1)} %pad_maximum_fusion.refs_0_), channel_id=1, source_target_pairs={{0,2},{1,3},{2,0},{3,1},{4,6},{5,7},{6,4},{7,5},{8,10},{9,11},{10,... | collective-permute-start | bytes 1622024 | tf_op jit(solution)/shard_map/ppermute | solution.py:537
  18.3 24.6 %collective-permute-start.1 = (bf16[1056,256]{1,0:T(8,128)(2,1)S(1)}, bf16[1056,256]{1,0:T(8,128)(2,1)}, u32[]{:S(2)}, u32[]{:S(2)}) collective-permute-start(bf16[1056,256]{1,0:T(8,128)(2,1)S(1)} %pad_maximum_fusion.refs_0_), channel_id=1, source_target_pairs={{0,1},{1,2},{2,3},{3,0},{4,5},{5,6},{6,7},{7,4},{8,9},{9,10},{10,1... | collective-permute-start | bytes 1622024 | tf_op jit(solution)/shard_map/ppermute | solution.py:537
  18.6 24.3 %collective-permute-start.2 = (bf16[1056,256]{1,0:T(8,128)(2,1)S(1)}, bf16[1056,256]{1,0:T(8,128)(2,1)}, u32[]{:S(2)}, u32[]{:S(2)}) collective-permute-start(bf16[1056,256]{1,0:T(8,128)(2,1)S(1)} %pad_maximum_fusion.refs_0_), channel_id=1, source_target_pairs={{0,3},{1,0},{2,1},{3,2},{4,7},{5,4},{6,5},{7,6},{8,11},{9,8},{10,9... | collective-permute-start | bytes 1622024 | tf_op jit(solution)/shard_map/ppermute | solution.py:537
  43.5 7.3 %copy-start.12 = (s32[32,4]{0,1:T(4,128)S(1)}, s32[32,4]{0,1:T(4,128)}, u32[]{:S(2)}) copy-start(s32[32,4]{0,1:T(4,128)} %param.12) | copy-start | bytes 1540
  43.5 7.5 %copy-start.5 = (s32[1,32]{1,0:T(1,128)S(1)}, s32[1,32]{1,0:T(1,128)}, u32[]{:S(2)}) copy-start(s32[1,32]{1,0:T(1,128)} %param.10) | copy-start | bytes 388
  43.5 35.6 %all-to-all-start.1 = ((bf16[32,2,128,128]{3,2,1,0:T(8,128)(2,1)}), bf16[32,2,128,128]{3,2,1,0:T(8,128)(2,1)S(1)}, u32[]{:S(2)}, u32[]{:S(2)}) async-start(bf16[32,2,128,128]{3,2,1,0:T(8,128)(2,1)} %bitcast.30), calls=%async_computation.1 | async-start | bytes 4194304 | tf_op jit(solution)/shard_map/all_to_all | solution.py:544
  56.1 9.5 %collective-permute-start.3 = (bf16[1024,128]{1,0:T(8,128)(2,1)}, bf16[1024,128]{1,0:T(8,128)(2,1)S(1)}, u32[]{:S(2)}, u32[]{:S(2)}) collective-permute-start(bf16[1024,128]{1,0:T(8,128)(2,1)} %get-tuple-element.61), channel_id=1, source_target_pairs={{0,2},{1,3},{2,0},{3,1},{4,6},{5,7},{6,4},{7,5},{8,10},{9,11},{10,... | collective-permute-start | bytes 786440 | tf_op jit(solution)/shard_map/ppermute | solution.py:537
  58.0 13.9 %collective-permute-start.4 = (bf16[1024,128]{1,0:T(8,128)(2,1)}, bf16[1024,128]{1,0:T(8,128)(2,1)}, u32[]{:S(2)}, u32[]{:S(2)}) collective-permute-start(bf16[1024,128]{1,0:T(8,128)(2,1)} %get-tuple-element.62), channel_id=1, source_target_pairs={{0,1},{1,2},{2,3},{3,0},{4,5},{5,6},{6,7},{7,4},{8,9},{9,10},{10,1... | collective-permute-start | bytes 786440 | tf_op jit(solution)/shard_map/ppermute | solution.py:537
  59.1 12.8 %collective-permute-start.5 = (bf16[1024,128]{1,0:T(8,128)(2,1)}, bf16[1024,128]{1,0:T(8,128)(2,1)}, u32[]{:S(2)}, u32[]{:S(2)}) collective-permute-start(bf16[1024,128]{1,0:T(8,128)(2,1)} %get-tuple-element.63), channel_id=1, source_target_pairs={{0,3},{1,0},{2,1},{3,2},{4,7},{5,4},{6,5},{7,6},{8,11},{9,8},{10,9... | collective-permute-start | bytes 786440 | tf_op jit(solution)/shard_map/ppermute | solution.py:537
  62.7 0.7 copy-start.1
  63.4 1.3 copy-start.6
  64.7 0.8 copy-start.8
  82.3 8.6 %collective-permute-start.6 = (bf16[1024,128]{1,0:T(8,128)(2,1)S(1)}, bf16[1024,128]{1,0:T(8,128)(2,1)S(1)}, u32[]{:S(2)}, u32[]{:S(2)}) collective-permute-start(bf16[1024,128]{1,0:T(8,128)(2,1)S(1)} %get-tuple-element.69), channel_id=1, source_target_pairs={{0,2},{1,3},{2,0},{3,1},{4,6},{5,7},{6,4},{7,5},{8,10},{9,11},{10,... | collective-permute-start | bytes 786440 | tf_op jit(solution)/shard_map/ppermute | solution.py:537
  84.2 13.6 %collective-permute-start.7 = (bf16[1024,128]{1,0:T(8,128)(2,1)S(1)}, bf16[1024,128]{1,0:T(8,128)(2,1)S(1)}, u32[]{:S(2)}, u32[]{:S(2)}) collective-permute-start(bf16[1024,128]{1,0:T(8,128)(2,1)S(1)} %get-tuple-element.70), channel_id=1, source_target_pairs={{0,1},{1,2},{2,3},{3,0},{4,5},{5,6},{6,7},{7,4},{8,9},{9,10},{10,1... | collective-permute-start | bytes 786440 | tf_op jit(solution)/shard_map/ppermute | solution.py:537
  85.3 12.4 %copy-start.7 = (bf16[1024,1024]{1,0:T(8,128)(2,1)S(1)}, bf16[1024,1024]{1,0:T(8,128)(2,1)}, u32[]{:S(2)}) copy-start(bf16[1024,1024]{1,0:T(8,128)(2,1)} %copy-done.6) | copy-start | bytes 6291460
  85.3 12.4 %copy-start.9 = (f32[1024,1]{1,0:T(8,128)S(1)}, f32[1024,1]{1,0:T(8,128)}, u32[]{:S(2)}) copy-start(f32[1024,1]{1,0:T(8,128)} %copy-done.8) | copy-start | bytes 12292
  85.3 12.4 %collective-permute-start.8 = (bf16[1024,128]{1,0:T(8,128)(2,1)S(1)}, bf16[1024,128]{1,0:T(8,128)(2,1)S(1)}, u32[]{:S(2)}, u32[]{:S(2)}) collective-permute-start(bf16[1024,128]{1,0:T(8,128)(2,1)S(1)} %get-tuple-element.71), channel_id=1, source_target_pairs={{0,3},{1,0},{2,1},{3,2},{4,7},{5,4},{6,5},{7,6},{8,11},{9,8},{10,9... | collective-permute-start | bytes 786440 | tf_op jit(solution)/shard_map/ppermute | solution.py:537
  89.2 20.6 %copy-start.4 = (s32[64]{0:T(128)S(1)}, s32[64]{0:T(128)}, u32[]{:S(2)}) copy-start(s32[64]{0:T(128)} %reshape.58.table) | copy-start | bytes 772
  89.2 35.4 %copy-start.3 = (s32[4096]{0:T(1024)S(1)}, s32[4096]{0:T(1024)}, u32[]{:S(2)}) copy-start(s32[4096]{0:T(1024)} %param.14) | copy-start | bytes 49156
  97.8 26.9 %copy-start = (bf16[32,4,128,128]{3,2,1,0:T(8,128)(2,1)S(1)}, bf16[32,4,128,128]{3,2,1,0:T(8,128)(2,1)}, u32[]{:S(2)}) copy-start(bf16[32,4,128,128]{3,2,1,0:T(8,128)(2,1)} %tiles.1) | copy-start | bytes 12582916
  101.8 4.7 %collective-permute-start.10 = (f32[8,16,128]{2,1,0:T(8,128)S(1)}, f32[8,16,128]{2,1,0:T(8,128)S(1)}, u32[]{:S(2)}, u32[]{:S(2)}) collective-permute-start(f32[8,16,128]{2,1,0:T(8,128)S(1)} %get-tuple-element.75.p0), channel_id=1, source_target_pairs={{0,2},{1,3},{2,0},{3,1},{4,6},{5,7},{6,4},{7,5},{8,10},{9,11},{10,... | collective-permute-start | bytes 196616 | tf_op jit(solution)/shard_map/ppermute | solution.py:537
  103.6 4.1 %collective-permute-start.11 = (f32[8,16,128]{2,1,0:T(8,128)S(1)}, f32[8,16,128]{2,1,0:T(8,128)S(1)}, u32[]{:S(2)}, u32[]{:S(2)}) collective-permute-start(f32[8,16,128]{2,1,0:T(8,128)S(1)} %get-tuple-element.75.p0), channel_id=1, source_target_pairs={{0,3},{1,0},{2,1},{3,2},{4,7},{5,4},{6,5},{7,6},{8,11},{9,8},{10,9... | collective-permute-start | bytes 196616 | tf_op jit(solution)/shard_map/ppermute | solution.py:537
  105.4 4.3 %collective-permute-start.9 = (f32[8,16,128]{2,1,0:T(8,128)S(1)}, f32[8,16,128]{2,1,0:T(8,128)S(1)}, u32[]{:S(2)}, u32[]{:S(2)}) collective-permute-start(f32[8,16,128]{2,1,0:T(8,128)S(1)} %get-tuple-element.75.p0), channel_id=1, source_target_pairs={{0,1},{1,2},{2,3},{3,0},{4,5},{5,6},{6,7},{7,4},{8,9},{9,10},{10,1... | collective-permute-start | bytes 196616 | tf_op jit(solution)/shard_map/ppermute | solution.py:537
  124.6 15.4 %copy-start.2 = (bf16[1024,16]{1,0:T(8,128)(2,1)S(1)}, bf16[1024,16]{1,0:T(8,128)(2,1)}, u32[]{:S(2)}) copy-start(bf16[1024,16]{1,0:T(8,128)(2,1)} %copy-done.1) | copy-start | bytes 98308
  145.9 3.2 %collective-permute-start.12 = (bf16[16,4,32,256]{3,2,1,0:T(8,128)(2,1)S(1)}, bf16[16,4,32,256]{3,2,1,0:T(8,128)(2,1)S(1)}, u32[]{:S(2)}, u32[]{:S(2)}) collective-permute-start(bf16[16,4,32,256]{3,2,1,0:T(8,128)(2,1)S(1)} %big_gradient.3), channel_id=1, source_target_pairs={{0,4},{4,0},{8,12},{12,8},{16,20},{20,16},{24,28},{28,24},{32,36},... | collective-permute-start | bytes 3145736 | tf_op jit(solution)/shard_map/ppermute | solution.py:540
  146.1 2.9 %collective-permute-start.13 = (f32[24,1024]{1,0:T(8,128)S(1)}, f32[24,1024]{1,0:T(8,128)S(1)}, u32[]{:S(2)}, u32[]{:S(2)}) collective-permute-start(f32[24,1024]{1,0:T(8,128)S(1)} %get-tuple-element.84.small), channel_id=1, source_target_pairs={{0,4},{4,0},{8,12},{12,8},{16,20},{20,16},{24,28},{28,24},{32,36},... | collective-permute-start | bytes 294920 | tf_op jit(solution)/shard_map/ppermute | solution.py:540
  180.6 2.2 %collective-permute-start.14 = (f32[16,256]{1,0:T(8,128)S(1)}, f32[16,256]{1,0:T(8,128)S(1)}, u32[]{:S(2)}, u32[]{:S(2)}) collective-permute-start(f32[16,256]{1,0:T(8,128)S(1)} %get-tuple-element.86.a), channel_id=1, source_target_pairs={{0,4},{4,0},{8,12},{12,8},{16,20},{20,16},{24,28},{28,24},{32,36},... | collective-permute-start | bytes 49160 | tf_op jit(solution)/shard_map/ppermute | solution.py:540
